TPU v7x, 32 devices: a whole 2x2x4 slice. The times are simulated.
32 devices in a mesh: row: 4 (over y, x), col: 8 (over z, core).
Axes of the slice: x: 2, y: 2, z: 4, core: 2. Of those that a mesh axis runs over, the one named last changes fastest.
Arguments:
- normals: float32 [12288, 12288], P('row', 'col'), may hold values from -1 to 4, as said below
- design: float32 [128, 12288], P('row', 'col'), may hold values from -0.5 to 0.5
- filter_blocks: float32 [2, 32, 32], replicated, may hold values from -4 to 4, as said below
- regular: float32 [12288], replicated, may hold values from 0.1 to 1
Outputs:
- factored: float32 [12288, 12288], P('row', 'col')
Inputs may be any that keep to these rules, and one draw needn't show every extreme that they name: normals is symmetric; each diagonal entry is at least 1 and each off-diagonal entry has magnitude at most 1 / 256. filter_blocks[0][i, j] = f[i - j] for i >= j and 0 above the diagonal; filter_blocks[1][i, j] = f[32 + i - j] for j >= i and 0 below; f holds the 33 taps of one causal filter with f[0] at least 1.
All inputs are finite; a program needn't handle non-finite values.
Results may differ from a plain program's by a relative error of at most 0.00007.
Values sent between devices are 32-bit elements; how exact they have to be, the bound alone decides.
No kernel may reach another device: no remote copies, remote signals or barrier semaphores. Data moves between devices by JAX's collectives and lax.ppermute only.
A program may use at most 128 MiB of HBM per device.

v0:
```python
import jax
import jax.numpy as jnp
from jax import lax
from jax.sharding import PartitionSpec as P

B = 256
P_SIZE = 32


def passed_along(value, axis, by):
    peers = lax.axis_size(axis)
    pairs = [(i, i + by) for i in range(peers) if 0 <= i + by < peers]
    return lax.ppermute(value, axis, pairs)


def broadcast(block, axis, holder):
    block = jnp.where(lax.axis_index(axis) == holder, block, jnp.zeros_like(block))
    return lax.psum(block, axis)


def contract_rows(left_side, right_side):
    return lax.dot_general(
        left_side,
        right_side,
        (((0,), (0,)), ((), ())),
        precision=lax.Precision.HIGHEST,
        preferred_element_type=jnp.float32,
    )


def body(normals, design, filter_blocks, regular):
    highest = lax.Precision.HIGHEST
    rows_here, cols_here = normals.shape
    obs_here = design.shape[0]
    row_index = lax.axis_index("row")
    col_index = lax.axis_index("col")
    tiles_per_row = lax.axis_size("col") // lax.axis_size("row")
    prior_rows = passed_along(design, "row", 1)
    blocks = design.reshape(obs_here // P_SIZE, P_SIZE, cols_here)
    before = jnp.concatenate([prior_rows[None], blocks[:-1]], axis=0)
    filtered = jnp.einsum("ij,bjc->bic", filter_blocks[0], blocks, precision=highest)
    filtered = filtered + jnp.einsum("ij,bjc->bic", filter_blocks[1], before, precision=highest)
    filtered = filtered.reshape(obs_here, cols_here)
    columns = lax.all_gather(filtered, "row", axis=0, tiled=True)
    pieces = [
        broadcast(columns, "col", row_index * tiles_per_row + offset)
        for offset in range(tiles_per_row)
    ]
    left_side = jnp.concatenate(pieces, axis=1)
    gram_tile = contract_rows(left_side, columns)
    row_pos = row_index * rows_here + jnp.arange(rows_here, dtype=jnp.int32)
    col_pos = col_index * cols_here + jnp.arange(cols_here, dtype=jnp.int32)
    reg_rows = lax.dynamic_slice_in_dim(regular, row_index * rows_here, rows_here)
    system = normals + gram_tile
    system = system + jnp.where(row_pos[:, None] == col_pos[None, :], reg_rows[:, None], 0.0)
    top_strip = broadcast(system[:B], "row", 0)
    corner = broadcast(top_strip[:, :B], "col", 0)
    factor = jnp.linalg.cholesky(corner)
    inverse = jax.scipy.linalg.solve_triangular(factor, jnp.eye(B, dtype=jnp.float32), lower=True)
    col_panel = lax.dot_general(
        top_strip,
        inverse,
        (((0,), (1,)), ((), ())),
        precision=highest,
        preferred_element_type=jnp.float32,
    )
    block_here = broadcast(system[:, :B], "col", 0)
    row_panel = jnp.dot(
        block_here, inverse.T, precision=highest, preferred_element_type=jnp.float32
    )
    update = lax.dot_general(
        row_panel,
        col_panel,
        (((1,), (1,)), ((), ())),
        precision=highest,
        preferred_element_type=jnp.float32,
    )
    trailing = system - update
    padded = jnp.pad(row_panel, ((0, 0), (0, cols_here - B)))
    return jnp.where(col_pos[None, :] < B, padded, trailing)


def solution(mesh):
    in_specs = (P("row", "col"), P("row", "col"), P(), P())
    out_specs = P("row", "col")
    return jax.shard_map(body, mesh=mesh, in_specs=in_specs, out_specs=out_specs, check_vma=False)
```

profile of v0, /device:TPU:0, one launch (start us, length us, event | category | flops | bytes accessed | tf_op | source)
XLA Modules:
  0.0 391.5 jit_solution(11564744289418291511)
XLA Ops:
  6.5 4.8 %collective-permute-start = (f32[32,1536]{1,0:T(8,128)}, f32[32,1536]{1,0:T(8,128)S(1)}, u32[]{:S(2)}, u32[]{:S(2)}) collective-permute-start(f32[32,1536]{1,0:T(8,128)} %param.5), channel_id=1, source_target_pairs={{0,8},{8,16},{16,24},{1,9},{9,17},{17,25},{2,10},{10,18},{18,26},{... | collective-permute-start | bytes 589832 | tf_op jit(solution)/shard_map/ppermute | solution.py:13
  12.7 3.2 collective-permute-done
  16.9 13.6 %all-gather = f32[1,128,1536]{2,1,0:T(8,128)S(1)} all-gather(f32[1,32,1536]{2,1,0:T(8,128)S(1)} %fusion), channel_id=2, replica_groups=mesh['row'=4,'col'=8] {'row'}, dimensions={1}, use_global_device_ids=true | all-gather | bytes 983040 | tf_op jit(solution)/shard_map/all_gather | solution.py:44
  30.5 1.3 bitcast_select_fusion.1
  31.9 18.7 %copy.5 = f32[3072,1536]{0,1:T(8,128)} copy(f32[3072,1536]{1,0:T(8,128)} %param.4) | data formatting | bytes 37748736 | tf_op args[0]
  51.3 42.9 %all-reduce.12.cloned.1.call-done = (f32[128,1536]{1,0:T(8,128)}, f32[128,1536]{1,0:T(8,128)}) async-done(((f32[128,1536]{1,0:T(8,128)}, f32[128,1536]{1,0:T(8,128)}), (f32[128,1536]{1,0:T(8,128)}, f32[128,1536]{1,0:T(8,128)})) %all-reduce.12.cloned.1.call-update) | async-done | bytes 1572880 | tf_op jit(solution)/shard_map/psum | solution.py:18
  94.2 20.0 %select_add_fusion = f32[3072,1536]{0,1:T(8,128)S(1)} fusion(f32[3072,1536]{0,1:T(8,128)} %copy.5, f32[3072]{0:T(1024)S(1)} %dynamic_slice.3, s32[3072]{0:T(1024)S(1)} %iota_add_fusion, s32[1536]{0:T(1024)S(1)} %iota_add_fusion.1, f32[128,1536]{1,0:T(8,128)} %get-tuple-element.27, f32[128,1536]{1,0:T(8,128)} %get-tuple-element.28, ...), kind=kOutput, calls=%fused_computation.3 | convolution fusion | flops 7267024896 | bytes 40138752 | tf_op jit(solution)/shard_map/dot_general | solution.py:22
  114.2 6.8 %copy-done = f32[3072,1536]{0,1:T(8,128)} copy-done((f32[3072,1536]{0,1:T(8,128)}, f32[3072,1536]{0,1:T(8,128)S(1)}, u32[]{:S(2)}) %copy-start) | copy-done | bytes 18874392
  121.0 1.4 slice_select_fusion.1
  122.7 3.9 %slice_select_fusion = f32[3072,256]{0,1:T(8,128)} fusion(f32[3072,1536]{0,1:T(8,128)} %copy-done, pred[]{:T(512)S(6)} %eq.31), kind=kLoop, calls=%fused_computation.4 | loop fusion | flops 786432 | bytes 6291457 | tf_op jit(solution)/shard_map/jit(_where)/select_n | solution.py:17
  126.6 56.3 %all-reduce.8.cloned.1.call-done = f32[256,1536]{0,1:T(8,128)} async-done(((f32[256,1536]{0,1:T(8,128)}), f32[256,1536]{0,1:T(8,128)}) %all-reduce.8.cloned.1.call-update) | async-done | bytes 1572880 | tf_op jit(solution)/shard_map/psum | solution.py:18
  182.9 1.7 slice_select_fusion.2
  184.7 82.9 %all-reduce.10.cloned.1.call-done = (f32[3072,256]{0,1:T(8,128)}, f32[256,256]{0,1:T(8,128)}) async-done(((f32[3072,256]{0,1:T(8,128)}, f32[256,256]{0,1:T(8,128)}), (f32[3072,256]{0,1:T(8,128)}, f32[256,256]{0,1:T(8,128)})) %all-reduce.10.cloned.1.call-update) | async-done | bytes 3407888 | tf_op jit(solution)/shard_map/psum | solution.py:18
  269.7 11.7 %cholesky.49 = f32[128,128]{1,0:T(8,128)S(1)} custom-call(f32[128,128]{1,0:T(8,128)S(1)} %cholesky.115), custom_call_target="Cholesky" | custom-call | tf_op jit(solution)/shard_map/jit(cholesky)/cholesky | solution.py:58
  281.5 9.8 %custom-call.15 = f32[1,128,128]{1,2,0:T(8,128)S(1)} custom-call(f32[1,128,128]{2,1,0:T(8,128)S(1)} %get-tuple-element.34), custom_call_target="InvertDiagBlocksLowerTriangular" | custom-call | tf_op jit(solution)/shard_map/jit(cholesky)/cholesky | solution.py:58
  291.9 11.7 %cholesky.103 = f32[128,128]{1,0:T(8,128)S(1)} custom-call(f32[128,128]{1,0:T(8,128)S(1)} %convolution_subtract_fusion.1), custom_call_target="Cholesky" | custom-call | tf_op jit(solution)/shard_map/jit(cholesky)/cholesky | solution.py:58
  305.8 4.2 %while.1 = (s32[]{:T(128)}, f32[256,256]{0,1:T(8,128)S(1)}, s32[2,2]{1,0:T(2,128)S(1)}, f32[2,128,128]{2,1,0:T(8,128)S(1)}, s32[]{:T(128)}) while((s32[]{:T(128)}, f32[256,256]{0,1:T(8,128)S(1)}, s32[2,2]{1,0:T(2,128)S(1)}, f32[2,128,128]{2,1,0:T(8,128)S(1)}, s32[]{:T(128)}) %tuple.23), condition=%wide.while_cond, body=%wide.while_body.sunk | while | flops 2 | bytes 393329 | solution.py:59
  306.6 1.3 dynamic-slice.7
  310.0 19.7 %custom-call.16 = f32[2,128,128]{1,2,0:T(8,128)S(1)} custom-call(f32[2,128,128]{2,1,0:T(8,128)S(1)} %get-tuple-element.12), custom_call_target="InvertDiagBlocksLowerTriangular" | custom-call | tf_op jit(solution)/shard_map/jit(_solve_triangular)/triangular_solve | solution.py:59
  330.6 7.0 %fusion.7 = f32[3072,256]{1,0:T(8,128)S(1)} fusion(f32[3072,256]{0,1:T(8,128)} %get-tuple-element.25, f32[128,256]{1,0:T(8,128)S(1)} %fusion.11, f32[128,256]{1,0:T(8,128)S(1)} %fusion.8), kind=kOutput, calls=%fused_computation.24 | convolution fusion | flops 2415984640 | bytes 6553600 | tf_op jit(solution)/shard_map/dot_general | solution.py:68
  337.6 2.4 copy.12
  339.9 3.0 fusion.6
  343.0 23.3 %subtract_select_fusion = f32[3072,1536]{0,1:T(8,128)} fusion(f32[3072,1536]{0,1:T(8,128)} %copy-done, f32[3072,256]{0,1:T(8,128)S(1)} %copy-done.1, f32[3072,256]{1,0:T(8,128)S(1)} %fusion.7, f32[1536,256]{1,0:T(8,128)S(1)} %fusion.6, pred[1536]{0:T(1024)(128)(4,1)S(1)} %broadcast_compare_fusion), kind=kOutput, calls=%fused_computation.2 | convolution fusion | flops 14504951808 | bytes 45614592 | tf_op jit(solution)/shard_map/dot_general | solution.py:71
  366.3 18.6 %copy.14 = f32[3072,1536]{1,0:T(8,128)} copy(f32[3072,1536]{0,1:T(8,128)} %subtract_select_fusion) | data formatting | bytes 37748736 | tf_op jit(solution)/shard_map/jit(_where)/select_n | solution.py:80
  (46 shorter events, 10.6 us)
Async XLA Ops:
  6.5 87.6 %all-reduce.12.cloned.1.call-start = ((), (), s32[]{:S(2)}) async-start(), calls=%async_computation.2 | async-start | bytes 3145728 | tf_op jit(solution)/shard_map/psum | solution.py:18
  6.5 9.3 %collective-permute-start = (f32[32,1536]{1,0:T(8,128)}, f32[32,1536]{1,0:T(8,128)S(1)}, u32[]{:S(2)}, u32[]{:S(2)}) collective-permute-start(f32[32,1536]{1,0:T(8,128)} %param.5), channel_id=1, source_target_pairs={{0,8},{8,16},{16,24},{1,9},{9,17},{17,25},{2,10},{10,18},{18,26},{... | collective-permute-start | bytes 589832 | tf_op jit(solution)/shard_map/ppermute | solution.py:13
  31.9 151.0 %all-reduce.8.cloned.1.call-start = ((), (), s32[]{:S(2)}) async-start(), calls=%async_computation | async-start | bytes 3145728 | tf_op jit(solution)/shard_map/psum | solution.py:18
  114.2 6.9 %copy-start = (f32[3072,1536]{0,1:T(8,128)}, f32[3072,1536]{0,1:T(8,128)S(1)}, u32[]{:S(2)}) copy-start(f32[3072,1536]{0,1:T(8,128)S(1)} %select_add_fusion) | copy-start | bytes 56623108
  122.4 145.1 %all-reduce.10.cloned.1.call-start = ((), (), s32[]{:S(2)}) async-start(), calls=%async_computation.1 | async-start | bytes 6815744 | tf_op jit(solution)/shard_map/psum | solution.py:18
  339.9 3.0 copy-start.1
Sparse Core Ops, SparseCore 0:
  32.0 62.1 all-reduce.11
  122.6 60.2 all-reduce.7
  185.5 82.0 all-reduce.9
where the time goes:
time: 392 us; the launch traced here: 391 us
  waiting for transfers between devices  185 us (47%)
  other arithmetic  63.1 us (16%)
  matrix products  56.9 us (15%)
  local copies, waits for them, and re-layouts  52.7 us (13%)
  between operations  14.5 us (4%)
  blocking collectives  13.6 us (3%)
  starting transfers between devices  5.11 us (1%)
    psum x3, waiting for transfers between devices, broadcast(): return lax.psum(block, axis)  182 us
    another operation x6, other arithmetic, body(): factor = jnp.linalg.cholesky(corner)  34 us
    unnamed x5, local copies, waits for them, and re-layouts  25.5 us
    dot_general x1, matrix products, body(): lax.dot_general(row_panel, col_panel, (((1,), (1,)), ((), ())), precision...  23.3 us
    dot_general x1, matrix products, contract_rows(): lax.dot_general(left_side, right_side, (((0,), (0,)), ((), ())), precisio...  20 us
    another operation x3, other arithmetic, body(): jax.scipy.linalg.solve_triangular(factor, jnp.eye(B, dtype=jnp.float32),...  19.7 us
    select_n x1, local copies, waits for them, and re-layouts, body(): return jnp.where(col_pos[None, :] < B, padded, trailing)  18.6 us
    all_gather x1, blocking collectives, body(): columns = lax.all_gather(filtered, 'row', axis=0, tiled=True)  13.6 us
  transfers between devices with their start and end apart: 4, of which 4 were waited for; matrix products, arithmetic and copies ran while one was open for 6% of the time, Pallas kernels for 0%

commit v1 on v0

v1 whole, which is shorter than its diff:
```python
import functools

import jax
import jax.numpy as jnp
from jax import lax
from jax.experimental import pallas as pl
from jax.experimental.pallas import tpu as pltpu
from jax.sharding import PartitionSpec as P

B = 256
P_SIZE = 32
STRIP = 32
CHUNKS = 4
HIGHEST = lax.Precision.HIGHEST


def exact_dot(left, right, left_dim, right_dim):
    return lax.dot_general(
        left,
        right,
        (((left_dim,), (right_dim,)), ((), ())),
        precision=HIGHEST,
        preferred_element_type=jnp.float32,
    )


def split(value):
    high = value.astype(jnp.bfloat16)
    low = (value - high.astype(jnp.float32)).astype(jnp.bfloat16)
    return high, low


def split_dot(left, right):
    left_high, left_low = split(left)
    right_high, right_low = split(right)
    wide = functools.partial(jnp.dot, preferred_element_type=jnp.float32)
    return wide(left_high, right_high) + (wide(left_high, right_low) + wide(left_low, right_high))


def corner_kernel(corner_ref, design_ref, filter_ref, regular_ref, inverse_ref, lead_ref, upper):
    first = exact_dot(filter_ref[...], design_ref[...], 1, 0)
    row_pos = lax.broadcasted_iota(jnp.int32, (B, B), 0)
    col_pos = lax.broadcasted_iota(jnp.int32, (B, B), 1)
    system = corner_ref[...] + exact_dot(first, first, 0, 0)
    system = system + jnp.where(row_pos == col_pos, regular_ref[...], 0.0)
    identity = jnp.where(row_pos == col_pos, 1.0, 0.0)
    sub = lax.broadcasted_iota(jnp.int32, (STRIP, 1), 0)
    half = B // 2
    for start in range(0, B, STRIP):
        rows = slice(start, start + STRIP)
        strip = jnp.concatenate([system[rows, :], identity[rows, :]], axis=1)
        if start:
            done = upper[:start, :]
            strip = strip - exact_dot(done[:, rows], done, 0, 0)
        low = 0 if start < half else half
        wide = 3 * half
        held = strip[:, low : low + wide]
        for j in range(STRIP):
            at = start + j - low
            pivot = held[j : j + 1, at : at + 1]
            coef = jnp.where(sub > j, held[:, at : at + 1] / pivot, 0.0)
            held = held - coef * held[j : j + 1, :]
        lane = lax.broadcasted_iota(jnp.int32, (STRIP, wide), 1)
        on_diag = lane == sub + (start - low)
        diag = jnp.sum(jnp.where(on_diag, held, 0.0), axis=1, keepdims=True)
        held = held / jnp.sqrt(diag)
        zero = jnp.zeros((STRIP, half), jnp.float32)
        parts = [held, zero] if low == 0 else [zero, held]
        upper[rows, :] = jnp.concatenate(parts, axis=1)
    inverse = upper[:, B:]
    inverse_ref[...] = inverse
    lead_ref[...] = exact_dot(first, inverse, 1, 1)


def corner_factor(corner, design, filter_matrix, regular):
    obs = design.shape[0]
    return pl.pallas_call(
        corner_kernel,
        out_shape=[
            jax.ShapeDtypeStruct((B, B), jnp.float32),
            jax.ShapeDtypeStruct((obs, B), jnp.float32),
        ],
        scratch_shapes=[pltpu.VMEM((B, 2 * B), jnp.float32)],
        compiler_params=pltpu.CompilerParams(vmem_limit_bytes=24 * 2**20),
        cost_estimate=pl.CostEstimate(flops=4 * 10**9, bytes_accessed=2**20, transcendentals=0),
        name="corner_factor",
    )(corner, design, filter_matrix, regular)


def tile_kernel(count, place_ref, *refs):
    normals_ref, mine_ref, theirs_ref = refs[:3]
    row_parts = refs[3 : 3 + count]
    col_parts = refs[3 + count : 3 + 2 * count]
    strip_refs = refs[3 + 2 * count : 5 + 2 * count]
    filter_ref, inverse_ref, lead_ref, regular_ref, lead_reg_ref = refs[5 + 2 * count : 10 + 2 * count]
    out_ref, right_side = refs[10 + 2 * count :]
    step = pl.program_id(0)
    per_half = pl.num_programs(0) // 2
    row_index, col_index = place_ref[0], place_ref[1]
    block, cols = out_ref.shape
    obs = filter_ref.shape[0]
    rows_here = block * pl.num_programs(0)
    inverse = inverse_ref[...]
    lead = lead_ref[...]

    @pl.when(step == 0)
    def _():
        design = jnp.concatenate([part[...] for part in col_parts], axis=0)
        filtered = split_dot(filter_ref[...], design)
        strip = jnp.concatenate([part[...] for part in strip_refs], axis=0)
        row_pos = lax.broadcasted_iota(jnp.int32, (B, cols), 0)
        col_pos = lax.broadcasted_iota(jnp.int32, (B, cols), 1) + col_index * cols
        strip = strip + jnp.where(row_pos == col_pos, regular_ref[...], 0.0)
        panel = split_dot(inverse, strip) + split_dot(lead.T, filtered)
        filtered_high, filtered_low = split(filtered)
        panel_high, panel_low = split(-panel)
        right_side[:obs, :] = filtered_high
        right_side[obs : 2 * obs, :] = filtered_low
        right_side[2 * obs : 2 * obs + B, :] = panel_high
        right_side[2 * obs + B : 2 * obs + 2 * B, :] = panel_low
        right_side[2 * obs + 2 * B : 2 * obs + 3 * B, :] = panel_high
        right_side[2 * obs + 3 * B :, :] = filtered_high

    own_core = lax.rem(col_index, 2)
    half_index = jnp.where(step < per_half, own_core, 1 - own_core)
    row_block = half_index * per_half + lax.rem(step, per_half)
    first_row = row_index * rows_here + row_block * block
    first_col = col_index * cols
    design = jnp.concatenate([part[...] for part in row_parts], axis=0)
    filtered = split_dot(filter_ref[...], design).T
    system = jnp.where(step < per_half, mine_ref[...], theirs_ref[...])
    row_pos = lax.broadcasted_iota(jnp.int32, (block, B), 0) + first_row
    col_pos = lax.broadcasted_iota(jnp.int32, (block, B), 1)
    system = system + jnp.where(row_pos == col_pos, lead_reg_ref[...], 0.0)
    panel = split_dot(system, inverse.T) + split_dot(filtered, lead)
    filtered_high, filtered_low = split(filtered)
    panel_high, panel_low = split(panel)
    left_side = jnp.concatenate(
        [filtered_high, filtered_high, panel_high, panel_high, panel_low, filtered_low], axis=1
    )
    out_ref[...] = normals_ref[...] + jnp.dot(
        left_side, right_side[...], preferred_element_type=jnp.float32
    )

    @pl.when((first_row < first_col + cols) & (first_col < first_row + block))
    def _():
        row_pos = lax.broadcasted_iota(jnp.int32, (block, cols), 0) + first_row
        col_pos = lax.broadcasted_iota(jnp.int32, (block, cols), 1) + first_col
        out_ref[...] = out_ref[...] + jnp.where(row_pos == col_pos, regular_ref[...], 0.0)

    @pl.when(col_index == 0)
    def _():
        out_ref[:, :B] = panel


def tile_update(place, normals, mine, theirs, row_parts, col_parts, strips, filter_matrix, inverse, lead, regular, lead_reg):
    rows, cols = normals.shape
    block = 256 if cols % 256 == 0 else 128
    per_half = rows // 2 // block
    count = len(row_parts)
    obs_here = row_parts[0].shape[0]
    obs = filter_matrix.shape[0]

    def row_block(i, place):
        own_core = lax.rem(place[1], 2)
        half_index = jnp.where(i < per_half, own_core, 1 - own_core)
        return half_index * per_half + lax.rem(i, per_half)

    def whole(array):
        return pl.BlockSpec(array.shape, lambda i, place: (0,) * array.ndim)

    tile_spec = pl.BlockSpec((block, cols), lambda i, place: (row_block(i, place), 0))
    in_specs = [
        tile_spec,
        pl.BlockSpec((block, B), lambda i, place: (jnp.minimum(i, per_half - 1), 0)),
        pl.BlockSpec((block, B), lambda i, place: (jnp.maximum(i - per_half, 0), 0)),
    ]
    in_specs += [pl.BlockSpec((obs_here, block), lambda i, place: (0, row_block(i, place)))] * count
    rest = [*col_parts, *strips, filter_matrix, inverse, lead, regular, lead_reg]
    in_specs += [whole(array) for array in rest]
    return pl.pallas_call(
        functools.partial(tile_kernel, count),
        grid_spec=pltpu.PrefetchScalarGridSpec(
            num_scalar_prefetch=1,
            grid=(2 * per_half,),
            in_specs=in_specs,
            out_specs=tile_spec,
            scratch_shapes=[pltpu.VMEM((3 * (obs + B), cols), jnp.bfloat16)],
        ),
        out_shape=jax.ShapeDtypeStruct((rows, cols), jnp.float32),
        compiler_params=pltpu.CompilerParams(vmem_limit_bytes=48 * 2**20),
        cost_estimate=pl.CostEstimate(
            flops=6 * rows * cols * (obs + B), bytes_accessed=8 * rows * cols, transcendentals=0
        ),
        name="tile_update",
    )(place, normals, mine, theirs, *row_parts, *rest)


def shifted(value, axis, by):
    peers = lax.axis_size(axis)
    return lax.ppermute(value, axis, [(i, (i + by) % peers) for i in range(peers)])


def spread(value, axis, bits):
    peers = lax.axis_size(axis)
    me = lax.axis_index(axis)
    reached = [0]
    for bit in bits:
        pairs = [(i, i | bit) for i in reached if i | bit < peers]
        got = lax.ppermute(value, axis, pairs)
        value = jnp.where((me & bit) != 0, got, value)
        reached += [to for _, to in pairs]
    return value


def filter_matrix_of(filter_blocks, sources):
    count = sources.shape[0]
    lag = jnp.arange(count, dtype=jnp.int32)[:, None] - sources[None, :]
    lag = lag[:, None, :, None]
    own = filter_blocks[0][None, :, None, :]
    prior = filter_blocks[1][None, :, None, :]
    blocks = jnp.where(lag == 0, own, jnp.where(lag == 1, prior, 0.0))
    return blocks.reshape(count * P_SIZE, count * P_SIZE)


def row_strip_halves(normals):
    rows = normals.shape[0]
    half = rows // 2
    peers = lax.axis_size("col")
    col_index = lax.axis_index("col")
    chips = peers // 2
    chip = col_index // 2
    own = normals[:, :B]
    second = lax.ppermute(own[half:], "col", [(0, 1)])
    source = jnp.where(col_index == 0, own[:half], second)
    size = half // CHUNKS
    along = [(c, c + 2) for c in range(peers - 2)]
    received = []
    for step in range(CHUNKS + chips - 2):
        send = received[-1] if received else source[:size]
        if 0 < step < CHUNKS:
            send = jnp.where(chip == 0, source[step * size : (step + 1) * size], send)
        received.append(lax.ppermute(send, "col", along))
    arrived = lax.dynamic_slice_in_dim(
        jnp.concatenate(received, axis=0), jnp.maximum(chip - 1, 0) * size, half, axis=0
    )
    mine = jnp.where(chip == 0, source, arrived)
    theirs = lax.ppermute(mine, "col", [(c, c ^ 1) for c in range(peers)])
    return mine, theirs


def body(normals, design, filter_blocks, regular):
    rows_here, cols_here = normals.shape
    obs_here = design.shape[0]
    row_peers = lax.axis_size("row")
    row_index = lax.axis_index("row")
    col_index = lax.axis_index("col")
    blocks_here = obs_here // P_SIZE

    at_first = col_index == 0
    time_block = jnp.arange(row_peers, dtype=jnp.int32)[:, None, None]
    lead_design = jnp.where((time_block == row_index) & at_first, design[None, :, :B], 0.0)
    lead_corner = jnp.where(at_first & (row_index == 0), normals[:B, :B], 0.0)
    lead = jnp.concatenate([lead_design.reshape(row_peers * obs_here, B), lead_corner], axis=0)
    lead = lax.psum(lead, ("row", "col"))
    obs = row_peers * obs_here

    col_parts = [design] + [shifted(design, "row", s) for s in range(1, row_peers)]
    time_rows = lax.all_gather(design, "col", axis=1, tiled=True)
    row_parts = []
    for s in range(row_peers):
        to = (row_index + s) % row_peers
        part = lax.dynamic_slice_in_dim(time_rows, to * rows_here, rows_here, axis=1)
        row_parts.append(shifted(part, "row", s) if s else part)

    bits = [1 << i for i in range((row_peers - 1).bit_length())]
    strips = [
        spread(normals[: B // 2], "row", bits),
        spread(normals[B // 2 : B], "row", bits[::-1]),
    ]
    mine, theirs = row_strip_halves(normals)

    positions = jnp.arange(obs // P_SIZE, dtype=jnp.int32)
    plain = filter_matrix_of(filter_blocks, positions)
    passed = positions // blocks_here
    order = ((row_index - passed) % row_peers) * blocks_here + positions % blocks_here
    arranged = filter_matrix_of(filter_blocks, order)
    lead_reg = regular[:B].reshape(1, B)
    inverse, lead_filtered = corner_factor(lead[obs:], lead[:obs], plain, lead_reg)
    own_reg = lax.dynamic_slice_in_dim(regular, col_index * cols_here, cols_here).reshape(1, cols_here)
    place = jnp.stack([row_index, col_index]).astype(jnp.int32)
    return tile_update(
        place, normals, mine, theirs, row_parts, col_parts, strips, arranged, inverse, lead_filtered, own_reg, lead_reg
    )


def solution(mesh):
    in_specs = (P("row", "col"), P("row", "col"), P(), P())
    out_specs = P("row", "col")
    return jax.shard_map(body, mesh=mesh, in_specs=in_specs, out_specs=out_specs, check_vma=False)
```

time: 392 us -> 292 us (0.74)
  matrix products: 56.9 us -> 0 us
  Pallas kernels: 0 us -> 53 us
  other arithmetic: 63.1 us -> 10.1 us
  starting transfers between devices: 5.11 us -> 56.3 us
  local copies, waits for them, and re-layouts: 52.7 us -> 10.4 us
  waiting for transfers between devices: 185 us -> 146 us
  blocking collectives: 13.6 us -> 0 us
    psum x3 -> x1, waiting for transfers between devices: 182 us -> 92.7 us  [body(): lead = lax.psum(lead, ('row', 'col'))]
    dot_general x6 -> x0, matrix products: 55.6 us -> none  [the longest x1 23.3 us: body(): lax.dot_general(row_panel, col_panel, (((1,), (1,)), ((), ())), precision...]
    another operation x9 -> x1, other arithmetic: 53.7 us -> 0.08 us  [body(): place = jnp.stack([row_index, col_index]).astype(jnp.int32)]
    pallas_call x0 -> x2, Pallas kernels: none -> 53 us  [the longest x1 28.4 us: tile_update(): pl.pallas_call(functools.partial(tile_kernel, count), grid_spec=pltpu.Pre...]
    ppermute x1 -> x18, starting transfers between devices: 4.84 us -> 56.3 us  [the longest x6 23.4 us: row_strip_halves(): received.append(lax.ppermute(send, 'col', along))]
    ppermute x1 -> x18, waiting for transfers between devices: 3.17 us -> 53.3 us  [the longest x6 28 us: row_strip_halves(): received.append(lax.ppermute(send, 'col', along))]
    unnamed x5 -> x10, local copies, waits for them, and re-layouts: 25.5 us -> 0.07 us
    select_n x1 -> x2, local copies, waits for them, and re-layouts: 18.6 us -> 0.32 us  [filter_matrix_of(): blocks = jnp.where(lag == 0, own, jnp.where(lag == 1, prior, 0.0))]
  transfers between devices with their start and end apart: 4 -> 20, of which waited for: 4 -> 8; matrix products, arithmetic and copies ran while one was open for 6% -> 6% of each run, Pallas kernels for 0% -> 8%
where the time goes in v1:
time: 292 us; the launch traced here: 291 us
  waiting for transfers between devices  146 us (50%)
  starting transfers between devices  56.3 us (19%)
  Pallas kernels  53 us (18%)
  between operations  15.3 us (5%)
  local copies, waits for them, and re-layouts  10.4 us (4%)
  other arithmetic  10.1 us (3%)
    psum x1, waiting for transfers between devices, body(): lead = lax.psum(lead, ('row', 'col'))  92.7 us
    pallas_call x1, Pallas kernels, tile_update(): pl.pallas_call(functools.partial(tile_kernel, count), grid_spec=pltpu.Pre...  28.4 us
    ppermute x6, waiting for transfers between devices, row_strip_halves(): received.append(lax.ppermute(send, 'col', along))  28 us
    pallas_call x1, Pallas kernels, corner_factor(): pl.pallas_call(corner_kernel, out_shape=[jax.ShapeDtypeStruct((B, B), jnp...  24.5 us
    ppermute x6, starting transfers between devices, row_strip_halves(): received.append(lax.ppermute(send, 'col', along))  23.4 us
    ppermute x6, starting transfers between devices, shifted(): lax.ppermute(value, axis, [(i, (i + by) % peers) for i in range(peers)])  17.2 us
    ppermute x4, starting transfers between devices, spread(): got = lax.ppermute(value, axis, pairs)  13.2 us
    ppermute x4, waiting for transfers between devices, spread(): got = lax.ppermute(value, axis, pairs)  13.1 us
  transfers between devices with their start and end apart: 20, of which 8 were waited for; matrix products, arithmetic and copies ran while one was open for 6% of the time, Pallas kernels for 8%

profile of v1, /device:TPU:0, one launch (start us, length us, event | category | flops | bytes accessed | tf_op | source)
XLA Modules:
  0.0 291.2 jit_solution(7971204817377074481)
XLA Ops:
  8.9 2.5 collective-permute-start
  11.4 2.9 collective-permute-done
  18.2 8.1 %collective-permute-done.1 = f32[384,256]{1,0:T(8,128)S(1)} collective-permute-done((f32[384,256]{1,0:T(8,128)S(1)}, f32[384,256]{1,0:T(8,128)S(1)}, u32[]{:S(2)}, u32[]{:S(2)}) %collective-permute-start.1) | collective-permute-done | bytes 393248 | tf_op jit(solution)/shard_map/ppermute | solution.py:243
  27.2 4.4 %collective-permute-start.2 = (f32[384,256]{1,0:T(8,128)S(1)}, f32[384,256]{1,0:T(8,128)S(1)}, u32[]{:S(2)}, u32[]{:S(2)}) collective-permute-start(f32[384,256]{1,0:T(8,128)S(1)} %get-tuple-element.21), channel_id=1, source_target_pairs={{0,2},{1,3},{2,4},{3,5},{4,6},{5,7},{8,10},{9,11},{10,12},{11,13},... | collective-permute-start | bytes 1179656 | tf_op jit(solution)/shard_map/ppermute | solution.py:243
  33.5 3.3 %collective-permute-start.13 = (f32[32,1536]{1,0:T(8,128)}, f32[32,1536]{1,0:T(8,128)S(1)}, u32[]{:S(2)}, u32[]{:S(2)}) collective-permute-start(f32[32,1536]{1,0:T(8,128)} %refs_7_.1), channel_id=1, source_target_pairs={{0,24},{8,0},{16,8},{24,16},{1,25},{9,1},{17,9},{25,17},{2,26},{10... | collective-permute-start | bytes 589832 | tf_op jit(solution)/shard_map/ppermute | solution.py:201
  37.4 2.8 collective-permute-done.2
  41.0 4.5 %collective-permute-start.3 = (f32[384,256]{1,0:T(8,128)S(1)}, f32[384,256]{1,0:T(8,128)S(1)}, u32[]{:S(2)}, u32[]{:S(2)}) collective-permute-start(f32[384,256]{1,0:T(8,128)S(1)} %get-tuple-element.19), channel_id=1, source_target_pairs={{0,2},{1,3},{2,4},{3,5},{4,6},{5,7},{8,10},{9,11},{10,12},{11,13},... | collective-permute-start | bytes 1179656 | tf_op jit(solution)/shard_map/ppermute | solution.py:243
  45.5 2.6 fusion.5
  48.1 4.3 %collective-permute-start.16 = (f32[128,1536]{1,0:T(8,128)}, f32[128,1536]{1,0:T(8,128)S(1)}, u32[]{:S(2)}, u32[]{:S(2)}) collective-permute-start(f32[128,1536]{1,0:T(8,128)} %get-tuple-element.11), channel_id=1, source_target_pairs={{0,16},{1,17},{2,18},{3,19},{4,20},{5,21},{6,22},{7,23}} | collective-permute-start | bytes 2359304 | tf_op jit(solution)/shard_map/ppermute | solution.py:210
  53.8 8.8 %collective-permute-done.3 = f32[384,256]{1,0:T(8,128)S(1)} collective-permute-done((f32[384,256]{1,0:T(8,128)S(1)}, f32[384,256]{1,0:T(8,128)S(1)}, u32[]{:S(2)}, u32[]{:S(2)}) %collective-permute-start.3) | collective-permute-done | bytes 393248 | tf_op jit(solution)/shard_map/ppermute | solution.py:243
  63.5 5.3 %collective-permute-start.4 = (f32[384,256]{1,0:T(8,128)S(1)}, f32[384,256]{1,0:T(8,128)S(1)}, u32[]{:S(2)}, u32[]{:S(2)}) collective-permute-start(f32[384,256]{1,0:T(8,128)S(1)} %get-tuple-element.17), channel_id=1, source_target_pairs={{0,2},{1,3},{2,4},{3,5},{4,6},{5,7},{8,10},{9,11},{10,12},{11,13},... | collective-permute-start | bytes 1179656 | tf_op jit(solution)/shard_map/ppermute | solution.py:243
  68.8 8.2 %collective-permute-done.4 = f32[384,256]{1,0:T(8,128)S(1)} collective-permute-done((f32[384,256]{1,0:T(8,128)S(1)}, f32[384,256]{1,0:T(8,128)S(1)}, u32[]{:S(2)}, u32[]{:S(2)}) %collective-permute-start.4) | collective-permute-done | bytes 393248 | tf_op jit(solution)/shard_map/ppermute | solution.py:243
  77.0 4.5 %collective-permute-start.5 = (f32[384,256]{1,0:T(8,128)S(1)}, f32[384,256]{1,0:T(8,128)S(1)}, u32[]{:S(2)}, u32[]{:S(2)}) collective-permute-start(f32[384,256]{1,0:T(8,128)S(1)} %collective-permute-done.4), channel_id=1, source_target_pairs={{0,2},{1,3},{2,4},{3,5},{4,6},{5,7},{8,10},{9,11},{10,12},{11,13},... | collective-permute-start | bytes 1179656 | tf_op jit(solution)/shard_map/ppermute | solution.py:243
  83.7 92.7 %all-reduce.2.cloned.1.call-done = f32[384,256]{1,0:T(8,128)} async-done(((f32[384,256]{1,0:T(8,128)}), f32[384,256]{1,0:T(8,128)}) %all-reduce.2.cloned.1.call-update) | async-done | bytes 393232 | tf_op jit(solution)/shard_map/psum | solution.py:265
  179.8 3.3 %collective-permute-start.6 = (f32[384,256]{1,0:T(8,128)S(1)}, f32[384,256]{1,0:T(8,128)S(1)}, u32[]{:S(2)}, u32[]{:S(2)}) collective-permute-start(f32[384,256]{1,0:T(8,128)S(1)} %collective-permute-done.5), channel_id=1, source_target_pairs={{0,2},{1,3},{2,4},{3,5},{4,6},{5,7},{8,10},{9,11},{10,12},{11,13},... | collective-permute-start | bytes 1179656 | tf_op jit(solution)/shard_map/ppermute | solution.py:243
  183.2 2.5 broadcast_select_fusion.2
  185.6 3.5 %collective-permute-start.17 = (f32[128,1536]{1,0:T(8,128)S(1)}, f32[128,1536]{1,0:T(8,128)S(1)}, u32[]{:S(2)}, u32[]{:S(2)}) collective-permute-start(f32[128,1536]{1,0:T(8,128)S(1)} %get-tuple-element.9), channel_id=1, source_target_pairs={{0,8},{16,24},{1,9},{17,25},{2,10},{18,26},{3,11},{19,27},{4,12},{... | collective-permute-start | bytes 2359304 | tf_op jit(solution)/shard_map/ppermute | solution.py:210
  189.6 24.5 %corner_factor.1 = (f32[256,256]{1,0:T(8,128)S(1)}, f32[128,256]{1,0:T(8,128)S(1)}) custom-call(f32[256,256]{1,0:T(8,128)S(1)} %slice.69.corner_ref, f32[128,256]{1,0:T(8,128)S(1)} %slice.70.design_ref, f32[128,128]{1,0:T(8,128)S(1)} %select_n.183.filter_ref, f32[1,256]{1,0:T(1,128)S(1)} %bitcast.9), custom_call_target="tpu_custom_call" | custom-call | flops 4000000000 | bytes 1048576 | tf_op jit(solution)/shard_map/corner_factor/pallas_call | solution.py:77
  214.1 4.0 %collective-permute-start.15 = (f32[128,1536]{1,0:T(8,128)}, f32[128,1536]{1,0:T(8,128)}, u32[]{:S(2)}, u32[]{:S(2)}) collective-permute-start(f32[128,1536]{1,0:T(8,128)} %get-tuple-element.10), channel_id=1, source_target_pairs={{0,16},{8,24},{1,17},{9,25},{2,18},{10,26},{3,19},{11,27},{4,20},{... | collective-permute-start | bytes 2359304 | tf_op jit(solution)/shard_map/ppermute | solution.py:210
  219.8 2.4 collective-permute-start.9
  222.3 13.1 %collective-permute-done.15 = f32[128,1536]{1,0:T(8,128)} collective-permute-done((f32[128,1536]{1,0:T(8,128)}, f32[128,1536]{1,0:T(8,128)}, u32[]{:S(2)}, u32[]{:S(2)}) %collective-permute-start.15) | collective-permute-done | bytes 786464 | tf_op jit(solution)/shard_map/ppermute | solution.py:210
  235.4 9.4 %collective-permute-start.8 = (f32[32,3072]{1,0:T(8,128)S(1)}, f32[32,3072]{1,0:T(8,128)S(1)}, u32[]{:S(2)}, u32[]{:S(2)}) collective-permute-start(f32[32,3072]{1,0:T(8,128)S(1)} %get-tuple-element.15), channel_id=1, source_target_pairs={{0,8},{8,16},{16,24},{24,0},{1,9},{9,17},{17,25},{25,1},{2,10},{10... | collective-permute-start | bytes 1179656 | tf_op jit(solution)/shard_map/ppermute | solution.py:201
  246.0 9.3 %collective-permute-done.8.refs_4_ = f32[32,3072]{1,0:T(8,128)S(1)} collective-permute-done((f32[32,3072]{1,0:T(8,128)S(1)}, f32[32,3072]{1,0:T(8,128)S(1)}, u32[]{:S(2)}, u32[]{:S(2)}) %collective-permute-start.8) | collective-permute-done | bytes 393248 | tf_op jit(solution)/shard_map/ppermute | solution.py:201
  255.3 28.4 %tile_update.1 = f32[3072,1536]{1,0:T(8,128)} custom-call(s32[2]{0:T(128)S(1)} %pad_add_fusion.place_ref, f32[3072,1536]{1,0:T(8,128)} %refs_0_.1, f32[1536,256]{1,0:T(8,128)S(1)} %dynamic-slice_select_fusion.refs_1_, f32[1536,256]{1,0:T(8,128)} %collective-permute-done.7.refs_2_, f32[32,3072]{1,0:T(8,128)S(1)} %get-tuple-element.16.refs_3_, ...), custom_call_target="tpu_custom_call" | custom-call | flops 10871635968 | bytes 37748736 | tf_op jit(solution)/shard_map/tile_update/pallas_call | solution.py:181
  (63 shorter events, 20.3 us)
Async XLA Ops:
  7.4 169.0 %all-reduce.2.cloned.1.call-start = ((), (), s32[]{:S(2)}) async-start(), calls=%async_computation.1 | async-start | bytes 786432 | tf_op jit(solution)/shard_map/psum | solution.py:265
  8.9 5.4 %collective-permute-start = (f32[1536,256]{1,0:T(8,128)S(1)}, f32[1536,256]{1,0:T(8,128)S(1)}, u32[]{:S(2)}, u32[]{:S(2)}) collective-permute-start(f32[1536,256]{1,0:T(8,128)S(1)} %slice.51), channel_id=1, source_target_pairs={{0,1},{8,9},{16,17},{24,25}} | collective-permute-start | bytes 4718600 | tf_op jit(solution)/shard_map/ppermute | solution.py:234
  15.9 46.8 %copy-start = (f32[1536,256]{1,0:T(8,128)}, f32[1536,256]{1,0:T(8,128)S(1)}, u32[]{:S(2)}) copy-start(f32[1536,256]{1,0:T(8,128)S(1)} %slice_select_fusion) | copy-start | bytes 4718596
  15.9 10.5 %collective-permute-start.1 = (f32[384,256]{1,0:T(8,128)S(1)}, f32[384,256]{1,0:T(8,128)S(1)}, u32[]{:S(2)}, u32[]{:S(2)}) collective-permute-start(f32[384,256]{1,0:T(8,128)S(1)} %slice.65), channel_id=1, source_target_pairs={{0,2},{1,3},{2,4},{3,5},{4,6},{5,7},{8,10},{9,11},{10,12},{11,13},... | collective-permute-start | bytes 1179656 | tf_op jit(solution)/shard_map/ppermute | solution.py:243
  27.2 13.0 %collective-permute-start.2 = (f32[384,256]{1,0:T(8,128)S(1)}, f32[384,256]{1,0:T(8,128)S(1)}, u32[]{:S(2)}, u32[]{:S(2)}) collective-permute-start(f32[384,256]{1,0:T(8,128)S(1)} %get-tuple-element.21), channel_id=1, source_target_pairs={{0,2},{1,3},{2,4},{3,5},{4,6},{5,7},{8,10},{9,11},{10,12},{11,13},... | collective-permute-start | bytes 1179656 | tf_op jit(solution)/shard_map/ppermute | solution.py:243
  33.4 184.8 %all-gather.2.cloned.1.call-start = ((), (), s32[]{:S(2)}) async-start(), calls=%async_computation | async-start | bytes 1769472 | tf_op jit(solution)/shard_map/all_gather | solution.py:269
  33.5 186.3 %collective-permute-start.13 = (f32[32,1536]{1,0:T(8,128)}, f32[32,1536]{1,0:T(8,128)S(1)}, u32[]{:S(2)}, u32[]{:S(2)}) collective-permute-start(f32[32,1536]{1,0:T(8,128)} %refs_7_.1), channel_id=1, source_target_pairs={{0,24},{8,0},{16,8},{24,16},{1,25},{9,1},{17,9},{25,17},{2,26},{10... | collective-permute-start | bytes 589832 | tf_op jit(solution)/shard_map/ppermute | solution.py:201
  36.8 183.0 %collective-permute-start.12 = (f32[32,1536]{1,0:T(8,128)}, f32[32,1536]{1,0:T(8,128)S(1)}, u32[]{:S(2)}, u32[]{:S(2)}) collective-permute-start(f32[32,1536]{1,0:T(8,128)} %refs_7_.1), channel_id=1, source_target_pairs={{0,16},{8,24},{16,0},{24,8},{1,17},{9,25},{17,1},{25,9},{2,18},{10... | collective-permute-start | bytes 589832 | tf_op jit(solution)/shard_map/ppermute | solution.py:201
  41.0 27.8 %copy-start.3 = (f32[2,32,32]{2,1,0:T(8,128)S(1)}, f32[2,32,32]{2,1,0:T(8,128)}, u32[]{:S(2)}) copy-start(f32[2,32,32]{2,1,0:T(8,128)} %param.6) | copy-start | bytes 24580
  41.0 21.7 %collective-permute-start.3 = (f32[384,256]{1,0:T(8,128)S(1)}, f32[384,256]{1,0:T(8,128)S(1)}, u32[]{:S(2)}, u32[]{:S(2)}) collective-permute-start(f32[384,256]{1,0:T(8,128)S(1)} %get-tuple-element.19), channel_id=1, source_target_pairs={{0,2},{1,3},{2,4},{3,5},{4,6},{5,7},{8,10},{9,11},{10,12},{11,13},... | collective-permute-start | bytes 1179656 | tf_op jit(solution)/shard_map/ppermute | solution.py:243
  48.1 130.1 %collective-permute-start.16 = (f32[128,1536]{1,0:T(8,128)}, f32[128,1536]{1,0:T(8,128)S(1)}, u32[]{:S(2)}, u32[]{:S(2)}) collective-permute-start(f32[128,1536]{1,0:T(8,128)} %get-tuple-element.11), channel_id=1, source_target_pairs={{0,16},{1,17},{2,18},{3,19},{4,20},{5,21},{6,22},{7,23}} | collective-permute-start | bytes 2359304 | tf_op jit(solution)/shard_map/ppermute | solution.py:210
  52.5 130.7 %collective-permute-start.14 = (f32[128,1536]{1,0:T(8,128)}, f32[128,1536]{1,0:T(8,128)S(1)}, u32[]{:S(2)}, u32[]{:S(2)}) collective-permute-start(f32[128,1536]{1,0:T(8,128)} %get-tuple-element.12), channel_id=1, source_target_pairs={{0,8},{1,9},{2,10},{3,11},{4,12},{5,13},{6,14},{7,15}} | collective-permute-start | bytes 2359304 | tf_op jit(solution)/shard_map/ppermute | solution.py:210
  63.5 13.6 %collective-permute-start.4 = (f32[384,256]{1,0:T(8,128)S(1)}, f32[384,256]{1,0:T(8,128)S(1)}, u32[]{:S(2)}, u32[]{:S(2)}) collective-permute-start(f32[384,256]{1,0:T(8,128)S(1)} %get-tuple-element.17), channel_id=1, source_target_pairs={{0,2},{1,3},{2,4},{3,5},{4,6},{5,7},{8,10},{9,11},{10,12},{11,13},... | collective-permute-start | bytes 1179656 | tf_op jit(solution)/shard_map/ppermute | solution.py:243
  77.0 102.8 %collective-permute-start.5 = (f32[384,256]{1,0:T(8,128)S(1)}, f32[384,256]{1,0:T(8,128)S(1)}, u32[]{:S(2)}, u32[]{:S(2)}) collective-permute-start(f32[384,256]{1,0:T(8,128)S(1)} %collective-permute-done.4), channel_id=1, source_target_pairs={{0,2},{1,3},{2,4},{3,5},{4,6},{5,7},{8,10},{9,11},{10,12},{11,13},... | collective-permute-start | bytes 1179656 | tf_op jit(solution)/shard_map/ppermute | solution.py:243
  178.3 10.9 %copy-start.2 = (f32[2304,256]{1,0:T(8,128)S(1)}, f32[2304,256]{1,0:T(8,128)}, u32[]{:S(2)}) copy-start(f32[2304,256]{1,0:T(8,128)} %get-tuple-element.18) | copy-start | bytes 7077892
  178.3 67.7 %collective-permute-start.11 = (f32[32,1536]{1,0:T(8,128)}, f32[32,1536]{1,0:T(8,128)S(1)}, u32[]{:S(2)}, u32[]{:S(2)}) collective-permute-start(f32[32,1536]{1,0:T(8,128)} %refs_7_.1), channel_id=1, source_target_pairs={{0,8},{8,16},{16,24},{24,0},{1,9},{9,17},{17,25},{25,1},{2,10},{10... | collective-permute-start | bytes 589832 | tf_op jit(solution)/shard_map/ppermute | solution.py:201
  179.8 9.4 %collective-permute-start.6 = (f32[384,256]{1,0:T(8,128)S(1)}, f32[384,256]{1,0:T(8,128)S(1)}, u32[]{:S(2)}, u32[]{:S(2)}) collective-permute-start(f32[384,256]{1,0:T(8,128)S(1)} %collective-permute-done.5), channel_id=1, source_target_pairs={{0,2},{1,3},{2,4},{3,5},{4,6},{5,7},{8,10},{9,11},{10,12},{11,13},... | collective-permute-start | bytes 1179656 | tf_op jit(solution)/shard_map/ppermute | solution.py:243
  185.6 3.7 %copy-start.1 = (f32[1536,256]{1,0:T(8,128)S(1)}, f32[1536,256]{1,0:T(8,128)}, u32[]{:S(2)}) copy-start(f32[1536,256]{1,0:T(8,128)} %copy-done) | copy-start | bytes 4718596
  185.6 28.5 %collective-permute-start.17 = (f32[128,1536]{1,0:T(8,128)S(1)}, f32[128,1536]{1,0:T(8,128)S(1)}, u32[]{:S(2)}, u32[]{:S(2)}) collective-permute-start(f32[128,1536]{1,0:T(8,128)S(1)} %get-tuple-element.9), channel_id=1, source_target_pairs={{0,8},{16,24},{1,9},{17,25},{2,10},{18,26},{3,11},{19,27},{4,12},{... | collective-permute-start | bytes 2359304 | tf_op jit(solution)/shard_map/ppermute | solution.py:210
  189.5 65.8 %collective-permute-start.7 = (f32[1536,256]{1,0:T(8,128)S(1)}, f32[1536,256]{1,0:T(8,128)}, u32[]{:S(2)}, u32[]{:S(2)}) collective-permute-start(f32[1536,256]{1,0:T(8,128)S(1)} %dynamic-slice_select_fusion.refs_1_), channel_id=1, source_target_pairs={{0,1},{1,0},{2,3},{3,2},{4,5},{5,4},{6,7},{7,6},{8,9},{9,8},{10,11... | collective-permute-start | bytes 4718600 | tf_op jit(solution)/shard_map/ppermute | solution.py:248
  214.1 21.2 %collective-permute-start.15 = (f32[128,1536]{1,0:T(8,128)}, f32[128,1536]{1,0:T(8,128)}, u32[]{:S(2)}, u32[]{:S(2)}) collective-permute-start(f32[128,1536]{1,0:T(8,128)} %get-tuple-element.10), channel_id=1, source_target_pairs={{0,16},{8,24},{1,17},{9,25},{2,18},{10,26},{3,19},{11,27},{4,20},{... | collective-permute-start | bytes 2359304 | tf_op jit(solution)/shard_map/ppermute | solution.py:210
  219.8 26.2 %collective-permute-start.10 = (f32[32,3072]{1,0:T(8,128)S(1)}, f32[32,3072]{1,0:T(8,128)S(1)}, u32[]{:S(2)}, u32[]{:S(2)}) collective-permute-start(f32[32,3072]{1,0:T(8,128)S(1)} %get-tuple-element.13), channel_id=1, source_target_pairs={{0,24},{8,0},{16,8},{24,16},{1,25},{9,1},{17,9},{25,17},{2,26},{10... | collective-permute-start | bytes 1179656 | tf_op jit(solution)/shard_map/ppermute | solution.py:201
  219.8 26.2 %collective-permute-start.9 = (f32[32,3072]{1,0:T(8,128)S(1)}, f32[32,3072]{1,0:T(8,128)S(1)}, u32[]{:S(2)}, u32[]{:S(2)}) collective-permute-start(f32[32,3072]{1,0:T(8,128)S(1)} %get-tuple-element.14), channel_id=1, source_target_pairs={{0,16},{8,24},{16,0},{24,8},{1,17},{9,25},{17,1},{25,9},{2,18},{10... | collective-permute-start | bytes 1179656 | tf_op jit(solution)/shard_map/ppermute | solution.py:201
  235.4 19.9 %collective-permute-start.8 = (f32[32,3072]{1,0:T(8,128)S(1)}, f32[32,3072]{1,0:T(8,128)S(1)}, u32[]{:S(2)}, u32[]{:S(2)}) collective-permute-start(f32[32,3072]{1,0:T(8,128)S(1)} %get-tuple-element.15), channel_id=1, source_target_pairs={{0,8},{8,16},{16,24},{24,0},{1,9},{9,17},{17,25},{25,1},{2,10},{10... | collective-permute-start | bytes 1179656 | tf_op jit(solution)/shard_map/ppermute | solution.py:201
Sparse Core Ops, SparseCore 0:
  33.6 142.7 all-reduce.1
Sparse Core Ops, SparseCore 1:
  37.4 27.0 all-gather.1

commit v2 on v1

v2 whole, which is shorter than its diff:
```python
import functools

import jax
import jax.numpy as jnp
from jax import lax
from jax.experimental import pallas as pl
from jax.experimental.pallas import tpu as pltpu
from jax.sharding import PartitionSpec as P

B = 256
P_SIZE = 32
STRIP = 32
HIGHEST = lax.Precision.HIGHEST


def exact_dot(left, right, left_dim, right_dim):
    return lax.dot_general(
        left,
        right,
        (((left_dim,), (right_dim,)), ((), ())),
        precision=HIGHEST,
        preferred_element_type=jnp.float32,
    )


def split(value):
    high = value.astype(jnp.bfloat16)
    low = (value - high.astype(jnp.float32)).astype(jnp.bfloat16)
    return high, low


def split_dot(left, right):
    left_high, left_low = split(left)
    right_high, right_low = split(right)
    wide = functools.partial(jnp.dot, preferred_element_type=jnp.float32)
    return wide(left_high, right_high) + (wide(left_high, right_low) + wide(left_low, right_high))


def corner_kernel(joined_ref, filter_ref, regular_ref, inverse_ref, lead_ref, upper):
    obs = filter_ref.shape[0]
    first = exact_dot(filter_ref[...], joined_ref[:obs, :], 1, 0)
    row_pos = lax.broadcasted_iota(jnp.int32, (B, B), 0)
    col_pos = lax.broadcasted_iota(jnp.int32, (B, B), 1)
    system = joined_ref[obs:, :] + exact_dot(first, first, 0, 0)
    system = system + jnp.where(row_pos == col_pos, regular_ref[...], 0.0)
    identity = jnp.where(row_pos == col_pos, 1.0, 0.0)
    sub = lax.broadcasted_iota(jnp.int32, (STRIP, 1), 0)
    half = B // 2
    for start in range(0, B, STRIP):
        rows = slice(start, start + STRIP)
        strip = jnp.concatenate([system[rows, :], identity[rows, :]], axis=1)
        if start:
            done = upper[:start, :]
            strip = strip - exact_dot(done[:, rows], done, 0, 0)
        low = 0 if start < half else half
        wide = 3 * half
        held = strip[:, low : low + wide]
        for j in range(STRIP):
            at = start + j - low
            pivot = held[j : j + 1, at : at + 1]
            coef = jnp.where(sub > j, held[:, at : at + 1] / pivot, 0.0)
            held = held - coef * held[j : j + 1, :]
        lane = lax.broadcasted_iota(jnp.int32, (STRIP, wide), 1)
        on_diag = lane == sub + (start - low)
        diag = jnp.sum(jnp.where(on_diag, held, 0.0), axis=1, keepdims=True)
        held = held / jnp.sqrt(diag)
        zero = jnp.zeros((STRIP, half), jnp.float32)
        parts = [held, zero] if low == 0 else [zero, held]
        upper[rows, :] = jnp.concatenate(parts, axis=1)
    inverse = upper[:, B:]
    inverse_ref[...] = inverse.T
    lead_ref[...] = exact_dot(first, inverse, 1, 1)


def corner_factor(joined, filter_matrix, regular):
    obs = filter_matrix.shape[0]
    return pl.pallas_call(
        corner_kernel,
        out_shape=[
            jax.ShapeDtypeStruct((B, B), jnp.float32),
            jax.ShapeDtypeStruct((obs, B), jnp.float32),
        ],
        scratch_shapes=[pltpu.VMEM((B, 2 * B), jnp.float32)],
        compiler_params=pltpu.CompilerParams(vmem_limit_bytes=24 * 2**20),
        cost_estimate=pl.CostEstimate(flops=4 * 10**9, bytes_accessed=2**20, transcendentals=0),
        name="corner_factor",
    )(joined, filter_matrix, regular)


def right_kernel(count, place_ref, *refs):
    col_parts = refs[:count]
    high_ref, low_ref, filter_ref, inverse_ref, lead_ref, regular_ref, out_ref = refs[count:]
    cols = out_ref.shape[1]
    obs = filter_ref.shape[0]
    design = jnp.concatenate([part[...] for part in col_parts], axis=0)
    filtered = split_dot(filter_ref[...], design)
    strip = jnp.concatenate([high_ref[...], low_ref[...]], axis=0)
    row_pos = lax.broadcasted_iota(jnp.int32, (B, cols), 0)
    col_pos = lax.broadcasted_iota(jnp.int32, (B, cols), 1) + place_ref[1] * cols
    strip = strip + jnp.where(row_pos == col_pos, regular_ref[...], 0.0)
    panel = split_dot(inverse_ref[...].T, strip) + split_dot(lead_ref[...].T, filtered)
    filtered_high, filtered_low = split(filtered)
    panel_high, panel_low = split(-panel)
    out_ref[:obs, :] = filtered_high
    out_ref[obs : 2 * obs, :] = filtered_low
    out_ref[2 * obs : 2 * obs + B, :] = panel_high
    out_ref[2 * obs + B : 2 * obs + 2 * B, :] = panel_low
    out_ref[2 * obs + 2 * B : 2 * obs + 3 * B, :] = panel_high
    out_ref[2 * obs + 3 * B :, :] = filtered_high


def right_side(place, col_parts, strips, filter_matrix, inverse, lead, regular):
    count = len(col_parts)
    cols = strips[0].shape[1]
    depth = 3 * (filter_matrix.shape[0] + B)
    specs = [pl.BlockSpec(memory_space=pltpu.SMEM)]
    specs += [pl.BlockSpec(memory_space=pltpu.VMEM)] * (count + 6)
    return pl.pallas_call(
        functools.partial(right_kernel, count),
        in_specs=specs,
        out_specs=pl.BlockSpec(memory_space=pltpu.VMEM),
        out_shape=jax.ShapeDtypeStruct((depth, cols), jnp.bfloat16),
        compiler_params=pltpu.CompilerParams(vmem_limit_bytes=32 * 2**20),
        cost_estimate=pl.CostEstimate(
            flops=3 * 2 * cols * B * depth // 3, bytes_accessed=4 * cols * depth, transcendentals=0
        ),
        name="right_side",
    )(place, *col_parts, *strips, filter_matrix, inverse, lead, regular)


def tile_kernel(of_own, place_ref, *refs):
    if not of_own:
        refs = refs[1:]
    normals_ref, strip_ref, design_ref, right_ref = refs[:4]
    filter_ref, inverse_ref, lead_ref, regular_ref, lead_reg_ref, out_ref, left_ref = refs[4:]
    step = pl.program_id(0)
    steps = pl.num_programs(0)
    row_index, col_index = place_ref[0], place_ref[1]
    block, cols = out_ref.shape
    half = steps * block
    obs = filter_ref.shape[0]
    own_core = lax.rem(col_index, 2)
    half_index = own_core if of_own else 1 - own_core
    half_row = (2 * row_index + half_index) * half
    first_row = half_row + step * block
    first_col = col_index * cols

    @pl.when(step == 0)
    def _():
        filtered = split_dot(filter_ref[...], design_ref[...]).T
        row_pos = lax.broadcasted_iota(jnp.int32, (half, B), 0) + half_row
        col_pos = lax.broadcasted_iota(jnp.int32, (half, B), 1)
        system = strip_ref[...] + jnp.where(row_pos == col_pos, lead_reg_ref[...], 0.0)
        panel = split_dot(system, inverse_ref[...]) + split_dot(filtered, lead_ref[...])
        filtered_high, filtered_low = split(filtered)
        panel_high, panel_low = split(panel)
        left_ref[:, :obs] = filtered_high
        left_ref[:, obs : 2 * obs] = filtered_high
        left_ref[:, 2 * obs : 2 * obs + B] = panel_high
        left_ref[:, 2 * obs + B : 2 * obs + 2 * B] = panel_high
        left_ref[:, 2 * obs + 2 * B : 2 * obs + 3 * B] = panel_low
        left_ref[:, 2 * obs + 3 * B :] = filtered_low

    rows = pl.ds(pl.multiple_of(step * block, block), block)
    out_ref[...] = normals_ref[...] + jnp.dot(
        left_ref[rows, :], right_ref[...], preferred_element_type=jnp.float32
    )

    @pl.when((first_row < first_col + cols) & (first_col < first_row + block))
    def _():
        row_pos = lax.broadcasted_iota(jnp.int32, (block, cols), 0) + first_row
        col_pos = lax.broadcasted_iota(jnp.int32, (block, cols), 1) + first_col
        out_ref[...] = out_ref[...] + jnp.where(row_pos == col_pos, regular_ref[...], 0.0)

    @pl.when(col_index == 0)
    def _():
        panel_high = left_ref[rows, 2 * obs : 2 * obs + B].astype(jnp.float32)
        panel_low = left_ref[rows, 2 * obs + 2 * B : 2 * obs + 3 * B].astype(jnp.float32)
        out_ref[:, :B] = panel_high + panel_low


def block_rows(half):
    return max(size for size in range(128, 513, 128) if half % size == 0)


def tile_half(place, before, normals, strip, design, right, filter_matrix, inverse, lead, regular, lead_reg):
    rows, cols = normals.shape
    half = rows // 2
    block = block_rows(half)
    steps = half // block
    depth = right.shape[0]
    of_own = before is None

    def tile_block(i, place):
        own_core = lax.rem(place[1], 2)
        half_index = own_core if of_own else 1 - own_core
        return half_index * steps + i, 0

    def whole(array):
        return pl.BlockSpec(array.shape, lambda i, place: (0,) * array.ndim)

    tile_spec = pl.BlockSpec((block, cols), tile_block)
    rest = [strip, design, right, filter_matrix, inverse, lead, regular, lead_reg]
    in_specs = [tile_spec] + [whole(array) for array in rest]
    operands = [normals, *rest]
    if not of_own:
        in_specs = [pl.BlockSpec(memory_space=pl.ANY)] + in_specs
        operands = [before] + operands
    return pl.pallas_call(
        functools.partial(tile_kernel, of_own),
        grid_spec=pltpu.PrefetchScalarGridSpec(
            num_scalar_prefetch=1,
            grid=(steps,),
            in_specs=in_specs,
            out_specs=tile_spec,
            scratch_shapes=[pltpu.VMEM((half, depth), jnp.bfloat16)],
        ),
        out_shape=jax.ShapeDtypeStruct((rows, cols), jnp.float32),
        input_output_aliases={} if of_own else {1: 0},
        compiler_params=pltpu.CompilerParams(vmem_limit_bytes=44 * 2**20),
        cost_estimate=pl.CostEstimate(
            flops=2 * half * cols * depth, bytes_accessed=8 * half * cols, transcendentals=0
        ),
        name="tile_own" if of_own else "tile_other",
    )(place, *operands)


def shifted(value, axis, by):
    peers = lax.axis_size(axis)
    return lax.ppermute(value, axis, [(i, (i + by) % peers) for i in range(peers)])


def spread(value, axis, bits):
    peers = lax.axis_size(axis)
    me = lax.axis_index(axis)
    reached = [0]
    for bit in bits:
        pairs = [(i, i | bit) for i in reached if i | bit < peers]
        got = lax.ppermute(value, axis, pairs)
        value = jnp.where((me & bit) != 0, got, value)
        reached += [to for _, to in pairs]
    return value


def filter_matrix_of(filter_blocks, sources):
    count = sources.shape[0]
    lag = jnp.arange(count, dtype=jnp.int32)[:, None] - sources[None, :]
    lag = lag[:, None, :, None]
    own = filter_blocks[0][None, :, None, :]
    prior = filter_blocks[1][None, :, None, :]
    blocks = jnp.where(lag == 0, own, jnp.where(lag == 1, prior, 0.0))
    return blocks.reshape(count * P_SIZE, count * P_SIZE)


def row_strip_piece(normals):
    peers = lax.axis_size("col")
    chips = peers // 2
    half = normals.shape[0] // 2
    size = half // chips
    arrived = None
    for c in reversed(range(1, peers)):
        first = (c % 2) * half + (c // 2) * size
        got = lax.ppermute(normals[first : first + size, :B], "col", [(0, c)])
        arrived = got if arrived is None else arrived + got
    return jnp.where(lax.axis_index("col") == 0, normals[:size, :B], arrived)


def other_core(value):
    return lax.ppermute(value, "col", [(c, c ^ 1) for c in range(lax.axis_size("col"))])


def leading_parts(normals, design):
    row_peers, col_peers = lax.axis_size("row"), lax.axis_size("col")
    row_index, col_index = lax.axis_index("row"), lax.axis_index("col")
    obs_here = design.shape[0]
    held = jnp.concatenate([design[:, :B], normals[:B, :B]], axis=0)
    reached = [0]
    for bit in reversed([1 << i for i in range(1, (col_peers - 1).bit_length())]):
        pairs = [(i, i | bit) for i in reached if i | bit < col_peers]
        got = lax.ppermute(held, "col", pairs)
        held = jnp.where((col_index & bit) != 0, got, held)
        reached += [to for _, to in pairs]
    times, block = [held[:obs_here]], held[obs_here:]
    for s in range(1, row_peers):
        pairs = [
            (i * col_peers + c, (i + s) % row_peers * col_peers + c)
            for i in range(row_peers)
            for c in range(0, col_peers, 2)
        ]
        got = lax.ppermute(held, ("row", "col"), pairs)
        times.append(got[:obs_here])
        block = jnp.where(row_index == s, got[obs_here:], block)
    held = jnp.concatenate([*times, block], axis=0)
    got = lax.ppermute(held, "col", [(c, c + 1) for c in range(0, col_peers, 2)])
    return jnp.where(col_index % 2 == 1, got, held)


def body(normals, design, filter_blocks, regular):
    rows_here, cols_here = normals.shape
    obs_here = design.shape[0]
    row_peers = lax.axis_size("row")
    row_index = lax.axis_index("row")
    col_peers = lax.axis_size("col")
    col_index = lax.axis_index("col")
    blocks_here = obs_here // P_SIZE
    obs = row_peers * obs_here
    cores = [list(range(k, col_peers, 2)) for k in range(2)]

    lead = leading_parts(normals, design)
    piece = row_strip_piece(normals)

    time_rows = lax.all_gather(design, "col", axis=1, tiled=True, axis_index_groups=cores)
    col_parts = [design] + [shifted(design, "row", s) for s in range(1, row_peers)]

    bits = [1 << i for i in range((row_peers - 1).bit_length())]
    strips = [
        spread(normals[: B // 2], "row", bits),
        spread(normals[B // 2 : B], "row", bits[::-1]),
    ]
    row_parts = []
    for s in range(row_peers):
        to = (row_index + s) % row_peers
        part = lax.dynamic_slice_in_dim(time_rows, to * cols_here, cols_here, axis=1)
        row_parts.append(shifted(part, "row", s) if s else part)
    own_design = jnp.concatenate(row_parts, axis=0)
    other_design = other_core(own_design)
    own_strip = lax.all_gather(piece, "col", axis=0, tiled=True, axis_index_groups=cores)
    other_strip = other_core(own_strip)

    positions = jnp.arange(obs // P_SIZE, dtype=jnp.int32)
    passed = positions // blocks_here
    order = ((row_index - passed) % row_peers) * blocks_here + positions % blocks_here
    filters = filter_matrix_of(filter_blocks, order)
    lead_reg = regular[:B].reshape(1, B)
    own_reg = lax.dynamic_slice_in_dim(regular, col_index * cols_here, cols_here).reshape(1, cols_here)
    place = jnp.stack([row_index, col_index]).astype(jnp.int32)
    inverse, lead_filtered = corner_factor(lead, filters, lead_reg)
    right = right_side(place, col_parts, strips, filters, inverse, lead_filtered, own_reg)
    shared = [right, filters, inverse, lead_filtered, own_reg, lead_reg]
    out = tile_half(place, None, normals, own_strip, own_design, *shared)
    return tile_half(place, out, normals, other_strip, other_design, *shared)


def solution(mesh):
    in_specs = (P("row", "col"), P("row", "col"), P(), P())
    out_specs = P("row", "col")
    return jax.shard_map(body, mesh=mesh, in_specs=in_specs, out_specs=out_specs, check_vma=False)
```

time: 292 us -> 187 us (0.64)
  waiting for transfers between devices: 146 us -> 18.7 us
  blocking collectives: 0 us -> 22.1 us
  other arithmetic: 10.1 us -> 7.15 us
    psum x1 -> x0, waiting for transfers between devices: 92.7 us -> none  [body(): lead = lax.psum(lead, ('row', 'col'))]
    all_gather x0 -> x1, blocking collectives: none -> 22.1 us  [body(): lax.all_gather(design, 'col', axis=1, tiled=True, axis_index_groups=cores)]
    ppermute x4, waiting for transfers between devices: 13.1 us -> 0.01 us  [spread(): got = lax.ppermute(value, axis, pairs)]
    ppermute x8 -> x15, waiting for transfers between devices: 30.9 us -> 18.4 us  [the longest x3 18.4 us: leading_parts(): got = lax.ppermute(held, ('row', 'col'), pairs)]
    ppermute x8 -> x15, starting transfers between devices: 25.9 us -> 36.5 us  [the longest x7 17.4 us: row_strip_piece(): got = lax.ppermute(normals[first:first + size, :B], 'col', [(0, c)])]
    ppermute x6, starting transfers between devices: 17.2 us -> 7.61 us  [shifted(): lax.ppermute(value, axis, [(i, (i + by) % peers) for i in range(peers)])]
    ppermute x6, waiting for transfers between devices: 9.27 us -> 0.27 us  [shifted(): lax.ppermute(value, axis, [(i, (i + by) % peers) for i in range(peers)])]
    pallas_call x1 -> x3, Pallas kernels: 28.4 us -> 30.4 us  [the longest x2 27.9 us: tile_half(): pl.pallas_call(functools.partial(tile_kernel, of_own), grid_spec=pltpu.Pr...]
  transfers between devices with their start and end apart: 20 -> 26, of which waited for: 8 -> 3; matrix products, arithmetic and copies ran while one was open for 6% -> 9% of each run, Pallas kernels for 8% -> 22%
where the time goes in v2:
time: 187 us; the launch traced here: 186 us
  starting transfers between devices  56.7 us (30%)
  Pallas kernels  55 us (29%)
  blocking collectives  22.1 us (12%)
  waiting for transfers between devices  18.7 us (10%)
  between operations  13.7 us (7%)
  local copies, waits for them, and re-layouts  12.9 us (7%)
  other arithmetic  7.15 us (4%)
    pallas_call x2, Pallas kernels, tile_half(): pl.pallas_call(functools.partial(tile_kernel, of_own), grid_spec=pltpu.Pr...  27.9 us
    pallas_call x1, Pallas kernels, corner_factor(): pl.pallas_call(corner_kernel, out_shape=[jax.ShapeDtypeStruct((B, B), jnp...  24.5 us
    all_gather x1, blocking collectives, body(): lax.all_gather(design, 'col', axis=1, tiled=True, axis_index_groups=cores)  22.1 us
    ppermute x3, waiting for transfers between devices, leading_parts(): got = lax.ppermute(held, ('row', 'col'), pairs)  18.4 us
    ppermute x7, starting transfers between devices, row_strip_piece(): got = lax.ppermute(normals[first:first + size, :B], 'col', [(0, c)])  17.4 us
    ppermute x4, starting transfers between devices, spread(): got = lax.ppermute(value, axis, pairs)  12.6 us
    ppermute x2, starting transfers between devices, leading_parts(): got = lax.ppermute(held, 'col', pairs)  10.9 us
    ppermute x6, starting transfers between devices, shifted(): lax.ppermute(value, axis, [(i, (i + by) % peers) for i in range(peers)])  7.61 us
  transfers between devices with their start and end apart: 26, of which 3 were waited for; matrix products, arithmetic and copies ran while one was open for 9% of the time, Pallas kernels for 22%

profile of v2, /device:TPU:0, one launch (start us, length us, event | category | flops | bytes accessed | tf_op | source)
XLA Modules:
  0.0 186.2 jit_solution(6120105471979136416)
XLA Ops:
  8.4 6.7 %collective-permute-start.17 = (f32[288,256]{1,0:T(8,128)S(1)}, f32[288,256]{1,0:T(8,128)}, u32[]{:S(2)}, u32[]{:S(2)}) collective-permute-start(f32[288,256]{1,0:T(8,128)S(1)} %pad_maximum_fusion.1), channel_id=1, source_target_pairs={{0,4},{8,12},{16,20},{24,28}} | collective-permute-start | bytes 884744 | tf_op jit(solution)/shard_map/ppermute | solution.py:280
  15.0 3.3 %fusion.7 = (f32[384,256]{1,0:T(8,128)}, f32[384,256]{1,0:T(8,128)}, f32[384,256]{1,0:T(8,128)}, f32[384,256]{1,0:T(8,128)}, f32[384,256]{1,0:T(8,128)}, /*index=5*/f32[384,256]{1,0:T(8,128)}, f32[384,256]{1,0:T(8,128)}) fusion(f32[3072,1536]{1,0:T(8,128)} %refs_1_.1), kind=kLoop, calls=%fused_computation.34 | loop fusion | bytes 5505024 | tf_op jit(solution)/shard_map/slice | solution.py:263
  21.3 2.1 %collective-permute-start.5 = (f32[384,256]{1,0:T(8,128)}, f32[384,256]{1,0:T(8,128)}, u32[]{:S(2)}, u32[]{:S(2)}) collective-permute-start(f32[384,256]{1,0:T(8,128)} %get-tuple-element.15), channel_id=1, source_target_pairs={{0,2},{8,10},{16,18},{24,26}} | collective-permute-start | bytes 1179656 | tf_op jit(solution)/shard_map/ppermute | solution.py:263
  23.4 2.0 %collective-permute-start.4 = (f32[384,256]{1,0:T(8,128)}, f32[384,256]{1,0:T(8,128)}, u32[]{:S(2)}, u32[]{:S(2)}) collective-permute-start(f32[384,256]{1,0:T(8,128)} %get-tuple-element.16), channel_id=1, source_target_pairs={{0,3},{8,11},{16,19},{24,27}} | collective-permute-start | bytes 1179656 | tf_op jit(solution)/shard_map/ppermute | solution.py:263
  25.5 2.4 %fusion.6 = (f32[128,1536]{1,0:T(8,128)}, f32[128,1536]{1,0:T(8,128)S(1)}) fusion(f32[3072,1536]{1,0:T(8,128)} %refs_1_.1), kind=kLoop, calls=%fused_computation.33 | loop fusion | bytes 3145728 | tf_op jit(solution)/shard_map/slice | solution.py:318
  28.6 22.1 %all_gather.7 = f32[32,6144]{1,0:T(8,128)S(1)} all-gather(f32[32,1536]{1,0:T(8,128)} %refs_0_.2), channel_id=1, replica_groups={{0,2,4,6},{1,3,5,7},{8,10,12,14},{9,11,13,15},{16,18,20,22},{17,19,21,2..., dimensions={1}, use_global_device_ids=true | all-gather | bytes 983040 | tf_op jit(solution)/shard_map/all_gather | solution.py:312
  50.7 4.2 %collective-permute-start.18 = (f32[288,256]{1,0:T(8,128)S(1)}, f32[288,256]{1,0:T(8,128)}, u32[]{:S(2)}, u32[]{:S(2)}) collective-permute-start(f32[288,256]{1,0:T(8,128)S(1)} %broadcast_select_fusion.5), channel_id=1, source_target_pairs={{0,2},{4,6},{8,10},{12,14},{16,18},{20,22},{24,26},{28,30}} | collective-permute-start | bytes 884744 | tf_op jit(solution)/shard_map/ppermute | solution.py:280
  55.8 6.2 %collective-permute-start.3 = (f32[384,256]{1,0:T(8,128)}, f32[384,256]{1,0:T(8,128)}, u32[]{:S(2)}, u32[]{:S(2)}) collective-permute-start(f32[384,256]{1,0:T(8,128)} %get-tuple-element.17), channel_id=1, source_target_pairs={{0,4},{8,12},{16,20},{24,28}} | collective-permute-start | bytes 1179656 | tf_op jit(solution)/shard_map/ppermute | solution.py:263
  62.1 2.0 %collective-permute-start.2 = (f32[384,256]{1,0:T(8,128)}, f32[384,256]{1,0:T(8,128)}, u32[]{:S(2)}, u32[]{:S(2)}) collective-permute-start(f32[384,256]{1,0:T(8,128)} %get-tuple-element.18), channel_id=1, source_target_pairs={{0,5},{8,13},{16,21},{24,29}} | collective-permute-start | bytes 1179656 | tf_op jit(solution)/shard_map/ppermute | solution.py:263
  64.1 2.1 %collective-permute-start = (f32[384,256]{1,0:T(8,128)}, f32[384,256]{1,0:T(8,128)}, u32[]{:S(2)}, u32[]{:S(2)}) collective-permute-start(f32[384,256]{1,0:T(8,128)} %get-tuple-element.19), channel_id=1, source_target_pairs={{0,7},{8,15},{16,23},{24,31}} | collective-permute-start | bytes 1179656 | tf_op jit(solution)/shard_map/ppermute | solution.py:263
  68.1 2.5 %collective-permute-start.12 = (f32[32,1536]{1,0:T(8,128)}, f32[32,1536]{1,0:T(8,128)S(1)}, u32[]{:S(2)}, u32[]{:S(2)}) collective-permute-start(f32[32,1536]{1,0:T(8,128)} %refs_0_.2), channel_id=1, source_target_pairs={{0,24},{8,0},{16,8},{24,16},{1,25},{9,1},{17,9},{25,17},{2,26},{10... | collective-permute-start | bytes 589832 | tf_op jit(solution)/shard_map/ppermute | solution.py:230
  70.6 2.4 %collective-permute-start.15 = (f32[128,1536]{1,0:T(8,128)}, f32[128,1536]{1,0:T(8,128)S(1)}, u32[]{:S(2)}, u32[]{:S(2)}) collective-permute-start(f32[128,1536]{1,0:T(8,128)} %get-tuple-element.11), channel_id=1, source_target_pairs={{0,16},{1,17},{2,18},{3,19},{4,20},{5,21},{6,22},{7,23}} | collective-permute-start | bytes 2359304 | tf_op jit(solution)/shard_map/ppermute | solution.py:239
  76.4 2.8 %add_select_fusion = f32[384,256]{1,0:T(8,128)} fusion(f32[384,256]{1,0:T(8,128)} %copy-done.4, f32[384,256]{1,0:T(8,128)} %collective-permute-done.5, f32[384,256]{1,0:T(8,128)} %collective-permute-done.4, f32[384,256]{1,0:T(8,128)} %collective-permute-done.3, f32[384,256]{1,0:T(8,128)} %collective-permute-done.2, f32[384,256]{1,0:T(8,128)} %collective-permute-done, ...), kind=kLoop, calls=%fused_computation.1 | loop fusion | flops 688128 | bytes 3538945 | tf_op jit(solution)/shard_map/jit(_where)/select_n | solution.py:265
  79.2 2.4 %collective-permute-start.20 = (f32[288,256]{1,0:T(8,128)S(1)}, f32[288,256]{1,0:T(8,128)S(1)}, u32[]{:S(2)}, u32[]{:S(2)}) collective-permute-start(f32[288,256]{1,0:T(8,128)S(1)} %broadcast_select_fusion.6), channel_id=1, source_target_pairs={{0,16},{2,18},{4,20},{6,22},{8,24},{10,26},{12,28},{14,30},{16,0},... | collective-permute-start | bytes 884744 | tf_op jit(solution)/shard_map/ppermute | solution.py:290
  81.6 11.9 %collective-permute-done.19 = f32[288,256]{1,0:T(8,128)} collective-permute-done((f32[288,256]{1,0:T(8,128)S(1)}, f32[288,256]{1,0:T(8,128)}, u32[]{:S(2)}, u32[]{:S(2)}) %collective-permute-start.19) | collective-permute-done | bytes 294944 | tf_op jit(solution)/shard_map/ppermute | solution.py:290
  96.2 6.5 %collective-permute-done.21 = f32[288,256]{1,0:T(8,128)S(1)} collective-permute-done((f32[288,256]{1,0:T(8,128)S(1)}, f32[288,256]{1,0:T(8,128)S(1)}, u32[]{:S(2)}, u32[]{:S(2)}) %collective-permute-start.21) | collective-permute-done | bytes 294944 | tf_op jit(solution)/shard_map/ppermute | solution.py:290
  104.7 2.0 %collective-permute-start.7 = (f32[32,1536]{1,0:T(8,128)}, f32[32,1536]{1,0:T(8,128)S(1)}, u32[]{:S(2)}, u32[]{:S(2)}) collective-permute-start(f32[32,1536]{1,0:T(8,128)} %get-tuple-element.23), channel_id=1, source_target_pairs={{0,8},{8,16},{16,24},{24,0},{1,9},{9,17},{17,25},{25,1},{2,10},{10... | collective-permute-start | bytes 589832 | tf_op jit(solution)/shard_map/ppermute | solution.py:230
  109.6 2.1 %collective-permute-start.11 = (f32[32,1536]{1,0:T(8,128)S(1)}, f32[32,1536]{1,0:T(8,128)S(1)}, u32[]{:S(2)}, u32[]{:S(2)}) collective-permute-start(f32[32,1536]{1,0:T(8,128)S(1)} %copy-done.1), channel_id=1, source_target_pairs={{0,16},{8,24},{16,0},{24,8},{1,17},{9,25},{17,1},{25,9},{2,18},{10... | collective-permute-start | bytes 589832 | tf_op jit(solution)/shard_map/ppermute | solution.py:230
  112.0 4.0 %collective-permute-start.16 = (f32[128,1536]{1,0:T(8,128)S(1)}, f32[128,1536]{1,0:T(8,128)}, u32[]{:S(2)}, u32[]{:S(2)}) collective-permute-start(f32[128,1536]{1,0:T(8,128)S(1)} %get-tuple-element.9), channel_id=1, source_target_pairs={{0,8},{16,24},{1,9},{17,25},{2,10},{18,26},{3,11},{19,27},{4,12},{... | collective-permute-start | bytes 2359304 | tf_op jit(solution)/shard_map/ppermute | solution.py:239
  116.1 4.8 %collective-permute-start.14 = (f32[128,1536]{1,0:T(8,128)S(1)}, f32[128,1536]{1,0:T(8,128)}, u32[]{:S(2)}, u32[]{:S(2)}) collective-permute-start(f32[128,1536]{1,0:T(8,128)S(1)} %get-tuple-element.10), channel_id=1, source_target_pairs={{0,16},{8,24},{1,17},{9,25},{2,18},{10,26},{3,19},{11,27},{4,20},{... | collective-permute-start | bytes 2359304 | tf_op jit(solution)/shard_map/ppermute | solution.py:239
  120.9 24.5 %corner_factor.1 = (f32[256,256]{1,0:T(8,128)S(1)}, f32[128,256]{1,0:T(8,128)S(1)}) custom-call(f32[384,256]{1,0:T(8,128)S(1)} %broadcast_select_fusion.4.joined_ref, f32[128,128]{1,0:T(8,128)S(1)} %select_n.159.filter_ref.refs_6_.refs_4_.refs_5_, f32[1,256]{1,0:T(1,128)S(1)} %bitcast.7), custom_call_target="tpu_custom_call" | custom-call | flops 4000000000 | bytes 1048576 | tf_op jit(solution)/shard_map/corner_factor/pallas_call | solution.py:77
  147.5 2.5 %right_side.1.refs_3_.refs_4_ = bf16[1152,1536]{1,0:T(8,128)(2,1)S(1)} custom-call(s32[2]{0:T(128)S(1)} %pad_add_fusion.place_ref, f32[32,1536]{1,0:T(8,128)S(1)} %copy-done.1, f32[32,1536]{1,0:T(8,128)S(1)} %collective-permute-done.10.refs_1_, f32[32,1536]{1,0:T(8,128)S(1)} %collective-permute-done.11.refs_2_, ...), custom_call_target="tpu_custom_call" | custom-call | flops 905969664 | bytes 7077888 | tf_op jit(solution)/shard_map/right_side/pallas_call | solution.py:118
  151.4 14.4 %tile_own.1.refs_0_ = f32[3072,1536]{1,0:T(8,128)} custom-call(s32[2]{0:T(128)S(1)} %pad_add_fusion.place_ref, f32[3072,1536]{1,0:T(8,128)} %refs_1_.1, f32[1536,256]{1,0:T(8,128)S(1)} %copy-done, f32[128,1536]{1,0:T(8,128)S(1)} %pad_maximum_fusion.refs_2_, bf16[1152,1536]{1,0:T(8,128)(2,1)S(1)} %right_side.1.refs_3_.refs_4_, ...), custom_call_target="tpu_custom_call" | custom-call | flops 5435817984 | bytes 18874368 | tf_op jit(solution)/shard_map/tile_own/pallas_call | solution.py:209
  165.8 13.5 %tile_other.1 = f32[3072,1536]{1,0:T(8,128)} custom-call(s32[2]{0:T(128)S(1)} %pad_add_fusion.place_ref, f32[3072,1536]{1,0:T(8,128)} %tile_own.1.refs_0_, f32[3072,1536]{1,0:T(8,128)} %refs_1_.1, f32[1536,256]{1,0:T(8,128)S(1)} %collective-permute-done.23.refs_2_, f32[128,1536]{1,0:T(8,128)S(1)} %collective-permute-done.24.refs_3_, ...), custom_call_target="tpu_custom_call", output_to_operand_aliasing={{}: (1, {})} | custom-call | flops 5435817984 | bytes 18874368 | tf_op jit(solution)/shard_map/tile_other/pallas_call | solution.py:209
  (72 shorter events, 23.0 us)
Async XLA Ops:
  6.5 139.0 %all-gather.2.cloned.1.call-start = ((), (), s32[]{:S(2)}) async-start(), calls=%async_computation | async-start | bytes 1966080 | tf_op jit(solution)/shard_map/all_gather | solution.py:327
  8.4 42.3 %collective-permute-start.17 = (f32[288,256]{1,0:T(8,128)S(1)}, f32[288,256]{1,0:T(8,128)}, u32[]{:S(2)}, u32[]{:S(2)}) collective-permute-start(f32[288,256]{1,0:T(8,128)S(1)} %pad_maximum_fusion.1), channel_id=1, source_target_pairs={{0,4},{8,12},{16,20},{24,28}} | collective-permute-start | bytes 884744 | tf_op jit(solution)/shard_map/ppermute | solution.py:280
  18.3 37.5 %collective-permute-start.1 = (f32[384,256]{1,0:T(8,128)}, f32[384,256]{1,0:T(8,128)S(1)}, u32[]{:S(2)}, u32[]{:S(2)}) collective-permute-start(f32[384,256]{1,0:T(8,128)} %get-tuple-element.13), channel_id=1, source_target_pairs={{0,6},{8,14},{16,22},{24,30}} | collective-permute-start | bytes 1179656 | tf_op jit(solution)/shard_map/ppermute | solution.py:263
  20.0 42.0 %collective-permute-start.6 = (f32[384,256]{1,0:T(8,128)}, f32[384,256]{1,0:T(8,128)S(1)}, u32[]{:S(2)}, u32[]{:S(2)}) collective-permute-start(f32[384,256]{1,0:T(8,128)} %get-tuple-element.14), channel_id=1, source_target_pairs={{0,1},{8,9},{16,17},{24,25}} | collective-permute-start | bytes 1179656 | tf_op jit(solution)/shard_map/ppermute | solution.py:263
  21.3 46.7 %collective-permute-start.5 = (f32[384,256]{1,0:T(8,128)}, f32[384,256]{1,0:T(8,128)}, u32[]{:S(2)}, u32[]{:S(2)}) collective-permute-start(f32[384,256]{1,0:T(8,128)} %get-tuple-element.15), channel_id=1, source_target_pairs={{0,2},{8,10},{16,18},{24,26}} | collective-permute-start | bytes 1179656 | tf_op jit(solution)/shard_map/ppermute | solution.py:263
  23.4 47.2 %collective-permute-start.4 = (f32[384,256]{1,0:T(8,128)}, f32[384,256]{1,0:T(8,128)}, u32[]{:S(2)}, u32[]{:S(2)}) collective-permute-start(f32[384,256]{1,0:T(8,128)} %get-tuple-element.16), channel_id=1, source_target_pairs={{0,3},{8,11},{16,19},{24,27}} | collective-permute-start | bytes 1179656 | tf_op jit(solution)/shard_map/ppermute | solution.py:263
  50.7 13.4 %collective-permute-start.18 = (f32[288,256]{1,0:T(8,128)S(1)}, f32[288,256]{1,0:T(8,128)}, u32[]{:S(2)}, u32[]{:S(2)}) collective-permute-start(f32[288,256]{1,0:T(8,128)S(1)} %broadcast_select_fusion.5), channel_id=1, source_target_pairs={{0,2},{4,6},{8,10},{12,14},{16,18},{20,22},{24,26},{28,30}} | collective-permute-start | bytes 884744 | tf_op jit(solution)/shard_map/ppermute | solution.py:280
  55.8 17.2 %collective-permute-start.3 = (f32[384,256]{1,0:T(8,128)}, f32[384,256]{1,0:T(8,128)}, u32[]{:S(2)}, u32[]{:S(2)}) collective-permute-start(f32[384,256]{1,0:T(8,128)} %get-tuple-element.17), channel_id=1, source_target_pairs={{0,4},{8,12},{16,20},{24,28}} | collective-permute-start | bytes 1179656 | tf_op jit(solution)/shard_map/ppermute | solution.py:263
  62.1 12.4 %collective-permute-start.2 = (f32[384,256]{1,0:T(8,128)}, f32[384,256]{1,0:T(8,128)}, u32[]{:S(2)}, u32[]{:S(2)}) collective-permute-start(f32[384,256]{1,0:T(8,128)} %get-tuple-element.18), channel_id=1, source_target_pairs={{0,5},{8,13},{16,21},{24,29}} | collective-permute-start | bytes 1179656 | tf_op jit(solution)/shard_map/ppermute | solution.py:263
  64.1 12.3 %collective-permute-start = (f32[384,256]{1,0:T(8,128)}, f32[384,256]{1,0:T(8,128)}, u32[]{:S(2)}, u32[]{:S(2)}) collective-permute-start(f32[384,256]{1,0:T(8,128)} %get-tuple-element.19), channel_id=1, source_target_pairs={{0,7},{8,15},{16,23},{24,31}} | collective-permute-start | bytes 1179656 | tf_op jit(solution)/shard_map/ppermute | solution.py:263
  68.1 79.4 %collective-permute-start.12 = (f32[32,1536]{1,0:T(8,128)}, f32[32,1536]{1,0:T(8,128)S(1)}, u32[]{:S(2)}, u32[]{:S(2)}) collective-permute-start(f32[32,1536]{1,0:T(8,128)} %refs_0_.2), channel_id=1, source_target_pairs={{0,24},{8,0},{16,8},{24,16},{1,25},{9,1},{17,9},{25,17},{2,26},{10... | collective-permute-start | bytes 589832 | tf_op jit(solution)/shard_map/ppermute | solution.py:230
  70.6 34.1 %collective-permute-start.15 = (f32[128,1536]{1,0:T(8,128)}, f32[128,1536]{1,0:T(8,128)S(1)}, u32[]{:S(2)}, u32[]{:S(2)}) collective-permute-start(f32[128,1536]{1,0:T(8,128)} %get-tuple-element.11), channel_id=1, source_target_pairs={{0,16},{1,17},{2,18},{3,19},{4,20},{5,21},{6,22},{7,23}} | collective-permute-start | bytes 2359304 | tf_op jit(solution)/shard_map/ppermute | solution.py:239
  73.1 33.6 %collective-permute-start.13 = (f32[128,1536]{1,0:T(8,128)S(1)}, f32[128,1536]{1,0:T(8,128)S(1)}, u32[]{:S(2)}, u32[]{:S(2)}) collective-permute-start(f32[128,1536]{1,0:T(8,128)S(1)} %get-tuple-element.12), channel_id=1, source_target_pairs={{0,8},{1,9},{2,10},{3,11},{4,12},{5,13},{6,14},{7,15}} | collective-permute-start | bytes 2359304 | tf_op jit(solution)/shard_map/ppermute | solution.py:239
  74.4 19.1 %collective-permute-start.19 = (f32[288,256]{1,0:T(8,128)S(1)}, f32[288,256]{1,0:T(8,128)}, u32[]{:S(2)}, u32[]{:S(2)}) collective-permute-start(f32[288,256]{1,0:T(8,128)S(1)} %broadcast_select_fusion.6), channel_id=1, source_target_pairs={{0,8},{2,10},{4,12},{6,14},{8,16},{10,18},{12,20},{14,22},{16,24},... | collective-permute-start | bytes 884744 | tf_op jit(solution)/shard_map/ppermute | solution.py:290
  79.2 17.0 %collective-permute-start.20 = (f32[288,256]{1,0:T(8,128)S(1)}, f32[288,256]{1,0:T(8,128)S(1)}, u32[]{:S(2)}, u32[]{:S(2)}) collective-permute-start(f32[288,256]{1,0:T(8,128)S(1)} %broadcast_select_fusion.6), channel_id=1, source_target_pairs={{0,16},{2,18},{4,20},{6,22},{8,24},{10,26},{12,28},{14,30},{16,0},... | collective-permute-start | bytes 884744 | tf_op jit(solution)/shard_map/ppermute | solution.py:290
  93.5 9.2 %collective-permute-start.21 = (f32[288,256]{1,0:T(8,128)S(1)}, f32[288,256]{1,0:T(8,128)S(1)}, u32[]{:S(2)}, u32[]{:S(2)}) collective-permute-start(f32[288,256]{1,0:T(8,128)S(1)} %broadcast_select_fusion.6), channel_id=1, source_target_pairs={{0,24},{2,26},{4,28},{6,30},{8,0},{10,2},{12,4},{14,6},{16,8},{18,... | collective-permute-start | bytes 884744 | tf_op jit(solution)/shard_map/ppermute | solution.py:290
  96.2 13.4 %collective-permute-start.9 = (f32[32,1536]{1,0:T(8,128)}, f32[32,1536]{1,0:T(8,128)S(1)}, u32[]{:S(2)}, u32[]{:S(2)}) collective-permute-start(f32[32,1536]{1,0:T(8,128)} %get-tuple-element.21), channel_id=1, source_target_pairs={{0,24},{8,0},{16,8},{24,16},{1,25},{9,1},{17,9},{25,17},{2,26},{10... | collective-permute-start | bytes 589832 | tf_op jit(solution)/shard_map/ppermute | solution.py:230
  106.7 9.4 %collective-permute-start.22 = (f32[384,256]{1,0:T(8,128)S(1)}, f32[384,256]{1,0:T(8,128)S(1)}, u32[]{:S(2)}, u32[]{:S(2)}) collective-permute-start(f32[384,256]{1,0:T(8,128)S(1)} %fusion.2), channel_id=1, source_target_pairs={{0,1},{2,3},{4,5},{6,7},{8,9},{10,11},{12,13},{14,15},{16,17},{18,... | collective-permute-start | bytes 1179656 | tf_op jit(solution)/shard_map/ppermute | solution.py:294
  109.6 37.9 %collective-permute-start.11 = (f32[32,1536]{1,0:T(8,128)S(1)}, f32[32,1536]{1,0:T(8,128)S(1)}, u32[]{:S(2)}, u32[]{:S(2)}) collective-permute-start(f32[32,1536]{1,0:T(8,128)S(1)} %copy-done.1), channel_id=1, source_target_pairs={{0,16},{8,24},{16,0},{24,8},{1,17},{9,25},{17,1},{25,9},{2,18},{10... | collective-permute-start | bytes 589832 | tf_op jit(solution)/shard_map/ppermute | solution.py:230
  111.7 35.8 %collective-permute-start.10 = (f32[32,1536]{1,0:T(8,128)S(1)}, f32[32,1536]{1,0:T(8,128)S(1)}, u32[]{:S(2)}, u32[]{:S(2)}) collective-permute-start(f32[32,1536]{1,0:T(8,128)S(1)} %copy-done.1), channel_id=1, source_target_pairs={{0,8},{8,16},{16,24},{24,0},{1,9},{9,17},{17,25},{25,1},{2,10},{10... | collective-permute-start | bytes 589832 | tf_op jit(solution)/shard_map/ppermute | solution.py:230
  112.0 33.5 %collective-permute-start.16 = (f32[128,1536]{1,0:T(8,128)S(1)}, f32[128,1536]{1,0:T(8,128)}, u32[]{:S(2)}, u32[]{:S(2)}) collective-permute-start(f32[128,1536]{1,0:T(8,128)S(1)} %get-tuple-element.9), channel_id=1, source_target_pairs={{0,8},{16,24},{1,9},{17,25},{2,10},{18,26},{3,11},{19,27},{4,12},{... | collective-permute-start | bytes 2359304 | tf_op jit(solution)/shard_map/ppermute | solution.py:239
  116.1 30.7 %collective-permute-start.14 = (f32[128,1536]{1,0:T(8,128)S(1)}, f32[128,1536]{1,0:T(8,128)}, u32[]{:S(2)}, u32[]{:S(2)}) collective-permute-start(f32[128,1536]{1,0:T(8,128)S(1)} %get-tuple-element.10), channel_id=1, source_target_pairs={{0,16},{8,24},{1,17},{9,25},{2,18},{10,26},{3,19},{11,27},{4,20},{... | collective-permute-start | bytes 2359304 | tf_op jit(solution)/shard_map/ppermute | solution.py:239
  145.5 20.3 %collective-permute-start.23 = (f32[1536,256]{1,0:T(8,128)}, f32[1536,256]{1,0:T(8,128)S(1)}, u32[]{:S(2)}, u32[]{:S(2)}) collective-permute-start(f32[1536,256]{1,0:T(8,128)} %all-gather.2.cloned.1.call-done.refs_1_), channel_id=1, source_target_pairs={{0,1},{1,0},{2,3},{3,2},{4,5},{5,4},{6,7},{7,6},{8,9},{9,8},{10,11... | collective-permute-start | bytes 4718600 | tf_op jit(solution)/shard_map/ppermute | solution.py:269
  146.9 19.0 %collective-permute-start.24 = (f32[128,1536]{1,0:T(8,128)S(1)}, f32[128,1536]{1,0:T(8,128)S(1)}, u32[]{:S(2)}, u32[]{:S(2)}) collective-permute-start(f32[128,1536]{1,0:T(8,128)S(1)} %pad_maximum_fusion.refs_2_), channel_id=1, source_target_pairs={{0,1},{1,0},{2,3},{3,2},{4,5},{5,4},{6,7},{7,6},{8,9},{9,8},{10,11... | collective-permute-start | bytes 2359304 | tf_op jit(solution)/shard_map/ppermute | solution.py:269
  (7 other events, 179.9 us)
Sparse Core Ops, SparseCore 0:
  79.3 37.4 all-gather.1

commit v3 on v2

v3 whole, which is shorter than its diff:
```python
import functools

import jax
import jax.numpy as jnp
from jax import lax
from jax.experimental import pallas as pl
from jax.experimental.pallas import tpu as pltpu
from jax.sharding import PartitionSpec as P

B = 256
P_SIZE = 32
STRIP = 32
PIVOTS = 4
HIGHEST = lax.Precision.HIGHEST


def exact_dot(left, right, left_dim, right_dim):
    return lax.dot_general(
        left,
        right,
        (((left_dim,), (right_dim,)), ((), ())),
        precision=HIGHEST,
        preferred_element_type=jnp.float32,
    )


def split(value):
    high = value.astype(jnp.bfloat16)
    low = (value - high.astype(jnp.float32)).astype(jnp.bfloat16)
    return high, low


def split_dot(left, right):
    left_high, left_low = split(left)
    right_high, right_low = split(right)
    wide = functools.partial(jnp.dot, preferred_element_type=jnp.float32)
    return wide(left_high, right_high) + (wide(left_high, right_low) + wide(left_low, right_high))


def corner_kernel(joined_ref, filter_ref, regular_ref, inverse_ref, lead_ref, upper):
    obs = filter_ref.shape[0]
    filtered = exact_dot(filter_ref[...], joined_ref[:obs, :], 1, 0)
    row_pos = lax.broadcasted_iota(jnp.int32, (B, B), 0)
    col_pos = lax.broadcasted_iota(jnp.int32, (B, B), 1)
    system = joined_ref[obs:, :] + exact_dot(filtered, filtered, 0, 0)
    system = system + jnp.where(row_pos == col_pos, regular_ref[...], 0.0)
    identity = jnp.where(row_pos == col_pos, 1.0, 0.0)
    half = B // 2
    sub = lax.broadcasted_iota(jnp.int32, (STRIP, half), 0)
    lane = lax.broadcasted_iota(jnp.int32, (STRIP, half), 1)
    zero = jnp.zeros((STRIP, half), jnp.float32)
    for start in range(0, B, STRIP):
        rows = slice(start, start + STRIP)
        strip = jnp.concatenate([system[rows, :], identity[rows, :]], axis=1)
        if start:
            done = upper[:start, :]
            strip = strip - exact_dot(done[:, rows], done, 0, 0)
        low = 0 if start < half else half
        held = [strip[:, at : at + half] for at in range(low, low + 3 * half, half)]
        for first in range(0, STRIP, PIVOTS):
            at = start + first - low
            columns = [
                jnp.broadcast_to(held[0][:, at + q : at + q + 1], (STRIP, half)) for q in range(PIVOTS)
            ]
            pivot_rows = [[part[first + q : first + q + 1, :] for part in held] for q in range(PIVOTS)]
            for q in range(PIVOTS):
                j = first + q
                coef = jnp.where(sub > j, columns[q] * (1.0 / columns[q][j : j + 1, :]), 0.0)
                for m in range(q + 1, PIVOTS):
                    columns[m] = columns[m] - coef * columns[m][j : j + 1, :]
                    scale = coef[first + m : first + m + 1, :]
                    pivot_rows[m] = [
                        row - scale * other for row, other in zip(pivot_rows[m], pivot_rows[q])
                    ]
                held = [part - coef * row for part, row in zip(held, pivot_rows[q])]
        diag = jnp.sum(jnp.where(lane == sub + (start - low), held[0], 0.0), axis=1, keepdims=True)
        held = [part / jnp.sqrt(diag) for part in held]
        upper[rows, :] = jnp.concatenate([*held, zero] if low == 0 else [zero, *held], axis=1)
    inverse = upper[:, B:]
    inverse_ref[...] = inverse.T
    lead_ref[...] = exact_dot(filtered, inverse, 1, 1)


def corner_factor(joined, filter_matrix, regular):
    obs = filter_matrix.shape[0]
    return pl.pallas_call(
        corner_kernel,
        out_shape=[
            jax.ShapeDtypeStruct((B, B), jnp.float32),
            jax.ShapeDtypeStruct((obs, B), jnp.float32),
        ],
        scratch_shapes=[pltpu.VMEM((B, 2 * B), jnp.float32)],
        compiler_params=pltpu.CompilerParams(vmem_limit_bytes=24 * 2**20),
        cost_estimate=pl.CostEstimate(flops=4 * 10**9, bytes_accessed=2**20, transcendentals=0),
        name="corner_factor",
    )(joined, filter_matrix, regular)


def right_kernel(count, place_ref, *refs):
    col_parts = refs[:count]
    high_ref, low_ref, filter_ref, inverse_ref, lead_ref, regular_ref, out_ref = refs[count:]
    cols = out_ref.shape[1]
    obs = filter_ref.shape[0]
    obs_here = obs // count
    design = jnp.concatenate([part[:obs_here, :] for part in col_parts], axis=0)
    filtered = split_dot(filter_ref[...], design)
    strip = jnp.concatenate([high_ref[...], low_ref[...]], axis=0)
    row_pos = lax.broadcasted_iota(jnp.int32, (B, cols), 0)
    col_pos = lax.broadcasted_iota(jnp.int32, (B, cols), 1) + place_ref[1] * cols
    strip = strip + jnp.where(row_pos == col_pos, regular_ref[...], 0.0)
    panel = split_dot(inverse_ref[...].T, strip) + split_dot(lead_ref[...].T, filtered)
    filtered_high, filtered_low = split(filtered)
    panel_high, panel_low = split(-panel)
    out_ref[:obs, :] = filtered_high
    out_ref[obs : 2 * obs, :] = filtered_low
    out_ref[2 * obs : 2 * obs + B, :] = panel_high
    out_ref[2 * obs + B : 2 * obs + 2 * B, :] = panel_low
    out_ref[2 * obs + 2 * B : 2 * obs + 3 * B, :] = panel_high
    out_ref[2 * obs + 3 * B :, :] = filtered_high

    @pl.when(place_ref[1] == 0)
    def _():
        out_ref[:, :B] = jnp.zeros((out_ref.shape[0], B), jnp.bfloat16)
        row_pos = lax.broadcasted_iota(jnp.int32, (B, B), 0)
        identity = jnp.where(row_pos == lax.broadcasted_iota(jnp.int32, (B, B), 1), 1.0, 0.0)
        identity = identity.astype(jnp.bfloat16)
        out_ref[2 * obs : 2 * obs + B, :B] = identity
        out_ref[2 * obs + 2 * B : 2 * obs + 3 * B, :B] = identity


def right_side(place, col_parts, strips, filter_matrix, inverse, lead, regular):
    count = len(col_parts)
    cols = strips[0].shape[1]
    depth = 3 * (filter_matrix.shape[0] + B)
    specs = [pl.BlockSpec(memory_space=pltpu.SMEM)]
    specs += [pl.BlockSpec(memory_space=pltpu.VMEM)] * (count + 6)
    return pl.pallas_call(
        functools.partial(right_kernel, count),
        in_specs=specs,
        out_specs=pl.BlockSpec(memory_space=pltpu.VMEM),
        out_shape=jax.ShapeDtypeStruct((depth, cols), jnp.bfloat16),
        compiler_params=pltpu.CompilerParams(vmem_limit_bytes=32 * 2**20),
        cost_estimate=pl.CostEstimate(
            flops=2 * cols * B * depth, bytes_accessed=4 * cols * depth, transcendentals=0
        ),
        name="right_side",
    )(place, *col_parts, *strips, filter_matrix, inverse, lead, regular)


def tile_kernel(units, again, place_ref, blocks_ref, *refs):
    if again:
        refs = refs[1:]
    count = len(units)
    normals_ref = refs[0]
    strip_refs = refs[1 : 1 + count]
    design_refs = refs[1 + count : 3 + count]
    right_ref, filter_ref, inverse_ref, lead_ref, regular_ref, lead_reg_ref = refs[3 + count : 9 + count]
    out_ref, left_ref = refs[9 + count :]
    step = pl.program_id(0)
    row_index, col_index = place_ref[0], place_ref[1]
    block, cols = out_ref.shape
    row_blocks = 2 * cols // block
    obs = filter_ref.shape[0]
    first_col = col_index * cols

    @pl.when(step == 0)
    def _():
        for unit, other in enumerate(units):
            in_half = lax.rem(blocks_ref[unit], row_blocks // 2)
            here = pl.ds(pl.multiple_of(in_half * block, block), block)
            filtered = split_dot(filter_ref[...], design_refs[other][:, here]).T
            first_row = (row_index * row_blocks + blocks_ref[unit]) * block
            row_pos = lax.broadcasted_iota(jnp.int32, (block, B), 0) + first_row
            col_pos = lax.broadcasted_iota(jnp.int32, (block, B), 1)
            system = strip_refs[unit][...] + jnp.where(row_pos == col_pos, lead_reg_ref[...], 0.0)
            panel = split_dot(system, inverse_ref[...]) + split_dot(filtered, lead_ref[...])
            filtered_high, filtered_low = split(filtered)
            panel_high, panel_low = split(panel)
            rows = slice(unit * block, (unit + 1) * block)
            left_ref[rows, :obs] = filtered_high
            left_ref[rows, obs : 2 * obs] = filtered_high
            left_ref[rows, 2 * obs : 2 * obs + B] = panel_high
            left_ref[rows, 2 * obs + B : 2 * obs + 2 * B] = panel_high
            left_ref[rows, 2 * obs + 2 * B : 2 * obs + 3 * B] = panel_low
            left_ref[rows, 2 * obs + 3 * B :] = filtered_low

    first_row = (row_index * row_blocks + blocks_ref[step]) * block
    rows = pl.ds(pl.multiple_of(step * block, block), block)
    col_pos = lax.broadcasted_iota(jnp.int32, (1, cols), 1) + first_col
    keep = jnp.where(col_pos < B, 0.0, 1.0)
    out_ref[...] = normals_ref[...] * keep + jnp.dot(
        left_ref[rows, :], right_ref[...], preferred_element_type=jnp.float32
    )

    @pl.when((first_row < first_col + cols) & (first_col < first_row + block))
    def _():
        row_pos = lax.broadcasted_iota(jnp.int32, (block, cols), 0) + first_row
        on_diag = (row_pos == col_pos) & (col_pos >= B)
        out_ref[...] = out_ref[...] + jnp.where(on_diag, regular_ref[...], 0.0)


def tile_rows(place, blocks, before, normals, units, strips, designs, right, filter_matrix, inverse, lead, regular, lead_reg):
    rows, cols = normals.shape
    block = strips[0].shape[0]
    depth = right.shape[0]
    again = before is not None

    def whole(array):
        return pl.BlockSpec(array.shape, lambda i, place, blocks: (0,) * array.ndim)

    tile_spec = pl.BlockSpec((block, cols), lambda i, place, blocks: (blocks[i], 0))
    rest = [*strips, *designs, right, filter_matrix, inverse, lead, regular, lead_reg]
    in_specs = [tile_spec] + [whole(array) for array in rest]
    operands = [normals, *rest]
    if again:
        in_specs = [pl.BlockSpec(memory_space=pl.ANY)] + in_specs
        operands = [before] + operands
    count = len(units)
    return pl.pallas_call(
        functools.partial(tile_kernel, units, again),
        grid_spec=pltpu.PrefetchScalarGridSpec(
            num_scalar_prefetch=2,
            grid=(count,),
            in_specs=in_specs,
            out_specs=tile_spec,
            scratch_shapes=[pltpu.VMEM((count * block, depth), jnp.bfloat16)],
        ),
        out_shape=jax.ShapeDtypeStruct((rows, cols), jnp.float32),
        input_output_aliases={2: 0} if again else {},
        compiler_params=pltpu.CompilerParams(vmem_limit_bytes=44 * 2**20),
        cost_estimate=pl.CostEstimate(
            flops=2 * count * block * cols * depth, bytes_accessed=8 * count * block * cols, transcendentals=0
        ),
        name="tile_rest" if again else "tile_first",
    )(place, blocks, *operands)


def shifted(value, axis, by):
    peers = lax.axis_size(axis)
    return lax.ppermute(value, axis, [(i, (i + by) % peers) for i in range(peers)])


def spread(value, axis, bits):
    peers = lax.axis_size(axis)
    me = lax.axis_index(axis)
    reached = [0]
    for bit in bits:
        pairs = [(i, i | bit) for i in reached if i | bit < peers]
        got = lax.ppermute(value, axis, pairs)
        value = jnp.where((me & bit) != 0, got, value)
        reached += [to for _, to in pairs]
    return value


def filter_matrix_of(filter_blocks, sources):
    count = sources.shape[0]
    lag = jnp.arange(count, dtype=jnp.int32)[:, None] - sources[None, :]
    lag = lag[:, None, :, None]
    own = filter_blocks[0][None, :, None, :]
    prior = filter_blocks[1][None, :, None, :]
    blocks = jnp.where(lag == 0, own, jnp.where(lag == 1, prior, 0.0))
    return blocks.reshape(count * P_SIZE, count * P_SIZE)


def other_core(value):
    return lax.ppermute(value, "col", [(c, c ^ 1) for c in range(lax.axis_size("col"))])


def row_strip(normals):
    peers = lax.axis_size("col")
    chips = peers // 2
    half = normals.shape[0] // 2
    col_index = lax.axis_index("col")
    chip = col_index // 2
    own = normals[:half, :B]
    second = lax.ppermute(normals[half:, :B], "col", [(0, 1)])
    if chips > 4:
        cores = [list(range(k, peers, 2)) for k in range(2)]
        size = half // chips
        arrived = own[:size]
        for c in range(1, peers):
            first = (c % 2) * half + (c // 2) * size
            got = lax.ppermute(normals[first : first + size, :B], "col", [(0, c)])
            arrived = jnp.where(col_index == c, got, arrived)
        return [(jnp.int32(0), lax.all_gather(arrived, "col", axis=0, tiled=True, axis_index_groups=cores))]
    count = chips - 1
    size = half // count
    arrived = None
    for c in reversed(range(2, peers)):
        first = (c % 2) * half + (c // 2 - 1) * size
        got = lax.ppermute(normals[first : first + size, :B], "col", [(0, c)])
        arrived = got if arrived is None else arrived + got
    local = jnp.where(col_index == 0, own, second)
    at_source = chip == 0
    mine = jnp.where(at_source, local[:size], arrived)
    pieces = [(jnp.where(at_source, 0, chip - 1), mine)]
    for s in range(1, count):
        pairs = [
            (2 * (1 + i) + k, 2 * (1 + (i + s) % count) + k) for i in range(count) for k in range(2)
        ]
        got = lax.ppermute(mine, "col", pairs)
        which = -s % count
        piece = jnp.where(at_source, local[which * size : (which + 1) * size], got)
        pieces.append((jnp.where(at_source, which, (chip - 1 - s) % count), piece))
    return pieces


def leading_parts(normals, design):
    row_peers, col_peers = lax.axis_size("row"), lax.axis_size("col")
    row_index, col_index = lax.axis_index("row"), lax.axis_index("col")
    obs_here = design.shape[0]
    held = jnp.concatenate([design[:, :B], normals[:B, :B]], axis=0)
    reached = [0]
    for bit in reversed([1 << i for i in range(1, (col_peers - 1).bit_length())]):
        pairs = [(i, i | bit) for i in reached if i | bit < col_peers]
        got = lax.ppermute(held, "col", pairs)
        held = jnp.where((col_index & bit) != 0, got, held)
        reached += [to for _, to in pairs]
    times, block = [held[:obs_here]], held[obs_here:]
    for s in range(1, row_peers):
        pairs = [
            (i * col_peers + c, (i + s) % row_peers * col_peers + c)
            for i in range(row_peers)
            for c in range(0, col_peers, 2)
        ]
        got = lax.ppermute(held, ("row", "col"), pairs)
        times.append(got[:obs_here])
        block = jnp.where(row_index == s, got[obs_here:], block)
    held = jnp.concatenate([*times, block], axis=0)
    got = lax.ppermute(held, "col", [(c, c + 1) for c in range(0, col_peers, 2)])
    return jnp.where(col_index % 2 == 1, got, held)


def body(normals, design, filter_blocks, regular):
    cols_here = normals.shape[1]
    obs_here = design.shape[0]
    row_peers = lax.axis_size("row")
    row_index = lax.axis_index("row")
    chips = lax.axis_size("col") // 2
    col_index = lax.axis_index("col")
    blocks_here = obs_here // P_SIZE
    obs = row_peers * obs_here

    lead = leading_parts(normals, design)
    pieces = row_strip(normals)

    along = [design] + [shifted(design, "col", 2 * s) for s in range(1, chips)]
    along = jnp.stack(along)
    parts = []
    for s in range(row_peers):
        back = (col_index // 2 - (row_index + s)) % chips
        far = lax.dynamic_index_in_dim(along, back, 0, keepdims=False)
        part = jnp.concatenate([design, far], axis=0)
        parts.append(shifted(part, "row", s) if s else part)
    own_design = jnp.concatenate([part[obs_here:] for part in parts], axis=0)
    designs = [own_design, other_core(own_design)]

    bits = [1 << i for i in range((row_peers - 1).bit_length())]
    strips = [
        spread(normals[: B // 2], "row", bits),
        spread(normals[B // 2 : B], "row", bits[::-1]),
    ]

    positions = jnp.arange(obs // P_SIZE, dtype=jnp.int32)
    passed = positions // blocks_here
    order = ((row_index - passed) % row_peers) * blocks_here + positions % blocks_here
    filters = filter_matrix_of(filter_blocks, order)
    lead_reg = regular[:B].reshape(1, B)
    own_reg = lax.dynamic_slice_in_dim(regular, col_index * cols_here, cols_here).reshape(1, cols_here)
    place = jnp.stack([row_index, col_index]).astype(jnp.int32)
    inverse, lead_filtered = corner_factor(lead, filters, lead_reg)
    right = right_side(place, parts, strips, filters, inverse, lead_filtered, own_reg)
    shared = [right, filters, inverse, lead_filtered, own_reg, lead_reg]

    core = col_index % 2
    out = None
    for group in (pieces[:1], pieces[1:]):
        if group:
            rows, blocks = [], []
            for other in range(2):
                for which, piece in group:
                    rows.append(other_core(piece) if other else piece)
                    blocks.append(((1 - core) if other else core) * len(pieces) + which)
            units = [0] * len(group) + [1] * len(group)
            blocks = jnp.stack(blocks).astype(jnp.int32)
            out = tile_rows(place, blocks, out, normals, units, rows, designs, *shared)
    return out


def solution(mesh):
    in_specs = (P("row", "col"), P("row", "col"), P(), P())
    out_specs = P("row", "col")
    return jax.shard_map(body, mesh=mesh, in_specs=in_specs, out_specs=out_specs, check_vma=False)
```

time: 187 us -> 168 us (0.90)
  the two profiles are of different devices: /device:TPU:0 before, /device:TPU:11 now
where the time goes in v3:
time: 168 us; the launch traced here: 167 us
  waiting for transfers between devices  58 us (35%)
  starting transfers between devices  44.4 us (26%)
  Pallas kernels  43.9 us (26%)
  local copies, waits for them, and re-layouts  12.2 us (7%)
  other arithmetic  8.07 us (5%)
    pallas_call x2, Pallas kernels, tile_rows(): pl.pallas_call(functools.partial(tile_kernel, units, again), grid_spec=pl...  27.3 us
    ppermute x1, waiting for transfers between devices, leading_parts(): lax.ppermute(held, 'col', [(c, c + 1) for c in range(0, col_peers, 2)])  18.9 us
    ppermute x2, starting transfers between devices, row_strip(): got = lax.ppermute(mine, 'col', pairs)  18.3 us
    ppermute x2, waiting for transfers between devices, row_strip(): got = lax.ppermute(mine, 'col', pairs)  15.1 us
    ppermute x6, waiting for transfers between devices, shifted(): lax.ppermute(value, axis, [(i, (i + by) % peers) for i in range(peers)])  14.4 us
    pallas_call x1, Pallas kernels, corner_factor(): pl.pallas_call(corner_kernel, out_shape=[jax.ShapeDtypeStruct((B, B), jnp...  14.1 us
    ppermute x4, waiting for transfers between devices, spread(): got = lax.ppermute(value, axis, pairs)  9.58 us
    ppermute x6, starting transfers between devices, shifted(): lax.ppermute(value, axis, [(i, (i + by) % peers) for i in range(peers)])  8.28 us
  transfers between devices with their start and end apart: 29, of which 6 were waited for; matrix products, arithmetic and copies ran while one was open for 12% of the time, Pallas kernels for 16%

profile of v3, /device:TPU:11, one launch (start us, length us, event | category | flops | bytes accessed | tf_op | source)
XLA Modules:
  0.0 167.2 jit_solution(2007319394334466201)
XLA Ops:
  0.2 2.3 %collective-permute-start.9 = (f32[32,1536]{1,0:T(8,128)}, f32[32,1536]{1,0:T(8,128)S(1)}, u32[]{:S(2)}, u32[]{:S(2)}) collective-permute-start(f32[32,1536]{1,0:T(8,128)} %param.5), channel_id=1, source_target_pairs={{0,4},{1,5},{2,6},{3,7},{4,0},{5,1},{6,2},{7,3},{8,12},{9,13},{10,... | collective-permute-start | bytes 589832 | tf_op jit(solution)/shard_map/ppermute | solution.py:240
  2.5 2.2 %collective-permute-start.8 = (f32[32,1536]{1,0:T(8,128)}, f32[32,1536]{1,0:T(8,128)S(1)}, u32[]{:S(2)}, u32[]{:S(2)}) collective-permute-start(f32[32,1536]{1,0:T(8,128)} %param.5), channel_id=1, source_target_pairs={{0,2},{1,3},{2,4},{3,5},{4,6},{5,7},{6,0},{7,1},{8,10},{9,11},{10,... | collective-permute-start | bytes 589832 | tf_op jit(solution)/shard_map/ppermute | solution.py:240
  7.2 2.6 %fusion.6 = (f32[128,1536]{1,0:T(8,128)}, f32[128,1536]{1,0:T(8,128)}) fusion(f32[3072,1536]{1,0:T(8,128)} %refs_1_.1), kind=kLoop, calls=%fused_computation.43 | loop fusion | bytes 3145728 | tf_op jit(solution)/shard_map/slice | solution.py:361
  9.8 1.7 collective-permute-start.17
  11.5 3.6 %fusion.7 = (f32[512,256]{1,0:T(8,128)}, f32[512,256]{1,0:T(8,128)}, f32[512,256]{1,0:T(8,128)}, f32[512,256]{1,0:T(8,128)}, f32[512,256]{1,0:T(8,128)}, /*index=5*/f32[512,256]{1,0:T(8,128)}) fusion(f32[3072,1536]{1,0:T(8,128)} %refs_1_.1), kind=kLoop, calls=%fused_computation.44 | loop fusion | bytes 6291456 | tf_op jit(solution)/shard_map/slice | solution.py:291
  15.9 6.5 %collective-permute-done.8 = f32[32,1536]{1,0:T(8,128)S(1)} collective-permute-done((f32[32,1536]{1,0:T(8,128)}, f32[32,1536]{1,0:T(8,128)S(1)}, u32[]{:S(2)}, u32[]{:S(2)}) %collective-permute-start.8) | collective-permute-done | bytes 196640 | tf_op jit(solution)/shard_map/ppermute | solution.py:240
  25.8 1.4 collective-permute-start.20
  27.5 2.1 %collective-permute-start.11 = (f32[64,1536]{1,0:T(8,128)}, f32[64,1536]{1,0:T(8,128)S(1)}, u32[]{:S(2)}, u32[]{:S(2)}) collective-permute-start(f32[64,1536]{1,0:T(8,128)} %get-tuple-element.28), channel_id=1, source_target_pairs={{0,8},{8,16},{16,24},{24,0},{1,9},{9,17},{17,25},{25,1},{2,10},{10... | collective-permute-start | bytes 1179656 | tf_op jit(solution)/shard_map/ppermute | solution.py:240
  29.7 1.5 slice.88
  33.9 7.8 %collective-permute-done.12.refs_2_ = f32[64,1536]{1,0:T(8,128)S(1)} collective-permute-done((f32[64,1536]{1,0:T(8,128)}, f32[64,1536]{1,0:T(8,128)S(1)}, u32[]{:S(2)}, u32[]{:S(2)}) %collective-permute-start.12) | collective-permute-done | bytes 393248 | tf_op jit(solution)/shard_map/ppermute | solution.py:240
  48.8 1.3 collective-permute-start.5
  50.1 9.6 %collective-permute-done.15 = f32[128,1536]{1,0:T(8,128)S(1)} collective-permute-done((f32[128,1536]{1,0:T(8,128)}, f32[128,1536]{1,0:T(8,128)S(1)}, u32[]{:S(2)}, u32[]{:S(2)}) %collective-permute-start.15) | collective-permute-done | bytes 786464 | tf_op jit(solution)/shard_map/ppermute | solution.py:249
  60.9 1.6 broadcast_select_fusion.2
  62.6 18.9 %collective-permute-done.24 = f32[384,256]{1,0:T(8,128)S(1)} collective-permute-done((f32[384,256]{1,0:T(8,128)S(1)}, f32[384,256]{1,0:T(8,128)S(1)}, u32[]{:S(2)}, u32[]{:S(2)}) %collective-permute-start.24) | collective-permute-done | bytes 393248 | tf_op jit(solution)/shard_map/ppermute | solution.py:330
  82.3 14.1 %corner_factor.1 = (f32[256,256]{1,0:T(8,128)S(1)}, f32[128,256]{1,0:T(8,128)S(1)}) custom-call(f32[384,256]{1,0:T(8,128)S(1)} %broadcast_select_fusion.4.joined_ref, f32[128,128]{1,0:T(8,128)S(1)} %select_n.215.filter_ref.refs_6_.refs_9_, f32[1,256]{1,0:T(1,128)S(1)} %bitcast.25), custom_call_target="tpu_custom_call" | custom-call | flops 4000000000 | bytes 1048576 | tf_op jit(solution)/shard_map/corner_factor/pallas_call | solution.py:86
  99.2 1.6 slice_select_fusion
  101.4 1.3 collective-permute-start.16
  103.0 16.2 %collective-permute-start.26 = (f32[512,256]{1,0:T(8,128)S(1)}, f32[512,256]{1,0:T(8,128)S(1)}, u32[]{:S(2)}, u32[]{:S(2)}) collective-permute-start(f32[512,256]{1,0:T(8,128)S(1)} %slice_select_fusion.3.refs_1_), channel_id=1, source_target_pairs={{2,6},{3,7},{4,2},{5,3},{6,4},{7,5},{10,14},{11,15},{12,10},{13,11... | collective-permute-start | bytes 1572872 | tf_op jit(solution)/shard_map/ppermute | solution.py:301
  119.2 2.1 %collective-permute-start.25 = (f32[512,256]{1,0:T(8,128)S(1)}, f32[512,256]{1,0:T(8,128)S(1)}, u32[]{:S(2)}, u32[]{:S(2)}) collective-permute-start(f32[512,256]{1,0:T(8,128)S(1)} %slice_select_fusion.3.refs_1_), channel_id=1, source_target_pairs={{2,4},{3,5},{4,6},{5,7},{6,2},{7,3},{10,12},{11,13},{12,14},{13,15... | collective-permute-start | bytes 1572872 | tf_op jit(solution)/shard_map/ppermute | solution.py:301
  121.5 9.5 %collective-permute-done.26 = f32[512,256]{1,0:T(8,128)S(1)} collective-permute-done((f32[512,256]{1,0:T(8,128)S(1)}, f32[512,256]{1,0:T(8,128)S(1)}, u32[]{:S(2)}, u32[]{:S(2)}) %collective-permute-start.26) | collective-permute-done | bytes 524320 | tf_op jit(solution)/shard_map/ppermute | solution.py:301
  131.0 5.6 %collective-permute-done.25 = f32[512,256]{1,0:T(8,128)S(1)} collective-permute-done((f32[512,256]{1,0:T(8,128)S(1)}, f32[512,256]{1,0:T(8,128)S(1)}, u32[]{:S(2)}, u32[]{:S(2)}) %collective-permute-start.25) | collective-permute-done | bytes 524320 | tf_op jit(solution)/shard_map/ppermute | solution.py:301
  137.4 2.5 %right_side.1.refs_5_.refs_8_ = bf16[1152,1536]{1,0:T(8,128)(2,1)S(1)} custom-call(s32[2]{0:T(128)S(1)} %pad_add_fusion.place_ref, f32[64,1536]{1,0:T(8,128)S(1)} %get-tuple-element.25.refs_0_, f32[64,1536]{1,0:T(8,128)S(1)} %collective-permute-done.11.refs_1_, f32[64,1536]{1,0:T(8,128)S(1)} %collective-permute-done.12.refs_2_, ...), custom_call_target="tpu_custom_call" | custom-call | flops 905969664 | bytes 7077888 | tf_op jit(solution)/shard_map/right_side/pallas_call | solution.py:137
  139.9 10.2 %tile_first.1.refs_0_ = f32[3072,1536]{1,0:T(8,128)} custom-call(s32[2]{0:T(128)S(1)} %pad_add_fusion.place_ref, s32[2]{0:T(128)S(1)} %pad_add_fusion.2.blocks_ref, f32[3072,1536]{1,0:T(8,128)} %refs_1_.1, f32[512,256]{1,0:T(8,128)S(1)} %slice_select_fusion.3.refs_1_, f32[512,256]{1,0:T(8,128)S(1)} %collective-permute-done.7.refs_2_, ...), custom_call_target="tpu_custom_call" | custom-call | flops 3623878656 | bytes 12582912 | tf_op jit(solution)/shard_map/tile_first/pallas_call | solution.py:219
  150.1 17.1 %tile_rest.1 = f32[3072,1536]{1,0:T(8,128)} custom-call(s32[2]{0:T(128)S(1)} %pad_add_fusion.place_ref, s32[4]{0:T(128)S(1)} %pad_add_fusion.1.blocks_ref, f32[3072,1536]{1,0:T(8,128)} %tile_first.1.refs_0_, f32[3072,1536]{1,0:T(8,128)} %refs_1_.1, f32[512,256]{1,0:T(8,128)S(1)} %get-tuple-element.20.refs_2_, ...), custom_call_target="tpu_custom_call", output_to_operand_aliasing={{}: (2, {})} | custom-call | flops 7247757312 | bytes 25165824 | tf_op jit(solution)/shard_map/tile_rest/pallas_call | solution.py:219
  (92 shorter events, 23.2 us)
Async XLA Ops:
  0.0 15.9 %collective-permute-start.10 = (f32[32,1536]{1,0:T(8,128)}, f32[32,1536]{1,0:T(8,128)S(1)}, u32[]{:S(2)}, u32[]{:S(2)}) collective-permute-start(f32[32,1536]{1,0:T(8,128)} %param.5), channel_id=1, source_target_pairs={{0,6},{1,7},{2,0},{3,1},{4,2},{5,3},{6,4},{7,5},{8,14},{9,15},{10,... | collective-permute-start | bytes 589832 | tf_op jit(solution)/shard_map/ppermute | solution.py:240
  0.2 15.8 %collective-permute-start.9 = (f32[32,1536]{1,0:T(8,128)}, f32[32,1536]{1,0:T(8,128)S(1)}, u32[]{:S(2)}, u32[]{:S(2)}) collective-permute-start(f32[32,1536]{1,0:T(8,128)} %param.5), channel_id=1, source_target_pairs={{0,4},{1,5},{2,6},{3,7},{4,0},{5,1},{6,2},{7,3},{8,12},{9,13},{10,... | collective-permute-start | bytes 589832 | tf_op jit(solution)/shard_map/ppermute | solution.py:240
  2.5 20.0 %collective-permute-start.8 = (f32[32,1536]{1,0:T(8,128)}, f32[32,1536]{1,0:T(8,128)S(1)}, u32[]{:S(2)}, u32[]{:S(2)}) collective-permute-start(f32[32,1536]{1,0:T(8,128)} %param.5), channel_id=1, source_target_pairs={{0,2},{1,3},{2,4},{3,5},{4,6},{5,7},{6,0},{7,1},{8,10},{9,11},{10,... | collective-permute-start | bytes 589832 | tf_op jit(solution)/shard_map/ppermute | solution.py:240
  6.5 18.5 %collective-permute-start.19 = (f32[288,256]{1,0:T(8,128)S(1)}, f32[288,256]{1,0:T(8,128)S(1)}, u32[]{:S(2)}, u32[]{:S(2)}) collective-permute-start(f32[288,256]{1,0:T(8,128)S(1)} %pad_maximum_fusion.6), channel_id=1, source_target_pairs={{0,4},{8,12},{16,20},{24,28}} | collective-permute-start | bytes 884744 | tf_op jit(solution)/shard_map/ppermute | solution.py:316
  9.8 39.0 %collective-permute-start.17 = (f32[128,1536]{1,0:T(8,128)}, f32[128,1536]{1,0:T(8,128)}, u32[]{:S(2)}, u32[]{:S(2)}) collective-permute-start(f32[128,1536]{1,0:T(8,128)} %get-tuple-element.11), channel_id=1, source_target_pairs={{0,16},{1,17},{2,18},{3,19},{4,20},{5,21},{6,22},{7,23}} | collective-permute-start | bytes 2359304 | tf_op jit(solution)/shard_map/ppermute | solution.py:249
  23.8 18.0 %collective-permute-start.12 = (f32[64,1536]{1,0:T(8,128)}, f32[64,1536]{1,0:T(8,128)S(1)}, u32[]{:S(2)}, u32[]{:S(2)}) collective-permute-start(f32[64,1536]{1,0:T(8,128)} %get-tuple-element.26), channel_id=1, source_target_pairs={{0,16},{8,24},{16,0},{24,8},{1,17},{9,25},{17,1},{25,9},{2,18},{10... | collective-permute-start | bytes 1179656 | tf_op jit(solution)/shard_map/ppermute | solution.py:240
  25.8 17.3 %collective-permute-start.20 = (f32[288,256]{1,0:T(8,128)}, f32[288,256]{1,0:T(8,128)}, u32[]{:S(2)}, u32[]{:S(2)}) collective-permute-start(f32[288,256]{1,0:T(8,128)} %broadcast_select_fusion.5), channel_id=1, source_target_pairs={{0,2},{4,6},{8,10},{12,14},{16,18},{20,22},{24,26},{28,30}} | collective-permute-start | bytes 884744 | tf_op jit(solution)/shard_map/ppermute | solution.py:316
  27.2 17.6 %collective-permute-start.13 = (f32[64,1536]{1,0:T(8,128)}, f32[64,1536]{1,0:T(8,128)S(1)}, u32[]{:S(2)}, u32[]{:S(2)}) collective-permute-start(f32[64,1536]{1,0:T(8,128)} %get-tuple-element.27), channel_id=1, source_target_pairs={{0,24},{8,0},{16,8},{24,16},{1,25},{9,1},{17,9},{25,17},{2,26},{10... | collective-permute-start | bytes 1179656 | tf_op jit(solution)/shard_map/ppermute | solution.py:240
  27.5 18.1 %collective-permute-start.11 = (f32[64,1536]{1,0:T(8,128)}, f32[64,1536]{1,0:T(8,128)S(1)}, u32[]{:S(2)}, u32[]{:S(2)}) collective-permute-start(f32[64,1536]{1,0:T(8,128)} %get-tuple-element.28), channel_id=1, source_target_pairs={{0,8},{8,16},{16,24},{24,0},{1,9},{9,17},{17,25},{25,1},{2,10},{10... | collective-permute-start | bytes 1179656 | tf_op jit(solution)/shard_map/ppermute | solution.py:240
  41.7 17.9 %collective-permute-start.15 = (f32[128,1536]{1,0:T(8,128)}, f32[128,1536]{1,0:T(8,128)S(1)}, u32[]{:S(2)}, u32[]{:S(2)}) collective-permute-start(f32[128,1536]{1,0:T(8,128)} %get-tuple-element.12), channel_id=1, source_target_pairs={{0,8},{1,9},{2,10},{3,11},{4,12},{5,13},{6,14},{7,15}} | collective-permute-start | bytes 2359304 | tf_op jit(solution)/shard_map/ppermute | solution.py:249
  43.1 54.8 %collective-permute-start = (f32[1536,256]{1,0:T(8,128)S(1)}, f32[1536,256]{1,0:T(8,128)S(1)}, u32[]{:S(2)}, u32[]{:S(2)}) collective-permute-start(f32[1536,256]{1,0:T(8,128)S(1)} %slice.88), channel_id=1, source_target_pairs={{0,1},{8,9},{16,17},{24,25}} | collective-permute-start | bytes 4718600 | tf_op jit(solution)/shard_map/ppermute | solution.py:276
  47.2 49.2 %collective-permute-start.2 = (f32[512,256]{1,0:T(8,128)S(1)}, f32[512,256]{1,0:T(8,128)S(1)}, u32[]{:S(2)}, u32[]{:S(2)}) collective-permute-start(f32[512,256]{1,0:T(8,128)S(1)} %copy-done.6), channel_id=1, source_target_pairs={{0,6},{8,14},{16,22},{24,30}} | collective-permute-start | bytes 1572872 | tf_op jit(solution)/shard_map/ppermute | solution.py:291
  48.0 49.2 %collective-permute-start.6 = (f32[512,256]{1,0:T(8,128)S(1)}, f32[512,256]{1,0:T(8,128)S(1)}, u32[]{:S(2)}, u32[]{:S(2)}) collective-permute-start(f32[512,256]{1,0:T(8,128)S(1)} %copy-done.5), channel_id=1, source_target_pairs={{0,2},{8,10},{16,18},{24,26}} | collective-permute-start | bytes 1572872 | tf_op jit(solution)/shard_map/ppermute | solution.py:291
  48.8 52.0 %collective-permute-start.5 = (f32[512,256]{1,0:T(8,128)S(1)}, f32[512,256]{1,0:T(8,128)S(1)}, u32[]{:S(2)}, u32[]{:S(2)}) collective-permute-start(f32[512,256]{1,0:T(8,128)S(1)} %copy-done.4), channel_id=1, source_target_pairs={{0,3},{8,11},{16,19},{24,27}} | collective-permute-start | bytes 1572872 | tf_op jit(solution)/shard_map/ppermute | solution.py:291
  59.7 21.9 %collective-permute-start.24 = (f32[384,256]{1,0:T(8,128)S(1)}, f32[384,256]{1,0:T(8,128)S(1)}, u32[]{:S(2)}, u32[]{:S(2)}) collective-permute-start(f32[384,256]{1,0:T(8,128)S(1)} %fusion.2), channel_id=1, source_target_pairs={{0,1},{2,3},{4,5},{6,7},{8,9},{10,11},{12,13},{14,15},{16,17},{18,... | collective-permute-start | bytes 1179656 | tf_op jit(solution)/shard_map/ppermute | solution.py:330
  81.5 19.8 %collective-permute-start.4 = (f32[512,256]{1,0:T(8,128)S(1)}, f32[512,256]{1,0:T(8,128)S(1)}, u32[]{:S(2)}, u32[]{:S(2)}) collective-permute-start(f32[512,256]{1,0:T(8,128)S(1)} %copy-done.3), channel_id=1, source_target_pairs={{0,4},{8,12},{16,20},{24,28}} | collective-permute-start | bytes 1572872 | tf_op jit(solution)/shard_map/ppermute | solution.py:291
  97.9 23.4 %collective-permute-start.18 = (f32[128,1536]{1,0:T(8,128)S(1)}, f32[128,1536]{1,0:T(8,128)S(1)}, u32[]{:S(2)}, u32[]{:S(2)}) collective-permute-start(f32[128,1536]{1,0:T(8,128)S(1)} %get-tuple-element.9), channel_id=1, source_target_pairs={{0,8},{16,24},{1,9},{17,25},{2,10},{18,26},{3,11},{19,27},{4,12},{... | collective-permute-start | bytes 2359304 | tf_op jit(solution)/shard_map/ppermute | solution.py:249
  100.8 39.1 %collective-permute-start.14 = (f32[128,1536]{1,0:T(8,128)S(1)}, f32[128,1536]{1,0:T(8,128)S(1)}, u32[]{:S(2)}, u32[]{:S(2)}) collective-permute-start(f32[128,1536]{1,0:T(8,128)S(1)} %pad_maximum_fusion.1.refs_3_.refs_6_), channel_id=1, source_target_pairs={{0,1},{1,0},{2,3},{3,2},{4,5},{5,4},{6,7},{7,6},{8,9},{9,8},{10,11... | collective-permute-start | bytes 2359304 | tf_op jit(solution)/shard_map/ppermute | solution.py:266
  101.4 35.9 %collective-permute-start.16 = (f32[128,1536]{1,0:T(8,128)S(1)}, f32[128,1536]{1,0:T(8,128)S(1)}, u32[]{:S(2)}, u32[]{:S(2)}) collective-permute-start(f32[128,1536]{1,0:T(8,128)S(1)} %get-tuple-element.10), channel_id=1, source_target_pairs={{0,16},{8,24},{1,17},{9,25},{2,18},{10,26},{3,19},{11,27},{4,20},{... | collective-permute-start | bytes 2359304 | tf_op jit(solution)/shard_map/ppermute | solution.py:249
  103.0 28.0 %collective-permute-start.26 = (f32[512,256]{1,0:T(8,128)S(1)}, f32[512,256]{1,0:T(8,128)S(1)}, u32[]{:S(2)}, u32[]{:S(2)}) collective-permute-start(f32[512,256]{1,0:T(8,128)S(1)} %slice_select_fusion.3.refs_1_), channel_id=1, source_target_pairs={{2,6},{3,7},{4,2},{5,3},{6,4},{7,5},{10,14},{11,15},{12,10},{13,11... | collective-permute-start | bytes 1572872 | tf_op jit(solution)/shard_map/ppermute | solution.py:301
  119.2 17.4 %collective-permute-start.25 = (f32[512,256]{1,0:T(8,128)S(1)}, f32[512,256]{1,0:T(8,128)S(1)}, u32[]{:S(2)}, u32[]{:S(2)}) collective-permute-start(f32[512,256]{1,0:T(8,128)S(1)} %slice_select_fusion.3.refs_1_), channel_id=1, source_target_pairs={{2,4},{3,5},{4,6},{5,7},{6,2},{7,3},{10,12},{11,13},{12,14},{13,15... | collective-permute-start | bytes 1572872 | tf_op jit(solution)/shard_map/ppermute | solution.py:301
  121.3 18.6 %collective-permute-start.7 = (f32[512,256]{1,0:T(8,128)S(1)}, f32[512,256]{1,0:T(8,128)S(1)}, u32[]{:S(2)}, u32[]{:S(2)}) collective-permute-start(f32[512,256]{1,0:T(8,128)S(1)} %slice_select_fusion.3.refs_1_), channel_id=1, source_target_pairs={{0,1},{1,0},{2,3},{3,2},{4,5},{5,4},{6,7},{7,6},{8,9},{9,8},{10,11... | collective-permute-start | bytes 1572872 | tf_op jit(solution)/shard_map/ppermute | solution.py:266
  136.7 13.4 %collective-permute-start.28 = (f32[512,256]{1,0:T(8,128)S(1)}, f32[512,256]{1,0:T(8,128)S(1)}, u32[]{:S(2)}, u32[]{:S(2)}) collective-permute-start(f32[512,256]{1,0:T(8,128)S(1)} %get-tuple-element.19.refs_3_), channel_id=1, source_target_pairs={{0,1},{1,0},{2,3},{3,2},{4,5},{5,4},{6,7},{7,6},{8,9},{9,8},{10,11... | collective-permute-start | bytes 1572872 | tf_op jit(solution)/shard_map/ppermute | solution.py:266
  136.8 13.3 %collective-permute-start.27 = (f32[512,256]{1,0:T(8,128)S(1)}, f32[512,256]{1,0:T(8,128)S(1)}, u32[]{:S(2)}, u32[]{:S(2)}) collective-permute-start(f32[512,256]{1,0:T(8,128)S(1)} %get-tuple-element.20.refs_2_), channel_id=1, source_target_pairs={{0,1},{1,0},{2,3},{3,2},{4,5},{5,4},{6,7},{7,6},{8,9},{9,8},{10,11... | collective-permute-start | bytes 1572872 | tf_op jit(solution)/shard_map/ppermute | solution.py:266
  (13 other events, 141.2 us)

commit v4 on v3

v4 whole, which is shorter than its diff:
```python
import functools

import jax
import jax.numpy as jnp
from jax import lax
from jax.experimental import pallas as pl
from jax.experimental.pallas import tpu as pltpu
from jax.sharding import PartitionSpec as P

B = 256
P_SIZE = 32
STRIP = 32
PIVOTS = 4
HIGHEST = lax.Precision.HIGHEST


def exact_dot(left, right, left_dim, right_dim):
    return lax.dot_general(
        left,
        right,
        (((left_dim,), (right_dim,)), ((), ())),
        precision=HIGHEST,
        preferred_element_type=jnp.float32,
    )


def split(value):
    high = value.astype(jnp.bfloat16)
    low = (value - high.astype(jnp.float32)).astype(jnp.bfloat16)
    return high, low


def split_dot(left, right):
    left_high, left_low = split(left)
    right_high, right_low = split(right)
    wide = functools.partial(jnp.dot, preferred_element_type=jnp.float32)
    return wide(left_high, right_high) + (wide(left_high, right_low) + wide(left_low, right_high))


def corner_kernel(block_ref, design_ref, filter_ref, regular_ref, inverse_ref, upper):
    filtered = exact_dot(filter_ref[...], design_ref[...], 1, 0)
    row_pos = lax.broadcasted_iota(jnp.int32, (B, B), 0)
    col_pos = lax.broadcasted_iota(jnp.int32, (B, B), 1)
    system = block_ref[...] + exact_dot(filtered, filtered, 0, 0)
    system = system + jnp.where(row_pos == col_pos, regular_ref[...], 0.0)
    identity = jnp.where(row_pos == col_pos, 1.0, 0.0)
    half = B // 2
    sub = lax.broadcasted_iota(jnp.int32, (STRIP, half), 0)
    lane = lax.broadcasted_iota(jnp.int32, (STRIP, half), 1)
    zero = jnp.zeros((STRIP, half), jnp.float32)
    for start in range(0, B, STRIP):
        rows = slice(start, start + STRIP)
        strip = jnp.concatenate([system[rows, :], identity[rows, :]], axis=1)
        if start:
            done = upper[:start, :]
            strip = strip - exact_dot(done[:, rows], done, 0, 0)
        low = 0 if start < half else half
        held = [strip[:, at : at + half] for at in range(low, low + 3 * half, half)]
        for first in range(0, STRIP, PIVOTS):
            at = start + first - low
            columns = [
                jnp.broadcast_to(held[0][:, at + q : at + q + 1], (STRIP, half)) for q in range(PIVOTS)
            ]
            pivot_rows = [[part[first + q : first + q + 1, :] for part in held] for q in range(PIVOTS)]
            for q in range(PIVOTS):
                j = first + q
                coef = jnp.where(sub > j, columns[q] * (1.0 / columns[q][j : j + 1, :]), 0.0)
                for m in range(q + 1, PIVOTS):
                    columns[m] = columns[m] - coef * columns[m][j : j + 1, :]
                    scale = coef[first + m : first + m + 1, :]
                    pivot_rows[m] = [
                        row - scale * other for row, other in zip(pivot_rows[m], pivot_rows[q])
                    ]
                held = [part - coef * row for part, row in zip(held, pivot_rows[q])]
        diag = jnp.sum(jnp.where(lane == sub + (start - low), held[0], 0.0), axis=1, keepdims=True)
        held = [part / jnp.sqrt(diag) for part in held]
        upper[rows, :] = jnp.concatenate([*held, zero] if low == 0 else [zero, *held], axis=1)
    inverse_ref[...] = upper[:, B:].T


def corner_factor(block, design, filter_matrix, regular):
    return pl.pallas_call(
        corner_kernel,
        out_shape=jax.ShapeDtypeStruct((B, B), jnp.float32),
        scratch_shapes=[pltpu.VMEM((B, 2 * B), jnp.float32)],
        compiler_params=pltpu.CompilerParams(vmem_limit_bytes=4 * 2**20),
        cost_estimate=pl.CostEstimate(flops=10**9, bytes_accessed=2**20, transcendentals=0),
        name="corner_factor",
    )(block, design, filter_matrix, regular)


def right_kernel(place_ref, high_ref, low_ref, gram_ref, inverse_ref, out_ref):
    strip = jnp.concatenate([high_ref[...], low_ref[...]], axis=0) + gram_ref[...]
    panel_high, panel_low = split(-split_dot(inverse_ref[...].T, strip))
    out_ref[:B, :] = panel_high
    out_ref[B : 2 * B, :] = panel_low
    out_ref[2 * B :, :] = panel_high

    @pl.when(place_ref[1] == 0)
    def _():
        row_pos = lax.broadcasted_iota(jnp.int32, (B, B), 0)
        identity = jnp.where(row_pos == lax.broadcasted_iota(jnp.int32, (B, B), 1), 1.0, 0.0)
        identity = identity.astype(jnp.bfloat16)
        out_ref[:B, :B] = identity
        out_ref[B : 2 * B, :B] = jnp.zeros((B, B), jnp.bfloat16)
        out_ref[2 * B :, :B] = identity


def right_side(place, strips, gram_rows, inverse):
    cols = gram_rows.shape[1]
    return pl.pallas_call(
        right_kernel,
        in_specs=[pl.BlockSpec(memory_space=pltpu.SMEM)] + [pl.BlockSpec(memory_space=pltpu.VMEM)] * 4,
        out_specs=pl.BlockSpec(memory_space=pltpu.VMEM),
        out_shape=jax.ShapeDtypeStruct((3 * B, cols), jnp.bfloat16),
        compiler_params=pltpu.CompilerParams(vmem_limit_bytes=20 * 2**20),
        cost_estimate=pl.CostEstimate(
            flops=6 * cols * B * B, bytes_accessed=12 * cols * B, transcendentals=0
        ),
        name="right_side",
    )(place, *strips, gram_rows, inverse)


def filter_kernel(count, place_ref, *refs):
    parts = refs[:count]
    other_ref, filter_ref, regular_ref, lead_reg_ref = refs[count : count + 4]
    left_ref, right_ref, gram_rows_ref, gram_cols_ref = refs[count + 4 :]
    row_index, col_index = place_ref[0], place_ref[1]
    cols = right_ref.shape[1]
    obs = filter_ref.shape[0]
    core = lax.rem(col_index, 2)
    design = jnp.concatenate([part[...] for part in parts], axis=0)
    filtered = split_dot(filter_ref[...], design)
    here, rows_own, lead = filtered[:, :cols], filtered[:, cols : 2 * cols], filtered[:, 2 * cols :]
    row_pos = lax.broadcasted_iota(jnp.int32, (B, cols), 0)
    col_pos = lax.broadcasted_iota(jnp.int32, (1, cols), 1) + col_index * cols
    gram_rows_ref[...] = split_dot(lead.T, here) + jnp.where(row_pos == col_pos, regular_ref[...], 0.0)
    high, low = split(jnp.where(col_pos < B, 0.0, here))
    right_ref[:obs, :] = high
    right_ref[obs : 2 * obs, :] = low
    right_ref[2 * obs :, :] = high
    rows_other = split_dot(filter_ref[...], other_ref[...])
    for half, value in ((core, rows_own), (1 - core, rows_other)):
        value = value.T
        high, low = split(value)
        rows = pl.ds(pl.multiple_of(half * cols, cols), cols)
        left_ref[rows, :obs] = high
        left_ref[rows, obs : 2 * obs] = high
        left_ref[rows, 2 * obs :] = low
        row_pos = lax.broadcasted_iota(jnp.int32, (cols, B), 0) + (2 * row_index + half) * cols
        lead_pos = lax.broadcasted_iota(jnp.int32, (cols, B), 1)
        gram_cols_ref[rows, :] = split_dot(value, lead) + jnp.where(
            row_pos == lead_pos, lead_reg_ref[...], 0.0
        )


def filter_sides(place, parts, other, filter_matrix, regular, lead_reg):
    cols = other.shape[1]
    obs = filter_matrix.shape[0]
    vmem = pl.BlockSpec(memory_space=pltpu.VMEM)
    return pl.pallas_call(
        functools.partial(filter_kernel, len(parts)),
        in_specs=[pl.BlockSpec(memory_space=pltpu.SMEM)] + [vmem] * (len(parts) + 4),
        out_specs=[vmem] * 4,
        out_shape=[
            jax.ShapeDtypeStruct((2 * cols, 3 * obs), jnp.bfloat16),
            jax.ShapeDtypeStruct((3 * obs, cols), jnp.bfloat16),
            jax.ShapeDtypeStruct((B, cols), jnp.float32),
            jax.ShapeDtypeStruct((2 * cols, B), jnp.float32),
        ],
        compiler_params=pltpu.CompilerParams(vmem_limit_bytes=20 * 2**20),
        cost_estimate=pl.CostEstimate(
            flops=18 * cols * obs * B, bytes_accessed=24 * cols * B, transcendentals=0
        ),
        name="filter_sides",
    )(place, *parts, other, filter_matrix, regular, lead_reg)


def gram_kernel(place_ref, normals_ref, left_ref, right_ref, regular_ref, out_ref):
    step = pl.program_id(0)
    block, cols = out_ref.shape
    first_col = place_ref[1] * cols
    col_pos = lax.broadcasted_iota(jnp.int32, (1, cols), 1) + first_col
    keep = jnp.where(col_pos < B, 0.0, 1.0)
    out_ref[...] = normals_ref[...] * keep + jnp.dot(
        left_ref[...], right_ref[...], preferred_element_type=jnp.float32
    )
    first_row = (place_ref[0] * pl.num_programs(0) + step) * block

    @pl.when((first_row < first_col + cols) & (first_col < first_row + block))
    def _():
        row_pos = lax.broadcasted_iota(jnp.int32, (block, cols), 0) + first_row
        on_diag = (row_pos == col_pos) & (col_pos >= B)
        out_ref[...] = out_ref[...] + jnp.where(on_diag, regular_ref[...], 0.0)


def block_rows(half):
    return max(size for size in range(128, 513, 128) if half % size == 0)


def gram_tile(place, normals, left, right, regular):
    rows, cols = normals.shape
    block = block_rows(rows // 2)
    depth = right.shape[0]
    tile_spec = pl.BlockSpec((block, cols), lambda i, place: (i, 0))
    return pl.pallas_call(
        gram_kernel,
        grid_spec=pltpu.PrefetchScalarGridSpec(
            num_scalar_prefetch=1,
            grid=(rows // block,),
            in_specs=[
                tile_spec,
                pl.BlockSpec((block, depth), lambda i, place: (i, 0)),
                pl.BlockSpec((depth, cols), lambda i, place: (0, 0), pipeline_mode=pl.Buffered(1)),
                pl.BlockSpec((1, cols), lambda i, place: (0, 0)),
            ],
            out_specs=tile_spec,
        ),
        out_shape=pltpu.VMEM((rows, cols), jnp.float32),
        compiler_params=pltpu.CompilerParams(vmem_limit_bytes=8 * 2**20),
        cost_estimate=pl.CostEstimate(
            flops=2 * rows * cols * depth, bytes_accessed=4 * rows * cols, transcendentals=0
        ),
        name="gram_tile",
    )(place, normals, left, right, regular)


def tile_kernel(count, block_ids_ref, place_ref, system_ref, *refs):
    here_refs, sent_refs = refs[:count], refs[count : 2 * count]
    gram_ref, right_ref, inverse_ref, out_ref = refs[2 * count :]
    step = pl.program_id(0)
    block = out_ref.shape[0]
    per_piece = pl.num_programs(0) // count
    even = lax.rem(place_ref[1], 2) == 0
    slot = step // per_piece
    rows = pl.ds(pl.multiple_of(lax.rem(step, per_piece) * block, block), block)
    strip = jnp.where(even, here_refs[0][rows, :], sent_refs[0][rows, :])
    for i in range(1, count):
        strip = jnp.where(slot == i, jnp.where(even, here_refs[i][rows, :], sent_refs[i][rows, :]), strip)
    panel = split_dot(strip + gram_ref[...], inverse_ref[...])
    high, low = split(panel)
    left = jnp.concatenate([high, high, low], axis=1)
    out_ref[...] = system_ref[...] + jnp.dot(left, right_ref[...], preferred_element_type=jnp.float32)


def tile_rows(place, block_ids, system, here, sent, gram_cols, right, inverse):
    rows, cols = system.shape
    count = len(here)
    block = rows // block_ids.shape[0]

    def whole(array):
        return pl.BlockSpec(
            array.shape, lambda i, ids, place: (0,) * array.ndim, pipeline_mode=pl.Buffered(1)
        )

    tile_spec = pl.BlockSpec((block, cols), lambda i, ids, place: (ids[i], 0))
    gram_spec = pl.BlockSpec((block, B), lambda i, ids, place: (ids[i], 0))
    return pl.pallas_call(
        functools.partial(tile_kernel, count),
        grid_spec=pltpu.PrefetchScalarGridSpec(
            num_scalar_prefetch=2,
            grid=(block_ids.shape[0],),
            in_specs=[tile_spec]
            + [whole(array) for array in [*here, *sent]]
            + [gram_spec, whole(right), whole(inverse)],
            out_specs=tile_spec,
        ),
        out_shape=jax.ShapeDtypeStruct((rows, cols), jnp.float32),
        compiler_params=pltpu.CompilerParams(vmem_limit_bytes=16 * 2**20),
        cost_estimate=pl.CostEstimate(
            flops=6 * rows * cols * B, bytes_accessed=4 * rows * cols, transcendentals=0
        ),
        name="tile_rows",
    )(block_ids, place, system, *here, *sent, gram_cols, right, inverse)


def shifted(value, axis, by):
    peers = lax.axis_size(axis)
    return lax.ppermute(value, axis, [(i, (i + by) % peers) for i in range(peers)])


def spread(value, axis, bits):
    peers = lax.axis_size(axis)
    me = lax.axis_index(axis)
    reached = [0]
    for bit in bits:
        pairs = [(i, i | bit) for i in reached if i | bit < peers]
        got = lax.ppermute(value, axis, pairs)
        value = jnp.where((me & bit) != 0, got, value)
        reached += [to for _, to in pairs]
    return value


def filter_matrix_of(filter_blocks, sources):
    count = sources.shape[0]
    lag = jnp.arange(count, dtype=jnp.int32)[:, None] - sources[None, :]
    lag = lag[:, None, :, None]
    own = filter_blocks[0][None, :, None, :]
    prior = filter_blocks[1][None, :, None, :]
    blocks = jnp.where(lag == 0, own, jnp.where(lag == 1, prior, 0.0))
    return blocks.reshape(count * P_SIZE, count * P_SIZE)


def to_odd_core(value):
    return lax.ppermute(value, "col", [(c, c + 1) for c in range(0, lax.axis_size("col"), 2)])


def row_strip(normals):
    peers = lax.axis_size("col")
    chips = peers // 2
    rows = normals.shape[0]
    col_index = lax.axis_index("col")
    chip = col_index // 2
    if chips > 4:
        size = rows // chips
        share = normals[:size, :B]
        for z in range(1, chips):
            got = lax.ppermute(normals[z * size : (z + 1) * size, :B], "col", [(0, 2 * z)])
            share = jnp.where(chip == z, got, share)
        cores = [list(range(k, peers, 2)) for k in range(2)]
        return [(jnp.int32(0), lax.all_gather(share, "col", axis=0, tiled=True, axis_index_groups=cores))]
    count = chips - 1
    size = rows // count
    local = [normals[i * size : (i + 1) * size, :B] for i in range(count)]
    arrived = None
    for i in reversed(range(count)):
        got = lax.ppermute(local[i], "col", [(0, 2 * (1 + i))])
        arrived = got if arrived is None else arrived + got
    at_source = chip == 0
    mine = jnp.where(at_source, local[0], arrived)
    pieces = [(jnp.where(at_source, 0, chip - 1), mine)]
    for s in range(1, count):
        pairs = [(2 * (1 + i), 2 * (1 + (i + s) % count)) for i in range(count)]
        got = lax.ppermute(mine, "col", pairs)
        which = -s % count
        piece = jnp.where(at_source, local[which], got)
        pieces.append((jnp.where(at_source, which, (chip - 1 - s) % count), piece))
    return pieces


def leading_block(normals):
    row_peers, col_peers = lax.axis_size("row"), lax.axis_size("col")
    here = lax.axis_index("row") * col_peers + lax.axis_index("col")
    total = row_peers * col_peers
    held = normals[:B, :B]
    reached = [0]
    bits = [1 << i for i in range((total - 1).bit_length())]
    bits = [b for b in reversed(bits) if 1 < b < col_peers] + [b for b in bits if b >= col_peers] + [1]
    for bit in bits:
        pairs = [(i, i | bit) for i in reached if i | bit < total]
        got = lax.ppermute(held, ("row", "col"), pairs)
        held = jnp.where((here & bit) != 0, got, held)
        reached += [to for _, to in pairs]
    return held


def body(normals, design, filter_blocks, regular):
    rows_here, cols_here = normals.shape
    obs_here = design.shape[0]
    row_peers = lax.axis_size("row")
    row_index = lax.axis_index("row")
    col_index = lax.axis_index("col")
    blocks_here = obs_here // P_SIZE
    obs = row_peers * obs_here
    core = col_index % 2

    corner = leading_block(normals)
    pieces = row_strip(normals)

    along = lax.all_gather(design, "col", axis=1, tiled=True)
    parts = []
    for s in range(row_peers):
        to = (row_index + s) % row_peers
        far = lax.dynamic_slice_in_dim(along, to * rows_here + core * cols_here, cols_here, axis=1)
        part = jnp.concatenate([design, far, along[:, :B]], axis=1)
        parts.append(shifted(part, "row", s) if s else part)
    own = jnp.concatenate([part[:, cols_here : 2 * cols_here] for part in parts], axis=0)
    other = lax.ppermute(own, "col", [(c, c ^ 1) for c in range(lax.axis_size("col"))])
    lead = jnp.concatenate([part[:, 2 * cols_here :] for part in parts], axis=0)

    bits = [1 << i for i in range((row_peers - 1).bit_length())]
    strips = [
        spread(normals[: B // 2], "row", bits),
        spread(normals[B // 2 : B], "row", bits[::-1]),
    ]

    positions = jnp.arange(obs // P_SIZE, dtype=jnp.int32)
    passed = positions // blocks_here
    order = ((row_index - passed) % row_peers) * blocks_here + positions % blocks_here
    filters = filter_matrix_of(filter_blocks, order)
    lead_reg = regular[:B].reshape(1, B)
    own_reg = lax.dynamic_slice_in_dim(regular, col_index * cols_here, cols_here).reshape(1, cols_here)
    place = jnp.stack([row_index, col_index]).astype(jnp.int32)
    inverse = corner_factor(corner, lead, filters, lead_reg)
    gram_left, gram_right, gram_rows, gram_cols = filter_sides(place, parts, other, filters, own_reg, lead_reg)
    system = gram_tile(place, normals, gram_left, gram_right, own_reg)
    system = pltpu.with_memory_space_constraint(system, pltpu.VMEM)
    right = right_side(place, strips, gram_rows, inverse)

    here = [piece for _, piece in pieces]
    sent = [to_odd_core(piece) for piece in here]
    per_piece = here[0].shape[0] // block_rows(rows_here // 2)
    which = jnp.stack([index for index, _ in pieces])
    block_ids = which[:, None] * per_piece + jnp.arange(per_piece, dtype=jnp.int32)[None, :]
    block_ids = block_ids.reshape(-1).astype(jnp.int32)
    return tile_rows(place, block_ids, system, here, sent, gram_cols, right, inverse)


def solution(mesh):
    in_specs = (P("row", "col"), P("row", "col"), P(), P())
    out_specs = P("row", "col")
    return jax.shard_map(body, mesh=mesh, in_specs=in_specs, out_specs=out_specs, check_vma=False)
```

time: 168 us -> 186 us (1.11)
  the two profiles are of different devices: /device:TPU:11 before, /device:TPU:0 now
where the time goes in v4:
time: 186 us; the launch traced here: 185 us
  starting transfers between devices  51.2 us (28%)
  waiting for transfers between devices  45.6 us (25%)
  Pallas kernels  40.9 us (22%)
  local copies, waits for them, and re-layouts  22.4 us (12%)
  between operations  13.8 us (7%)
  other arithmetic  11.3 us (6%)
    ppermute x5, waiting for transfers between devices, leading_block(): got = lax.ppermute(held, ('row', 'col'), pairs)  25.9 us
    ppermute x3, waiting for transfers between devices, shifted(): lax.ppermute(value, axis, [(i, (i + by) % peers) for i in range(peers)])  19 us
    pallas_call x1, Pallas kernels, tile_rows(): pl.pallas_call(functools.partial(tile_kernel, count), grid_spec=pltpu.Pre...  13.9 us
    pallas_call x1, Pallas kernels, corner_factor(): pl.pallas_call(corner_kernel, out_shape=jax.ShapeDtypeStruct((B, B), jnp....  13.9 us
    ppermute x5, starting transfers between devices, leading_block(): got = lax.ppermute(held, ('row', 'col'), pairs)  13.2 us
    ppermute x3, starting transfers between devices, row_strip(): got = lax.ppermute(local[i], 'col', [(0, 2 * (1 + i))])  13 us
    ppermute x4, starting transfers between devices, spread(): got = lax.ppermute(value, axis, pairs)  11.5 us
    unnamed x18, local copies, waits for them, and re-layouts  11.1 us
  transfers between devices with their start and end apart: 22, of which 4 were waited for; matrix products, arithmetic and copies ran while one was open for 12% of the time, Pallas kernels for 15%

profile of v4, /device:TPU:0, one launch (start us, length us, event | category | flops | bytes accessed | tf_op | source)
XLA Modules:
  0.0 185.2 jit_solution(9008573455512396217)
XLA Ops:
  8.2 6.6 %collective-permute-start.16 = (f32[256,256]{1,0:T(8,128)S(1)}, f32[256,256]{1,0:T(8,128)}, u32[]{:S(2)}, u32[]{:S(2)}) collective-permute-start(f32[256,256]{1,0:T(8,128)S(1)} %slice.63), channel_id=1, source_target_pairs={{0,4}} | collective-permute-start | bytes 786440 | tf_op jit(solution)/shard_map/ppermute | solution.py:351
  16.4 2.2 %collective-permute-start.14 = (f32[128,1536]{1,0:T(8,128)S(1)}, f32[128,1536]{1,0:T(8,128)}, u32[]{:S(2)}, u32[]{:S(2)}) collective-permute-start(f32[128,1536]{1,0:T(8,128)S(1)} %get-tuple-element.15), channel_id=1, source_target_pairs={{0,16},{1,17},{2,18},{3,19},{4,20},{5,21},{6,22},{7,23}} | collective-permute-start | bytes 2359304 | tf_op jit(solution)/shard_map/ppermute | solution.py:288
  18.6 2.2 %collective-permute-start.12 = (f32[128,1536]{1,0:T(8,128)S(1)}, f32[128,1536]{1,0:T(8,128)}, u32[]{:S(2)}, u32[]{:S(2)}) collective-permute-start(f32[128,1536]{1,0:T(8,128)S(1)} %get-tuple-element.16), channel_id=1, source_target_pairs={{0,8},{1,9},{2,10},{3,11},{4,12},{5,13},{6,14},{7,15}} | collective-permute-start | bytes 2359304 | tf_op jit(solution)/shard_map/ppermute | solution.py:288
  20.8 3.4 %fusion.4 = (f32[1024,256]{1,0:T(8,128)}, f32[1024,256]{1,0:T(8,128)}, f32[1024,256]{1,0:T(8,128)S(1)}) fusion(f32[3072,1536]{1,0:T(8,128)} %normals_ref.1), kind=kLoop, calls=%fused_computation.40 | loop fusion | bytes 6291456 | tf_op jit(solution)/shard_map/slice | solution.py:324
  24.2 3.9 %collective-permute-start.5 = (f32[1024,256]{1,0:T(8,128)}, f32[1024,256]{1,0:T(8,128)}, u32[]{:S(2)}, u32[]{:S(2)}) collective-permute-start(f32[1024,256]{1,0:T(8,128)} %get-tuple-element.19), channel_id=1, source_target_pairs={{0,4},{8,12},{16,20},{24,28}} | collective-permute-start | bytes 3145736 | tf_op jit(solution)/shard_map/ppermute | solution.py:327
  28.1 2.6 %collective-permute-start.4 = (f32[1024,256]{1,0:T(8,128)}, f32[1024,256]{1,0:T(8,128)}, u32[]{:S(2)}, u32[]{:S(2)}) collective-permute-start(f32[1024,256]{1,0:T(8,128)} %get-tuple-element.20), channel_id=1, source_target_pairs={{0,6},{8,14},{16,22},{24,30}} | collective-permute-start | bytes 3145736 | tf_op jit(solution)/shard_map/ppermute | solution.py:327
  31.9 2.0 %collective-permute-start.17 = (f32[256,256]{1,0:T(8,128)S(1)}, f32[256,256]{1,0:T(8,128)}, u32[]{:S(2)}, u32[]{:S(2)}) collective-permute-start(f32[256,256]{1,0:T(8,128)S(1)} %broadcast_select_fusion.6), channel_id=1, source_target_pairs={{0,2},{4,6}} | collective-permute-start | bytes 786440 | tf_op jit(solution)/shard_map/ppermute | solution.py:351
  34.6 22.9 %collective-permute-done.17 = f32[256,256]{1,0:T(8,128)} collective-permute-done((f32[256,256]{1,0:T(8,128)S(1)}, f32[256,256]{1,0:T(8,128)}, u32[]{:S(2)}, u32[]{:S(2)}) %collective-permute-start.17) | collective-permute-done | bytes 262176 | tf_op jit(solution)/shard_map/ppermute | solution.py:351
  59.8 2.9 %collective-permute-done.18 = f32[256,256]{1,0:T(8,128)S(1)} collective-permute-done((f32[256,256]{1,0:T(8,128)S(1)}, f32[256,256]{1,0:T(8,128)S(1)}, u32[]{:S(2)}, u32[]{:S(2)}) %collective-permute-start.18) | collective-permute-done | bytes 262176 | tf_op jit(solution)/shard_map/ppermute | solution.py:351
  62.8 6.4 %collective-permute-start.6 = (f32[1024,256]{1,0:T(8,128)S(1)}, f32[1024,256]{1,0:T(8,128)}, u32[]{:S(2)}, u32[]{:S(2)}) collective-permute-start(f32[1024,256]{1,0:T(8,128)S(1)} %get-tuple-element.21), channel_id=1, source_target_pairs={{0,2},{8,10},{16,18},{24,26}} | collective-permute-start | bytes 3145736 | tf_op jit(solution)/shard_map/ppermute | solution.py:327
  72.2 5.5 %collective-permute-start.15 = (f32[128,1536]{1,0:T(8,128)S(1)}, f32[128,1536]{1,0:T(8,128)}, u32[]{:S(2)}, u32[]{:S(2)}) collective-permute-start(f32[128,1536]{1,0:T(8,128)S(1)} %get-tuple-element.13), channel_id=1, source_target_pairs={{0,8},{16,24},{1,9},{17,25},{2,10},{18,26},{3,11},{19,27},{4,12},{... | collective-permute-start | bytes 2359304 | tf_op jit(solution)/shard_map/ppermute | solution.py:288
  78.5 2.0 %collective-permute-start.20 = (f32[256,256]{1,0:T(8,128)}, f32[256,256]{1,0:T(8,128)}, u32[]{:S(2)}, u32[]{:S(2)}) collective-permute-start(f32[256,256]{1,0:T(8,128)} %broadcast_select_fusion.9), channel_id=1, source_target_pairs={{0,1},{4,5},{2,3},{6,7},{8,9},{12,13},{10,11},{14,15},{16,17},{20,... | collective-permute-start | bytes 786440 | tf_op jit(solution)/shard_map/ppermute | solution.py:351
  85.0 2.4 %add_select_fusion.refs_0_ = f32[1024,256]{1,0:T(8,128)S(1)} fusion(f32[1024,256]{1,0:T(8,128)} %collective-permute-done.6, f32[1024,256]{1,0:T(8,128)} %collective-permute-done.4, f32[1024,256]{1,0:T(8,128)} %collective-permute-done.5, pred[]{:T(512)S(6)} %eq.30, f32[3072,1536]{1,0:T(8,128)} %normals_ref.1), kind=kLoop, calls=%fused_computation | loop fusion | flops 786432 | bytes 5242881 | tf_op jit(solution)/shard_map/jit(_where)/select_n | solution.py:330
  97.2 8.2 %collective-permute-done.refs_1_ = f32[32,3328]{1,0:T(8,128)S(1)} collective-permute-done((f32[32,3328]{1,0:T(8,128)}, f32[32,3328]{1,0:T(8,128)S(1)}, u32[]{:S(2)}, u32[]{:S(2)}) %collective-permute-start) | collective-permute-done | bytes 426016 | tf_op jit(solution)/shard_map/ppermute | solution.py:279
  105.4 2.3 %collective-permute-start.9 = (f32[1024,256]{1,0:T(8,128)S(1)}, f32[1024,256]{1,0:T(8,128)}, u32[]{:S(2)}, u32[]{:S(2)}) collective-permute-start(f32[1024,256]{1,0:T(8,128)S(1)} %add_select_fusion.refs_0_), channel_id=1, source_target_pairs={{0,1},{2,3},{4,5},{6,7},{8,9},{10,11},{12,13},{14,15},{16,17},{18,... | collective-permute-start | bytes 3145736 | tf_op jit(solution)/shard_map/ppermute | solution.py:305
  107.7 10.8 %collective-permute-done.1.refs_2_ = f32[32,3328]{1,0:T(8,128)S(1)} collective-permute-done((f32[32,3328]{1,0:T(8,128)}, f32[32,3328]{1,0:T(8,128)S(1)}, u32[]{:S(2)}, u32[]{:S(2)}) %collective-permute-start.1) | collective-permute-done | bytes 426016 | tf_op jit(solution)/shard_map/ppermute | solution.py:279
  118.7 1.8 broadcast_select_fusion
  120.5 3.4 %collective-permute-start.11 = (f32[1024,256]{1,0:T(8,128)S(1)}, f32[1024,256]{1,0:T(8,128)}, u32[]{:S(2)}, u32[]{:S(2)}) collective-permute-start(f32[1024,256]{1,0:T(8,128)S(1)} %get-tuple-element.17.refs_2_), channel_id=1, source_target_pairs={{0,1},{2,3},{4,5},{6,7},{8,9},{10,11},{12,13},{14,15},{16,17},{18,... | collective-permute-start | bytes 3145736 | tf_op jit(solution)/shard_map/ppermute | solution.py:305
  123.9 2.3 %collective-permute-start.10 = (f32[1024,256]{1,0:T(8,128)S(1)}, f32[1024,256]{1,0:T(8,128)}, u32[]{:S(2)}, u32[]{:S(2)}) collective-permute-start(f32[1024,256]{1,0:T(8,128)S(1)} %get-tuple-element.18.refs_1_), channel_id=1, source_target_pairs={{0,1},{2,3},{4,5},{6,7},{8,9},{10,11},{12,13},{14,15},{16,17},{18,... | collective-permute-start | bytes 3145736 | tf_op jit(solution)/shard_map/ppermute | solution.py:305
  126.3 13.9 %corner_factor.1.inverse_ref.refs_8_ = f32[256,256]{1,0:T(8,128)S(1)} custom-call(f32[256,256]{1,0:T(8,128)S(1)} %broadcast_select_fusion.10.block_ref, f32[128,256]{1,0:T(8,128)S(1)} %pad_maximum_fusion.9.design_ref, f32[128,128]{1,0:T(8,128)S(1)} %select_n.180.refs_5_.filter_ref, f32[1,256]{1,0:T(1,128)S(1)} %bitcast.10), custom_call_target="tpu_custom_call" | custom-call | flops 1000000000 | bytes 1048576 | tf_op jit(solution)/shard_map/corner_factor/pallas_call | solution.py:82
  142.3 3.9 %filter_sides.1 = (bf16[3072,384]{1,0:T(8,128)(2,1)S(1)}, bf16[384,1536]{1,0:T(8,128)(2,1)S(1)}, f32[256,1536]{1,0:T(8,128)S(1)}, f32[3072,256]{1,0:T(8,128)S(1)}) custom-call(s32[2]{0:T(128)S(1)} %pad_add_fusion.place_ref, f32[32,3328]{1,0:T(8,128)S(1)} %copy-done.5, f32[32,3328]{1,0:T(8,128)S(1)} %collective-permute-done.refs_1_, ...), custom_call_target="tpu_custom_call" | custom-call | flops 905969664 | bytes 9437184 | tf_op jit(solution)/shard_map/filter_sides/pallas_call | solution.py:161
  149.7 6.4 %copy-done = f32[3072,1536]{1,0:T(8,128)S(1)} copy-done((f32[3072,1536]{1,0:T(8,128)S(1)}, f32[3072,1536]{1,0:T(8,128)}, u32[]{:S(2)}) %copy-start) | copy-done | bytes 18874392
  156.0 7.4 %gram_tile.1.system_ref = f32[3072,1536]{1,0:T(8,128)S(1)} custom-call(s32[2]{0:T(128)S(1)} %pad_add_fusion.place_ref, f32[3072,1536]{1,0:T(8,128)S(1)} %copy-done, bf16[3072,384]{1,0:T(8,128)(2,1)S(1)} %get-tuple-element.9.left_ref, bf16[384,1536]{1,0:T(8,128)(2,1)S(1)} %get-tuple-element.10.right_ref, f32[1,1536]{1,0:T(1,128)S(1)} %reshape.99.refs_6_.regular_ref), custom_call_target="tpu_custom_call" | custom-call | flops 3623878656 | bytes 18874368 | tf_op jit(solution)/shard_map/gram_tile/pallas_call | solution.py:206
  164.4 13.9 %tile_rows.1 = f32[3072,1536]{1,0:T(8,128)} custom-call(s32[6]{0:T(128)S(1)} %add.113.block_ids_ref, s32[2]{0:T(128)S(1)} %pad_add_fusion.place_ref, f32[3072,1536]{1,0:T(8,128)S(1)} %gram_tile.1.system_ref, f32[1024,256]{1,0:T(8,128)S(1)} %add_select_fusion.refs_0_, f32[1024,256]{1,0:T(8,128)S(1)} %get-tuple-element.18.refs_1_, ...), custom_call_target="tpu_custom_call" | custom-call | flops 7247757312 | bytes 18874368 | tf_op jit(solution)/shard_map/tile_rows/pallas_call | solution.py:258
  (80 shorter events, 31.8 us)
Async XLA Ops:
  6.5 76.0 %copy-start.8 = (f32[32,1536]{1,0:T(8,128)S(1)}, f32[32,1536]{1,0:T(8,128)}, u32[]{:S(2)}) copy-start(f32[32,1536]{1,0:T(8,128)} %param.5) | copy-start | bytes 589828
  6.5 73.9 %all-gather.2.cloned.1.call-start = ((), (), s32[]{:S(2)}) async-start(), calls=%async_computation | async-start | bytes 1769472 | tf_op jit(solution)/shard_map/all_gather | solution.py:370
  8.2 22.7 %collective-permute-start.16 = (f32[256,256]{1,0:T(8,128)S(1)}, f32[256,256]{1,0:T(8,128)}, u32[]{:S(2)}, u32[]{:S(2)}) collective-permute-start(f32[256,256]{1,0:T(8,128)S(1)} %slice.63), channel_id=1, source_target_pairs={{0,4}} | collective-permute-start | bytes 786440 | tf_op jit(solution)/shard_map/ppermute | solution.py:351
  16.4 52.9 %collective-permute-start.14 = (f32[128,1536]{1,0:T(8,128)S(1)}, f32[128,1536]{1,0:T(8,128)}, u32[]{:S(2)}, u32[]{:S(2)}) collective-permute-start(f32[128,1536]{1,0:T(8,128)S(1)} %get-tuple-element.15), channel_id=1, source_target_pairs={{0,16},{1,17},{2,18},{3,19},{4,20},{5,21},{6,22},{7,23}} | collective-permute-start | bytes 2359304 | tf_op jit(solution)/shard_map/ppermute | solution.py:288
  18.6 52.0 %collective-permute-start.12 = (f32[128,1536]{1,0:T(8,128)S(1)}, f32[128,1536]{1,0:T(8,128)}, u32[]{:S(2)}, u32[]{:S(2)}) collective-permute-start(f32[128,1536]{1,0:T(8,128)S(1)} %get-tuple-element.16), channel_id=1, source_target_pairs={{0,8},{1,9},{2,10},{3,11},{4,12},{5,13},{6,14},{7,15}} | collective-permute-start | bytes 2359304 | tf_op jit(solution)/shard_map/ppermute | solution.py:288
  24.2 59.7 %collective-permute-start.5 = (f32[1024,256]{1,0:T(8,128)}, f32[1024,256]{1,0:T(8,128)}, u32[]{:S(2)}, u32[]{:S(2)}) collective-permute-start(f32[1024,256]{1,0:T(8,128)} %get-tuple-element.19), channel_id=1, source_target_pairs={{0,4},{8,12},{16,20},{24,28}} | collective-permute-start | bytes 3145736 | tf_op jit(solution)/shard_map/ppermute | solution.py:327
  28.1 56.8 %collective-permute-start.4 = (f32[1024,256]{1,0:T(8,128)}, f32[1024,256]{1,0:T(8,128)}, u32[]{:S(2)}, u32[]{:S(2)}) collective-permute-start(f32[1024,256]{1,0:T(8,128)} %get-tuple-element.20), channel_id=1, source_target_pairs={{0,6},{8,14},{16,22},{24,30}} | collective-permute-start | bytes 3145736 | tf_op jit(solution)/shard_map/ppermute | solution.py:327
  31.9 25.7 %collective-permute-start.17 = (f32[256,256]{1,0:T(8,128)S(1)}, f32[256,256]{1,0:T(8,128)}, u32[]{:S(2)}, u32[]{:S(2)}) collective-permute-start(f32[256,256]{1,0:T(8,128)S(1)} %broadcast_select_fusion.6), channel_id=1, source_target_pairs={{0,2},{4,6}} | collective-permute-start | bytes 786440 | tf_op jit(solution)/shard_map/ppermute | solution.py:351
  57.6 5.2 %collective-permute-start.18 = (f32[256,256]{1,0:T(8,128)S(1)}, f32[256,256]{1,0:T(8,128)S(1)}, u32[]{:S(2)}, u32[]{:S(2)}) collective-permute-start(f32[256,256]{1,0:T(8,128)S(1)} %broadcast_select_fusion.7), channel_id=1, source_target_pairs={{0,8},{4,12},{2,10},{6,14}} | collective-permute-start | bytes 786440 | tf_op jit(solution)/shard_map/ppermute | solution.py:351
  62.8 22.2 %collective-permute-start.6 = (f32[1024,256]{1,0:T(8,128)S(1)}, f32[1024,256]{1,0:T(8,128)}, u32[]{:S(2)}, u32[]{:S(2)}) collective-permute-start(f32[1024,256]{1,0:T(8,128)S(1)} %get-tuple-element.21), channel_id=1, source_target_pairs={{0,2},{8,10},{16,18},{24,26}} | collective-permute-start | bytes 3145736 | tf_op jit(solution)/shard_map/ppermute | solution.py:327
  69.3 8.5 %collective-permute-start.19 = (f32[256,256]{1,0:T(8,128)S(1)}, f32[256,256]{1,0:T(8,128)S(1)}, u32[]{:S(2)}, u32[]{:S(2)}) collective-permute-start(f32[256,256]{1,0:T(8,128)S(1)} %broadcast_select_fusion.8), channel_id=1, source_target_pairs={{0,16},{4,20},{2,18},{6,22},{8,24},{12,28},{10,26},{14,30}} | collective-permute-start | bytes 786440 | tf_op jit(solution)/shard_map/ppermute | solution.py:351
  72.2 23.8 %collective-permute-start.15 = (f32[128,1536]{1,0:T(8,128)S(1)}, f32[128,1536]{1,0:T(8,128)}, u32[]{:S(2)}, u32[]{:S(2)}) collective-permute-start(f32[128,1536]{1,0:T(8,128)S(1)} %get-tuple-element.13), channel_id=1, source_target_pairs={{0,8},{16,24},{1,9},{17,25},{2,10},{18,26},{3,11},{19,27},{4,12},{... | collective-permute-start | bytes 2359304 | tf_op jit(solution)/shard_map/ppermute | solution.py:288
  78.5 15.0 %collective-permute-start.20 = (f32[256,256]{1,0:T(8,128)}, f32[256,256]{1,0:T(8,128)}, u32[]{:S(2)}, u32[]{:S(2)}) collective-permute-start(f32[256,256]{1,0:T(8,128)} %broadcast_select_fusion.9), channel_id=1, source_target_pairs={{0,1},{4,5},{2,3},{6,7},{8,9},{12,13},{10,11},{14,15},{16,17},{20,... | collective-permute-start | bytes 786440 | tf_op jit(solution)/shard_map/ppermute | solution.py:351
  83.8 13.2 %collective-permute-start.2 = (f32[32,3328]{1,0:T(8,128)}, f32[32,3328]{1,0:T(8,128)S(1)}, u32[]{:S(2)}, u32[]{:S(2)}) collective-permute-start(f32[32,3328]{1,0:T(8,128)} %get-tuple-element.26), channel_id=1, source_target_pairs={{0,24},{8,0},{16,8},{24,16},{1,25},{9,1},{17,9},{25,17},{2,26},{10... | collective-permute-start | bytes 1277960 | tf_op jit(solution)/shard_map/ppermute | solution.py:279
  87.4 31.3 %collective-permute-start.8 = (f32[1024,256]{1,0:T(8,128)S(1)}, f32[1024,256]{1,0:T(8,128)}, u32[]{:S(2)}, u32[]{:S(2)}) collective-permute-start(f32[1024,256]{1,0:T(8,128)S(1)} %add_select_fusion.refs_0_), channel_id=1, source_target_pairs={{2,6},{4,2},{6,4},{10,14},{12,10},{14,12},{18,22},{20,18},{22,20},... | collective-permute-start | bytes 3145736 | tf_op jit(solution)/shard_map/ppermute | solution.py:334
  89.1 29.6 %collective-permute-start.7 = (f32[1024,256]{1,0:T(8,128)S(1)}, f32[1024,256]{1,0:T(8,128)}, u32[]{:S(2)}, u32[]{:S(2)}) collective-permute-start(f32[1024,256]{1,0:T(8,128)S(1)} %add_select_fusion.refs_0_), channel_id=1, source_target_pairs={{2,4},{4,6},{6,2},{10,12},{12,14},{14,10},{18,20},{20,22},{22,18},... | collective-permute-start | bytes 3145736 | tf_op jit(solution)/shard_map/ppermute | solution.py:334
  93.5 32.7 %collective-permute-start.13 = (f32[128,1536]{1,0:T(8,128)S(1)}, f32[128,1536]{1,0:T(8,128)S(1)}, u32[]{:S(2)}, u32[]{:S(2)}) collective-permute-start(f32[128,1536]{1,0:T(8,128)S(1)} %get-tuple-element.14), channel_id=1, source_target_pairs={{0,16},{8,24},{1,17},{9,25},{2,18},{10,26},{3,19},{11,27},{4,20},{... | collective-permute-start | bytes 2359304 | tf_op jit(solution)/shard_map/ppermute | solution.py:288
  96.0 9.4 %collective-permute-start = (f32[32,3328]{1,0:T(8,128)}, f32[32,3328]{1,0:T(8,128)S(1)}, u32[]{:S(2)}, u32[]{:S(2)}) collective-permute-start(f32[32,3328]{1,0:T(8,128)} %get-tuple-element.27), channel_id=1, source_target_pairs={{0,8},{8,16},{16,24},{24,0},{1,9},{9,17},{17,25},{25,1},{2,10},{10... | collective-permute-start | bytes 1277960 | tf_op jit(solution)/shard_map/ppermute | solution.py:279
  97.1 43.1 %copy-start.6 = (f32[32,3328]{1,0:T(8,128)}, f32[32,3328]{1,0:T(8,128)S(1)}, u32[]{:S(2)}) copy-start(f32[32,3328]{1,0:T(8,128)S(1)} %collective-permute-done.2.refs_3_) | copy-start | bytes 1277956
  97.1 21.4 %collective-permute-start.1 = (f32[32,3328]{1,0:T(8,128)}, f32[32,3328]{1,0:T(8,128)S(1)}, u32[]{:S(2)}, u32[]{:S(2)}) collective-permute-start(f32[32,3328]{1,0:T(8,128)} %get-tuple-element.28), channel_id=1, source_target_pairs={{0,16},{8,24},{16,0},{24,8},{1,17},{9,25},{17,1},{25,9},{2,18},{10... | collective-permute-start | bytes 1277960 | tf_op jit(solution)/shard_map/ppermute | solution.py:279
  105.4 58.1 %collective-permute-start.9 = (f32[1024,256]{1,0:T(8,128)S(1)}, f32[1024,256]{1,0:T(8,128)}, u32[]{:S(2)}, u32[]{:S(2)}) collective-permute-start(f32[1024,256]{1,0:T(8,128)S(1)} %add_select_fusion.refs_0_), channel_id=1, source_target_pairs={{0,1},{2,3},{4,5},{6,7},{8,9},{10,11},{12,13},{14,15},{16,17},{18,... | collective-permute-start | bytes 3145736 | tf_op jit(solution)/shard_map/ppermute | solution.py:305
  118.6 21.6 %collective-permute-start.3 = (f32[128,1536]{1,0:T(8,128)S(1)}, f32[128,1536]{1,0:T(8,128)S(1)}, u32[]{:S(2)}, u32[]{:S(2)}) collective-permute-start(f32[128,1536]{1,0:T(8,128)S(1)} %pad_maximum_fusion.4), channel_id=1, source_target_pairs={{0,1},{1,0},{2,3},{3,2},{4,5},{5,4},{6,7},{7,6},{8,9},{9,8},{10,11... | collective-permute-start | bytes 2359304 | tf_op jit(solution)/shard_map/ppermute | solution.py:378
  120.5 42.9 %collective-permute-start.11 = (f32[1024,256]{1,0:T(8,128)S(1)}, f32[1024,256]{1,0:T(8,128)}, u32[]{:S(2)}, u32[]{:S(2)}) collective-permute-start(f32[1024,256]{1,0:T(8,128)S(1)} %get-tuple-element.17.refs_2_), channel_id=1, source_target_pairs={{0,1},{2,3},{4,5},{6,7},{8,9},{10,11},{12,13},{14,15},{16,17},{18,... | collective-permute-start | bytes 3145736 | tf_op jit(solution)/shard_map/ppermute | solution.py:305
  123.9 39.6 %collective-permute-start.10 = (f32[1024,256]{1,0:T(8,128)S(1)}, f32[1024,256]{1,0:T(8,128)}, u32[]{:S(2)}, u32[]{:S(2)}) collective-permute-start(f32[1024,256]{1,0:T(8,128)S(1)} %get-tuple-element.18.refs_1_), channel_id=1, source_target_pairs={{0,1},{2,3},{4,5},{6,7},{8,9},{10,11},{12,13},{14,15},{16,17},{18,... | collective-permute-start | bytes 3145736 | tf_op jit(solution)/shard_map/ppermute | solution.py:305
  (7 other events, 28.0 us)
Sparse Core Ops, SparseCore 0:
  9.0 27.7 all-gather.1

commit v5 on v4

--- a/solution.py
+++ b/solution.py
@@ -274,6 +274,10 @@
     )(block_ids, place, system, *here, *sent, gram_cols, right, inverse)
 
 
+def after(value, earlier):
+    return lax.optimization_barrier((value, earlier))[0]
+
+
 def shifted(value, axis, by):
     peers = lax.axis_size(axis)
     return lax.ppermute(value, axis, [(i, (i + by) % peers) for i in range(peers)])
@@ -305,7 +309,7 @@
     return lax.ppermute(value, "col", [(c, c + 1) for c in range(0, lax.axis_size("col"), 2)])
 
 
-def row_strip(normals):
+def row_strip(normals, earlier):
     peers = lax.axis_size("col")
     chips = peers // 2
     rows = normals.shape[0]
@@ -322,6 +326,7 @@
     count = chips - 1
     size = rows // count
     local = [normals[i * size : (i + 1) * size, :B] for i in range(count)]
+    local = after(local, earlier)
     arrived = None
     for i in reversed(range(count)):
         got = lax.ppermute(local[i], "col", [(0, 2 * (1 + i))])
@@ -338,20 +343,15 @@
     return pieces
 
 
-def leading_block(normals):
+def doubled(value, bits, reached):
     row_peers, col_peers = lax.axis_size("row"), lax.axis_size("col")
     here = lax.axis_index("row") * col_peers + lax.axis_index("col")
-    total = row_peers * col_peers
-    held = normals[:B, :B]
-    reached = [0]
-    bits = [1 << i for i in range((total - 1).bit_length())]
-    bits = [b for b in reversed(bits) if 1 < b < col_peers] + [b for b in bits if b >= col_peers] + [1]
     for bit in bits:
-        pairs = [(i, i | bit) for i in reached if i | bit < total]
-        got = lax.ppermute(held, ("row", "col"), pairs)
-        held = jnp.where((here & bit) != 0, got, held)
-        reached += [to for _, to in pairs]
-    return held
+        pairs = [(i, i | bit) for i in reached if i | bit < row_peers * col_peers]
+        got = lax.ppermute(value, ("row", "col"), pairs)
+        value = jnp.where((here & bit) != 0, got, value)
+        reached = reached + [to for _, to in pairs]
+    return value, reached
 
 
 def body(normals, design, filter_blocks, regular):
@@ -364,8 +364,13 @@
     obs = row_peers * obs_here
     core = col_index % 2
 
-    corner = leading_block(normals)
-    pieces = row_strip(normals)
+    col_peers = lax.axis_size("col")
+    index_bits = [1 << i for i in range((row_peers * col_peers - 1).bit_length())]
+    along_z = [bit for bit in reversed(index_bits) if 1 < bit < col_peers]
+    block, reached = doubled(normals[:B, :B], along_z, [0])
+    even_corner, reached = doubled(block, [bit for bit in index_bits if bit >= col_peers], reached)
+    corner, _ = doubled(even_corner, [1], reached)
+    pieces = row_strip(normals, block)
 
     along = lax.all_gather(design, "col", axis=1, tiled=True)
     parts = []
@@ -379,10 +384,8 @@
     lead = jnp.concatenate([part[:, 2 * cols_here :] for part in parts], axis=0)
 
     bits = [1 << i for i in range((row_peers - 1).bit_length())]
-    strips = [
-        spread(normals[: B // 2], "row", bits),
-        spread(normals[B // 2 : B], "row", bits[::-1]),
-    ]
+    halves = after([normals[: B // 2], normals[B // 2 : B]], even_corner)
+    strips = [spread(halves[0], "row", bits), spread(halves[1], "row", bits[::-1])]
 
     positions = jnp.arange(obs // P_SIZE, dtype=jnp.int32)
     passed = positions // blocks_here

time: 186 us -> 184 us (0.989)
  the two profiles are of different devices: /device:TPU:0 before, /device:TPU:10 now
where the time goes in v5:
time: 184 us; the launch traced here: 183 us
  starting transfers between devices  54.5 us (30%)
  Pallas kernels  40.8 us (22%)
  waiting for transfers between devices  39.3 us (21%)
  local copies, waits for them, and re-layouts  18.6 us (10%)
  other arithmetic  16.2 us (9%)
  between operations  13.9 us (8%)
    ppermute x2, starting transfers between devices, row_strip(): got = lax.ppermute(mine, 'col', pairs)  27.8 us
    ppermute x5, waiting for transfers between devices, doubled(): got = lax.ppermute(value, ('row', 'col'), pairs)  21.5 us
    pallas_call x1, Pallas kernels, tile_rows(): pl.pallas_call(functools.partial(tile_kernel, count), grid_spec=pltpu.Pre...  13.9 us
    pallas_call x1, Pallas kernels, corner_factor(): pl.pallas_call(corner_kernel, out_shape=jax.ShapeDtypeStruct((B, B), jnp....  13.9 us
    ppermute x2, waiting for transfers between devices, row_strip(): got = lax.ppermute(mine, 'col', pairs)  10.8 us
    unnamed x20, local copies, waits for them, and re-layouts  9 us
    pallas_call x1, Pallas kernels, gram_tile(): pl.pallas_call(gram_kernel, grid_spec=pltpu.PrefetchScalarGridSpec(num_sc...  7.42 us
    ppermute x3, starting transfers between devices, to_odd_core(): lax.ppermute(value, 'col', [(c, c + 1) for c in range(0, lax.axis_size('c...  6.82 us
  transfers between devices with their start and end apart: 22, of which 4 were waited for; matrix products, arithmetic and copies ran while one was open for 14% of the time, Pallas kernels for 15%

profile of v5, /device:TPU:10, one launch (start us, length us, event | category | flops | bytes accessed | tf_op | source)
XLA Modules:
  0.0 183.3 jit_solution(447883923815623897)
XLA Ops:
  8.9 2.7 %fusion.3 = (f32[128,1536]{1,0:T(8,128)}, f32[128,1536]{1,0:T(8,128)}) fusion(f32[3072,1536]{1,0:T(8,128)} %normals_ref.1), kind=kLoop, calls=%fused_computation.39 | loop fusion | bytes 3145728 | tf_op jit(solution)/shard_map/slice | solution.py:387
  13.3 2.1 %fusion.4 = (f32[1024,256]{1,0:T(8,128)S(1)}, f32[1024,256]{1,0:T(8,128)S(1)}, f32[1024,256]{1,0:T(8,128)S(1)}) fusion(f32[3072,1536]{1,0:T(8,128)} %normals_ref.1), kind=kLoop, calls=%fused_computation.40 | loop fusion | bytes 6291456 | tf_op jit(solution)/shard_map/slice | solution.py:328
  16.9 21.5 %collective-permute-done.14 = f32[256,256]{1,0:T(8,128)} collective-permute-done((f32[256,256]{1,0:T(8,128)S(1)}, f32[256,256]{1,0:T(8,128)}, u32[]{:S(2)}, u32[]{:S(2)}) %collective-permute-start.14) | collective-permute-done | bytes 262176 | tf_op jit(solution)/shard_map/ppermute | solution.py:351
  38.3 1.7 broadcast_select_fusion.7
  40.0 2.0 %collective-permute-start.15 = (f32[256,256]{1,0:T(8,128)}, f32[256,256]{1,0:T(8,128)}, u32[]{:S(2)}, u32[]{:S(2)}) collective-permute-start(f32[256,256]{1,0:T(8,128)} %broadcast_select_fusion.7), channel_id=1, source_target_pairs={{0,16},{4,20},{2,18},{6,22},{8,24},{12,28},{10,26},{14,30}} | collective-permute-start | bytes 786440 | tf_op jit(solution)/shard_map/ppermute | solution.py:351
  46.8 1.7 broadcast_select_fusion.8
  48.5 2.0 %collective-permute-start.20 = (f32[256,256]{1,0:T(8,128)}, f32[256,256]{1,0:T(8,128)}, u32[]{:S(2)}, u32[]{:S(2)}) collective-permute-start(f32[256,256]{1,0:T(8,128)} %broadcast_select_fusion.8), channel_id=1, source_target_pairs={{0,1},{4,5},{2,3},{6,7},{8,9},{12,13},{10,11},{14,15},{16,17},{20,... | collective-permute-start | bytes 786440 | tf_op jit(solution)/shard_map/ppermute | solution.py:351
  55.5 3.4 %collective-permute-done.8 = f32[1024,256]{1,0:T(8,128)} collective-permute-done((f32[1024,256]{1,0:T(8,128)S(1)}, f32[1024,256]{1,0:T(8,128)}, u32[]{:S(2)}, u32[]{:S(2)}) %collective-permute-start.8) | collective-permute-done | bytes 1048608 | tf_op jit(solution)/shard_map/ppermute | solution.py:332
  58.9 2.1 %add_select_fusion.refs_0_ = f32[1024,256]{1,0:T(8,128)S(1)} fusion(f32[1024,256]{1,0:T(8,128)} %copy-done.5, f32[1024,256]{1,0:T(8,128)} %collective-permute-done.8, f32[1024,256]{1,0:T(8,128)} %collective-permute-done.6, f32[1024,256]{1,0:T(8,128)} %collective-permute-done.7, pred[]{:T(512)S(6)} %eq.30), kind=kLoop, calls=%fused_computation | loop fusion | flops 786432 | bytes 5242881 | tf_op jit(solution)/shard_map/jit(_where)/select_n | solution.py:335
  61.0 15.5 %collective-permute-start.10 = (f32[1024,256]{1,0:T(8,128)S(1)}, f32[1024,256]{1,0:T(8,128)}, u32[]{:S(2)}, u32[]{:S(2)}) collective-permute-start(f32[1024,256]{1,0:T(8,128)S(1)} %add_select_fusion.refs_0_), channel_id=1, source_target_pairs={{2,6},{4,2},{6,4},{10,14},{12,10},{14,12},{18,22},{20,18},{22,20},... | collective-permute-start | bytes 3145736 | tf_op jit(solution)/shard_map/ppermute | solution.py:339
  76.5 12.3 %collective-permute-start.9 = (f32[1024,256]{1,0:T(8,128)S(1)}, f32[1024,256]{1,0:T(8,128)}, u32[]{:S(2)}, u32[]{:S(2)}) collective-permute-start(f32[1024,256]{1,0:T(8,128)S(1)} %add_select_fusion.refs_0_), channel_id=1, source_target_pairs={{2,4},{4,6},{6,2},{10,12},{12,14},{14,10},{18,20},{20,22},{22,18},... | collective-permute-start | bytes 3145736 | tf_op jit(solution)/shard_map/ppermute | solution.py:339
  88.9 2.1 %broadcast_select_fusion.3 = f32[128,1536]{1,0:T(8,128)} fusion(f32[128,1536]{1,0:T(8,128)} %collective-permute-done.16, f32[128,1536]{1,0:T(8,128)S(1)} %copy-done.8, pred[]{:T(512)S(6)} %ne.103), kind=kLoop, calls=%fused_computation.13 | loop fusion | flops 196608 | bytes 2359297 | tf_op jit(solution)/shard_map/jit(_where)/select_n | solution.py:293
  91.0 2.2 %collective-permute-start.17 = (f32[128,1536]{1,0:T(8,128)}, f32[128,1536]{1,0:T(8,128)}, u32[]{:S(2)}, u32[]{:S(2)}) collective-permute-start(f32[128,1536]{1,0:T(8,128)} %broadcast_select_fusion.3), channel_id=1, source_target_pairs={{0,16},{8,24},{1,17},{9,25},{2,18},{10,26},{3,19},{11,27},{4,20},{... | collective-permute-start | bytes 2359304 | tf_op jit(solution)/shard_map/ppermute | solution.py:292
  97.4 2.9 %collective-permute-start = (f32[32,3328]{1,0:T(8,128)S(1)}, f32[32,3328]{1,0:T(8,128)S(1)}, u32[]{:S(2)}, u32[]{:S(2)}) collective-permute-start(f32[32,3328]{1,0:T(8,128)S(1)} %get-tuple-element.33), channel_id=1, source_target_pairs={{0,8},{8,16},{16,24},{24,0},{1,9},{9,17},{17,25},{25,1},{2,10},{10... | collective-permute-start | bytes 1277960 | tf_op jit(solution)/shard_map/ppermute | solution.py:283
  101.7 10.8 %collective-permute-done.9 = f32[1024,256]{1,0:T(8,128)} collective-permute-done((f32[1024,256]{1,0:T(8,128)S(1)}, f32[1024,256]{1,0:T(8,128)}, u32[]{:S(2)}, u32[]{:S(2)}) %collective-permute-start.9) | collective-permute-done | bytes 1048608 | tf_op jit(solution)/shard_map/ppermute | solution.py:339
  115.2 2.3 %collective-permute-start.11 = (f32[1024,256]{1,0:T(8,128)S(1)}, f32[1024,256]{1,0:T(8,128)}, u32[]{:S(2)}, u32[]{:S(2)}) collective-permute-start(f32[1024,256]{1,0:T(8,128)S(1)} %add_select_fusion.refs_0_), channel_id=1, source_target_pairs={{0,1},{2,3},{4,5},{6,7},{8,9},{10,11},{12,13},{14,15},{16,17},{18,... | collective-permute-start | bytes 3145736 | tf_op jit(solution)/shard_map/ppermute | solution.py:309
  117.5 2.3 %collective-permute-start.13 = (f32[1024,256]{1,0:T(8,128)S(1)}, f32[1024,256]{1,0:T(8,128)}, u32[]{:S(2)}, u32[]{:S(2)}) collective-permute-start(f32[1024,256]{1,0:T(8,128)S(1)} %broadcast_select_fusion.refs_2_), channel_id=1, source_target_pairs={{0,1},{2,3},{4,5},{6,7},{8,9},{10,11},{12,13},{14,15},{16,17},{18,... | collective-permute-start | bytes 3145736 | tf_op jit(solution)/shard_map/ppermute | solution.py:309
  119.8 2.3 %collective-permute-start.12 = (f32[1024,256]{1,0:T(8,128)S(1)}, f32[1024,256]{1,0:T(8,128)}, u32[]{:S(2)}, u32[]{:S(2)}) collective-permute-start(f32[1024,256]{1,0:T(8,128)S(1)} %broadcast_select_fusion.1.refs_1_), channel_id=1, source_target_pairs={{0,1},{2,3},{4,5},{6,7},{8,9},{10,11},{12,13},{14,15},{16,17},{18,... | collective-permute-start | bytes 3145736 | tf_op jit(solution)/shard_map/ppermute | solution.py:309
  123.5 2.9 %collective-permute-done.19 = f32[128,1536]{1,0:T(8,128)S(1)} collective-permute-done((f32[128,1536]{1,0:T(8,128)S(1)}, f32[128,1536]{1,0:T(8,128)S(1)}, u32[]{:S(2)}, u32[]{:S(2)}) %collective-permute-start.19) | collective-permute-done | bytes 786464 | tf_op jit(solution)/shard_map/ppermute | solution.py:292
  126.5 13.9 %corner_factor.1.inverse_ref.refs_8_ = f32[256,256]{1,0:T(8,128)S(1)} custom-call(f32[256,256]{1,0:T(8,128)S(1)} %broadcast_select_fusion.6.block_ref, f32[128,256]{1,0:T(8,128)S(1)} %pad_maximum_fusion.9.design_ref, f32[128,128]{1,0:T(8,128)S(1)} %select_n.180.refs_5_.filter_ref, f32[1,256]{1,0:T(1,128)S(1)} %bitcast.10), custom_call_target="tpu_custom_call" | custom-call | flops 1000000000 | bytes 1048576 | tf_op jit(solution)/shard_map/corner_factor/pallas_call | solution.py:82
  140.4 3.9 %filter_sides.1 = (bf16[3072,384]{1,0:T(8,128)(2,1)S(1)}, bf16[384,1536]{1,0:T(8,128)(2,1)S(1)}, f32[256,1536]{1,0:T(8,128)S(1)}, f32[3072,256]{1,0:T(8,128)S(1)}) custom-call(s32[2]{0:T(128)S(1)} %pad_add_fusion.place_ref, f32[32,3328]{1,0:T(8,128)S(1)} %get-tuple-element.35.refs_0_, f32[32,3328]{1,0:T(8,128)S(1)} %collective-permute-done.refs_1_, ...), custom_call_target="tpu_custom_call" | custom-call | flops 905969664 | bytes 9437184 | tf_op jit(solution)/shard_map/filter_sides/pallas_call | solution.py:161
  147.7 6.4 %copy-done = f32[3072,1536]{1,0:T(8,128)S(1)} copy-done((f32[3072,1536]{1,0:T(8,128)S(1)}, f32[3072,1536]{1,0:T(8,128)}, u32[]{:S(2)}) %copy-start) | copy-done | bytes 18874392
  154.1 7.4 %gram_tile.1.system_ref = f32[3072,1536]{1,0:T(8,128)S(1)} custom-call(s32[2]{0:T(128)S(1)} %pad_add_fusion.place_ref, f32[3072,1536]{1,0:T(8,128)S(1)} %copy-done, bf16[3072,384]{1,0:T(8,128)(2,1)S(1)} %get-tuple-element.14.left_ref, bf16[384,1536]{1,0:T(8,128)(2,1)S(1)} %get-tuple-element.15.right_ref, f32[1,1536]{1,0:T(1,128)S(1)} %reshape.99.refs_6_.regular_ref), custom_call_target="tpu_custom_call" | custom-call | flops 3623878656 | bytes 18874368 | tf_op jit(solution)/shard_map/gram_tile/pallas_call | solution.py:206
  162.5 13.9 %tile_rows.1 = f32[3072,1536]{1,0:T(8,128)} custom-call(s32[6]{0:T(128)S(1)} %add.115.block_ids_ref, s32[2]{0:T(128)S(1)} %pad_add_fusion.place_ref, f32[3072,1536]{1,0:T(8,128)S(1)} %gram_tile.1.system_ref, f32[1024,256]{1,0:T(8,128)S(1)} %add_select_fusion.refs_0_, f32[1024,256]{1,0:T(8,128)S(1)} %broadcast_select_fusion.1.refs_1_, ...), custom_call_target="tpu_custom_call" | custom-call | flops 7247757312 | bytes 18874368 | tf_op jit(solution)/shard_map/tile_rows/pallas_call | solution.py:258
  (84 shorter events, 29.2 us)
Async XLA Ops:
  6.5 87.7 %all-gather.2.cloned.1.call-start = ((), (), s32[]{:S(2)}) async-start(), calls=%async_computation | async-start | bytes 1769472 | tf_op jit(solution)/shard_map/all_gather | solution.py:375
  8.2 3.4 %collective-permute-start.4 = (f32[256,256]{1,0:T(8,128)S(1)}, f32[256,256]{1,0:T(8,128)S(1)}, u32[]{:S(2)}, u32[]{:S(2)}) collective-permute-start(f32[256,256]{1,0:T(8,128)S(1)} %slice.61), channel_id=1, source_target_pairs={{0,4}} | collective-permute-start | bytes 786440 | tf_op jit(solution)/shard_map/ppermute | solution.py:351
  12.6 2.8 %collective-permute-start.5 = (f32[256,256]{1,0:T(8,128)S(1)}, f32[256,256]{1,0:T(8,128)S(1)}, u32[]{:S(2)}, u32[]{:S(2)}) collective-permute-start(f32[256,256]{1,0:T(8,128)S(1)} %broadcast_select_fusion.9), channel_id=1, source_target_pairs={{0,2},{4,6}} | collective-permute-start | bytes 786440 | tf_op jit(solution)/shard_map/ppermute | solution.py:351
  15.4 43.5 %copy-start.5 = (f32[1024,256]{1,0:T(8,128)}, f32[1024,256]{1,0:T(8,128)S(1)}, u32[]{:S(2)}) copy-start(f32[1024,256]{1,0:T(8,128)S(1)} %get-tuple-element.16) | copy-start | bytes 3145732
  15.5 22.9 %collective-permute-start.14 = (f32[256,256]{1,0:T(8,128)S(1)}, f32[256,256]{1,0:T(8,128)}, u32[]{:S(2)}, u32[]{:S(2)}) collective-permute-start(f32[256,256]{1,0:T(8,128)S(1)} %broadcast_select_fusion.10), channel_id=1, source_target_pairs={{0,8},{4,12},{2,10},{6,14}} | collective-permute-start | bytes 786440 | tf_op jit(solution)/shard_map/ppermute | solution.py:351
  40.0 6.8 %collective-permute-start.15 = (f32[256,256]{1,0:T(8,128)}, f32[256,256]{1,0:T(8,128)}, u32[]{:S(2)}, u32[]{:S(2)}) collective-permute-start(f32[256,256]{1,0:T(8,128)} %broadcast_select_fusion.7), channel_id=1, source_target_pairs={{0,16},{4,20},{2,18},{6,22},{8,24},{12,28},{10,26},{14,30}} | collective-permute-start | bytes 786440 | tf_op jit(solution)/shard_map/ppermute | solution.py:351
  42.1 16.8 %collective-permute-start.8 = (f32[1024,256]{1,0:T(8,128)S(1)}, f32[1024,256]{1,0:T(8,128)}, u32[]{:S(2)}, u32[]{:S(2)}) collective-permute-start(f32[1024,256]{1,0:T(8,128)S(1)} %get-tuple-element.16), channel_id=1, source_target_pairs={{0,2},{8,10},{16,18},{24,26}} | collective-permute-start | bytes 3145736 | tf_op jit(solution)/shard_map/ppermute | solution.py:332
  43.4 15.5 %collective-permute-start.6 = (f32[1024,256]{1,0:T(8,128)S(1)}, f32[1024,256]{1,0:T(8,128)}, u32[]{:S(2)}, u32[]{:S(2)}) collective-permute-start(f32[1024,256]{1,0:T(8,128)S(1)} %get-tuple-element.17), channel_id=1, source_target_pairs={{0,6},{8,14},{16,22},{24,30}} | collective-permute-start | bytes 3145736 | tf_op jit(solution)/shard_map/ppermute | solution.py:332
  45.0 13.9 %collective-permute-start.7 = (f32[1024,256]{1,0:T(8,128)S(1)}, f32[1024,256]{1,0:T(8,128)}, u32[]{:S(2)}, u32[]{:S(2)}) collective-permute-start(f32[1024,256]{1,0:T(8,128)S(1)} %get-tuple-element.18), channel_id=1, source_target_pairs={{0,4},{8,12},{16,20},{24,28}} | collective-permute-start | bytes 3145736 | tf_op jit(solution)/shard_map/ppermute | solution.py:332
  48.5 5.2 %collective-permute-start.20 = (f32[256,256]{1,0:T(8,128)}, f32[256,256]{1,0:T(8,128)}, u32[]{:S(2)}, u32[]{:S(2)}) collective-permute-start(f32[256,256]{1,0:T(8,128)} %broadcast_select_fusion.8), channel_id=1, source_target_pairs={{0,1},{4,5},{2,3},{6,7},{8,9},{12,13},{10,11},{14,15},{16,17},{20,... | collective-permute-start | bytes 786440 | tf_op jit(solution)/shard_map/ppermute | solution.py:351
  50.5 38.4 %collective-permute-start.16 = (f32[128,1536]{1,0:T(8,128)}, f32[128,1536]{1,0:T(8,128)}, u32[]{:S(2)}, u32[]{:S(2)}) collective-permute-start(f32[128,1536]{1,0:T(8,128)} %get-tuple-element.20), channel_id=1, source_target_pairs={{0,8},{1,9},{2,10},{3,11},{4,12},{5,13},{6,14},{7,15}} | collective-permute-start | bytes 2359304 | tf_op jit(solution)/shard_map/ppermute | solution.py:292
  53.7 39.5 %collective-permute-start.18 = (f32[128,1536]{1,0:T(8,128)}, f32[128,1536]{1,0:T(8,128)S(1)}, u32[]{:S(2)}, u32[]{:S(2)}) collective-permute-start(f32[128,1536]{1,0:T(8,128)} %get-tuple-element.21), channel_id=1, source_target_pairs={{0,16},{1,17},{2,18},{3,19},{4,20},{5,21},{6,22},{7,23}} | collective-permute-start | bytes 2359304 | tf_op jit(solution)/shard_map/ppermute | solution.py:292
  55.5 37.7 %copy-start.7 = (f32[128,1536]{1,0:T(8,128)S(1)}, f32[128,1536]{1,0:T(8,128)}, u32[]{:S(2)}) copy-start(f32[128,1536]{1,0:T(8,128)} %get-tuple-element.21) | copy-start | bytes 2359300
  61.0 39.3 %collective-permute-start.10 = (f32[1024,256]{1,0:T(8,128)S(1)}, f32[1024,256]{1,0:T(8,128)}, u32[]{:S(2)}, u32[]{:S(2)}) collective-permute-start(f32[1024,256]{1,0:T(8,128)S(1)} %add_select_fusion.refs_0_), channel_id=1, source_target_pairs={{2,6},{4,2},{6,4},{10,14},{12,10},{14,12},{18,22},{20,18},{22,20},... | collective-permute-start | bytes 3145736 | tf_op jit(solution)/shard_map/ppermute | solution.py:339
  76.5 36.0 %collective-permute-start.9 = (f32[1024,256]{1,0:T(8,128)S(1)}, f32[1024,256]{1,0:T(8,128)}, u32[]{:S(2)}, u32[]{:S(2)}) collective-permute-start(f32[1024,256]{1,0:T(8,128)S(1)} %add_select_fusion.refs_0_), channel_id=1, source_target_pairs={{2,4},{4,6},{6,2},{10,12},{12,14},{14,10},{18,20},{20,22},{22,18},... | collective-permute-start | bytes 3145736 | tf_op jit(solution)/shard_map/ppermute | solution.py:339
  91.0 31.1 %collective-permute-start.17 = (f32[128,1536]{1,0:T(8,128)}, f32[128,1536]{1,0:T(8,128)}, u32[]{:S(2)}, u32[]{:S(2)}) collective-permute-start(f32[128,1536]{1,0:T(8,128)} %broadcast_select_fusion.3), channel_id=1, source_target_pairs={{0,16},{8,24},{1,17},{9,25},{2,18},{10,26},{3,19},{11,27},{4,20},{... | collective-permute-start | bytes 2359304 | tf_op jit(solution)/shard_map/ppermute | solution.py:292
  97.4 17.8 %collective-permute-start.2 = (f32[32,3328]{1,0:T(8,128)S(1)}, f32[32,3328]{1,0:T(8,128)S(1)}, u32[]{:S(2)}, u32[]{:S(2)}) collective-permute-start(f32[32,3328]{1,0:T(8,128)S(1)} %get-tuple-element.32), channel_id=1, source_target_pairs={{0,24},{8,0},{16,8},{24,16},{1,25},{9,1},{17,9},{25,17},{2,26},{10... | collective-permute-start | bytes 1277960 | tf_op jit(solution)/shard_map/ppermute | solution.py:283
  97.4 20.0 %collective-permute-start = (f32[32,3328]{1,0:T(8,128)S(1)}, f32[32,3328]{1,0:T(8,128)S(1)}, u32[]{:S(2)}, u32[]{:S(2)}) collective-permute-start(f32[32,3328]{1,0:T(8,128)S(1)} %get-tuple-element.33), channel_id=1, source_target_pairs={{0,8},{8,16},{16,24},{24,0},{1,9},{9,17},{17,25},{25,1},{2,10},{10... | collective-permute-start | bytes 1277960 | tf_op jit(solution)/shard_map/ppermute | solution.py:283
  100.4 19.4 %collective-permute-start.1 = (f32[32,3328]{1,0:T(8,128)S(1)}, f32[32,3328]{1,0:T(8,128)S(1)}, u32[]{:S(2)}, u32[]{:S(2)}) collective-permute-start(f32[32,3328]{1,0:T(8,128)S(1)} %get-tuple-element.34), channel_id=1, source_target_pairs={{0,16},{8,24},{16,0},{24,8},{1,17},{9,25},{17,1},{25,9},{2,18},{10... | collective-permute-start | bytes 1277960 | tf_op jit(solution)/shard_map/ppermute | solution.py:283
  112.5 13.9 %collective-permute-start.19 = (f32[128,1536]{1,0:T(8,128)S(1)}, f32[128,1536]{1,0:T(8,128)S(1)}, u32[]{:S(2)}, u32[]{:S(2)}) collective-permute-start(f32[128,1536]{1,0:T(8,128)S(1)} %copy-done.6), channel_id=1, source_target_pairs={{0,8},{16,24},{1,9},{17,25},{2,10},{18,26},{3,11},{19,27},{4,12},{... | collective-permute-start | bytes 2359304 | tf_op jit(solution)/shard_map/ppermute | solution.py:292
  115.2 46.4 %collective-permute-start.11 = (f32[1024,256]{1,0:T(8,128)S(1)}, f32[1024,256]{1,0:T(8,128)}, u32[]{:S(2)}, u32[]{:S(2)}) collective-permute-start(f32[1024,256]{1,0:T(8,128)S(1)} %add_select_fusion.refs_0_), channel_id=1, source_target_pairs={{0,1},{2,3},{4,5},{6,7},{8,9},{10,11},{12,13},{14,15},{16,17},{18,... | collective-permute-start | bytes 3145736 | tf_op jit(solution)/shard_map/ppermute | solution.py:309
  117.5 44.1 %collective-permute-start.13 = (f32[1024,256]{1,0:T(8,128)S(1)}, f32[1024,256]{1,0:T(8,128)}, u32[]{:S(2)}, u32[]{:S(2)}) collective-permute-start(f32[1024,256]{1,0:T(8,128)S(1)} %broadcast_select_fusion.refs_2_), channel_id=1, source_target_pairs={{0,1},{2,3},{4,5},{6,7},{8,9},{10,11},{12,13},{14,15},{16,17},{18,... | collective-permute-start | bytes 3145736 | tf_op jit(solution)/shard_map/ppermute | solution.py:309
  119.8 41.8 %collective-permute-start.12 = (f32[1024,256]{1,0:T(8,128)S(1)}, f32[1024,256]{1,0:T(8,128)}, u32[]{:S(2)}, u32[]{:S(2)}) collective-permute-start(f32[1024,256]{1,0:T(8,128)S(1)} %broadcast_select_fusion.1.refs_1_), channel_id=1, source_target_pairs={{0,1},{2,3},{4,5},{6,7},{8,9},{10,11},{12,13},{14,15},{16,17},{18,... | collective-permute-start | bytes 3145736 | tf_op jit(solution)/shard_map/ppermute | solution.py:309
  122.2 18.3 %collective-permute-start.3 = (f32[128,1536]{1,0:T(8,128)S(1)}, f32[128,1536]{1,0:T(8,128)S(1)}, u32[]{:S(2)}, u32[]{:S(2)}) collective-permute-start(f32[128,1536]{1,0:T(8,128)S(1)} %pad_maximum_fusion.4), channel_id=1, source_target_pairs={{0,1},{1,0},{2,3},{3,2},{4,5},{5,4},{6,7},{7,6},{8,9},{9,8},{10,11... | collective-permute-start | bytes 2359304 | tf_op jit(solution)/shard_map/ppermute | solution.py:383
  (8 other events, 79.6 us)
Sparse Core Ops, SparseCore 0:
  9.0 26.0 all-gather.1

commit v6 on v5

--- a/solution.py
+++ b/solution.py
@@ -89,8 +89,8 @@
     )(block, design, filter_matrix, regular)
 
 
-def right_kernel(place_ref, high_ref, low_ref, gram_ref, inverse_ref, out_ref):
-    strip = jnp.concatenate([high_ref[...], low_ref[...]], axis=0) + gram_ref[...]
+def right_kernel(place_ref, strip_ref, gram_ref, inverse_ref, out_ref):
+    strip = strip_ref[...] + gram_ref[...]
     panel_high, panel_low = split(-split_dot(inverse_ref[...].T, strip))
     out_ref[:B, :] = panel_high
     out_ref[B : 2 * B, :] = panel_low
@@ -106,11 +106,11 @@
         out_ref[2 * B :, :B] = identity
 
 
-def right_side(place, strips, gram_rows, inverse):
+def right_side(place, strip, gram_rows, inverse):
     cols = gram_rows.shape[1]
     return pl.pallas_call(
         right_kernel,
-        in_specs=[pl.BlockSpec(memory_space=pltpu.SMEM)] + [pl.BlockSpec(memory_space=pltpu.VMEM)] * 4,
+        in_specs=[pl.BlockSpec(memory_space=pltpu.SMEM)] + [pl.BlockSpec(memory_space=pltpu.VMEM)] * 3,
         out_specs=pl.BlockSpec(memory_space=pltpu.VMEM),
         out_shape=jax.ShapeDtypeStruct((3 * B, cols), jnp.bfloat16),
         compiler_params=pltpu.CompilerParams(vmem_limit_bytes=20 * 2**20),
@@ -118,7 +118,7 @@
             flops=6 * cols * B * B, bytes_accessed=12 * cols * B, transcendentals=0
         ),
         name="right_side",
-    )(place, *strips, gram_rows, inverse)
+    )(place, strip, gram_rows, inverse)
 
 
 def filter_kernel(count, place_ref, *refs):
@@ -216,7 +216,7 @@
             ],
             out_specs=tile_spec,
         ),
-        out_shape=pltpu.VMEM((rows, cols), jnp.float32),
+        out_shape=jax.ShapeDtypeStruct((rows, cols), jnp.float32),
         compiler_params=pltpu.CompilerParams(vmem_limit_bytes=8 * 2**20),
         cost_estimate=pl.CostEstimate(
             flops=2 * rows * cols * depth, bytes_accessed=4 * rows * cols, transcendentals=0
@@ -225,53 +225,36 @@
     )(place, normals, left, right, regular)
 
 
-def tile_kernel(count, block_ids_ref, place_ref, system_ref, *refs):
-    here_refs, sent_refs = refs[:count], refs[count : 2 * count]
-    gram_ref, right_ref, inverse_ref, out_ref = refs[2 * count :]
-    step = pl.program_id(0)
-    block = out_ref.shape[0]
-    per_piece = pl.num_programs(0) // count
-    even = lax.rem(place_ref[1], 2) == 0
-    slot = step // per_piece
-    rows = pl.ds(pl.multiple_of(lax.rem(step, per_piece) * block, block), block)
-    strip = jnp.where(even, here_refs[0][rows, :], sent_refs[0][rows, :])
-    for i in range(1, count):
-        strip = jnp.where(slot == i, jnp.where(even, here_refs[i][rows, :], sent_refs[i][rows, :]), strip)
-    panel = split_dot(strip + gram_ref[...], inverse_ref[...])
+def tile_kernel(system_ref, strip_ref, gram_ref, right_ref, inverse_ref, out_ref):
+    panel = split_dot(strip_ref[...] + gram_ref[...], inverse_ref[...])
     high, low = split(panel)
     left = jnp.concatenate([high, high, low], axis=1)
     out_ref[...] = system_ref[...] + jnp.dot(left, right_ref[...], preferred_element_type=jnp.float32)
 
 
-def tile_rows(place, block_ids, system, here, sent, gram_cols, right, inverse):
+def tile_rows(system, strip, gram_cols, right, inverse):
     rows, cols = system.shape
-    count = len(here)
-    block = rows // block_ids.shape[0]
-
-    def whole(array):
-        return pl.BlockSpec(
-            array.shape, lambda i, ids, place: (0,) * array.ndim, pipeline_mode=pl.Buffered(1)
-        )
-
-    tile_spec = pl.BlockSpec((block, cols), lambda i, ids, place: (ids[i], 0))
-    gram_spec = pl.BlockSpec((block, B), lambda i, ids, place: (ids[i], 0))
-    return pl.pallas_call(
-        functools.partial(tile_kernel, count),
-        grid_spec=pltpu.PrefetchScalarGridSpec(
-            num_scalar_prefetch=2,
-            grid=(block_ids.shape[0],),
-            in_specs=[tile_spec]
-            + [whole(array) for array in [*here, *sent]]
-            + [gram_spec, whole(right), whole(inverse)],
-            out_specs=tile_spec,
-        ),
+    block = block_rows(rows // 2)
+    tile_spec = pl.BlockSpec((block, cols), lambda i: (i, 0))
+    lead_spec = pl.BlockSpec((block, B), lambda i: (i, 0))
+    return pl.pallas_call(
+        tile_kernel,
+        grid=(rows // block,),
+        in_specs=[
+            tile_spec,
+            lead_spec,
+            lead_spec,
+            pl.BlockSpec(right.shape, lambda i: (0, 0), pipeline_mode=pl.Buffered(1)),
+            pl.BlockSpec(inverse.shape, lambda i: (0, 0), pipeline_mode=pl.Buffered(1)),
+        ],
+        out_specs=tile_spec,
         out_shape=jax.ShapeDtypeStruct((rows, cols), jnp.float32),
-        compiler_params=pltpu.CompilerParams(vmem_limit_bytes=16 * 2**20),
+        compiler_params=pltpu.CompilerParams(vmem_limit_bytes=22 * 2**20),
         cost_estimate=pl.CostEstimate(
             flops=6 * rows * cols * B, bytes_accessed=4 * rows * cols, transcendentals=0
         ),
         name="tile_rows",
-    )(block_ids, place, system, *here, *sent, gram_cols, right, inverse)
+    )(system, strip, gram_cols, right, inverse)
 
 
 def after(value, earlier):
@@ -281,18 +264,6 @@
 def shifted(value, axis, by):
     peers = lax.axis_size(axis)
     return lax.ppermute(value, axis, [(i, (i + by) % peers) for i in range(peers)])
-
-
-def spread(value, axis, bits):
-    peers = lax.axis_size(axis)
-    me = lax.axis_index(axis)
-    reached = [0]
-    for bit in bits:
-        pairs = [(i, i | bit) for i in reached if i | bit < peers]
-        got = lax.ppermute(value, axis, pairs)
-        value = jnp.where((me & bit) != 0, got, value)
-        reached += [to for _, to in pairs]
-    return value
 
 
 def filter_matrix_of(filter_blocks, sources):
@@ -305,42 +276,18 @@
     return blocks.reshape(count * P_SIZE, count * P_SIZE)
 
 
-def to_odd_core(value):
-    return lax.ppermute(value, "col", [(c, c + 1) for c in range(0, lax.axis_size("col"), 2)])
-
-
-def row_strip(normals, earlier):
+def row_strip_piece(normals):
     peers = lax.axis_size("col")
     chips = peers // 2
-    rows = normals.shape[0]
+    size = normals.shape[0] // chips
     col_index = lax.axis_index("col")
-    chip = col_index // 2
-    if chips > 4:
-        size = rows // chips
-        share = normals[:size, :B]
-        for z in range(1, chips):
-            got = lax.ppermute(normals[z * size : (z + 1) * size, :B], "col", [(0, 2 * z)])
-            share = jnp.where(chip == z, got, share)
-        cores = [list(range(k, peers, 2)) for k in range(2)]
-        return [(jnp.int32(0), lax.all_gather(share, "col", axis=0, tiled=True, axis_index_groups=cores))]
-    count = chips - 1
-    size = rows // count
-    local = [normals[i * size : (i + 1) * size, :B] for i in range(count)]
-    local = after(local, earlier)
     arrived = None
-    for i in reversed(range(count)):
-        got = lax.ppermute(local[i], "col", [(0, 2 * (1 + i))])
+    for z in reversed(range(1, chips)):
+        got = lax.ppermute(normals[z * size : (z + 1) * size, :B], "col", [(0, 2 * z)])
         arrived = got if arrived is None else arrived + got
-    at_source = chip == 0
-    mine = jnp.where(at_source, local[0], arrived)
-    pieces = [(jnp.where(at_source, 0, chip - 1), mine)]
-    for s in range(1, count):
-        pairs = [(2 * (1 + i), 2 * (1 + (i + s) % count)) for i in range(count)]
-        got = lax.ppermute(mine, "col", pairs)
-        which = -s % count
-        piece = jnp.where(at_source, local[which], got)
-        pieces.append((jnp.where(at_source, which, (chip - 1 - s) % count), piece))
-    return pieces
+    piece = jnp.where(col_index == 0, normals[:size, :B], arrived)
+    second = lax.ppermute(piece[size // 2 :], "col", [(c, c + 1) for c in range(0, peers, 2)])
+    return jnp.where(col_index % 2 == 0, piece[: size // 2], second)
 
 
 def doubled(value, bits, reached):
@@ -365,12 +312,15 @@
     core = col_index % 2
 
     col_peers = lax.axis_size("col")
+    piece = row_strip_piece(normals)
+    strip = lax.all_gather(piece, "col", axis=0, tiled=True)
+
     index_bits = [1 << i for i in range((row_peers * col_peers - 1).bit_length())]
-    along_z = [bit for bit in reversed(index_bits) if 1 < bit < col_peers]
-    block, reached = doubled(normals[:B, :B], along_z, [0])
-    even_corner, reached = doubled(block, [bit for bit in index_bits if bit >= col_peers], reached)
-    corner, _ = doubled(even_corner, [1], reached)
-    pieces = row_strip(normals, block)
+    block, reached = doubled(normals[:B, :B], [bit for bit in index_bits if bit >= col_peers], [0])
+    block = after(block, piece)
+    corner, _ = doubled(block, [bit for bit in reversed(index_bits) if bit < col_peers], reached)
+
+    col_strip = lax.psum(jnp.where(row_index == 0, normals[:B], 0.0), "row")
 
     along = lax.all_gather(design, "col", axis=1, tiled=True)
     parts = []
@@ -383,10 +333,6 @@
     other = lax.ppermute(own, "col", [(c, c ^ 1) for c in range(lax.axis_size("col"))])
     lead = jnp.concatenate([part[:, 2 * cols_here :] for part in parts], axis=0)
 
-    bits = [1 << i for i in range((row_peers - 1).bit_length())]
-    halves = after([normals[: B // 2], normals[B // 2 : B]], even_corner)
-    strips = [spread(halves[0], "row", bits), spread(halves[1], "row", bits[::-1])]
-
     positions = jnp.arange(obs // P_SIZE, dtype=jnp.int32)
     passed = positions // blocks_here
     order = ((row_index - passed) % row_peers) * blocks_here + positions % blocks_here
@@ -397,16 +343,8 @@
     inverse = corner_factor(corner, lead, filters, lead_reg)
     gram_left, gram_right, gram_rows, gram_cols = filter_sides(place, parts, other, filters, own_reg, lead_reg)
     system = gram_tile(place, normals, gram_left, gram_right, own_reg)
-    system = pltpu.with_memory_space_constraint(system, pltpu.VMEM)
-    right = right_side(place, strips, gram_rows, inverse)
-
-    here = [piece for _, piece in pieces]
-    sent = [to_odd_core(piece) for piece in here]
-    per_piece = here[0].shape[0] // block_rows(rows_here // 2)
-    which = jnp.stack([index for index, _ in pieces])
-    block_ids = which[:, None] * per_piece + jnp.arange(per_piece, dtype=jnp.int32)[None, :]
-    block_ids = block_ids.reshape(-1).astype(jnp.int32)
-    return tile_rows(place, block_ids, system, here, sent, gram_cols, right, inverse)
+    right = right_side(place, col_strip, gram_rows, inverse)
+    return tile_rows(system, strip, gram_cols, right, inverse)
 
 
 def solution(mesh):

time: 184 us -> 203 us (1.10)
  the two profiles are of different devices: /device:TPU:10 before, /device:TPU:0 now
where the time goes in v6:
time: 203 us; the launch traced here: 201 us
  waiting for transfers between devices  62.5 us (31%)
  local copies, waits for them, and re-layouts  41.6 us (20%)
  Pallas kernels  38.3 us (19%)
  starting transfers between devices  35.1 us (17%)
  between operations  15.3 us (8%)
  other arithmetic  7.74 us (4%)
    unnamed x40, local copies, waits for them, and re-layouts  35 us
    ppermute x3, waiting for transfers between devices, row_strip_piece(): lax.ppermute(normals[z * size:(z + 1) * size, :B], 'col', [(0, 2 * z)])  31.7 us
    ppermute x5, waiting for transfers between devices, doubled(): got = lax.ppermute(value, ('row', 'col'), pairs)  18.7 us
    pallas_call x1, Pallas kernels, corner_factor(): pl.pallas_call(corner_kernel, out_shape=jax.ShapeDtypeStruct((B, B), jnp....  13.9 us
    ppermute x3, starting transfers between devices, shifted(): lax.ppermute(value, axis, [(i, (i + by) % peers) for i in range(peers)])  13.3 us
    pallas_call x1, Pallas kernels, tile_rows(): pl.pallas_call(tile_kernel, grid=(rows // block,), in_specs=[tile_spec, l...  11.4 us
    ppermute x3, starting transfers between devices, row_strip_piece(): lax.ppermute(normals[z * size:(z + 1) * size, :B], 'col', [(0, 2 * z)])  10.4 us
    ppermute x5, starting transfers between devices, doubled(): got = lax.ppermute(value, ('row', 'col'), pairs)  10 us
  transfers between devices with their start and end apart: 16, of which 10 were waited for; matrix products, arithmetic and copies ran while one was open for 7% of the time, Pallas kernels for 13%

profile of v6, /device:TPU:0, one launch (start us, length us, event | category | flops | bytes accessed | tf_op | source)
XLA Modules:
  0.0 200.6 jit_solution(3899590348422861349)
XLA Ops:
  9.9 6.0 %collective-permute-start.5 = (f32[768,256]{1,0:T(8,128)S(1)}, f32[768,256]{1,0:T(8,128)S(1)}, u32[]{:S(2)}, u32[]{:S(2)}) collective-permute-start(f32[768,256]{1,0:T(8,128)S(1)} %get-tuple-element.15), channel_id=1, source_target_pairs={{0,4},{8,12},{16,20},{24,28}} | collective-permute-start | bytes 2359304 | tf_op jit(solution)/shard_map/ppermute | solution.py:286
  15.9 2.2 %collective-permute-start.6 = (f32[768,256]{1,0:T(8,128)S(1)}, f32[768,256]{1,0:T(8,128)}, u32[]{:S(2)}, u32[]{:S(2)}) collective-permute-start(f32[768,256]{1,0:T(8,128)S(1)} %get-tuple-element.16), channel_id=1, source_target_pairs={{0,2},{8,10},{16,18},{24,26}} | collective-permute-start | bytes 2359304 | tf_op jit(solution)/shard_map/ppermute | solution.py:286
  18.1 2.2 %collective-permute-start.4 = (f32[768,256]{1,0:T(8,128)S(1)}, f32[768,256]{1,0:T(8,128)}, u32[]{:S(2)}, u32[]{:S(2)}) collective-permute-start(f32[768,256]{1,0:T(8,128)S(1)} %get-tuple-element.17), channel_id=1, source_target_pairs={{0,6},{8,14},{16,22},{24,30}} | collective-permute-start | bytes 2359304 | tf_op jit(solution)/shard_map/ppermute | solution.py:286
  20.3 2.7 %slice_select_fusion = f32[256,1536]{1,0:T(8,128)} fusion(f32[3072,1536]{1,0:T(8,128)} %normals_ref.1, pred[]{:T(512)S(6)} %eq.39), kind=kLoop, calls=%fused_computation | loop fusion | flops 393216 | bytes 3145729 | tf_op jit(solution)/shard_map/jit(_where)/select_n | solution.py:323
  23.1 11.8 %collective-permute-done.5 = f32[768,256]{1,0:T(8,128)S(1)} collective-permute-done((f32[768,256]{1,0:T(8,128)S(1)}, f32[768,256]{1,0:T(8,128)S(1)}, u32[]{:S(2)}, u32[]{:S(2)}) %collective-permute-start.5) | collective-permute-done | bytes 786464 | tf_op jit(solution)/shard_map/ppermute | solution.py:286
  34.9 11.5 %collective-permute-done.6 = f32[768,256]{1,0:T(8,128)} collective-permute-done((f32[768,256]{1,0:T(8,128)S(1)}, f32[768,256]{1,0:T(8,128)}, u32[]{:S(2)}, u32[]{:S(2)}) %collective-permute-start.6) | collective-permute-done | bytes 786464 | tf_op jit(solution)/shard_map/ppermute | solution.py:286
  46.4 8.4 %collective-permute-done.4 = f32[768,256]{1,0:T(8,128)} collective-permute-done((f32[768,256]{1,0:T(8,128)S(1)}, f32[768,256]{1,0:T(8,128)}, u32[]{:S(2)}, u32[]{:S(2)}) %collective-permute-start.4) | collective-permute-done | bytes 786464 | tf_op jit(solution)/shard_map/ppermute | solution.py:286
  61.2 3.4 %collective-permute-start.8 = (f32[256,256]{1,0:T(8,128)S(1)}, f32[256,256]{1,0:T(8,128)S(1)}, u32[]{:S(2)}, u32[]{:S(2)}) collective-permute-start(f32[256,256]{1,0:T(8,128)S(1)} %slice.71), channel_id=1, source_target_pairs={{0,8}} | collective-permute-start | bytes 786440 | tf_op jit(solution)/shard_map/ppermute | solution.py:298
  64.6 3.8 %collective-permute-done.8 = f32[256,256]{1,0:T(8,128)S(1)} collective-permute-done((f32[256,256]{1,0:T(8,128)S(1)}, f32[256,256]{1,0:T(8,128)S(1)}, u32[]{:S(2)}, u32[]{:S(2)}) %collective-permute-start.8) | collective-permute-done | bytes 262176 | tf_op jit(solution)/shard_map/ppermute | solution.py:298
  70.8 7.0 %collective-permute-done.9 = f32[256,256]{1,0:T(8,128)S(1)} collective-permute-done((f32[256,256]{1,0:T(8,128)S(1)}, f32[256,256]{1,0:T(8,128)S(1)}, u32[]{:S(2)}, u32[]{:S(2)}) %collective-permute-start.9) | collective-permute-done | bytes 262176 | tf_op jit(solution)/shard_map/ppermute | solution.py:298
  80.7 7.9 %collective-permute-done.10 = f32[256,256]{1,0:T(8,128)S(1)} collective-permute-done((f32[256,256]{1,0:T(8,128)S(1)}, f32[256,256]{1,0:T(8,128)S(1)}, u32[]{:S(2)}, u32[]{:S(2)}) %collective-permute-start.10) | collective-permute-done | bytes 262176 | tf_op jit(solution)/shard_map/ppermute | solution.py:298
  88.6 2.0 %collective-permute-start.11 = (f32[256,256]{1,0:T(8,128)S(1)}, f32[256,256]{1,0:T(8,128)}, u32[]{:S(2)}, u32[]{:S(2)}) collective-permute-start(f32[256,256]{1,0:T(8,128)S(1)} %broadcast_select_fusion.2), channel_id=1, source_target_pairs={{0,2},{8,10},{16,18},{24,26},{4,6},{12,14},{20,22},{28,30}} | collective-permute-start | bytes 786440 | tf_op jit(solution)/shard_map/ppermute | solution.py:298
  92.9 12.7 %collective-permute-start.2 = (f32[32,3328]{1,0:T(8,128)S(1)}, f32[32,3328]{1,0:T(8,128)S(1)}, u32[]{:S(2)}, u32[]{:S(2)}) collective-permute-start(f32[32,3328]{1,0:T(8,128)S(1)} %get-tuple-element.22), channel_id=1, source_target_pairs={{0,24},{8,0},{16,8},{24,16},{1,25},{9,1},{17,9},{25,17},{2,26},{10... | collective-permute-start | bytes 1277960 | tf_op jit(solution)/shard_map/ppermute | solution.py:266
  106.3 2.0 collective-permute-start.12
  108.3 3.0 %collective-permute-done.2.refs_3_ = f32[32,3328]{1,0:T(8,128)S(1)} collective-permute-done((f32[32,3328]{1,0:T(8,128)S(1)}, f32[32,3328]{1,0:T(8,128)S(1)}, u32[]{:S(2)}, u32[]{:S(2)}) %collective-permute-start.2) | collective-permute-done | bytes 426016 | tf_op jit(solution)/shard_map/ppermute | solution.py:266
  111.3 5.1 %collective-permute-done.refs_1_ = f32[32,3328]{1,0:T(8,128)S(1)} collective-permute-done((f32[32,3328]{1,0:T(8,128)S(1)}, f32[32,3328]{1,0:T(8,128)S(1)}, u32[]{:S(2)}, u32[]{:S(2)}) %collective-permute-start) | collective-permute-done | bytes 426016 | tf_op jit(solution)/shard_map/ppermute | solution.py:266
  116.4 1.9 collective-permute-done.1.refs_2_
  119.7 13.9 %corner_factor.1.inverse_ref = f32[256,256]{1,0:T(8,128)S(1)} custom-call(f32[256,256]{1,0:T(8,128)S(1)} %broadcast_select_fusion.4.block_ref, f32[128,256]{1,0:T(8,128)S(1)} %pad_maximum_fusion.9.design_ref, f32[128,128]{1,0:T(8,128)S(1)} %select_n.140.refs_5_.filter_ref, f32[1,256]{1,0:T(1,128)S(1)} %bitcast.7), custom_call_target="tpu_custom_call" | custom-call | flops 1000000000 | bytes 1048576 | tf_op jit(solution)/shard_map/corner_factor/pallas_call | solution.py:82
  136.3 3.9 %filter_sides.1 = (bf16[3072,384]{1,0:T(8,128)(2,1)S(1)}, bf16[384,1536]{1,0:T(8,128)(2,1)S(1)}, f32[256,1536]{1,0:T(8,128)S(1)}, f32[3072,256]{1,0:T(8,128)S(1)}) custom-call(s32[2]{0:T(128)S(1)} %pad_add_fusion.place_ref, f32[32,3328]{1,0:T(8,128)S(1)} %get-tuple-element.25.refs_0_, f32[32,3328]{1,0:T(8,128)S(1)} %collective-permute-done.refs_1_, ...), custom_call_target="tpu_custom_call" | custom-call | flops 905969664 | bytes 9437184 | tf_op jit(solution)/shard_map/filter_sides/pallas_call | solution.py:161
  150.0 6.4 %copy-done.2 = f32[3072,1536]{1,0:T(8,128)S(1)} copy-done((f32[3072,1536]{1,0:T(8,128)S(1)}, f32[3072,1536]{1,0:T(8,128)}, u32[]{:S(2)}) %copy-start.2) | copy-done | bytes 18874392
  156.3 7.4 %gram_tile.1.system_ref = f32[3072,1536]{1,0:T(8,128)S(1)} custom-call(s32[2]{0:T(128)S(1)} %pad_add_fusion.place_ref, f32[3072,1536]{1,0:T(8,128)S(1)} %copy-done.2, bf16[3072,384]{1,0:T(8,128)(2,1)S(1)} %copy-done.7, bf16[384,1536]{1,0:T(8,128)(2,1)S(1)} %get-tuple-element.11.right_ref, f32[1,1536]{1,0:T(1,128)S(1)} %reshape.69.refs_6_.regular_ref), custom_call_target="tpu_custom_call" | custom-call | flops 3623878656 | bytes 18874368 | tf_op jit(solution)/shard_map/gram_tile/pallas_call | solution.py:206
  163.8 6.8 %copy-done = f32[3072,1536]{1,0:T(8,128)} copy-done((f32[3072,1536]{1,0:T(8,128)}, f32[3072,1536]{1,0:T(8,128)S(1)}, u32[]{:S(2)}) %copy-start) | copy-done | bytes 18874392
  170.6 6.4 %copy-done.1 = f32[3072,1536]{1,0:T(8,128)S(1)} copy-done((f32[3072,1536]{1,0:T(8,128)S(1)}, f32[3072,1536]{1,0:T(8,128)}, u32[]{:S(2)}) %copy-start.1) | copy-done | bytes 18874392
  181.7 11.4 %tile_rows.1 = f32[3072,1536]{1,0:T(8,128)} custom-call(f32[3072,1536]{1,0:T(8,128)S(1)} %copy-done.1, f32[3072,256]{1,0:T(8,128)S(1)} %copy-done.3, f32[3072,256]{1,0:T(8,128)S(1)} %copy-done.5, bf16[768,1536]{1,0:T(8,128)(2,1)S(1)} %right_side.1.right_ref, f32[256,256]{1,0:T(8,128)S(1)} %copy-done.13), custom_call_target="tpu_custom_call" | custom-call | flops 7247757312 | bytes 18874368 | tf_op jit(solution)/shard_map/tile_rows/pallas_call | solution.py:240
  (87 shorter events, 35.4 us)
Async XLA Ops:
  7.4 83.3 %all-gather.3.cloned.1.call-start = ((), (), s32[]{:S(2)}) async-start(), calls=%async_computation | async-start | bytes 1769472 | tf_op jit(solution)/shard_map/all_gather | solution.py:325
  8.1 136.4 %all-reduce.2.cloned.1.call-start = ((), (), s32[]{:S(2)}) async-start(), calls=%async_computation.2 | async-start | bytes 3145728 | tf_op jit(solution)/shard_map/psum | solution.py:323
  9.9 25.0 %collective-permute-start.5 = (f32[768,256]{1,0:T(8,128)S(1)}, f32[768,256]{1,0:T(8,128)S(1)}, u32[]{:S(2)}, u32[]{:S(2)}) collective-permute-start(f32[768,256]{1,0:T(8,128)S(1)} %get-tuple-element.15), channel_id=1, source_target_pairs={{0,4},{8,12},{16,20},{24,28}} | collective-permute-start | bytes 2359304 | tf_op jit(solution)/shard_map/ppermute | solution.py:286
  15.9 30.5 %collective-permute-start.6 = (f32[768,256]{1,0:T(8,128)S(1)}, f32[768,256]{1,0:T(8,128)}, u32[]{:S(2)}, u32[]{:S(2)}) collective-permute-start(f32[768,256]{1,0:T(8,128)S(1)} %get-tuple-element.16), channel_id=1, source_target_pairs={{0,2},{8,10},{16,18},{24,26}} | collective-permute-start | bytes 2359304 | tf_op jit(solution)/shard_map/ppermute | solution.py:286
  18.1 36.7 %collective-permute-start.4 = (f32[768,256]{1,0:T(8,128)S(1)}, f32[768,256]{1,0:T(8,128)}, u32[]{:S(2)}, u32[]{:S(2)}) collective-permute-start(f32[768,256]{1,0:T(8,128)S(1)} %get-tuple-element.17), channel_id=1, source_target_pairs={{0,6},{8,14},{16,22},{24,30}} | collective-permute-start | bytes 2359304 | tf_op jit(solution)/shard_map/ppermute | solution.py:286
  23.1 147.5 %all-gather.5.cloned.1.call-start = ((), (), s32[]{:S(2)}) async-start(), calls=%async_computation.1 | async-start | bytes 3538944 | tf_op jit(solution)/shard_map/all_gather | solution.py:316
  56.7 24.0 %copy-start.19 = (f32[2,32,32]{2,1,0:T(8,128)S(1)}, f32[2,32,32]{2,1,0:T(8,128)}, u32[]{:S(2)}) copy-start(f32[2,32,32]{2,1,0:T(8,128)} %param.6) | copy-start | bytes 24580
  56.7 2.6 %collective-permute-start.7 = (f32[384,256]{1,0:T(8,128)S(1)}, f32[384,256]{1,0:T(8,128)S(1)}, u32[]{:S(2)}, u32[]{:S(2)}) collective-permute-start(f32[384,256]{1,0:T(8,128)S(1)} %slice.80), channel_id=1, source_target_pairs={{0,1},{2,3},{4,5},{6,7},{8,9},{10,11},{12,13},{14,15},{16,17},{18,... | collective-permute-start | bytes 1179656 | tf_op jit(solution)/shard_map/ppermute | solution.py:289
  60.2 32.6 %copy-start.16 = (f32[32,1536]{1,0:T(8,128)S(1)}, f32[32,1536]{1,0:T(8,128)}, u32[]{:S(2)}) copy-start(f32[32,1536]{1,0:T(8,128)} %param.5) | copy-start | bytes 589828
  61.2 7.3 %collective-permute-start.8 = (f32[256,256]{1,0:T(8,128)S(1)}, f32[256,256]{1,0:T(8,128)S(1)}, u32[]{:S(2)}, u32[]{:S(2)}) collective-permute-start(f32[256,256]{1,0:T(8,128)S(1)} %slice.71), channel_id=1, source_target_pairs={{0,8}} | collective-permute-start | bytes 786440 | tf_op jit(solution)/shard_map/ppermute | solution.py:298
  69.4 8.4 %collective-permute-start.9 = (f32[256,256]{1,0:T(8,128)S(1)}, f32[256,256]{1,0:T(8,128)S(1)}, u32[]{:S(2)}, u32[]{:S(2)}) collective-permute-start(f32[256,256]{1,0:T(8,128)S(1)} %broadcast_select_fusion), channel_id=1, source_target_pairs={{0,16},{8,24}} | collective-permute-start | bytes 786440 | tf_op jit(solution)/shard_map/ppermute | solution.py:298
  77.8 10.8 %collective-permute-start.10 = (f32[256,256]{1,0:T(8,128)S(1)}, f32[256,256]{1,0:T(8,128)S(1)}, u32[]{:S(2)}, u32[]{:S(2)}) collective-permute-start(f32[256,256]{1,0:T(8,128)S(1)} %broadcast_select_fusion.1), channel_id=1, source_target_pairs={{0,4},{8,12},{16,20},{24,28}} | collective-permute-start | bytes 786440 | tf_op jit(solution)/shard_map/ppermute | solution.py:298
  88.6 17.6 %collective-permute-start.11 = (f32[256,256]{1,0:T(8,128)S(1)}, f32[256,256]{1,0:T(8,128)}, u32[]{:S(2)}, u32[]{:S(2)}) collective-permute-start(f32[256,256]{1,0:T(8,128)S(1)} %broadcast_select_fusion.2), channel_id=1, source_target_pairs={{0,2},{8,10},{16,18},{24,26},{4,6},{12,14},{20,22},{28,30}} | collective-permute-start | bytes 786440 | tf_op jit(solution)/shard_map/ppermute | solution.py:298
  91.4 14.8 %copy-start.17 = (f32[32,256]{1,0:T(8,128)}, f32[32,256]{1,0:T(8,128)S(1)}, u32[]{:S(2)}) copy-start(f32[32,256]{1,0:T(8,128)S(1)} %slice.75) | copy-start | bytes 98308
  92.9 18.4 %collective-permute-start.2 = (f32[32,3328]{1,0:T(8,128)S(1)}, f32[32,3328]{1,0:T(8,128)S(1)}, u32[]{:S(2)}, u32[]{:S(2)}) collective-permute-start(f32[32,3328]{1,0:T(8,128)S(1)} %get-tuple-element.22), channel_id=1, source_target_pairs={{0,24},{8,0},{16,8},{24,16},{1,25},{9,1},{17,9},{25,17},{2,26},{10... | collective-permute-start | bytes 1277960 | tf_op jit(solution)/shard_map/ppermute | solution.py:266
  105.6 10.8 %collective-permute-start = (f32[32,3328]{1,0:T(8,128)S(1)}, f32[32,3328]{1,0:T(8,128)S(1)}, u32[]{:S(2)}, u32[]{:S(2)}) collective-permute-start(f32[32,3328]{1,0:T(8,128)S(1)} %get-tuple-element.23), channel_id=1, source_target_pairs={{0,8},{8,16},{16,24},{24,0},{1,9},{9,17},{17,25},{25,1},{2,10},{10... | collective-permute-start | bytes 1277960 | tf_op jit(solution)/shard_map/ppermute | solution.py:266
  105.6 12.7 %collective-permute-start.1 = (f32[32,3328]{1,0:T(8,128)S(1)}, f32[32,3328]{1,0:T(8,128)S(1)}, u32[]{:S(2)}, u32[]{:S(2)}) collective-permute-start(f32[32,3328]{1,0:T(8,128)S(1)} %get-tuple-element.24), channel_id=1, source_target_pairs={{0,16},{8,24},{16,0},{24,8},{1,17},{9,25},{17,1},{25,9},{2,18},{10... | collective-permute-start | bytes 1277960 | tf_op jit(solution)/shard_map/ppermute | solution.py:266
  106.3 13.3 %collective-permute-start.12 = (f32[256,256]{1,0:T(8,128)S(1)}, f32[256,256]{1,0:T(8,128)}, u32[]{:S(2)}, u32[]{:S(2)}) collective-permute-start(f32[256,256]{1,0:T(8,128)S(1)} %broadcast_select_fusion.3), channel_id=1, source_target_pairs={{0,1},{8,9},{16,17},{24,25},{4,5},{12,13},{20,21},{28,29},{2,3},{1... | collective-permute-start | bytes 786440 | tf_op jit(solution)/shard_map/ppermute | solution.py:298
  111.2 8.4 %copy-start.18 = (f32[32,256]{1,0:T(8,128)S(1)}, f32[32,256]{1,0:T(8,128)}, u32[]{:S(2)}) copy-start(f32[32,256]{1,0:T(8,128)} %copy-done.17) | copy-start | bytes 98308
  119.2 15.1 %collective-permute-start.3 = (f32[128,1536]{1,0:T(8,128)}, f32[128,1536]{1,0:T(8,128)S(1)}, u32[]{:S(2)}, u32[]{:S(2)}) collective-permute-start(f32[128,1536]{1,0:T(8,128)} %pad_maximum_fusion.4), channel_id=1, source_target_pairs={{0,1},{1,0},{2,3},{3,2},{4,5},{5,4},{6,7},{7,6},{8,9},{9,8},{10,11... | collective-permute-start | bytes 2359304 | tf_op jit(solution)/shard_map/ppermute | solution.py:333
  149.9 6.4 %copy-start.2 = (f32[3072,1536]{1,0:T(8,128)S(1)}, f32[3072,1536]{1,0:T(8,128)}, u32[]{:S(2)}) copy-start(f32[3072,1536]{1,0:T(8,128)} %normals_ref.1) | copy-start | bytes 56623108
  163.7 6.9 %copy-start = (f32[3072,1536]{1,0:T(8,128)}, f32[3072,1536]{1,0:T(8,128)S(1)}, u32[]{:S(2)}) copy-start(f32[3072,1536]{1,0:T(8,128)S(1)} %gram_tile.1.system_ref) | copy-start | bytes 56623108
  170.6 6.4 %copy-start.1 = (f32[3072,1536]{1,0:T(8,128)S(1)}, f32[3072,1536]{1,0:T(8,128)}, u32[]{:S(2)}) copy-start(f32[3072,1536]{1,0:T(8,128)} %copy-done) | copy-start | bytes 56623108
  177.0 1.9 copy-start.3
  (12 other events, 15.3 us)
Sparse Core Ops, SparseCore 0:
  9.8 29.7 all-gather.2
  60.3 41.2 all-gather.4
Sparse Core Ops, SparseCore 1:
  23.1 69.4 all-reduce.1

commit v7 on v6

--- a/solution.py
+++ b/solution.py
@@ -83,7 +83,7 @@
         corner_kernel,
         out_shape=jax.ShapeDtypeStruct((B, B), jnp.float32),
         scratch_shapes=[pltpu.VMEM((B, 2 * B), jnp.float32)],
-        compiler_params=pltpu.CompilerParams(vmem_limit_bytes=4 * 2**20),
+        compiler_params=pltpu.CompilerParams(vmem_limit_bytes=8 * 2**20),
         cost_estimate=pl.CostEstimate(flops=10**9, bytes_accessed=2**20, transcendentals=0),
         name="corner_factor",
     )(block, design, filter_matrix, regular)
@@ -113,7 +113,7 @@
         in_specs=[pl.BlockSpec(memory_space=pltpu.SMEM)] + [pl.BlockSpec(memory_space=pltpu.VMEM)] * 3,
         out_specs=pl.BlockSpec(memory_space=pltpu.VMEM),
         out_shape=jax.ShapeDtypeStruct((3 * B, cols), jnp.bfloat16),
-        compiler_params=pltpu.CompilerParams(vmem_limit_bytes=20 * 2**20),
+        compiler_params=pltpu.CompilerParams(vmem_limit_bytes=24 * 2**20),
         cost_estimate=pl.CostEstimate(
             flops=6 * cols * B * B, bytes_accessed=12 * cols * B, transcendentals=0
         ),
@@ -121,16 +121,23 @@
     )(place, strip, gram_rows, inverse)
 
 
-def filter_kernel(count, place_ref, *refs):
-    parts = refs[:count]
-    other_ref, filter_ref, regular_ref, lead_reg_ref = refs[count : count + 4]
-    left_ref, right_ref, gram_rows_ref, gram_cols_ref = refs[count + 4 :]
+def filter_kernel(
+    place_ref,
+    joined_ref,
+    other_ref,
+    filter_ref,
+    regular_ref,
+    lead_reg_ref,
+    left_ref,
+    right_ref,
+    gram_rows_ref,
+    gram_cols_ref,
+):
     row_index, col_index = place_ref[0], place_ref[1]
     cols = right_ref.shape[1]
     obs = filter_ref.shape[0]
     core = lax.rem(col_index, 2)
-    design = jnp.concatenate([part[...] for part in parts], axis=0)
-    filtered = split_dot(filter_ref[...], design)
+    filtered = split_dot(filter_ref[...], joined_ref[...])
     here, rows_own, lead = filtered[:, :cols], filtered[:, cols : 2 * cols], filtered[:, 2 * cols :]
     row_pos = lax.broadcasted_iota(jnp.int32, (B, cols), 0)
     col_pos = lax.broadcasted_iota(jnp.int32, (1, cols), 1) + col_index * cols
@@ -154,13 +161,13 @@
         )
 
 
-def filter_sides(place, parts, other, filter_matrix, regular, lead_reg):
+def filter_sides(place, joined, other, filter_matrix, regular, lead_reg):
     cols = other.shape[1]
     obs = filter_matrix.shape[0]
     vmem = pl.BlockSpec(memory_space=pltpu.VMEM)
     return pl.pallas_call(
-        functools.partial(filter_kernel, len(parts)),
-        in_specs=[pl.BlockSpec(memory_space=pltpu.SMEM)] + [vmem] * (len(parts) + 4),
+        filter_kernel,
+        in_specs=[pl.BlockSpec(memory_space=pltpu.SMEM)] + [vmem] * 5,
         out_specs=[vmem] * 4,
         out_shape=[
             jax.ShapeDtypeStruct((2 * cols, 3 * obs), jnp.bfloat16),
@@ -168,12 +175,12 @@
             jax.ShapeDtypeStruct((B, cols), jnp.float32),
             jax.ShapeDtypeStruct((2 * cols, B), jnp.float32),
         ],
-        compiler_params=pltpu.CompilerParams(vmem_limit_bytes=20 * 2**20),
+        compiler_params=pltpu.CompilerParams(vmem_limit_bytes=32 * 2**20),
         cost_estimate=pl.CostEstimate(
             flops=18 * cols * obs * B, bytes_accessed=24 * cols * B, transcendentals=0
         ),
         name="filter_sides",
-    )(place, *parts, other, filter_matrix, regular, lead_reg)
+    )(place, joined, other, filter_matrix, regular, lead_reg)
 
 
 def gram_kernel(place_ref, normals_ref, left_ref, right_ref, regular_ref, out_ref):
@@ -216,8 +223,8 @@
             ],
             out_specs=tile_spec,
         ),
-        out_shape=jax.ShapeDtypeStruct((rows, cols), jnp.float32),
-        compiler_params=pltpu.CompilerParams(vmem_limit_bytes=8 * 2**20),
+        out_shape=pltpu.HBM((rows, cols), jnp.float32),
+        compiler_params=pltpu.CompilerParams(vmem_limit_bytes=16 * 2**20),
         cost_estimate=pl.CostEstimate(
             flops=2 * rows * cols * depth, bytes_accessed=4 * rows * cols, transcendentals=0
         ),
@@ -249,7 +256,7 @@
         ],
         out_specs=tile_spec,
         out_shape=jax.ShapeDtypeStruct((rows, cols), jnp.float32),
-        compiler_params=pltpu.CompilerParams(vmem_limit_bytes=22 * 2**20),
+        compiler_params=pltpu.CompilerParams(vmem_limit_bytes=32 * 2**20),
         cost_estimate=pl.CostEstimate(
             flops=6 * rows * cols * B, bytes_accessed=4 * rows * cols, transcendentals=0
         ),
@@ -261,30 +268,24 @@
     return lax.optimization_barrier((value, earlier))[0]
 
 
-def shifted(value, axis, by):
-    peers = lax.axis_size(axis)
-    return lax.ppermute(value, axis, [(i, (i + by) % peers) for i in range(peers)])
-
-
-def filter_matrix_of(filter_blocks, sources):
-    count = sources.shape[0]
-    lag = jnp.arange(count, dtype=jnp.int32)[:, None] - sources[None, :]
-    lag = lag[:, None, :, None]
+def filter_matrix_of(filter_blocks, count):
+    positions = jnp.arange(count, dtype=jnp.int32)
+    lag = (positions[:, None] - positions[None, :])[:, None, :, None]
     own = filter_blocks[0][None, :, None, :]
     prior = filter_blocks[1][None, :, None, :]
     blocks = jnp.where(lag == 0, own, jnp.where(lag == 1, prior, 0.0))
     return blocks.reshape(count * P_SIZE, count * P_SIZE)
 
 
-def row_strip_piece(normals):
+def row_strip_piece(normals, earlier):
     peers = lax.axis_size("col")
     chips = peers // 2
     size = normals.shape[0] // chips
     col_index = lax.axis_index("col")
-    arrived = None
-    for z in reversed(range(1, chips)):
-        got = lax.ppermute(normals[z * size : (z + 1) * size, :B], "col", [(0, 2 * z)])
-        arrived = got if arrived is None else arrived + got
+    arrived = [
+        lax.ppermute(normals[z * size : (z + 1) * size, :B], "col", [(0, 2 * z)]) for z in range(1, chips)
+    ]
+    arrived = sum(after(arrived, earlier))
     piece = jnp.where(col_index == 0, normals[:size, :B], arrived)
     second = lax.ppermute(piece[size // 2 :], "col", [(c, c + 1) for c in range(0, peers, 2)])
     return jnp.where(col_index % 2 == 0, piece[: size // 2], second)
@@ -307,44 +308,43 @@
     row_peers = lax.axis_size("row")
     row_index = lax.axis_index("row")
     col_index = lax.axis_index("col")
-    blocks_here = obs_here // P_SIZE
     obs = row_peers * obs_here
     core = col_index % 2
 
     col_peers = lax.axis_size("col")
-    piece = row_strip_piece(normals)
-    strip = lax.all_gather(piece, "col", axis=0, tiled=True)
+    col_strip = lax.psum(jnp.where(row_index == 0, normals[:B], 0.0), "row")
 
     index_bits = [1 << i for i in range((row_peers * col_peers - 1).bit_length())]
     block, reached = doubled(normals[:B, :B], [bit for bit in index_bits if bit >= col_peers], [0])
-    block = after(block, piece)
-    corner, _ = doubled(block, [bit for bit in reversed(index_bits) if bit < col_peers], reached)
-
-    col_strip = lax.psum(jnp.where(row_index == 0, normals[:B], 0.0), "row")
 
     along = lax.all_gather(design, "col", axis=1, tiled=True)
-    parts = []
-    for s in range(row_peers):
-        to = (row_index + s) % row_peers
-        far = lax.dynamic_slice_in_dim(along, to * rows_here + core * cols_here, cols_here, axis=1)
-        part = jnp.concatenate([design, far, along[:, :B]], axis=1)
-        parts.append(shifted(part, "row", s) if s else part)
-    own = jnp.concatenate([part[:, cols_here : 2 * cols_here] for part in parts], axis=0)
-    other = lax.ppermute(own, "col", [(c, c ^ 1) for c in range(lax.axis_size("col"))])
-    lead = jnp.concatenate([part[:, 2 * cols_here :] for part in parts], axis=0)
-
-    positions = jnp.arange(obs // P_SIZE, dtype=jnp.int32)
-    passed = positions // blocks_here
-    order = ((row_index - passed) % row_peers) * blocks_here + positions % blocks_here
-    filters = filter_matrix_of(filter_blocks, order)
+    along = along.reshape(obs_here, row_peers, 2, cols_here)
+    far = lax.dynamic_index_in_dim(along, core, 2, keepdims=False)
+    sent = [
+        jnp.concatenate([design, far[:, to], along[:, 0, 0, :B]], axis=1) for to in range(row_peers)
+    ]
+    joined = lax.all_to_all(jnp.stack(sent), "row", 0, 0, tiled=True)
+    joined = joined.reshape(obs, 2 * cols_here + B)
+
+    piece = row_strip_piece(normals, (block, joined))
+    strip = lax.all_gather(piece, "col", axis=0, tiled=True)
+
+    corner, _ = doubled(after(block, piece), [bit for bit in reversed(index_bits) if bit < col_peers], reached)
+
+    other = lax.ppermute(
+        joined[:, cols_here : 2 * cols_here], "col", [(c, c ^ 1) for c in range(col_peers)]
+    )
+    lead = joined[:, 2 * cols_here :]
+    filters = filter_matrix_of(filter_blocks, obs // P_SIZE)
     lead_reg = regular[:B].reshape(1, B)
     own_reg = lax.dynamic_slice_in_dim(regular, col_index * cols_here, cols_here).reshape(1, cols_here)
     place = jnp.stack([row_index, col_index]).astype(jnp.int32)
     inverse = corner_factor(corner, lead, filters, lead_reg)
-    gram_left, gram_right, gram_rows, gram_cols = filter_sides(place, parts, other, filters, own_reg, lead_reg)
-    system = gram_tile(place, normals, gram_left, gram_right, own_reg)
+    gram_left, gram_right, gram_rows, gram_cols = filter_sides(place, joined, other, filters, own_reg, lead_reg)
+    in_hbm = functools.partial(pltpu.with_memory_space_constraint, memory_space=pltpu.HBM)
+    system = gram_tile(place, in_hbm(normals), gram_left, gram_right, own_reg)
     right = right_side(place, col_strip, gram_rows, inverse)
-    return tile_rows(system, strip, gram_cols, right, inverse)
+    return tile_rows(in_hbm(system), strip, gram_cols, right, inverse)
 
 
 def solution(mesh):

time: 203 us -> 178 us (0.88)
  the two profiles are of different devices: /device:TPU:0 before, /device:TPU:24 now
where the time goes in v7:
time: 178 us; the launch traced here: 177 us
  waiting for transfers between devices  64 us (36%)
  Pallas kernels  54.4 us (31%)
  local copies, waits for them, and re-layouts  17.3 us (10%)
  starting transfers between devices  16 us (9%)
  between operations  15.2 us (9%)
  other arithmetic  10.1 us (6%)
    all_gather x1, waiting for transfers between devices, body(): along = lax.all_gather(design, 'col', axis=1, tiled=True)  33.2 us
    all_to_all x1, waiting for transfers between devices, body(): joined = lax.all_to_all(jnp.stack(sent), 'row', 0, 0, tiled=True)  23.7 us
    pallas_call x1, Pallas kernels, tile_rows(): pl.pallas_call(tile_kernel, grid=(rows // block,), in_specs=[tile_spec, l...  18.3 us
    pallas_call x1, Pallas kernels, gram_tile(): pl.pallas_call(gram_kernel, grid_spec=pltpu.PrefetchScalarGridSpec(num_sc...  16.8 us
    pallas_call x1, Pallas kernels, corner_factor(): pl.pallas_call(corner_kernel, out_shape=jax.ShapeDtypeStruct((B, B), jnp....  13.9 us
    unnamed x17, local copies, waits for them, and re-layouts  7.19 us
    ppermute x5, starting transfers between devices, doubled(): got = lax.ppermute(value, ('row', 'col'), pairs)  6.22 us
    ppermute x5, waiting for transfers between devices, doubled(): got = lax.ppermute(value, ('row', 'col'), pairs)  4.96 us
  transfers between devices with their start and end apart: 14, of which 4 were waited for; matrix products, arithmetic and copies ran while one was open for 11% of the time, Pallas kernels for 20%

profile of v7, /device:TPU:24, one launch (start us, length us, event | category | flops | bytes accessed | tf_op | source)
XLA Modules:
  0.0 176.9 jit_solution(1987812913959556135)
XLA Ops:
  9.1 1.4 collective-permute-start.4
  10.5 2.7 %fusion.6 = (f32[768,256]{1,0:T(8,128)}, f32[768,256]{1,0:T(8,128)S(1)}, f32[768,256]{1,0:T(8,128)S(1)}) fusion(f32[3072,1536]{1,0:T(8,128)} %normals_ref.1), kind=kLoop, calls=%fused_computation.35 | loop fusion | bytes 4718592 | tf_op jit(solution)/shard_map/slice | solution.py:286
  14.4 1.6 collective-permute-start.2
  16.0 1.6 collective-permute-start.1
  17.6 33.2 %all-gather.3.cloned.1.call-done = f32[32,12288]{1,0:T(8,128)} async-done(((f32[32,1536]{1,0:T(8,128)}), f32[32,12288]{1,0:T(8,128)}) %all-gather.3.cloned.1.call-update) | async-done | bytes 1572880 | tf_op jit(solution)/shard_map/all_gather | solution.py:320
  50.8 2.7 %reshape.47 = f32[32,4,2,1536]{3,2,1,0:T(2,128)S(1)} reshape(f32[32,12288]{1,0:T(8,128)} %all-gather.3.cloned.1.call-done) | data formatting | bytes 3145728 | tf_op jit(solution)/shard_map/reshape | solution.py:321
  56.6 3.6 %all-to-all-start = ((f32[4,32,3328]{2,1,0:T(8,128)}), f32[4,32,3328]{2,1,0:T(8,128)S(1)}, u32[]{:S(2)}, u32[]{:S(2)}) async-start(f32[4,32,3328]{2,1,0:T(8,128)} %pad_maximum_fusion), calls=%async_computation | async-start | bytes 3407872 | tf_op jit(solution)/shard_map/all_to_all | solution.py:326
  60.3 2.7 %slice_select_fusion = f32[256,1536]{1,0:T(8,128)} fusion(f32[3072,1536]{1,0:T(8,128)} %normals_ref.1, pred[]{:T(512)S(6)} %eq.32), kind=kLoop, calls=%fused_computation.1 | loop fusion | flops 393216 | bytes 3145729 | tf_op jit(solution)/shard_map/jit(_where)/select_n | solution.py:315
  64.1 1.4 collective-permute-start.5
  66.2 23.7 %all-to-all-done = f32[4,32,3328]{2,1,0:T(8,128)S(1)} async-done(((f32[4,32,3328]{2,1,0:T(8,128)}), f32[4,32,3328]{2,1,0:T(8,128)S(1)}, u32[]{:S(2)}, u32[]{:S(2)}) %all-to-all-start) | async-done | bytes 1703968 | tf_op jit(solution)/shard_map/all_to_all | solution.py:326
  90.0 2.1 %add_select_fusion = f32[768,256]{1,0:T(8,128)S(1)} fusion(f32[768,256]{1,0:T(8,128)} %collective-permute-done.3, f32[768,256]{1,0:T(8,128)} %collective-permute-done.1, f32[768,256]{1,0:T(8,128)} %collective-permute-done.2, f32[3072,1536]{1,0:T(8,128)} %normals_ref.1, pred[]{:T(512)S(6)} %eq.31), kind=kLoop, calls=%fused_computation.7 | loop fusion | flops 589824 | bytes 3932161 | tf_op jit(solution)/shard_map/jit(_where)/select_n | solution.py:289
  92.1 1.3 collective-permute-start.6
  93.4 1.3 collective-permute-done.6
  100.9 3.9 %filter_sides.1 = (bf16[3072,384]{1,0:T(8,128)(2,1)S(1)}, bf16[384,1536]{1,0:T(8,128)(2,1)S(1)}, f32[256,1536]{1,0:T(8,128)S(1)}, f32[3072,256]{1,0:T(8,128)S(1)}) custom-call(s32[2]{0:T(128)S(1)} %pad_add_fusion.place_ref, f32[128,3328]{1,0:T(8,128)S(1)} %bitcast.32, f32[128,1536]{1,0:T(8,128)S(1)} %collective-permute-done.other_ref, ...), custom_call_target="tpu_custom_call" | custom-call | flops 905969664 | bytes 9437184 | tf_op jit(solution)/shard_map/filter_sides/pallas_call | solution.py:168
  104.9 4.9 %collective-permute-done.8 = f32[256,256]{1,0:T(8,128)} collective-permute-done((f32[256,256]{1,0:T(8,128)S(1)}, f32[256,256]{1,0:T(8,128)}, u32[]{:S(2)}, u32[]{:S(2)}) %collective-permute-start.8) | collective-permute-done | bytes 262176 | tf_op jit(solution)/shard_map/ppermute | solution.py:299
  110.8 1.5 collective-permute-start.9
  112.3 16.8 %gram_tile.1.system_ref = f32[3072,1536]{1,0:T(8,128)} custom-call(s32[2]{0:T(128)S(1)} %pad_add_fusion.place_ref, f32[3072,1536]{1,0:T(8,128)} %normals_ref.1, bf16[3072,384]{1,0:T(8,128)(2,1)S(1)} %get-tuple-element.13.left_ref, bf16[384,1536]{1,0:T(8,128)(2,1)S(1)} %get-tuple-element.14.right_ref, f32[1,1536]{1,0:T(1,128)S(1)} %reshape.49.regular_ref), custom_call_target="tpu_custom_call" | custom-call | flops 3623878656 | bytes 18874368 | tf_op jit(solution)/shard_map/gram_tile/pallas_call | solution.py:213
  129.2 13.9 %corner_factor.1.inverse_ref = f32[256,256]{1,0:T(8,128)S(1)} custom-call(f32[256,256]{1,0:T(8,128)S(1)} %broadcast_select_fusion.2.block_ref, f32[128,256]{1,0:T(8,128)S(1)} %slice.83.design_ref, f32[128,128]{1,0:T(8,128)S(1)} %select_n.90.filter_ref, f32[1,256]{1,0:T(1,128)S(1)} %bitcast.34), custom_call_target="tpu_custom_call" | custom-call | flops 1000000000 | bytes 1048576 | tf_op jit(solution)/shard_map/corner_factor/pallas_call | solution.py:82
  143.1 1.4 copy-done.3
  144.5 1.4 copy-done.5
  145.9 1.5 right_side.1.right_ref
  147.4 1.9 %copy-done = f32[3072,256]{1,0:T(8,128)S(1)} copy-done((f32[3072,256]{1,0:T(8,128)S(1)}, f32[3072,256]{1,0:T(8,128)}, u32[]{:S(2)}) %copy-start) | copy-done | bytes 3145752
  149.3 1.9 %copy-done.2 = f32[3072,256]{1,0:T(8,128)S(1)} copy-done((f32[3072,256]{1,0:T(8,128)S(1)}, f32[3072,256]{1,0:T(8,128)}, u32[]{:S(2)}) %copy-start.2) | copy-done | bytes 3145752
  151.2 18.3 %tile_rows.1 = f32[3072,1536]{1,0:T(8,128)} custom-call(f32[3072,1536]{1,0:T(8,128)} %gram_tile.1.system_ref, f32[3072,256]{1,0:T(8,128)S(1)} %copy-done, f32[3072,256]{1,0:T(8,128)S(1)} %copy-done.2, bf16[768,1536]{1,0:T(8,128)(2,1)S(1)} %right_side.1.right_ref, f32[256,256]{1,0:T(8,128)S(1)} %corner_factor.1.inverse_ref), custom_call_target="tpu_custom_call" | custom-call | flops 7247757312 | bytes 18874368 | tf_op jit(solution)/shard_map/tile_rows/pallas_call | solution.py:247
  (57 shorter events, 15.1 us)
Async XLA Ops:
  7.4 43.4 %all-gather.3.cloned.1.call-start = ((), (), s32[]{:S(2)}) async-start(), calls=%async_computation.1 | async-start | bytes 1769472 | tf_op jit(solution)/shard_map/all_gather | solution.py:320
  9.1 54.0 %collective-permute-start.4 = (f32[256,256]{1,0:T(8,128)S(1)}, f32[256,256]{1,0:T(8,128)}, u32[]{:S(2)}, u32[]{:S(2)}) collective-permute-start(f32[256,256]{1,0:T(8,128)S(1)} %slice.70), channel_id=1, source_target_pairs={{0,8}} | collective-permute-start | bytes 786440 | tf_op jit(solution)/shard_map/ppermute | solution.py:299
  13.2 53.1 %collective-permute-start.3 = (f32[768,256]{1,0:T(8,128)}, f32[768,256]{1,0:T(8,128)}, u32[]{:S(2)}, u32[]{:S(2)}) collective-permute-start(f32[768,256]{1,0:T(8,128)} %get-tuple-element.21), channel_id=1, source_target_pairs={{0,6},{8,14},{16,22},{24,30}} | collective-permute-start | bytes 2359304 | tf_op jit(solution)/shard_map/ppermute | solution.py:286
  14.4 51.8 %collective-permute-start.2 = (f32[768,256]{1,0:T(8,128)S(1)}, f32[768,256]{1,0:T(8,128)}, u32[]{:S(2)}, u32[]{:S(2)}) collective-permute-start(f32[768,256]{1,0:T(8,128)S(1)} %get-tuple-element.22), channel_id=1, source_target_pairs={{0,4},{8,12},{16,20},{24,28}} | collective-permute-start | bytes 2359304 | tf_op jit(solution)/shard_map/ppermute | solution.py:286
  16.0 50.2 %collective-permute-start.1 = (f32[768,256]{1,0:T(8,128)S(1)}, f32[768,256]{1,0:T(8,128)}, u32[]{:S(2)}, u32[]{:S(2)}) collective-permute-start(f32[768,256]{1,0:T(8,128)S(1)} %get-tuple-element.23), channel_id=1, source_target_pairs={{0,2},{8,10},{16,18},{24,26}} | collective-permute-start | bytes 2359304 | tf_op jit(solution)/shard_map/ppermute | solution.py:286
  54.3 0.9 copy-start.6
  56.6 33.3 %all-to-all-start = ((f32[4,32,3328]{2,1,0:T(8,128)}), f32[4,32,3328]{2,1,0:T(8,128)S(1)}, u32[]{:S(2)}, u32[]{:S(2)}) async-start(f32[4,32,3328]{2,1,0:T(8,128)} %pad_maximum_fusion), calls=%async_computation | async-start | bytes 3407872 | tf_op jit(solution)/shard_map/all_to_all | solution.py:326
  60.2 82.9 %all-reduce.2.cloned.1.call-start = ((), (), s32[]{:S(2)}) async-start(), calls=%async_computation.3 | async-start | bytes 3145728 | tf_op jit(solution)/shard_map/psum | solution.py:315
  63.0 84.3 %all-gather.5.cloned.1.call-start = ((), (), s32[]{:S(2)}) async-start(), calls=%async_computation.2 | async-start | bytes 3538944 | tf_op jit(solution)/shard_map/all_gather | solution.py:330
  64.1 1.4 collective-permute-start.5
  92.1 5.5 %copy-start.7 = (f32[2,32,32]{2,1,0:T(8,128)S(1)}, f32[2,32,32]{2,1,0:T(8,128)}, u32[]{:S(2)}) copy-start(f32[2,32,32]{2,1,0:T(8,128)} %param.6) | copy-start | bytes 24580
  92.1 2.6 %collective-permute-start.6 = (f32[384,256]{1,0:T(8,128)S(1)}, f32[384,256]{1,0:T(8,128)S(1)}, u32[]{:S(2)}, u32[]{:S(2)}) collective-permute-start(f32[384,256]{1,0:T(8,128)S(1)} %slice.82), channel_id=1, source_target_pairs={{0,1},{2,3},{4,5},{6,7},{8,9},{10,11},{12,13},{14,15},{16,17},{18,... | collective-permute-start | bytes 1179656 | tf_op jit(solution)/shard_map/ppermute | solution.py:290
  95.6 2.0 %collective-permute-start.7 = (f32[256,256]{1,0:T(8,128)}, f32[256,256]{1,0:T(8,128)S(1)}, u32[]{:S(2)}, u32[]{:S(2)}) collective-permute-start(f32[256,256]{1,0:T(8,128)} %broadcast_select_fusion.4), channel_id=1, source_target_pairs={{0,4},{8,12},{16,20},{24,28}} | collective-permute-start | bytes 786440 | tf_op jit(solution)/shard_map/ppermute | solution.py:299
  97.3 3.6 %collective-permute-start = (f32[128,1536]{1,0:T(8,128)}, f32[128,1536]{1,0:T(8,128)S(1)}, u32[]{:S(2)}, u32[]{:S(2)}) collective-permute-start(f32[128,1536]{1,0:T(8,128)} %slice.80), channel_id=1, source_target_pairs={{0,1},{1,0},{2,3},{3,2},{4,5},{5,4},{6,7},{7,6},{8,9},{9,8},{10,11... | collective-permute-start | bytes 2359304 | tf_op jit(solution)/shard_map/ppermute | solution.py:334
  97.7 12.1 %collective-permute-start.8 = (f32[256,256]{1,0:T(8,128)S(1)}, f32[256,256]{1,0:T(8,128)}, u32[]{:S(2)}, u32[]{:S(2)}) collective-permute-start(f32[256,256]{1,0:T(8,128)S(1)} %broadcast_select_fusion), channel_id=1, source_target_pairs={{0,2},{8,10},{16,18},{24,26},{4,6},{12,14},{20,22},{28,30}} | collective-permute-start | bytes 786440 | tf_op jit(solution)/shard_map/ppermute | solution.py:299
  104.8 24.3 %copy-start.1 = (f32[3072,256]{1,0:T(8,128)}, f32[3072,256]{1,0:T(8,128)S(1)}, u32[]{:S(2)}) copy-start(f32[3072,256]{1,0:T(8,128)S(1)} %get-tuple-element.18.gram_ref) | copy-start | bytes 9437188
  104.8 24.3 %copy-start.4 = (f32[256,1536]{1,0:T(8,128)}, f32[256,1536]{1,0:T(8,128)S(1)}, u32[]{:S(2)}) copy-start(f32[256,1536]{1,0:T(8,128)S(1)} %get-tuple-element.19.gram_ref) | copy-start | bytes 4718596
  110.8 18.3 %collective-permute-start.9 = (f32[256,256]{1,0:T(8,128)S(1)}, f32[256,256]{1,0:T(8,128)S(1)}, u32[]{:S(2)}, u32[]{:S(2)}) collective-permute-start(f32[256,256]{1,0:T(8,128)S(1)} %broadcast_select_fusion.1), channel_id=1, source_target_pairs={{0,1},{8,9},{16,17},{24,25},{4,5},{12,13},{20,21},{28,29},{2,3},{1... | collective-permute-start | bytes 786440 | tf_op jit(solution)/shard_map/ppermute | solution.py:299
  143.1 1.4 copy-start.3
  144.5 1.4 copy-start.5
  147.4 1.9 %copy-start = (f32[3072,256]{1,0:T(8,128)S(1)}, f32[3072,256]{1,0:T(8,128)}, u32[]{:S(2)}) copy-start(f32[3072,256]{1,0:T(8,128)} %all-gather.5.cloned.1.call-done.strip_ref) | copy-start | bytes 9437188
  149.3 1.9 %copy-start.2 = (f32[3072,256]{1,0:T(8,128)S(1)}, f32[3072,256]{1,0:T(8,128)}, u32[]{:S(2)}) copy-start(f32[3072,256]{1,0:T(8,128)} %copy-done.1) | copy-start | bytes 9437188
Sparse Core Ops, SparseCore 0:
  9.8 40.9 all-gather.2
  95.7 37.1 all-gather.4
Sparse Core Ops, SparseCore 1:
  63.8 70.7 all-reduce.1

commit v8 on v7

--- a/solution.py
+++ b/solution.py
@@ -89,12 +89,13 @@
     )(block, design, filter_matrix, regular)
 
 
-def right_kernel(place_ref, strip_ref, gram_ref, inverse_ref, out_ref):
+def right_kernel(place_ref, strip_ref, gram_ref, inverse_ref, side_ref, out_ref):
     strip = strip_ref[...] + gram_ref[...]
     panel_high, panel_low = split(-split_dot(inverse_ref[...].T, strip))
     out_ref[:B, :] = panel_high
     out_ref[B : 2 * B, :] = panel_low
-    out_ref[2 * B :, :] = panel_high
+    out_ref[2 * B : 3 * B, :] = panel_high
+    out_ref[3 * B :, :] = side_ref[...]
 
     @pl.when(place_ref[1] == 0)
     def _():
@@ -103,22 +104,23 @@
         identity = identity.astype(jnp.bfloat16)
         out_ref[:B, :B] = identity
         out_ref[B : 2 * B, :B] = jnp.zeros((B, B), jnp.bfloat16)
-        out_ref[2 * B :, :B] = identity
-
-
-def right_side(place, strip, gram_rows, inverse):
+        out_ref[2 * B : 3 * B, :B] = identity
+
+
+def right_side(place, strip, gram_rows, inverse, side):
     cols = gram_rows.shape[1]
+    depth = 3 * B + side.shape[0]
     return pl.pallas_call(
         right_kernel,
-        in_specs=[pl.BlockSpec(memory_space=pltpu.SMEM)] + [pl.BlockSpec(memory_space=pltpu.VMEM)] * 3,
+        in_specs=[pl.BlockSpec(memory_space=pltpu.SMEM)] + [pl.BlockSpec(memory_space=pltpu.VMEM)] * 4,
         out_specs=pl.BlockSpec(memory_space=pltpu.VMEM),
-        out_shape=jax.ShapeDtypeStruct((3 * B, cols), jnp.bfloat16),
+        out_shape=jax.ShapeDtypeStruct((depth, cols), jnp.bfloat16),
         compiler_params=pltpu.CompilerParams(vmem_limit_bytes=24 * 2**20),
         cost_estimate=pl.CostEstimate(
             flops=6 * cols * B * B, bytes_accessed=12 * cols * B, transcendentals=0
         ),
         name="right_side",
-    )(place, strip, gram_rows, inverse)
+    )(place, strip, gram_rows, inverse, side)
 
 
 def filter_kernel(
@@ -183,16 +185,31 @@
     )(place, joined, other, filter_matrix, regular, lead_reg)
 
 
-def gram_kernel(place_ref, normals_ref, left_ref, right_ref, regular_ref, out_ref):
+def block_rows(half):
+    return max(size for size in range(128, 513, 128) if half % size == 0)
+
+
+def tile_kernel(count, block_ids_ref, place_ref, normals_ref, *refs):
+    here_refs, sent_refs = refs[:count], refs[count : 2 * count]
+    gram_ref, left_ref, right_ref, inverse_ref, regular_ref, out_ref = refs[2 * count :]
     step = pl.program_id(0)
     block, cols = out_ref.shape
+    per_piece = pl.num_programs(0) // count
+    even = lax.rem(place_ref[1], 2) == 0
+    slot = step // per_piece
+    rows = pl.ds(pl.multiple_of(lax.rem(step, per_piece) * block, block), block)
+    strip = jnp.where(even, here_refs[0][rows, :], sent_refs[0][rows, :])
+    for i in range(1, count):
+        strip = jnp.where(slot == i, jnp.where(even, here_refs[i][rows, :], sent_refs[i][rows, :]), strip)
+    high, low = split(split_dot(strip + gram_ref[...], inverse_ref[...]))
+    left = jnp.concatenate([high, high, low, left_ref[...]], axis=1)
+    first_row = (place_ref[0] * pl.num_programs(0) + block_ids_ref[step]) * block
     first_col = place_ref[1] * cols
     col_pos = lax.broadcasted_iota(jnp.int32, (1, cols), 1) + first_col
     keep = jnp.where(col_pos < B, 0.0, 1.0)
     out_ref[...] = normals_ref[...] * keep + jnp.dot(
-        left_ref[...], right_ref[...], preferred_element_type=jnp.float32
+        left, right_ref[...], preferred_element_type=jnp.float32
     )
-    first_row = (place_ref[0] * pl.num_programs(0) + step) * block
 
     @pl.when((first_row < first_col + cols) & (first_col < first_row + block))
     def _():
@@ -201,67 +218,36 @@
         out_ref[...] = out_ref[...] + jnp.where(on_diag, regular_ref[...], 0.0)
 
 
-def block_rows(half):
-    return max(size for size in range(128, 513, 128) if half % size == 0)
-
-
-def gram_tile(place, normals, left, right, regular):
+def tile_rows(place, block_ids, normals, here, sent, gram_cols, left, right, inverse, regular):
     rows, cols = normals.shape
-    block = block_rows(rows // 2)
-    depth = right.shape[0]
-    tile_spec = pl.BlockSpec((block, cols), lambda i, place: (i, 0))
+    count = len(here)
+    block = rows // block_ids.shape[0]
+
+    def whole(array):
+        return pl.BlockSpec(
+            array.shape, lambda i, ids, place: (0,) * array.ndim, pipeline_mode=pl.Buffered(1)
+        )
+
+    def listed(width):
+        return pl.BlockSpec((block, width), lambda i, ids, place: (ids[i], 0))
+
     return pl.pallas_call(
-        gram_kernel,
+        functools.partial(tile_kernel, count),
         grid_spec=pltpu.PrefetchScalarGridSpec(
-            num_scalar_prefetch=1,
-            grid=(rows // block,),
-            in_specs=[
-                tile_spec,
-                pl.BlockSpec((block, depth), lambda i, place: (i, 0)),
-                pl.BlockSpec((depth, cols), lambda i, place: (0, 0), pipeline_mode=pl.Buffered(1)),
-                pl.BlockSpec((1, cols), lambda i, place: (0, 0)),
-            ],
-            out_specs=tile_spec,
+            num_scalar_prefetch=2,
+            grid=(block_ids.shape[0],),
+            in_specs=[listed(cols)]
+            + [whole(array) for array in [*here, *sent]]
+            + [listed(B), listed(left.shape[1]), whole(right), whole(inverse), whole(regular)],
+            out_specs=listed(cols),
         ),
-        out_shape=pltpu.HBM((rows, cols), jnp.float32),
-        compiler_params=pltpu.CompilerParams(vmem_limit_bytes=16 * 2**20),
+        out_shape=jax.ShapeDtypeStruct((rows, cols), jnp.float32),
+        compiler_params=pltpu.CompilerParams(vmem_limit_bytes=40 * 2**20),
         cost_estimate=pl.CostEstimate(
-            flops=2 * rows * cols * depth, bytes_accessed=4 * rows * cols, transcendentals=0
-        ),
-        name="gram_tile",
-    )(place, normals, left, right, regular)
-
-
-def tile_kernel(system_ref, strip_ref, gram_ref, right_ref, inverse_ref, out_ref):
-    panel = split_dot(strip_ref[...] + gram_ref[...], inverse_ref[...])
-    high, low = split(panel)
-    left = jnp.concatenate([high, high, low], axis=1)
-    out_ref[...] = system_ref[...] + jnp.dot(left, right_ref[...], preferred_element_type=jnp.float32)
-
-
-def tile_rows(system, strip, gram_cols, right, inverse):
-    rows, cols = system.shape
-    block = block_rows(rows // 2)
-    tile_spec = pl.BlockSpec((block, cols), lambda i: (i, 0))
-    lead_spec = pl.BlockSpec((block, B), lambda i: (i, 0))
-    return pl.pallas_call(
-        tile_kernel,
-        grid=(rows // block,),
-        in_specs=[
-            tile_spec,
-            lead_spec,
-            lead_spec,
-            pl.BlockSpec(right.shape, lambda i: (0, 0), pipeline_mode=pl.Buffered(1)),
-            pl.BlockSpec(inverse.shape, lambda i: (0, 0), pipeline_mode=pl.Buffered(1)),
-        ],
-        out_specs=tile_spec,
-        out_shape=jax.ShapeDtypeStruct((rows, cols), jnp.float32),
-        compiler_params=pltpu.CompilerParams(vmem_limit_bytes=32 * 2**20),
-        cost_estimate=pl.CostEstimate(
-            flops=6 * rows * cols * B, bytes_accessed=4 * rows * cols, transcendentals=0
+            flops=2 * rows * cols * right.shape[0], bytes_accessed=8 * rows * cols, transcendentals=0
         ),
         name="tile_rows",
-    )(system, strip, gram_cols, right, inverse)
+    )(block_ids, place, normals, *here, *sent, gram_cols, left, right, inverse, regular)
 
 
 def after(value, earlier):
@@ -277,18 +263,39 @@
     return blocks.reshape(count * P_SIZE, count * P_SIZE)
 
 
-def row_strip_piece(normals, earlier):
+def to_odd_core(value):
+    return lax.ppermute(value, "col", [(c, c + 1) for c in range(0, lax.axis_size("col"), 2)])
+
+
+def row_strip(normals, earlier, later):
     peers = lax.axis_size("col")
     chips = peers // 2
-    size = normals.shape[0] // chips
+    rows = normals.shape[0]
     col_index = lax.axis_index("col")
-    arrived = [
-        lax.ppermute(normals[z * size : (z + 1) * size, :B], "col", [(0, 2 * z)]) for z in range(1, chips)
-    ]
-    arrived = sum(after(arrived, earlier))
-    piece = jnp.where(col_index == 0, normals[:size, :B], arrived)
-    second = lax.ppermute(piece[size // 2 :], "col", [(c, c + 1) for c in range(0, peers, 2)])
-    return jnp.where(col_index % 2 == 0, piece[: size // 2], second)
+    chip = col_index // 2
+    if chips > 4:
+        size = rows // chips
+        share = normals[:size, :B]
+        for z in range(1, chips):
+            got = lax.ppermute(normals[z * size : (z + 1) * size, :B], "col", [(0, 2 * z)])
+            share = jnp.where(chip == z, got, share)
+        cores = [list(range(k, peers, 2)) for k in range(2)]
+        return [(jnp.int32(0), lax.all_gather(share, "col", axis=0, tiled=True, axis_index_groups=cores))]
+    count = chips - 1
+    size = rows // count
+    local = after([normals[i * size : (i + 1) * size, :B] for i in range(count)], earlier)
+    arrived = [lax.ppermute(value, "col", [(0, 2 * (1 + i))]) for i, value in enumerate(local)]
+    arrived = sum(after(arrived, later))
+    at_source = chip == 0
+    mine = jnp.where(at_source, local[0], arrived)
+    pieces = [(jnp.where(at_source, 0, chip - 1), mine)]
+    for s in range(1, count):
+        pairs = [(2 * (1 + i), 2 * (1 + (i + s) % count)) for i in range(count)]
+        got = lax.ppermute(mine, "col", pairs)
+        which = -s % count
+        piece = jnp.where(at_source, local[which], got)
+        pieces.append((jnp.where(at_source, which, (chip - 1 - s) % count), piece))
+    return pieces
 
 
 def doubled(value, bits, reached):
@@ -314,22 +321,28 @@
     col_peers = lax.axis_size("col")
     col_strip = lax.psum(jnp.where(row_index == 0, normals[:B], 0.0), "row")
 
+    top = jnp.where(row_index == 0, normals[:B], 0.0)
+    col_strip = lax.psum(top, "row")
+
     index_bits = [1 << i for i in range((row_peers * col_peers - 1).bit_length())]
     block, reached = doubled(normals[:B, :B], [bit for bit in index_bits if bit >= col_peers], [0])
 
-    along = lax.all_gather(design, "col", axis=1, tiled=True)
+    along = after(lax.all_gather(design, "col", axis=1, tiled=True), block)
     along = along.reshape(obs_here, row_peers, 2, cols_here)
     far = lax.dynamic_index_in_dim(along, core, 2, keepdims=False)
     sent = [
         jnp.concatenate([design, far[:, to], along[:, 0, 0, :B]], axis=1) for to in range(row_peers)
     ]
-    joined = lax.all_to_all(jnp.stack(sent), "row", 0, 0, tiled=True)
+    sent = jnp.stack(sent)
+    joined = lax.all_to_all(sent, "row", 0, 0, tiled=True)
     joined = joined.reshape(obs, 2 * cols_here + B)
 
-    piece = row_strip_piece(normals, (block, joined))
-    strip = lax.all_gather(piece, "col", axis=0, tiled=True)
-
-    corner, _ = doubled(after(block, piece), [bit for bit in reversed(index_bits) if bit < col_peers], reached)
+    pieces = row_strip(normals, top, sent)
+    here = [piece for _, piece in pieces]
+    passed = [to_odd_core(piece) for piece in here]
+
+    z_and_core = [bit for bit in reversed(index_bits) if bit < col_peers]
+    corner, _ = doubled(after(block, here[0]), z_and_core, reached)
 
     other = lax.ppermute(
         joined[:, cols_here : 2 * cols_here], "col", [(c, c ^ 1) for c in range(col_peers)]
@@ -341,10 +354,14 @@
     place = jnp.stack([row_index, col_index]).astype(jnp.int32)
     inverse = corner_factor(corner, lead, filters, lead_reg)
     gram_left, gram_right, gram_rows, gram_cols = filter_sides(place, joined, other, filters, own_reg, lead_reg)
-    in_hbm = functools.partial(pltpu.with_memory_space_constraint, memory_space=pltpu.HBM)
-    system = gram_tile(place, in_hbm(normals), gram_left, gram_right, own_reg)
-    right = right_side(place, col_strip, gram_rows, inverse)
-    return tile_rows(in_hbm(system), strip, gram_cols, right, inverse)
+    right = right_side(place, col_strip, gram_rows, inverse, gram_right)
+    per_piece = here[0].shape[0] // block_rows(rows_here // 2)
+    which = jnp.stack([index for index, _ in pieces])
+    block_ids = which[:, None] * per_piece + jnp.arange(per_piece, dtype=jnp.int32)[None, :]
+    block_ids = block_ids.reshape(-1).astype(jnp.int32)
+    return tile_rows(
+        place, block_ids, normals, here, passed, gram_cols, gram_left, right, inverse, own_reg
+    )
 
 
 def solution(mesh):

time: 178 us -> 181 us (1.017)
  the two profiles are of different devices: /device:TPU:24 before, /device:TPU:0 now
where the time goes in v8:
time: 181 us; the launch traced here: 180 us
  waiting for transfers between devices  43.4 us (24%)
  Pallas kernels  43.1 us (24%)
  starting transfers between devices  40.3 us (22%)
  local copies, waits for them, and re-layouts  25.9 us (14%)
  between operations  15.2 us (8%)
  other arithmetic  12.3 us (7%)
    pallas_call x1, Pallas kernels, tile_rows(): pl.pallas_call(functools.partial(tile_kernel, count), grid_spec=pltpu.Pre...  22.7 us
    ppermute x3, waiting for transfers between devices, row_strip(): lax.ppermute(value, 'col', [(0, 2 * (1 + i))])  20.4 us
    ppermute x5, starting transfers between devices, doubled(): got = lax.ppermute(value, ('row', 'col'), pairs)  18.8 us
    pallas_call x1, Pallas kernels, corner_factor(): pl.pallas_call(corner_kernel, out_shape=jax.ShapeDtypeStruct((B, B), jnp....  13.9 us
    psum x1, waiting for transfers between devices, body(): col_strip = lax.psum(top, 'row')  11.9 us
    unnamed x31, local copies, waits for them, and re-layouts  11.2 us
    all_gather x1, waiting for transfers between devices, body(): along = after(lax.all_gather(design, 'col', axis=1, tiled=True), block)  7.29 us
    ppermute x3, starting transfers between devices, row_strip(): lax.ppermute(value, 'col', [(0, 2 * (1 + i))])  6.81 us
  transfers between devices with their start and end apart: 17, of which 7 were waited for; matrix products, arithmetic and copies ran while one was open for 14% of the time, Pallas kernels for 11%

profile of v8, /device:TPU:0, one launch (start us, length us, event | category | flops | bytes accessed | tf_op | source)
XLA Modules:
  0.0 180.1 jit_solution(9671131964111946632)
XLA Ops:
  9.1 4.9 %collective-permute-start.3 = (f32[256,256]{1,0:T(8,128)S(1)}, f32[256,256]{1,0:T(8,128)S(1)}, u32[]{:S(2)}, u32[]{:S(2)}) collective-permute-start(f32[256,256]{1,0:T(8,128)S(1)} %slice.52), channel_id=1, source_target_pairs={{0,8}} | collective-permute-start | bytes 786440 | tf_op jit(solution)/shard_map/ppermute | solution.py:306
  14.0 2.7 %slice_select_fusion = f32[256,1536]{1,0:T(8,128)} fusion(f32[3072,1536]{1,0:T(8,128)} %normals_ref.1, pred[]{:T(512)S(6)} %eq.27), kind=kLoop, calls=%fused_computation.1 | loop fusion | flops 393216 | bytes 3145729 | tf_op jit(solution)/shard_map/jit(_where)/select_n | solution.py:324
  18.8 2.0 %collective-permute-start.4 = (f32[256,256]{1,0:T(8,128)S(1)}, f32[256,256]{1,0:T(8,128)}, u32[]{:S(2)}, u32[]{:S(2)}) collective-permute-start(f32[256,256]{1,0:T(8,128)S(1)} %broadcast_select_fusion.5), channel_id=1, source_target_pairs={{0,16},{8,24}} | collective-permute-start | bytes 786440 | tf_op jit(solution)/shard_map/ppermute | solution.py:306
  20.8 2.2 %fusion.6 = (f32[1024,256]{1,0:T(8,128)S(1)}, f32[1024,256]{1,0:T(8,128)S(1)}, f32[1024,256]{1,0:T(8,128)S(1)}) fusion(f32[3072,1536]{1,0:T(8,128)} %normals_ref.1), kind=kLoop, calls=%fused_computation.38 | loop fusion | bytes 6291456 | tf_op jit(solution)/shard_map/slice | solution.py:286
  23.0 2.3 %collective-permute-start = (f32[1024,256]{1,0:T(8,128)S(1)}, f32[1024,256]{1,0:T(8,128)}, u32[]{:S(2)}, u32[]{:S(2)}) collective-permute-start(f32[1024,256]{1,0:T(8,128)S(1)} %get-tuple-element.17), channel_id=1, source_target_pairs={{0,2},{8,10},{16,18},{24,26}} | collective-permute-start | bytes 3145736 | tf_op jit(solution)/shard_map/ppermute | solution.py:287
  25.3 2.3 %collective-permute-start.1 = (f32[1024,256]{1,0:T(8,128)S(1)}, f32[1024,256]{1,0:T(8,128)}, u32[]{:S(2)}, u32[]{:S(2)}) collective-permute-start(f32[1024,256]{1,0:T(8,128)S(1)} %get-tuple-element.18), channel_id=1, source_target_pairs={{0,4},{8,12},{16,20},{24,28}} | collective-permute-start | bytes 3145736 | tf_op jit(solution)/shard_map/ppermute | solution.py:287
  27.6 2.3 %collective-permute-start.2 = (f32[1024,256]{1,0:T(8,128)S(1)}, f32[1024,256]{1,0:T(8,128)}, u32[]{:S(2)}, u32[]{:S(2)}) collective-permute-start(f32[1024,256]{1,0:T(8,128)S(1)} %get-tuple-element.19), channel_id=1, source_target_pairs={{0,6},{8,14},{16,22},{24,30}} | collective-permute-start | bytes 3145736 | tf_op jit(solution)/shard_map/ppermute | solution.py:287
  30.8 7.3 %all-gather.2.cloned.1.call-done = f32[32,12288]{1,0:T(8,128)} async-done(((f32[32,1536]{1,0:T(8,128)}), f32[32,12288]{1,0:T(8,128)}) %all-gather.2.cloned.1.call-update) | async-done | bytes 1572880 | tf_op jit(solution)/shard_map/all_gather | solution.py:330
  38.1 3.4 %reshape.77 = f32[32,4,2,1536]{3,2,1,0:T(2,128)} reshape(f32[32,12288]{1,0:T(8,128)} %all-gather.2.cloned.1.call-done) | data formatting | bytes 3145728 | tf_op jit(solution)/shard_map/reshape | solution.py:331
  41.5 2.2 %constant_dynamic-slice_fusion = f32[32,4,1,1536]{3,2,1,0:T(1,128)S(1)} fusion(f32[32,4,2,1536]{3,2,1,0:T(2,128)} %reshape.77, s32[]{:T(128)S(6)} %select_n.120), kind=kLoop, calls=%fused_computation.37 | loop fusion | bytes 1572868 | tf_op jit(solution)/shard_map/jit(dynamic_index_in_dim)/dynamic_slice | solution.py:332
  46.4 9.2 %collective-permute-done.1 = f32[1024,256]{1,0:T(8,128)} collective-permute-done((f32[1024,256]{1,0:T(8,128)S(1)}, f32[1024,256]{1,0:T(8,128)}, u32[]{:S(2)}, u32[]{:S(2)}) %collective-permute-start.1) | collective-permute-done | bytes 1048608 | tf_op jit(solution)/shard_map/ppermute | solution.py:287
  55.6 11.2 %collective-permute-done.2 = f32[1024,256]{1,0:T(8,128)} collective-permute-done((f32[1024,256]{1,0:T(8,128)S(1)}, f32[1024,256]{1,0:T(8,128)}, u32[]{:S(2)}, u32[]{:S(2)}) %collective-permute-start.2) | collective-permute-done | bytes 1048608 | tf_op jit(solution)/shard_map/ppermute | solution.py:287
  66.8 2.1 %add_select_fusion.refs_0_ = f32[1024,256]{1,0:T(8,128)S(1)} fusion(f32[1024,256]{1,0:T(8,128)S(1)} %get-tuple-element.17, f32[1024,256]{1,0:T(8,128)} %collective-permute-done.2, f32[1024,256]{1,0:T(8,128)} %collective-permute-done, f32[1024,256]{1,0:T(8,128)} %collective-permute-done.1, pred[]{:T(512)S(6)} %eq.26), kind=kLoop, calls=%fused_computation.2 | loop fusion | flops 786432 | bytes 5242881 | tf_op jit(solution)/shard_map/jit(_where)/select_n | solution.py:290
  70.8 4.5 %all-to-all-start = ((f32[4,32,3328]{2,1,0:T(8,128)}), f32[4,32,3328]{2,1,0:T(8,128)}, u32[]{:S(2)}, u32[]{:S(2)}) async-start(f32[4,32,3328]{2,1,0:T(8,128)} %pad_maximum_fusion), calls=%async_computation | async-start | bytes 3407872 | tf_op jit(solution)/shard_map/all_to_all | solution.py:337
  77.0 7.4 %collective-permute-start.11 = (f32[256,256]{1,0:T(8,128)S(1)}, f32[256,256]{1,0:T(8,128)S(1)}, u32[]{:S(2)}, u32[]{:S(2)}) collective-permute-start(f32[256,256]{1,0:T(8,128)S(1)} %broadcast_select_fusion.6), channel_id=1, source_target_pairs={{0,4},{8,12},{16,20},{24,28}} | collective-permute-start | bytes 786440 | tf_op jit(solution)/shard_map/ppermute | solution.py:306
  86.0 2.3 %collective-permute-start.7 = (f32[1024,256]{1,0:T(8,128)S(1)}, f32[1024,256]{1,0:T(8,128)}, u32[]{:S(2)}, u32[]{:S(2)}) collective-permute-start(f32[1024,256]{1,0:T(8,128)S(1)} %add_select_fusion.refs_0_), channel_id=1, source_target_pairs={{0,1},{2,3},{4,5},{6,7},{8,9},{10,11},{12,13},{14,15},{16,17},{18,... | collective-permute-start | bytes 3145736 | tf_op jit(solution)/shard_map/ppermute | solution.py:267
  90.7 2.3 %collective-permute-start.9 = (f32[1024,256]{1,0:T(8,128)S(1)}, f32[1024,256]{1,0:T(8,128)}, u32[]{:S(2)}, u32[]{:S(2)}) collective-permute-start(f32[1024,256]{1,0:T(8,128)S(1)} %broadcast_select_fusion.refs_2_), channel_id=1, source_target_pairs={{0,1},{2,3},{4,5},{6,7},{8,9},{10,11},{12,13},{14,15},{16,17},{18,... | collective-permute-start | bytes 3145736 | tf_op jit(solution)/shard_map/ppermute | solution.py:267
  93.1 2.3 %collective-permute-start.8 = (f32[1024,256]{1,0:T(8,128)S(1)}, f32[1024,256]{1,0:T(8,128)}, u32[]{:S(2)}, u32[]{:S(2)}) collective-permute-start(f32[1024,256]{1,0:T(8,128)S(1)} %broadcast_select_fusion.1.refs_1_), channel_id=1, source_target_pairs={{0,1},{2,3},{4,5},{6,7},{8,9},{10,11},{12,13},{14,15},{16,17},{18,... | collective-permute-start | bytes 3145736 | tf_op jit(solution)/shard_map/ppermute | solution.py:267
  96.7 2.1 %slice.68 = f32[128,1536]{1,0:T(8,128)} slice(f32[128,3328]{1,0:T(8,128)} %bitcast.14.joined_ref), slice={[0:128], [1536:3072]} | slice | bytes 1572864 | tf_op jit(solution)/shard_map/slice | solution.py:348
  100.5 3.1 %collective-permute-start.13 = (f32[256,256]{1,0:T(8,128)}, f32[256,256]{1,0:T(8,128)}, u32[]{:S(2)}, u32[]{:S(2)}) collective-permute-start(f32[256,256]{1,0:T(8,128)} %broadcast_select_fusion.3), channel_id=1, source_target_pairs={{0,1},{8,9},{16,17},{24,25},{4,5},{12,13},{20,21},{28,29},{2,3},{1... | collective-permute-start | bytes 786440 | tf_op jit(solution)/shard_map/ppermute | solution.py:306
  106.3 13.9 %corner_factor.1.inverse_ref.refs_9_ = f32[256,256]{1,0:T(8,128)S(1)} custom-call(f32[256,256]{1,0:T(8,128)S(1)} %broadcast_select_fusion.4.block_ref, f32[128,256]{1,0:T(8,128)S(1)} %slice.69.design_ref, f32[128,128]{1,0:T(8,128)S(1)} %select_n.126.filter_ref, f32[1,256]{1,0:T(1,128)S(1)} %bitcast.33), custom_call_target="tpu_custom_call" | custom-call | flops 1000000000 | bytes 1048576 | tf_op jit(solution)/shard_map/corner_factor/pallas_call | solution.py:82
  120.2 5.1 %filter_sides.1 = (bf16[3072,384]{1,0:T(8,128)(2,1)S(1)}, bf16[384,1536]{1,0:T(8,128)(2,1)S(1)}, f32[256,1536]{1,0:T(8,128)S(1)}, f32[3072,256]{1,0:T(8,128)S(1)}) custom-call(s32[2]{0:T(128)S(1)} %pad_add_fusion.place_ref, f32[128,3328]{1,0:T(8,128)} %bitcast.14.joined_ref, f32[128,1536]{1,0:T(8,128)} %collective-permute-done.10.other_ref, ...), custom_call_target="tpu_custom_call" | custom-call | flops 905969664 | bytes 9437184 | tf_op jit(solution)/shard_map/filter_sides/pallas_call | solution.py:170
  130.6 11.9 %all-reduce.2.cloned.1.call-done.strip_ref = f32[256,1536]{1,0:T(8,128)} async-done(((f32[256,1536]{1,0:T(8,128)}), f32[256,1536]{1,0:T(8,128)}) %all-reduce.2.cloned.1.call-update) | async-done | bytes 1572880 | tf_op jit(solution)/shard_map/psum | solution.py:325
  150.0 22.7 %tile_rows.1 = f32[3072,1536]{1,0:T(8,128)} custom-call(s32[6]{0:T(128)S(1)} %add.59.block_ids_ref, s32[2]{0:T(128)S(1)} %pad_add_fusion.place_ref, f32[3072,1536]{1,0:T(8,128)} %normals_ref.1, f32[1024,256]{1,0:T(8,128)S(1)} %add_select_fusion.refs_0_, f32[1024,256]{1,0:T(8,128)S(1)} %broadcast_select_fusion.1.refs_1_, ...), custom_call_target="tpu_custom_call" | custom-call | flops 10871635968 | bytes 37748736 | tf_op jit(solution)/shard_map/tile_rows/pallas_call | solution.py:234
  (78 shorter events, 33.5 us)
Async XLA Ops:
  7.4 30.7 %all-gather.2.cloned.1.call-start = ((), (), s32[]{:S(2)}) async-start(), calls=%async_computation.1 | async-start | bytes 1769472 | tf_op jit(solution)/shard_map/all_gather | solution.py:330
  8.1 134.5 %all-reduce.2.cloned.1.call-start = ((), (), s32[]{:S(2)}) async-start(), calls=%async_computation.2 | async-start | bytes 3145728 | tf_op jit(solution)/shard_map/psum | solution.py:325
  9.1 8.7 %collective-permute-start.3 = (f32[256,256]{1,0:T(8,128)S(1)}, f32[256,256]{1,0:T(8,128)S(1)}, u32[]{:S(2)}, u32[]{:S(2)}) collective-permute-start(f32[256,256]{1,0:T(8,128)S(1)} %slice.52), channel_id=1, source_target_pairs={{0,8}} | collective-permute-start | bytes 786440 | tf_op jit(solution)/shard_map/ppermute | solution.py:306
  18.8 11.0 %copy-start.12 = (f32[256,256]{1,0:T(8,128)}, f32[256,256]{1,0:T(8,128)S(1)}, u32[]{:S(2)}) copy-start(f32[256,256]{1,0:T(8,128)S(1)} %broadcast_select_fusion.5) | copy-start | bytes 786436
  18.8 11.0 %collective-permute-start.4 = (f32[256,256]{1,0:T(8,128)S(1)}, f32[256,256]{1,0:T(8,128)}, u32[]{:S(2)}, u32[]{:S(2)}) collective-permute-start(f32[256,256]{1,0:T(8,128)S(1)} %broadcast_select_fusion.5), channel_id=1, source_target_pairs={{0,16},{8,24}} | collective-permute-start | bytes 786440 | tf_op jit(solution)/shard_map/ppermute | solution.py:306
  23.0 18.5 %copy-start.10 = (f32[1024,256]{1,0:T(8,128)}, f32[1024,256]{1,0:T(8,128)S(1)}, u32[]{:S(2)}) copy-start(f32[1024,256]{1,0:T(8,128)S(1)} %get-tuple-element.19) | copy-start | bytes 3145732
  23.0 23.4 %collective-permute-start = (f32[1024,256]{1,0:T(8,128)S(1)}, f32[1024,256]{1,0:T(8,128)}, u32[]{:S(2)}, u32[]{:S(2)}) collective-permute-start(f32[1024,256]{1,0:T(8,128)S(1)} %get-tuple-element.17), channel_id=1, source_target_pairs={{0,2},{8,10},{16,18},{24,26}} | collective-permute-start | bytes 3145736 | tf_op jit(solution)/shard_map/ppermute | solution.py:287
  25.3 30.3 %collective-permute-start.1 = (f32[1024,256]{1,0:T(8,128)S(1)}, f32[1024,256]{1,0:T(8,128)}, u32[]{:S(2)}, u32[]{:S(2)}) collective-permute-start(f32[1024,256]{1,0:T(8,128)S(1)} %get-tuple-element.18), channel_id=1, source_target_pairs={{0,4},{8,12},{16,20},{24,28}} | collective-permute-start | bytes 3145736 | tf_op jit(solution)/shard_map/ppermute | solution.py:287
  27.6 39.3 %collective-permute-start.2 = (f32[1024,256]{1,0:T(8,128)S(1)}, f32[1024,256]{1,0:T(8,128)}, u32[]{:S(2)}, u32[]{:S(2)}) collective-permute-start(f32[1024,256]{1,0:T(8,128)S(1)} %get-tuple-element.19), channel_id=1, source_target_pairs={{0,6},{8,14},{16,22},{24,30}} | collective-permute-start | bytes 3145736 | tf_op jit(solution)/shard_map/ppermute | solution.py:287
  69.0 21.5 %collective-permute-start.6 = (f32[1024,256]{1,0:T(8,128)S(1)}, f32[1024,256]{1,0:T(8,128)}, u32[]{:S(2)}, u32[]{:S(2)}) collective-permute-start(f32[1024,256]{1,0:T(8,128)S(1)} %add_select_fusion.refs_0_), channel_id=1, source_target_pairs={{2,6},{4,2},{6,4},{10,14},{12,10},{14,12},{18,22},{20,18},{22,20},... | collective-permute-start | bytes 3145736 | tf_op jit(solution)/shard_map/ppermute | solution.py:294
  70.8 15.2 %copy-start.14 = (f32[2,32,32]{2,1,0:T(8,128)S(1)}, f32[2,32,32]{2,1,0:T(8,128)}, u32[]{:S(2)}) copy-start(f32[2,32,32]{2,1,0:T(8,128)} %param.6) | copy-start | bytes 24580
  70.8 25.9 %all-to-all-start = ((f32[4,32,3328]{2,1,0:T(8,128)}), f32[4,32,3328]{2,1,0:T(8,128)}, u32[]{:S(2)}, u32[]{:S(2)}) async-start(f32[4,32,3328]{2,1,0:T(8,128)} %pad_maximum_fusion), calls=%async_computation | async-start | bytes 3407872 | tf_op jit(solution)/shard_map/all_to_all | solution.py:337
  75.3 17.7 %collective-permute-start.5 = (f32[1024,256]{1,0:T(8,128)S(1)}, f32[1024,256]{1,0:T(8,128)}, u32[]{:S(2)}, u32[]{:S(2)}) collective-permute-start(f32[1024,256]{1,0:T(8,128)S(1)} %add_select_fusion.refs_0_), channel_id=1, source_target_pairs={{2,4},{4,6},{6,2},{10,12},{12,14},{14,10},{18,20},{20,22},{22,18},... | collective-permute-start | bytes 3145736 | tf_op jit(solution)/shard_map/ppermute | solution.py:294
  77.0 11.3 %collective-permute-start.11 = (f32[256,256]{1,0:T(8,128)S(1)}, f32[256,256]{1,0:T(8,128)S(1)}, u32[]{:S(2)}, u32[]{:S(2)}) collective-permute-start(f32[256,256]{1,0:T(8,128)S(1)} %broadcast_select_fusion.6), channel_id=1, source_target_pairs={{0,4},{8,12},{16,20},{24,28}} | collective-permute-start | bytes 786440 | tf_op jit(solution)/shard_map/ppermute | solution.py:306
  86.0 63.9 %collective-permute-start.7 = (f32[1024,256]{1,0:T(8,128)S(1)}, f32[1024,256]{1,0:T(8,128)}, u32[]{:S(2)}, u32[]{:S(2)}) collective-permute-start(f32[1024,256]{1,0:T(8,128)S(1)} %add_select_fusion.refs_0_), channel_id=1, source_target_pairs={{0,1},{2,3},{4,5},{6,7},{8,9},{10,11},{12,13},{14,15},{16,17},{18,... | collective-permute-start | bytes 3145736 | tf_op jit(solution)/shard_map/ppermute | solution.py:267
  89.1 3.9 %copy-start.11 = (f32[1024,256]{1,0:T(8,128)S(1)}, f32[1024,256]{1,0:T(8,128)}, u32[]{:S(2)}) copy-start(f32[1024,256]{1,0:T(8,128)} %copy-done.10) | copy-start | bytes 3145732
  89.1 9.7 %collective-permute-start.12 = (f32[256,256]{1,0:T(8,128)}, f32[256,256]{1,0:T(8,128)S(1)}, u32[]{:S(2)}, u32[]{:S(2)}) collective-permute-start(f32[256,256]{1,0:T(8,128)} %broadcast_select_fusion.2), channel_id=1, source_target_pairs={{0,2},{8,10},{16,18},{24,26},{4,6},{12,14},{20,22},{28,30}} | collective-permute-start | bytes 786440 | tf_op jit(solution)/shard_map/ppermute | solution.py:306
  90.7 59.3 %collective-permute-start.9 = (f32[1024,256]{1,0:T(8,128)S(1)}, f32[1024,256]{1,0:T(8,128)}, u32[]{:S(2)}, u32[]{:S(2)}) collective-permute-start(f32[1024,256]{1,0:T(8,128)S(1)} %broadcast_select_fusion.refs_2_), channel_id=1, source_target_pairs={{0,1},{2,3},{4,5},{6,7},{8,9},{10,11},{12,13},{14,15},{16,17},{18,... | collective-permute-start | bytes 3145736 | tf_op jit(solution)/shard_map/ppermute | solution.py:267
  93.1 56.9 %collective-permute-start.8 = (f32[1024,256]{1,0:T(8,128)S(1)}, f32[1024,256]{1,0:T(8,128)}, u32[]{:S(2)}, u32[]{:S(2)}) collective-permute-start(f32[1024,256]{1,0:T(8,128)S(1)} %broadcast_select_fusion.1.refs_1_), channel_id=1, source_target_pairs={{0,1},{2,3},{4,5},{6,7},{8,9},{10,11},{12,13},{14,15},{16,17},{18,... | collective-permute-start | bytes 3145736 | tf_op jit(solution)/shard_map/ppermute | solution.py:267
  98.8 21.4 %collective-permute-start.10 = (f32[128,1536]{1,0:T(8,128)}, f32[128,1536]{1,0:T(8,128)}, u32[]{:S(2)}, u32[]{:S(2)}) collective-permute-start(f32[128,1536]{1,0:T(8,128)} %slice.68), channel_id=1, source_target_pairs={{0,1},{1,0},{2,3},{3,2},{4,5},{5,4},{6,7},{7,6},{8,9},{9,8},{10,11... | collective-permute-start | bytes 2359304 | tf_op jit(solution)/shard_map/ppermute | solution.py:347
  100.5 3.9 %collective-permute-start.13 = (f32[256,256]{1,0:T(8,128)}, f32[256,256]{1,0:T(8,128)}, u32[]{:S(2)}, u32[]{:S(2)}) collective-permute-start(f32[256,256]{1,0:T(8,128)} %broadcast_select_fusion.3), channel_id=1, source_target_pairs={{0,1},{8,9},{16,17},{24,25},{4,5},{12,13},{20,21},{28,29},{2,3},{1... | collective-permute-start | bytes 786440 | tf_op jit(solution)/shard_map/ppermute | solution.py:306
  146.7 3.3 %copy-start.2 = (f32[3072,256]{1,0:T(8,128)S(1)}, f32[3072,256]{1,0:T(8,128)}, u32[]{:S(2)}) copy-start(f32[3072,256]{1,0:T(8,128)} %copy-done.1) | copy-start | bytes 9437188
  146.7 3.3 %copy-start.4 = (bf16[3072,384]{1,0:T(8,128)(2,1)S(1)}, bf16[3072,384]{1,0:T(8,128)(2,1)}, u32[]{:S(2)}) copy-start(bf16[3072,384]{1,0:T(8,128)(2,1)} %copy-done.3) | copy-start | bytes 7077892
  148.2 1.7 copy-start
  (8 other events, 10.7 us)
Sparse Core Ops, SparseCore 0:
  9.8 28.2 all-gather.1
Sparse Core Ops, SparseCore 1:
  70.7 71.8 all-reduce.1

commit v9 on v7

--- a/solution.py
+++ b/solution.py
@@ -124,6 +124,7 @@
 def filter_kernel(
     place_ref,
     joined_ref,
+    lead_ref,
     other_ref,
     filter_ref,
     regular_ref,
@@ -137,8 +138,9 @@
     cols = right_ref.shape[1]
     obs = filter_ref.shape[0]
     core = lax.rem(col_index, 2)
-    filtered = split_dot(filter_ref[...], joined_ref[...])
-    here, rows_own, lead = filtered[:, :cols], filtered[:, cols : 2 * cols], filtered[:, 2 * cols :]
+    filtered = split_dot(filter_ref[...], joined_ref[:, : 2 * cols])
+    here, rows_own = filtered[:, :cols], filtered[:, cols : 2 * cols]
+    lead = split_dot(filter_ref[...], lead_ref[...])
     row_pos = lax.broadcasted_iota(jnp.int32, (B, cols), 0)
     col_pos = lax.broadcasted_iota(jnp.int32, (1, cols), 1) + col_index * cols
     gram_rows_ref[...] = split_dot(lead.T, here) + jnp.where(row_pos == col_pos, regular_ref[...], 0.0)
@@ -161,13 +163,13 @@
         )
 
 
-def filter_sides(place, joined, other, filter_matrix, regular, lead_reg):
+def filter_sides(place, joined, lead, other, filter_matrix, regular, lead_reg):
     cols = other.shape[1]
     obs = filter_matrix.shape[0]
     vmem = pl.BlockSpec(memory_space=pltpu.VMEM)
     return pl.pallas_call(
         filter_kernel,
-        in_specs=[pl.BlockSpec(memory_space=pltpu.SMEM)] + [vmem] * 5,
+        in_specs=[pl.BlockSpec(memory_space=pltpu.SMEM)] + [vmem] * 6,
         out_specs=[vmem] * 4,
         out_shape=[
             jax.ShapeDtypeStruct((2 * cols, 3 * obs), jnp.bfloat16),
@@ -180,7 +182,7 @@
             flops=18 * cols * obs * B, bytes_accessed=24 * cols * B, transcendentals=0
         ),
         name="filter_sides",
-    )(place, joined, other, filter_matrix, regular, lead_reg)
+    )(place, joined, lead, other, filter_matrix, regular, lead_reg)
 
 
 def gram_kernel(place_ref, normals_ref, left_ref, right_ref, regular_ref, out_ref):
@@ -277,20 +279,6 @@
     return blocks.reshape(count * P_SIZE, count * P_SIZE)
 
 
-def row_strip_piece(normals, earlier):
-    peers = lax.axis_size("col")
-    chips = peers // 2
-    size = normals.shape[0] // chips
-    col_index = lax.axis_index("col")
-    arrived = [
-        lax.ppermute(normals[z * size : (z + 1) * size, :B], "col", [(0, 2 * z)]) for z in range(1, chips)
-    ]
-    arrived = sum(after(arrived, earlier))
-    piece = jnp.where(col_index == 0, normals[:size, :B], arrived)
-    second = lax.ppermute(piece[size // 2 :], "col", [(c, c + 1) for c in range(0, peers, 2)])
-    return jnp.where(col_index % 2 == 0, piece[: size // 2], second)
-
-
 def doubled(value, bits, reached):
     row_peers, col_peers = lax.axis_size("row"), lax.axis_size("col")
     here = lax.axis_index("row") * col_peers + lax.axis_index("col")
@@ -314,33 +302,42 @@
     col_peers = lax.axis_size("col")
     col_strip = lax.psum(jnp.where(row_index == 0, normals[:B], 0.0), "row")
 
+    left_strip = jnp.where(col_index == 0, normals[:, :B], 0.0)
+    top_strip = jnp.where(row_index == 0, normals[:B], 0.0)
+    strip = lax.psum(left_strip, "col")
+    col_strip = lax.psum(top_strip, "row")
+
     index_bits = [1 << i for i in range((row_peers * col_peers - 1).bit_length())]
-    block, reached = doubled(normals[:B, :B], [bit for bit in index_bits if bit >= col_peers], [0])
-
-    along = lax.all_gather(design, "col", axis=1, tiled=True)
-    along = along.reshape(obs_here, row_peers, 2, cols_here)
-    far = lax.dynamic_index_in_dim(along, core, 2, keepdims=False)
-    sent = [
-        jnp.concatenate([design, far[:, to], along[:, 0, 0, :B]], axis=1) for to in range(row_peers)
-    ]
+    hops = [bit for bit in index_bits if bit >= col_peers]
+    hops += [bit for bit in reversed(index_bits) if 1 < bit < col_peers]
+    leading, reached = doubled(normals[:B, :B], hops, [0])
+
+    chips = col_peers // 2
+    design = after(design, (left_strip, top_strip))
+    along = [design]
+    for s in range(1, chips):
+        along.append(lax.ppermute(design, "col", [(c, (c + 2 * s) % col_peers) for c in range(col_peers)]))
+    along = jnp.stack(along)
+    lead = lax.dynamic_index_in_dim(along, col_index // 2, 0, keepdims=False)[:, :B]
+    sent = []
+    for to in range(row_peers):
+        far = lax.dynamic_index_in_dim(along, (col_index // 2 - to) % chips, 0, keepdims=False)
+        sent.append(jnp.concatenate([design, far, lead], axis=1))
     joined = lax.all_to_all(jnp.stack(sent), "row", 0, 0, tiled=True)
     joined = joined.reshape(obs, 2 * cols_here + B)
 
-    piece = row_strip_piece(normals, (block, joined))
-    strip = lax.all_gather(piece, "col", axis=0, tiled=True)
-
-    corner, _ = doubled(after(block, piece), [bit for bit in reversed(index_bits) if bit < col_peers], reached)
-
+    leading = jnp.concatenate([joined[:, 2 * cols_here :], leading], axis=0)
+    leading, _ = doubled(leading, [1], reached)
+    lead, corner = leading[:obs], leading[obs:]
     other = lax.ppermute(
         joined[:, cols_here : 2 * cols_here], "col", [(c, c ^ 1) for c in range(col_peers)]
     )
-    lead = joined[:, 2 * cols_here :]
     filters = filter_matrix_of(filter_blocks, obs // P_SIZE)
     lead_reg = regular[:B].reshape(1, B)
     own_reg = lax.dynamic_slice_in_dim(regular, col_index * cols_here, cols_here).reshape(1, cols_here)
     place = jnp.stack([row_index, col_index]).astype(jnp.int32)
     inverse = corner_factor(corner, lead, filters, lead_reg)
-    gram_left, gram_right, gram_rows, gram_cols = filter_sides(place, joined, other, filters, own_reg, lead_reg)
+    gram_left, gram_right, gram_rows, gram_cols = filter_sides(place, joined, lead, other, filters, own_reg, lead_reg)
     in_hbm = functools.partial(pltpu.with_memory_space_constraint, memory_space=pltpu.HBM)
     system = gram_tile(place, in_hbm(normals), gram_left, gram_right, own_reg)
     right = right_side(place, col_strip, gram_rows, inverse)

time: 178 us -> 202 us (1.13)
  the two profiles are of different devices: /device:TPU:24 before, /device:TPU:0 now
where the time goes in v9:
time: 202 us; the launch traced here: 201 us
  waiting for transfers between devices  81.7 us (40%)
  Pallas kernels  55 us (27%)
  starting transfers between devices  21.2 us (10%)
  local copies, waits for them, and re-layouts  19.5 us (10%)
  between operations  13.8 us (7%)
  other arithmetic  10.1 us (5%)
    psum x1, waiting for transfers between devices, body(): strip = lax.psum(left_strip, 'col')  51.1 us
    ppermute x5, waiting for transfers between devices, doubled(): got = lax.ppermute(value, ('row', 'col'), pairs)  19.4 us
    pallas_call x1, Pallas kernels, tile_rows(): pl.pallas_call(tile_kernel, grid=(rows // block,), in_specs=[tile_spec, l...  18.3 us
    pallas_call x1, Pallas kernels, gram_tile(): pl.pallas_call(gram_kernel, grid_spec=pltpu.PrefetchScalarGridSpec(num_sc...  17.2 us
    unnamed x30, local copies, waits for them, and re-layouts  15.8 us
    pallas_call x1, Pallas kernels, corner_factor(): pl.pallas_call(corner_kernel, out_shape=jax.ShapeDtypeStruct((B, B), jnp....  13.9 us
    ppermute x5, starting transfers between devices, doubled(): got = lax.ppermute(value, ('row', 'col'), pairs)  11.5 us
    ppermute x3, waiting for transfers between devices, body(): lax.ppermute(design, 'col', [(c, (c + 2 * s) % col_peers) for c in range(...  11.2 us
  transfers between devices with their start and end apart: 12, of which 5 were waited for; matrix products, arithmetic and copies ran while one was open for 4% of the time, Pallas kernels for 18%

profile of v9, /device:TPU:0, one launch (start us, length us, event | category | flops | bytes accessed | tf_op | source)
XLA Modules:
  0.0 201.3 jit_solution(8747308305154783210)
XLA Ops:
  6.5 2.7 %slice_select_fusion.1 = f32[256,1536]{1,0:T(8,128)} fusion(f32[3072,1536]{1,0:T(8,128)} %normals_ref.1, pred[]{:T(512)S(6)} %eq.28), kind=kLoop, calls=%fused_computation.2 | loop fusion | flops 393216 | bytes 3145729 | tf_op jit(solution)/shard_map/jit(_where)/select_n | solution.py:306
  9.2 3.8 %slice_select_fusion = f32[3072,256]{1,0:T(8,128)} fusion(f32[3072,1536]{1,0:T(8,128)} %normals_ref.1, pred[]{:T(512)S(6)} %eq.27), kind=kLoop, calls=%fused_computation | loop fusion | flops 786432 | bytes 6291457 | tf_op jit(solution)/shard_map/jit(_where)/select_n | solution.py:305
  13.0 5.0 %collective-permute-start.2 = (f32[32,1536]{1,0:T(8,128)S(1)}, f32[32,1536]{1,0:T(8,128)S(1)}, u32[]{:S(2)}, u32[]{:S(2)}) collective-permute-start(f32[32,1536]{1,0:T(8,128)S(1)} %copy-done.13), channel_id=1, source_target_pairs={{0,6},{1,7},{2,0},{3,1},{4,2},{5,3},{6,4},{7,5},{8,14},{9,15},{10,... | collective-permute-start | bytes 589832 | tf_op jit(solution)/shard_map/ppermute | solution.py:319
  20.1 3.4 %collective-permute-start.3 = (f32[256,256]{1,0:T(8,128)S(1)}, f32[256,256]{1,0:T(8,128)S(1)}, u32[]{:S(2)}, u32[]{:S(2)}) collective-permute-start(f32[256,256]{1,0:T(8,128)S(1)} %slice.37), channel_id=1, source_target_pairs={{0,8}} | collective-permute-start | bytes 786440 | tf_op jit(solution)/shard_map/ppermute | solution.py:287
  23.6 11.1 %collective-permute-done.1 = f32[32,1536]{1,0:T(8,128)S(1)} collective-permute-done((f32[32,1536]{1,0:T(8,128)S(1)}, f32[32,1536]{1,0:T(8,128)S(1)}, u32[]{:S(2)}, u32[]{:S(2)}) %collective-permute-start.1) | collective-permute-done | bytes 196640 | tf_op jit(solution)/shard_map/ppermute | solution.py:319
  36.1 3.4 %collective-permute-start.4 = (f32[256,256]{1,0:T(8,128)S(1)}, f32[256,256]{1,0:T(8,128)S(1)}, u32[]{:S(2)}, u32[]{:S(2)}) collective-permute-start(f32[256,256]{1,0:T(8,128)S(1)} %broadcast_select_fusion.1), channel_id=1, source_target_pairs={{0,16},{8,24}} | collective-permute-start | bytes 786440 | tf_op jit(solution)/shard_map/ppermute | solution.py:287
  39.5 1.3 pad_maximum_fusion
  40.9 3.6 %all-to-all-start = ((f32[4,32,3328]{2,1,0:T(8,128)}), f32[4,32,3328]{2,1,0:T(8,128)S(1)}, u32[]{:S(2)}, u32[]{:S(2)}) async-start(f32[4,32,3328]{2,1,0:T(8,128)} %pad_maximum_fusion), calls=%async_computation | async-start | bytes 3407872 | tf_op jit(solution)/shard_map/all_to_all | solution.py:326
  44.5 11.7 %collective-permute-done.4 = f32[256,256]{1,0:T(8,128)S(1)} collective-permute-done((f32[256,256]{1,0:T(8,128)S(1)}, f32[256,256]{1,0:T(8,128)S(1)}, u32[]{:S(2)}, u32[]{:S(2)}) %collective-permute-start.4) | collective-permute-done | bytes 262176 | tf_op jit(solution)/shard_map/ppermute | solution.py:287
  57.6 3.9 %collective-permute-done.5 = f32[256,256]{1,0:T(8,128)S(1)} collective-permute-done((f32[256,256]{1,0:T(8,128)S(1)}, f32[256,256]{1,0:T(8,128)S(1)}, u32[]{:S(2)}, u32[]{:S(2)}) %collective-permute-start.5) | collective-permute-done | bytes 262176 | tf_op jit(solution)/shard_map/ppermute | solution.py:287
  62.9 3.8 %collective-permute-done.6 = f32[256,256]{1,0:T(8,128)S(1)} collective-permute-done((f32[256,256]{1,0:T(8,128)S(1)}, f32[256,256]{1,0:T(8,128)S(1)}, u32[]{:S(2)}, u32[]{:S(2)}) %collective-permute-start.6) | collective-permute-done | bytes 262176 | tf_op jit(solution)/shard_map/ppermute | solution.py:287
  68.5 2.0 %collective-permute-start.7 = (f32[384,256]{1,0:T(8,128)}, f32[384,256]{1,0:T(8,128)}, u32[]{:S(2)}, u32[]{:S(2)}) collective-permute-start(f32[384,256]{1,0:T(8,128)} %pad_maximum_fusion.10), channel_id=1, source_target_pairs={{0,1},{8,9},{16,17},{24,25},{4,5},{12,13},{20,21},{28,29},{2,3},{1... | collective-permute-start | bytes 1179656 | tf_op jit(solution)/shard_map/ppermute | solution.py:287
  72.5 13.9 %corner_factor.1.inverse_ref = f32[256,256]{1,0:T(8,128)S(1)} custom-call(f32[256,256]{1,0:T(8,128)S(1)} %slice.48.block_ref, f32[128,256]{1,0:T(8,128)S(1)} %slice.46.lead_ref.design_ref, f32[128,128]{1,0:T(8,128)S(1)} %select_n.136.filter_ref, f32[1,256]{1,0:T(1,128)S(1)} %bitcast.33), custom_call_target="tpu_custom_call" | custom-call | flops 1000000000 | bytes 1048576 | tf_op jit(solution)/shard_map/corner_factor/pallas_call | solution.py:82
  89.2 4.0 %filter_sides.1 = (bf16[3072,384]{1,0:T(8,128)(2,1)S(1)}, bf16[384,1536]{1,0:T(8,128)(2,1)S(1)}, f32[256,1536]{1,0:T(8,128)S(1)}, f32[3072,256]{1,0:T(8,128)S(1)}) custom-call(s32[2]{0:T(128)S(1)} %pad_add_fusion.place_ref, f32[128,3328]{1,0:T(8,128)S(1)} %bitcast.32, f32[128,256]{1,0:T(8,128)S(1)} %slice.46.lead_ref.design_ref, f32[128,1536]{1,0:T(8,128)S(1)} %copy-done.12, ...), custom_call_target="tpu_custom_call" | custom-call | flops 905969664 | bytes 9437184 | tf_op jit(solution)/shard_map/filter_sides/pallas_call | solution.py:170
  93.2 1.7 copy-done.1
  94.8 1.4 copy-done.3
  97.4 1.4 copy-done.5
  98.8 1.6 copy-done.7
  101.4 1.6 right_side.1.right_ref
  103.1 17.2 %gram_tile.1.system_ref = f32[3072,1536]{1,0:T(8,128)} custom-call(s32[2]{0:T(128)S(1)} %pad_add_fusion.place_ref, f32[3072,1536]{1,0:T(8,128)} %normals_ref.1, bf16[3072,384]{1,0:T(8,128)(2,1)S(1)} %copy-done.4, bf16[384,1536]{1,0:T(8,128)(2,1)S(1)} %get-tuple-element.12.right_ref, f32[1,1536]{1,0:T(1,128)S(1)} %reshape.45.regular_ref), custom_call_target="tpu_custom_call" | custom-call | flops 3623878656 | bytes 18874368 | tf_op jit(solution)/shard_map/gram_tile/pallas_call | solution.py:215
  120.3 51.1 %all-reduce.3.cloned.1.call-done.strip_ref = f32[3072,256]{1,0:T(8,128)} async-done(((f32[3072,256]{1,0:T(8,128)}), f32[3072,256]{1,0:T(8,128)}) %all-reduce.3.cloned.1.call-update) | async-done | bytes 3145744 | tf_op jit(solution)/shard_map/psum | solution.py:307
  171.4 1.9 copy-done
  173.3 1.9 copy-done.2
  176.2 18.3 %tile_rows.1 = f32[3072,1536]{1,0:T(8,128)} custom-call(f32[3072,1536]{1,0:T(8,128)} %gram_tile.1.system_ref, f32[3072,256]{1,0:T(8,128)S(1)} %copy-done, f32[3072,256]{1,0:T(8,128)S(1)} %copy-done.2, bf16[768,1536]{1,0:T(8,128)(2,1)S(1)} %right_side.1.right_ref, f32[256,256]{1,0:T(8,128)S(1)} %copy-done.10), custom_call_target="tpu_custom_call" | custom-call | flops 7247757312 | bytes 18874368 | tf_op jit(solution)/shard_map/tile_rows/pallas_call | solution.py:249
  (63 shorter events, 15.6 us)
Async XLA Ops:
  6.5 90.9 %all-reduce.5.cloned.1.call-start = ((), (), s32[]{:S(2)}) async-start(), calls=%async_computation.2 | async-start | bytes 3145728 | tf_op jit(solution)/shard_map/psum | solution.py:308
  9.2 3.8 %copy-start.13 = (f32[32,1536]{1,0:T(8,128)S(1)}, f32[32,1536]{1,0:T(8,128)}, u32[]{:S(2)}) copy-start(f32[32,1536]{1,0:T(8,128)} %param.5) | copy-start | bytes 589828
  13.0 10.6 %collective-permute-start.2 = (f32[32,1536]{1,0:T(8,128)S(1)}, f32[32,1536]{1,0:T(8,128)S(1)}, u32[]{:S(2)}, u32[]{:S(2)}) collective-permute-start(f32[32,1536]{1,0:T(8,128)S(1)} %copy-done.13), channel_id=1, source_target_pairs={{0,6},{1,7},{2,0},{3,1},{4,2},{5,3},{6,4},{7,5},{8,14},{9,15},{10,... | collective-permute-start | bytes 589832 | tf_op jit(solution)/shard_map/ppermute | solution.py:319
  18.1 16.7 %collective-permute-start.1 = (f32[32,1536]{1,0:T(8,128)S(1)}, f32[32,1536]{1,0:T(8,128)S(1)}, u32[]{:S(2)}, u32[]{:S(2)}) collective-permute-start(f32[32,1536]{1,0:T(8,128)S(1)} %copy-done.13), channel_id=1, source_target_pairs={{0,4},{1,5},{2,6},{3,7},{4,0},{5,1},{6,2},{7,3},{8,12},{9,13},{10,... | collective-permute-start | bytes 589832 | tf_op jit(solution)/shard_map/ppermute | solution.py:319
  18.1 16.7 %collective-permute-start = (f32[32,1536]{1,0:T(8,128)S(1)}, f32[32,1536]{1,0:T(8,128)S(1)}, u32[]{:S(2)}, u32[]{:S(2)}) collective-permute-start(f32[32,1536]{1,0:T(8,128)S(1)} %copy-done.13), channel_id=1, source_target_pairs={{0,2},{1,3},{2,4},{3,5},{4,6},{5,7},{6,0},{7,1},{8,10},{9,11},{10,... | collective-permute-start | bytes 589832 | tf_op jit(solution)/shard_map/ppermute | solution.py:319
  20.1 15.0 %collective-permute-start.3 = (f32[256,256]{1,0:T(8,128)S(1)}, f32[256,256]{1,0:T(8,128)S(1)}, u32[]{:S(2)}, u32[]{:S(2)}) collective-permute-start(f32[256,256]{1,0:T(8,128)S(1)} %slice.37), channel_id=1, source_target_pairs={{0,8}} | collective-permute-start | bytes 786440 | tf_op jit(solution)/shard_map/ppermute | solution.py:287
  36.1 20.2 %collective-permute-start.4 = (f32[256,256]{1,0:T(8,128)S(1)}, f32[256,256]{1,0:T(8,128)S(1)}, u32[]{:S(2)}, u32[]{:S(2)}) collective-permute-start(f32[256,256]{1,0:T(8,128)S(1)} %broadcast_select_fusion.1), channel_id=1, source_target_pairs={{0,16},{8,24}} | collective-permute-start | bytes 786440 | tf_op jit(solution)/shard_map/ppermute | solution.py:287
  40.9 25.9 %all-to-all-start = ((f32[4,32,3328]{2,1,0:T(8,128)}), f32[4,32,3328]{2,1,0:T(8,128)S(1)}, u32[]{:S(2)}, u32[]{:S(2)}) async-start(f32[4,32,3328]{2,1,0:T(8,128)} %pad_maximum_fusion), calls=%async_computation | async-start | bytes 3407872 | tf_op jit(solution)/shard_map/all_to_all | solution.py:326
  44.4 127.0 %all-reduce.3.cloned.1.call-start = ((), (), s32[]{:S(2)}) async-start(), calls=%async_computation.1 | async-start | bytes 6291456 | tf_op jit(solution)/shard_map/psum | solution.py:307
  56.3 5.2 %collective-permute-start.5 = (f32[256,256]{1,0:T(8,128)S(1)}, f32[256,256]{1,0:T(8,128)S(1)}, u32[]{:S(2)}, u32[]{:S(2)}) collective-permute-start(f32[256,256]{1,0:T(8,128)S(1)} %broadcast_select_fusion.2), channel_id=1, source_target_pairs={{0,4},{8,12},{16,20},{24,28}} | collective-permute-start | bytes 786440 | tf_op jit(solution)/shard_map/ppermute | solution.py:287
  61.5 1.4 copy-start.14
  61.5 5.2 %collective-permute-start.6 = (f32[256,256]{1,0:T(8,128)S(1)}, f32[256,256]{1,0:T(8,128)S(1)}, u32[]{:S(2)}, u32[]{:S(2)}) collective-permute-start(f32[256,256]{1,0:T(8,128)S(1)} %broadcast_select_fusion.3), channel_id=1, source_target_pairs={{0,2},{8,10},{16,18},{24,26},{4,6},{12,14},{20,22},{28,30}} | collective-permute-start | bytes 786440 | tf_op jit(solution)/shard_map/ppermute | solution.py:287
  68.5 3.9 %collective-permute-start.7 = (f32[384,256]{1,0:T(8,128)}, f32[384,256]{1,0:T(8,128)}, u32[]{:S(2)}, u32[]{:S(2)}) collective-permute-start(f32[384,256]{1,0:T(8,128)} %pad_maximum_fusion.10), channel_id=1, source_target_pairs={{0,1},{8,9},{16,17},{24,25},{4,5},{12,13},{20,21},{28,29},{2,3},{1... | collective-permute-start | bytes 1179656 | tf_op jit(solution)/shard_map/ppermute | solution.py:287
  70.5 16.6 %collective-permute-start.8 = (f32[128,1536]{1,0:T(8,128)}, f32[128,1536]{1,0:T(8,128)S(1)}, u32[]{:S(2)}, u32[]{:S(2)}) collective-permute-start(f32[128,1536]{1,0:T(8,128)} %slice.47), channel_id=1, source_target_pairs={{0,1},{1,0},{2,3},{3,2},{4,5},{5,4},{6,7},{7,6},{8,9},{9,8},{10,11... | collective-permute-start | bytes 2359304 | tf_op jit(solution)/shard_map/ppermute | solution.py:332
  88.0 1.1 copy-start.12
  93.1 1.7 copy-start.1
  94.8 1.4 copy-start.3
  96.3 1.2 copy-start.6
  97.4 1.4 copy-start.5
  98.8 1.6 copy-start.7
  100.5 1.0 copy-start.9
  101.4 1.7 copy-start.4
  171.4 1.9 copy-start
  173.3 1.9 copy-start.2
  (3 other events, 2.6 us)
Sparse Core Ops, SparseCore 0:
  19.2 72.6 all-reduce.4
  94.4 76.9 all-reduce.2

commit v10 on v9

--- a/solution.py
+++ b/solution.py
@@ -89,12 +89,13 @@
     )(block, design, filter_matrix, regular)
 
 
-def right_kernel(place_ref, strip_ref, gram_ref, inverse_ref, out_ref):
-    strip = strip_ref[...] + gram_ref[...]
+def right_kernel(place_ref, high_ref, low_ref, gram_ref, inverse_ref, side_ref, out_ref):
+    strip = jnp.concatenate([high_ref[...], low_ref[...]], axis=0) + gram_ref[...]
     panel_high, panel_low = split(-split_dot(inverse_ref[...].T, strip))
     out_ref[:B, :] = panel_high
     out_ref[B : 2 * B, :] = panel_low
-    out_ref[2 * B :, :] = panel_high
+    out_ref[2 * B : 3 * B, :] = panel_high
+    out_ref[3 * B :, :] = side_ref[...]
 
     @pl.when(place_ref[1] == 0)
     def _():
@@ -103,22 +104,23 @@
         identity = identity.astype(jnp.bfloat16)
         out_ref[:B, :B] = identity
         out_ref[B : 2 * B, :B] = jnp.zeros((B, B), jnp.bfloat16)
-        out_ref[2 * B :, :B] = identity
-
-
-def right_side(place, strip, gram_rows, inverse):
+        out_ref[2 * B : 3 * B, :B] = identity
+
+
+def right_side(place, strips, gram_rows, inverse, side):
     cols = gram_rows.shape[1]
+    depth = 3 * B + side.shape[0]
     return pl.pallas_call(
         right_kernel,
-        in_specs=[pl.BlockSpec(memory_space=pltpu.SMEM)] + [pl.BlockSpec(memory_space=pltpu.VMEM)] * 3,
+        in_specs=[pl.BlockSpec(memory_space=pltpu.SMEM)] + [pl.BlockSpec(memory_space=pltpu.VMEM)] * 5,
         out_specs=pl.BlockSpec(memory_space=pltpu.VMEM),
-        out_shape=jax.ShapeDtypeStruct((3 * B, cols), jnp.bfloat16),
+        out_shape=jax.ShapeDtypeStruct((depth, cols), jnp.bfloat16),
         compiler_params=pltpu.CompilerParams(vmem_limit_bytes=24 * 2**20),
         cost_estimate=pl.CostEstimate(
             flops=6 * cols * B * B, bytes_accessed=12 * cols * B, transcendentals=0
         ),
         name="right_side",
-    )(place, strip, gram_rows, inverse)
+    )(place, *strips, gram_rows, inverse, side)
 
 
 def filter_kernel(
@@ -185,16 +187,22 @@
     )(place, joined, lead, other, filter_matrix, regular, lead_reg)
 
 
-def gram_kernel(place_ref, normals_ref, left_ref, right_ref, regular_ref, out_ref):
+def block_rows(half):
+    return max(size for size in range(128, 513, 128) if half % size == 0)
+
+
+def tile_kernel(place_ref, normals_ref, strip_ref, gram_ref, left_ref, right_ref, inverse_ref, regular_ref, out_ref):
     step = pl.program_id(0)
     block, cols = out_ref.shape
+    high, low = split(split_dot(strip_ref[...] + gram_ref[...], inverse_ref[...]))
+    left = jnp.concatenate([high, high, low, left_ref[...]], axis=1)
+    first_row = (place_ref[0] * pl.num_programs(0) + step) * block
     first_col = place_ref[1] * cols
     col_pos = lax.broadcasted_iota(jnp.int32, (1, cols), 1) + first_col
     keep = jnp.where(col_pos < B, 0.0, 1.0)
     out_ref[...] = normals_ref[...] * keep + jnp.dot(
-        left_ref[...], right_ref[...], preferred_element_type=jnp.float32
+        left, right_ref[...], preferred_element_type=jnp.float32
     )
-    first_row = (place_ref[0] * pl.num_programs(0) + step) * block
 
     @pl.when((first_row < first_col + cols) & (first_col < first_row + block))
     def _():
@@ -203,71 +211,48 @@
         out_ref[...] = out_ref[...] + jnp.where(on_diag, regular_ref[...], 0.0)
 
 
-def block_rows(half):
-    return max(size for size in range(128, 513, 128) if half % size == 0)
-
-
-def gram_tile(place, normals, left, right, regular):
+def tile_rows(place, normals, strip, gram_cols, left, right, inverse, regular):
     rows, cols = normals.shape
     block = block_rows(rows // 2)
-    depth = right.shape[0]
-    tile_spec = pl.BlockSpec((block, cols), lambda i, place: (i, 0))
+
+    def whole(array):
+        return pl.BlockSpec(array.shape, lambda i, place: (0,) * array.ndim, pipeline_mode=pl.Buffered(1))
+
+    def blocks(width):
+        return pl.BlockSpec((block, width), lambda i, place: (i, 0))
+
     return pl.pallas_call(
-        gram_kernel,
+        tile_kernel,
         grid_spec=pltpu.PrefetchScalarGridSpec(
             num_scalar_prefetch=1,
             grid=(rows // block,),
-            in_specs=[
-                tile_spec,
-                pl.BlockSpec((block, depth), lambda i, place: (i, 0)),
-                pl.BlockSpec((depth, cols), lambda i, place: (0, 0), pipeline_mode=pl.Buffered(1)),
-                pl.BlockSpec((1, cols), lambda i, place: (0, 0)),
-            ],
-            out_specs=tile_spec,
+            in_specs=[blocks(cols), blocks(B), blocks(B), blocks(left.shape[1])]
+            + [whole(array) for array in [right, inverse, regular]],
+            out_specs=blocks(cols),
         ),
-        out_shape=pltpu.HBM((rows, cols), jnp.float32),
-        compiler_params=pltpu.CompilerParams(vmem_limit_bytes=16 * 2**20),
-        cost_estimate=pl.CostEstimate(
-            flops=2 * rows * cols * depth, bytes_accessed=4 * rows * cols, transcendentals=0
-        ),
-        name="gram_tile",
-    )(place, normals, left, right, regular)
-
-
-def tile_kernel(system_ref, strip_ref, gram_ref, right_ref, inverse_ref, out_ref):
-    panel = split_dot(strip_ref[...] + gram_ref[...], inverse_ref[...])
-    high, low = split(panel)
-    left = jnp.concatenate([high, high, low], axis=1)
-    out_ref[...] = system_ref[...] + jnp.dot(left, right_ref[...], preferred_element_type=jnp.float32)
-
-
-def tile_rows(system, strip, gram_cols, right, inverse):
-    rows, cols = system.shape
-    block = block_rows(rows // 2)
-    tile_spec = pl.BlockSpec((block, cols), lambda i: (i, 0))
-    lead_spec = pl.BlockSpec((block, B), lambda i: (i, 0))
-    return pl.pallas_call(
-        tile_kernel,
-        grid=(rows // block,),
-        in_specs=[
-            tile_spec,
-            lead_spec,
-            lead_spec,
-            pl.BlockSpec(right.shape, lambda i: (0, 0), pipeline_mode=pl.Buffered(1)),
-            pl.BlockSpec(inverse.shape, lambda i: (0, 0), pipeline_mode=pl.Buffered(1)),
-        ],
-        out_specs=tile_spec,
         out_shape=jax.ShapeDtypeStruct((rows, cols), jnp.float32),
         compiler_params=pltpu.CompilerParams(vmem_limit_bytes=32 * 2**20),
         cost_estimate=pl.CostEstimate(
-            flops=6 * rows * cols * B, bytes_accessed=4 * rows * cols, transcendentals=0
+            flops=2 * rows * cols * right.shape[0], bytes_accessed=8 * rows * cols, transcendentals=0
         ),
         name="tile_rows",
-    )(system, strip, gram_cols, right, inverse)
+    )(place, normals, strip, gram_cols, left, right, inverse, regular)
 
 
 def after(value, earlier):
     return lax.optimization_barrier((value, earlier))[0]
+
+
+def spread(value, axis, bits):
+    peers = lax.axis_size(axis)
+    me = lax.axis_index(axis)
+    reached = [0]
+    for bit in bits:
+        pairs = [(i, i | bit) for i in reached if i | bit < peers]
+        got = lax.ppermute(value, axis, pairs)
+        value = jnp.where((me & bit) != 0, got, value)
+        reached += [to for _, to in pairs]
+    return value
 
 
 def filter_matrix_of(filter_blocks, count):
@@ -303,17 +288,19 @@
     col_strip = lax.psum(jnp.where(row_index == 0, normals[:B], 0.0), "row")
 
     left_strip = jnp.where(col_index == 0, normals[:, :B], 0.0)
-    top_strip = jnp.where(row_index == 0, normals[:B], 0.0)
     strip = lax.psum(left_strip, "col")
-    col_strip = lax.psum(top_strip, "row")
-
-    index_bits = [1 << i for i in range((row_peers * col_peers - 1).bit_length())]
-    hops = [bit for bit in index_bits if bit >= col_peers]
-    hops += [bit for bit in reversed(index_bits) if 1 < bit < col_peers]
-    leading, reached = doubled(normals[:B, :B], hops, [0])
+
+    bits = [1 << i for i in range((row_peers - 1).bit_length())]
+    halves = after([normals[: B // 2], normals[B // 2 : B]], left_strip)
+    strips = [spread(halves[0], "row", bits), spread(halves[1], "row", bits[::-1])]
+
+    leading = jnp.concatenate([half[:, :B] for half in strips], axis=0)
+    reached = [row * col_peers for row in range(row_peers)]
+    z_bits = [1 << i for i in range(1, (col_peers - 1).bit_length())]
+    leading, reached = doubled(leading, z_bits[::-1], reached)
 
     chips = col_peers // 2
-    design = after(design, (left_strip, top_strip))
+    design = after(design, left_strip)
     along = [design]
     for s in range(1, chips):
         along.append(lax.ppermute(design, "col", [(c, (c + 2 * s) % col_peers) for c in range(col_peers)]))
@@ -338,10 +325,8 @@
     place = jnp.stack([row_index, col_index]).astype(jnp.int32)
     inverse = corner_factor(corner, lead, filters, lead_reg)
     gram_left, gram_right, gram_rows, gram_cols = filter_sides(place, joined, lead, other, filters, own_reg, lead_reg)
-    in_hbm = functools.partial(pltpu.with_memory_space_constraint, memory_space=pltpu.HBM)
-    system = gram_tile(place, in_hbm(normals), gram_left, gram_right, own_reg)
-    right = right_side(place, col_strip, gram_rows, inverse)
-    return tile_rows(in_hbm(system), strip, gram_cols, right, inverse)
+    right = right_side(place, strips, gram_rows, inverse, gram_right)
+    return tile_rows(place, normals, strip, gram_cols, gram_left, right, inverse, own_reg)
 
 
 def solution(mesh):

time: 202 us -> 185 us (0.916)
  Pallas kernels: 55 us -> 40.2 us
  starting transfers between devices: 21.2 us -> 30.3 us
  local copies, waits for them, and re-layouts: 19.5 us -> 14.6 us
  other arithmetic: 10.1 us -> 6.75 us
  waiting for transfers between devices: 81.7 us -> 78.9 us
    ppermute x0 -> x4, waiting for transfers between devices: none -> 21.5 us  [spread(): got = lax.ppermute(value, axis, pairs)]
    pallas_call x2 -> x1, Pallas kernels: 35.5 us -> 20.7 us  [tile_rows(): pl.pallas_call(tile_kernel, grid_spec=pltpu.PrefetchScalarGridSpec(num_sc...]
    psum x1, waiting for transfers between devices: 51.1 us -> 37.5 us  [body(): strip = lax.psum(left_strip, 'col')]
    ppermute x0 -> x4, starting transfers between devices: none -> 12.7 us  [spread(): got = lax.ppermute(value, axis, pairs)]
    ppermute x5 -> x3, waiting for transfers between devices: 19.4 us -> 11.4 us  [doubled(): got = lax.ppermute(value, ('row', 'col'), pairs)]
    unnamed x30 -> x26, local copies, waits for them, and re-layouts: 15.8 us -> 10.4 us
    ppermute x5 -> x3, starting transfers between devices: 11.5 us -> 7.93 us  [doubled(): got = lax.ppermute(value, ('row', 'col'), pairs)]
    ppermute x3, waiting for transfers between devices: 11.2 us -> 8.55 us  [body(): lax.ppermute(design, 'col', [(c, (c + 2 * s) % col_peers) for c in range(...]
  transfers between devices with their start and end apart: 12 -> 13, of which waited for: 5 -> 7; matrix products, arithmetic and copies ran while one was open for 4% -> 4% of each run, Pallas kernels for 18% -> 11%
where the time goes in v10:
time: 185 us; the launch traced here: 184 us
  waiting for transfers between devices  78.9 us (43%)
  Pallas kernels  40.2 us (22%)
  starting transfers between devices  30.3 us (16%)
  local copies, waits for them, and re-layouts  14.6 us (8%)
  between operations  13.7 us (7%)
  other arithmetic  6.75 us (4%)
    psum x1, waiting for transfers between devices, body(): strip = lax.psum(left_strip, 'col')  37.5 us
    ppermute x4, waiting for transfers between devices, spread(): got = lax.ppermute(value, axis, pairs)  21.5 us
    pallas_call x1, Pallas kernels, tile_rows(): pl.pallas_call(tile_kernel, grid_spec=pltpu.PrefetchScalarGridSpec(num_sc...  20.7 us
    pallas_call x1, Pallas kernels, corner_factor(): pl.pallas_call(corner_kernel, out_shape=jax.ShapeDtypeStruct((B, B), jnp....  13.9 us
    ppermute x4, starting transfers between devices, spread(): got = lax.ppermute(value, axis, pairs)  12.7 us
    ppermute x3, waiting for transfers between devices, doubled(): got = lax.ppermute(value, ('row', 'col'), pairs)  11.4 us
    unnamed x26, local copies, waits for them, and re-layouts  10.4 us
    ppermute x3, waiting for transfers between devices, body(): lax.ppermute(design, 'col', [(c, (c + 2 * s) % col_peers) for c in range(...  8.55 us
  transfers between devices with their start and end apart: 13, of which 7 were waited for; matrix products, arithmetic and copies ran while one was open for 4% of the time, Pallas kernels for 11%

profile of v10, /device:TPU:0, one launch (start us, length us, event | category | flops | bytes accessed | tf_op | source)
XLA Modules:
  0.0 184.4 jit_solution(2014702181722188206)
XLA Ops:
  6.5 3.8 %slice_select_fusion = f32[3072,256]{1,0:T(8,128)} fusion(f32[3072,1536]{1,0:T(8,128)} %normals_ref.1, pred[]{:T(512)S(6)} %eq.24), kind=kLoop, calls=%fused_computation | loop fusion | flops 786432 | bytes 6291457 | tf_op jit(solution)/shard_map/jit(_where)/select_n | solution.py:290
  10.3 5.0 %collective-permute-start.2 = (f32[32,1536]{1,0:T(8,128)S(1)}, f32[32,1536]{1,0:T(8,128)S(1)}, u32[]{:S(2)}, u32[]{:S(2)}) collective-permute-start(f32[32,1536]{1,0:T(8,128)S(1)} %copy-done.11), channel_id=1, source_target_pairs={{0,6},{1,7},{2,0},{3,1},{4,2},{5,3},{6,4},{7,5},{8,14},{9,15},{10,... | collective-permute-start | bytes 589832 | tf_op jit(solution)/shard_map/ppermute | solution.py:306
  16.4 1.5 fusion.6
  17.9 3.4 %collective-permute-start.3 = (f32[128,1536]{1,0:T(8,128)S(1)}, f32[128,1536]{1,0:T(8,128)S(1)}, u32[]{:S(2)}, u32[]{:S(2)}) collective-permute-start(f32[128,1536]{1,0:T(8,128)S(1)} %get-tuple-element.13), channel_id=1, source_target_pairs={{0,8},{1,9},{2,10},{3,11},{4,12},{5,13},{6,14},{7,15}} | collective-permute-start | bytes 2359304 | tf_op jit(solution)/shard_map/ppermute | solution.py:252
  21.3 2.2 %collective-permute-start.5 = (f32[128,1536]{1,0:T(8,128)S(1)}, f32[128,1536]{1,0:T(8,128)}, u32[]{:S(2)}, u32[]{:S(2)}) collective-permute-start(f32[128,1536]{1,0:T(8,128)S(1)} %get-tuple-element.14), channel_id=1, source_target_pairs={{0,16},{1,17},{2,18},{3,19},{4,20},{5,21},{6,22},{7,23}} | collective-permute-start | bytes 2359304 | tf_op jit(solution)/shard_map/ppermute | solution.py:252
  23.5 8.5 %collective-permute-done.1 = f32[32,1536]{1,0:T(8,128)S(1)} collective-permute-done((f32[32,1536]{1,0:T(8,128)S(1)}, f32[32,1536]{1,0:T(8,128)S(1)}, u32[]{:S(2)}, u32[]{:S(2)}) %collective-permute-start.1) | collective-permute-done | bytes 196640 | tf_op jit(solution)/shard_map/ppermute | solution.py:306
  32.4 4.9 %collective-permute-done.3 = f32[128,1536]{1,0:T(8,128)S(1)} collective-permute-done((f32[128,1536]{1,0:T(8,128)S(1)}, f32[128,1536]{1,0:T(8,128)S(1)}, u32[]{:S(2)}, u32[]{:S(2)}) %collective-permute-start.3) | collective-permute-done | bytes 786464 | tf_op jit(solution)/shard_map/ppermute | solution.py:252
  37.3 2.2 %collective-permute-start.4 = (f32[128,1536]{1,0:T(8,128)S(1)}, f32[128,1536]{1,0:T(8,128)}, u32[]{:S(2)}, u32[]{:S(2)}) collective-permute-start(f32[128,1536]{1,0:T(8,128)S(1)} %broadcast_select_fusion.1), channel_id=1, source_target_pairs={{0,16},{8,24},{1,17},{9,25},{2,18},{10,26},{3,19},{11,27},{4,20},{... | collective-permute-start | bytes 2359304 | tf_op jit(solution)/shard_map/ppermute | solution.py:252
  40.1 4.8 %collective-permute-start.6 = (f32[128,1536]{1,0:T(8,128)S(1)}, f32[128,1536]{1,0:T(8,128)}, u32[]{:S(2)}, u32[]{:S(2)}) collective-permute-start(f32[128,1536]{1,0:T(8,128)S(1)} %broadcast_select_fusion.2), channel_id=1, source_target_pairs={{0,8},{16,24},{1,9},{17,25},{2,10},{18,26},{3,11},{19,27},{4,12},{... | collective-permute-start | bytes 2359304 | tf_op jit(solution)/shard_map/ppermute | solution.py:252
  46.2 3.6 %all-to-all-start = ((f32[4,32,3328]{2,1,0:T(8,128)}), f32[4,32,3328]{2,1,0:T(8,128)S(1)}, u32[]{:S(2)}, u32[]{:S(2)}) async-start(f32[4,32,3328]{2,1,0:T(8,128)} %pad_maximum_fusion), calls=%async_computation | async-start | bytes 3407872 | tf_op jit(solution)/shard_map/all_to_all | solution.py:313
  49.9 16.1 %collective-permute-done.4 = f32[128,1536]{1,0:T(8,128)} collective-permute-done((f32[128,1536]{1,0:T(8,128)S(1)}, f32[128,1536]{1,0:T(8,128)}, u32[]{:S(2)}, u32[]{:S(2)}) %collective-permute-start.4) | collective-permute-done | bytes 786464 | tf_op jit(solution)/shard_map/ppermute | solution.py:252
  68.1 3.8 %collective-permute-start.7 = (f32[256,256]{1,0:T(8,128)S(1)}, f32[256,256]{1,0:T(8,128)S(1)}, u32[]{:S(2)}, u32[]{:S(2)}) collective-permute-start(f32[256,256]{1,0:T(8,128)S(1)} %pad_maximum_fusion.11), channel_id=1, source_target_pairs={{0,4},{8,12},{16,20},{24,28}} | collective-permute-start | bytes 786440 | tf_op jit(solution)/shard_map/ppermute | solution.py:272
  71.9 3.8 %collective-permute-done.7 = f32[256,256]{1,0:T(8,128)S(1)} collective-permute-done((f32[256,256]{1,0:T(8,128)S(1)}, f32[256,256]{1,0:T(8,128)S(1)}, u32[]{:S(2)}, u32[]{:S(2)}) %collective-permute-start.7) | collective-permute-done | bytes 262176 | tf_op jit(solution)/shard_map/ppermute | solution.py:272
  75.8 2.0 %collective-permute-start.8 = (f32[256,256]{1,0:T(8,128)S(1)}, f32[256,256]{1,0:T(8,128)}, u32[]{:S(2)}, u32[]{:S(2)}) collective-permute-start(f32[256,256]{1,0:T(8,128)S(1)} %broadcast_select_fusion.5), channel_id=1, source_target_pairs={{0,2},{8,10},{16,18},{24,26},{4,6},{12,14},{20,22},{28,30}} | collective-permute-start | bytes 786440 | tf_op jit(solution)/shard_map/ppermute | solution.py:272
  78.8 7.6 %collective-permute-done.8 = f32[256,256]{1,0:T(8,128)} collective-permute-done((f32[256,256]{1,0:T(8,128)S(1)}, f32[256,256]{1,0:T(8,128)}, u32[]{:S(2)}, u32[]{:S(2)}) %collective-permute-start.8) | collective-permute-done | bytes 262176 | tf_op jit(solution)/shard_map/ppermute | solution.py:272
  87.3 2.1 %collective-permute-start.9 = (f32[384,256]{1,0:T(8,128)}, f32[384,256]{1,0:T(8,128)}, u32[]{:S(2)}, u32[]{:S(2)}) collective-permute-start(f32[384,256]{1,0:T(8,128)} %pad_maximum_fusion.10), channel_id=1, source_target_pairs={{0,1},{8,9},{16,17},{24,25},{4,5},{12,13},{20,21},{28,29},{2,3},{1... | collective-permute-start | bytes 1179656 | tf_op jit(solution)/shard_map/ppermute | solution.py:272
  91.3 4.0 %filter_sides.1 = (bf16[3072,384]{1,0:T(8,128)(2,1)S(1)}, bf16[384,1536]{1,0:T(8,128)(2,1)S(1)}, f32[256,1536]{1,0:T(8,128)S(1)}, f32[3072,256]{1,0:T(8,128)S(1)}) custom-call(s32[2]{0:T(128)S(1)} %pad_add_fusion.place_ref, f32[128,3328]{1,0:T(8,128)S(1)} %bitcast.32, f32[128,256]{1,0:T(8,128)S(1)} %slice.56.lead_ref.design_ref, ...), custom_call_target="tpu_custom_call" | custom-call | flops 905969664 | bytes 9437184 | tf_op jit(solution)/shard_map/filter_sides/pallas_call | solution.py:172
  96.8 13.9 %corner_factor.1.inverse_ref = f32[256,256]{1,0:T(8,128)S(1)} custom-call(f32[256,256]{1,0:T(8,128)S(1)} %slice.58.block_ref, f32[128,256]{1,0:T(8,128)S(1)} %slice.56.lead_ref.design_ref, f32[128,128]{1,0:T(8,128)S(1)} %select_n.138.filter_ref, f32[1,256]{1,0:T(1,128)S(1)} %bitcast.34), custom_call_target="tpu_custom_call" | custom-call | flops 1000000000 | bytes 1048576 | tf_op jit(solution)/shard_map/corner_factor/pallas_call | solution.py:82
  110.7 1.6 right_side.1.right_ref
  113.0 37.5 %all-reduce.2.cloned.1.call-done.strip_ref = f32[3072,256]{1,0:T(8,128)} async-done(((f32[3072,256]{1,0:T(8,128)}), f32[3072,256]{1,0:T(8,128)}) %all-reduce.2.cloned.1.call-update) | async-done | bytes 3145744 | tf_op jit(solution)/shard_map/psum | solution.py:291
  150.5 1.9 %copy-done.4 = f32[3072,256]{1,0:T(8,128)S(1)} copy-done((f32[3072,256]{1,0:T(8,128)S(1)}, f32[3072,256]{1,0:T(8,128)}, u32[]{:S(2)}) %copy-start.4) | copy-done | bytes 3145752
  152.3 1.9 %copy-done.6 = f32[3072,256]{1,0:T(8,128)S(1)} copy-done((f32[3072,256]{1,0:T(8,128)S(1)}, f32[3072,256]{1,0:T(8,128)}, u32[]{:S(2)}) %copy-start.6) | copy-done | bytes 3145752
  154.2 1.7 copy-done.8
  156.9 20.7 %tile_rows.1 = f32[3072,1536]{1,0:T(8,128)} custom-call(s32[2]{0:T(128)S(1)} %pad_add_fusion.place_ref, f32[3072,1536]{1,0:T(8,128)} %normals_ref.1, f32[3072,256]{1,0:T(8,128)S(1)} %copy-done.4, f32[3072,256]{1,0:T(8,128)S(1)} %copy-done.6, bf16[3072,384]{1,0:T(8,128)(2,1)S(1)} %copy-done.8, bf16[1152,1536]{1,0:T(8,128)(2,1)S(1)} %right_side.1.right_ref, ...), custom_call_target="tpu_custom_call" | custom-call | flops 10871635968 | bytes 37748736 | tf_op jit(solution)/shard_map/tile_rows/pallas_call | solution.py:224
  (63 shorter events, 12.2 us)
Async XLA Ops:
  6.5 3.8 %copy-start.11 = (f32[32,1536]{1,0:T(8,128)S(1)}, f32[32,1536]{1,0:T(8,128)}, u32[]{:S(2)}) copy-start(f32[32,1536]{1,0:T(8,128)} %param.5) | copy-start | bytes 589828
  10.3 13.2 %collective-permute-start.2 = (f32[32,1536]{1,0:T(8,128)S(1)}, f32[32,1536]{1,0:T(8,128)S(1)}, u32[]{:S(2)}, u32[]{:S(2)}) collective-permute-start(f32[32,1536]{1,0:T(8,128)S(1)} %copy-done.11), channel_id=1, source_target_pairs={{0,6},{1,7},{2,0},{3,1},{4,2},{5,3},{6,4},{7,5},{8,14},{9,15},{10,... | collective-permute-start | bytes 589832 | tf_op jit(solution)/shard_map/ppermute | solution.py:306
  15.4 16.7 %collective-permute-start.1 = (f32[32,1536]{1,0:T(8,128)S(1)}, f32[32,1536]{1,0:T(8,128)S(1)}, u32[]{:S(2)}, u32[]{:S(2)}) collective-permute-start(f32[32,1536]{1,0:T(8,128)S(1)} %copy-done.11), channel_id=1, source_target_pairs={{0,4},{1,5},{2,6},{3,7},{4,0},{5,1},{6,2},{7,3},{8,12},{9,13},{10,... | collective-permute-start | bytes 589832 | tf_op jit(solution)/shard_map/ppermute | solution.py:306
  15.4 16.7 %collective-permute-start = (f32[32,1536]{1,0:T(8,128)S(1)}, f32[32,1536]{1,0:T(8,128)S(1)}, u32[]{:S(2)}, u32[]{:S(2)}) collective-permute-start(f32[32,1536]{1,0:T(8,128)S(1)} %copy-done.11), channel_id=1, source_target_pairs={{0,2},{1,3},{2,4},{3,5},{4,6},{5,7},{6,0},{7,1},{8,10},{9,11},{10,... | collective-permute-start | bytes 589832 | tf_op jit(solution)/shard_map/ppermute | solution.py:306
  17.9 19.3 %collective-permute-start.3 = (f32[128,1536]{1,0:T(8,128)S(1)}, f32[128,1536]{1,0:T(8,128)S(1)}, u32[]{:S(2)}, u32[]{:S(2)}) collective-permute-start(f32[128,1536]{1,0:T(8,128)S(1)} %get-tuple-element.13), channel_id=1, source_target_pairs={{0,8},{1,9},{2,10},{3,11},{4,12},{5,13},{6,14},{7,15}} | collective-permute-start | bytes 2359304 | tf_op jit(solution)/shard_map/ppermute | solution.py:252
  21.3 18.7 %collective-permute-start.5 = (f32[128,1536]{1,0:T(8,128)S(1)}, f32[128,1536]{1,0:T(8,128)}, u32[]{:S(2)}, u32[]{:S(2)}) collective-permute-start(f32[128,1536]{1,0:T(8,128)S(1)} %get-tuple-element.14), channel_id=1, source_target_pairs={{0,16},{1,17},{2,18},{3,19},{4,20},{5,21},{6,22},{7,23}} | collective-permute-start | bytes 2359304 | tf_op jit(solution)/shard_map/ppermute | solution.py:252
  37.3 28.7 %collective-permute-start.4 = (f32[128,1536]{1,0:T(8,128)S(1)}, f32[128,1536]{1,0:T(8,128)}, u32[]{:S(2)}, u32[]{:S(2)}) collective-permute-start(f32[128,1536]{1,0:T(8,128)S(1)} %broadcast_select_fusion.1), channel_id=1, source_target_pairs={{0,16},{8,24},{1,17},{9,25},{2,18},{10,26},{3,19},{11,27},{4,20},{... | collective-permute-start | bytes 2359304 | tf_op jit(solution)/shard_map/ppermute | solution.py:252
  40.1 26.9 %collective-permute-start.6 = (f32[128,1536]{1,0:T(8,128)S(1)}, f32[128,1536]{1,0:T(8,128)}, u32[]{:S(2)}, u32[]{:S(2)}) collective-permute-start(f32[128,1536]{1,0:T(8,128)S(1)} %broadcast_select_fusion.2), channel_id=1, source_target_pairs={{0,8},{16,24},{1,9},{17,25},{2,10},{18,26},{3,11},{19,27},{4,12},{... | collective-permute-start | bytes 2359304 | tf_op jit(solution)/shard_map/ppermute | solution.py:252
  46.2 31.6 %all-to-all-start = ((f32[4,32,3328]{2,1,0:T(8,128)}), f32[4,32,3328]{2,1,0:T(8,128)S(1)}, u32[]{:S(2)}, u32[]{:S(2)}) async-start(f32[4,32,3328]{2,1,0:T(8,128)} %pad_maximum_fusion), calls=%async_computation | async-start | bytes 3407872 | tf_op jit(solution)/shard_map/all_to_all | solution.py:313
  49.8 100.6 %all-reduce.2.cloned.1.call-start = ((), (), s32[]{:S(2)}) async-start(), calls=%async_computation.1 | async-start | bytes 6291456 | tf_op jit(solution)/shard_map/psum | solution.py:291
  67.1 10.7 %copy-start.12 = (f32[2,32,32]{2,1,0:T(8,128)S(1)}, f32[2,32,32]{2,1,0:T(8,128)}, u32[]{:S(2)}) copy-start(f32[2,32,32]{2,1,0:T(8,128)} %param.6) | copy-start | bytes 24580
  67.1 0.9 copy-start.2
  68.1 7.7 %collective-permute-start.7 = (f32[256,256]{1,0:T(8,128)S(1)}, f32[256,256]{1,0:T(8,128)S(1)}, u32[]{:S(2)}, u32[]{:S(2)}) collective-permute-start(f32[256,256]{1,0:T(8,128)S(1)} %pad_maximum_fusion.11), channel_id=1, source_target_pairs={{0,4},{8,12},{16,20},{24,28}} | collective-permute-start | bytes 786440 | tf_op jit(solution)/shard_map/ppermute | solution.py:272
  75.8 10.6 %collective-permute-start.8 = (f32[256,256]{1,0:T(8,128)S(1)}, f32[256,256]{1,0:T(8,128)}, u32[]{:S(2)}, u32[]{:S(2)}) collective-permute-start(f32[256,256]{1,0:T(8,128)S(1)} %broadcast_select_fusion.5), channel_id=1, source_target_pairs={{0,2},{8,10},{16,18},{24,26},{4,6},{12,14},{20,22},{28,30}} | collective-permute-start | bytes 786440 | tf_op jit(solution)/shard_map/ppermute | solution.py:272
  78.8 12.4 %collective-permute-start.10 = (f32[128,1536]{1,0:T(8,128)}, f32[128,1536]{1,0:T(8,128)S(1)}, u32[]{:S(2)}, u32[]{:S(2)}) collective-permute-start(f32[128,1536]{1,0:T(8,128)} %slice.57), channel_id=1, source_target_pairs={{0,1},{1,0},{2,3},{3,2},{4,5},{5,4},{6,7},{7,6},{8,9},{9,8},{10,11... | collective-permute-start | bytes 2359304 | tf_op jit(solution)/shard_map/ppermute | solution.py:319
  87.3 3.9 %collective-permute-start.9 = (f32[384,256]{1,0:T(8,128)}, f32[384,256]{1,0:T(8,128)}, u32[]{:S(2)}, u32[]{:S(2)}) collective-permute-start(f32[384,256]{1,0:T(8,128)} %pad_maximum_fusion.10), channel_id=1, source_target_pairs={{0,1},{8,9},{16,17},{24,25},{4,5},{12,13},{20,21},{28,29},{2,3},{1... | collective-permute-start | bytes 1179656 | tf_op jit(solution)/shard_map/ppermute | solution.py:272
  95.3 1.5 copy-start.7
  96.8 13.9 %copy-start.5 = (f32[3072,256]{1,0:T(8,128)}, f32[3072,256]{1,0:T(8,128)S(1)}, u32[]{:S(2)}) copy-start(f32[3072,256]{1,0:T(8,128)S(1)} %get-tuple-element.15.gram_ref) | copy-start | bytes 9437188
  96.8 13.9 %copy-start.1 = (f32[128,1536]{1,0:T(8,128)S(1)}, f32[128,1536]{1,0:T(8,128)}, u32[]{:S(2)}) copy-start(f32[128,1536]{1,0:T(8,128)} %copy-done) | copy-start | bytes 2359300
  96.8 13.9 %copy-start.3 = (f32[128,1536]{1,0:T(8,128)S(1)}, f32[128,1536]{1,0:T(8,128)}, u32[]{:S(2)}) copy-start(f32[128,1536]{1,0:T(8,128)} %copy-done.2) | copy-start | bytes 2359300
  150.5 1.9 %copy-start.4 = (f32[3072,256]{1,0:T(8,128)S(1)}, f32[3072,256]{1,0:T(8,128)}, u32[]{:S(2)}) copy-start(f32[3072,256]{1,0:T(8,128)} %all-reduce.2.cloned.1.call-done.strip_ref) | copy-start | bytes 9437188
  152.3 1.9 %copy-start.6 = (f32[3072,256]{1,0:T(8,128)S(1)}, f32[3072,256]{1,0:T(8,128)}, u32[]{:S(2)}) copy-start(f32[3072,256]{1,0:T(8,128)} %copy-done.5) | copy-start | bytes 9437188
  154.2 1.7 copy-start.8
  155.9 0.9 copy-start.10
  (2 other events, 1.6 us)
Sparse Core Ops, SparseCore 0:
  72.1 78.3 all-reduce.1

commit v11 on v10

--- a/solution.py
+++ b/solution.py
@@ -89,8 +89,8 @@
     )(block, design, filter_matrix, regular)
 
 
-def right_kernel(place_ref, high_ref, low_ref, gram_ref, inverse_ref, side_ref, out_ref):
-    strip = jnp.concatenate([high_ref[...], low_ref[...]], axis=0) + gram_ref[...]
+def right_kernel(place_ref, strip_ref, gram_ref, inverse_ref, side_ref, out_ref):
+    strip = strip_ref[...] + gram_ref[...]
     panel_high, panel_low = split(-split_dot(inverse_ref[...].T, strip))
     out_ref[:B, :] = panel_high
     out_ref[B : 2 * B, :] = panel_low
@@ -107,12 +107,12 @@
         out_ref[2 * B : 3 * B, :B] = identity
 
 
-def right_side(place, strips, gram_rows, inverse, side):
+def right_side(place, strip, gram_rows, inverse, side):
     cols = gram_rows.shape[1]
     depth = 3 * B + side.shape[0]
     return pl.pallas_call(
         right_kernel,
-        in_specs=[pl.BlockSpec(memory_space=pltpu.SMEM)] + [pl.BlockSpec(memory_space=pltpu.VMEM)] * 5,
+        in_specs=[pl.BlockSpec(memory_space=pltpu.SMEM)] + [pl.BlockSpec(memory_space=pltpu.VMEM)] * 4,
         out_specs=pl.BlockSpec(memory_space=pltpu.VMEM),
         out_shape=jax.ShapeDtypeStruct((depth, cols), jnp.bfloat16),
         compiler_params=pltpu.CompilerParams(vmem_limit_bytes=24 * 2**20),
@@ -120,7 +120,7 @@
             flops=6 * cols * B * B, bytes_accessed=12 * cols * B, transcendentals=0
         ),
         name="right_side",
-    )(place, *strips, gram_rows, inverse, side)
+    )(place, strip, gram_rows, inverse, side)
 
 
 def filter_kernel(
@@ -243,18 +243,6 @@
     return lax.optimization_barrier((value, earlier))[0]
 
 
-def spread(value, axis, bits):
-    peers = lax.axis_size(axis)
-    me = lax.axis_index(axis)
-    reached = [0]
-    for bit in bits:
-        pairs = [(i, i | bit) for i in reached if i | bit < peers]
-        got = lax.ppermute(value, axis, pairs)
-        value = jnp.where((me & bit) != 0, got, value)
-        reached += [to for _, to in pairs]
-    return value
-
-
 def filter_matrix_of(filter_blocks, count):
     positions = jnp.arange(count, dtype=jnp.int32)
     lag = (positions[:, None] - positions[None, :])[:, None, :, None]
@@ -262,6 +250,20 @@
     prior = filter_blocks[1][None, :, None, :]
     blocks = jnp.where(lag == 0, own, jnp.where(lag == 1, prior, 0.0))
     return blocks.reshape(count * P_SIZE, count * P_SIZE)
+
+
+def row_strip_piece(normals, later):
+    peers = lax.axis_size("col")
+    chips = peers // 2
+    size = normals.shape[0] // chips
+    col_index = lax.axis_index("col")
+    arrived = [
+        lax.ppermute(normals[z * size : (z + 1) * size, :B], "col", [(0, 2 * z)]) for z in range(1, chips)
+    ]
+    arrived = sum(after(arrived, later))
+    piece = jnp.where(col_index == 0, normals[:size, :B], arrived)
+    second = lax.ppermute(piece[size // 2 :], "col", [(c, c + 1) for c in range(0, peers, 2)])
+    return jnp.where(col_index % 2 == 0, piece[: size // 2], second)
 
 
 def doubled(value, bits, reached):
@@ -287,20 +289,14 @@
     col_peers = lax.axis_size("col")
     col_strip = lax.psum(jnp.where(row_index == 0, normals[:B], 0.0), "row")
 
-    left_strip = jnp.where(col_index == 0, normals[:, :B], 0.0)
-    strip = lax.psum(left_strip, "col")
-
-    bits = [1 << i for i in range((row_peers - 1).bit_length())]
-    halves = after([normals[: B // 2], normals[B // 2 : B]], left_strip)
-    strips = [spread(halves[0], "row", bits), spread(halves[1], "row", bits[::-1])]
-
-    leading = jnp.concatenate([half[:, :B] for half in strips], axis=0)
-    reached = [row * col_peers for row in range(row_peers)]
-    z_bits = [1 << i for i in range(1, (col_peers - 1).bit_length())]
-    leading, reached = doubled(leading, z_bits[::-1], reached)
+    top_strip = jnp.where(row_index == 0, normals[:B], 0.0)
+    col_strip = lax.psum(top_strip, "row")
+
+    index_bits = [1 << i for i in range((row_peers * col_peers - 1).bit_length())]
+    leading, reached = doubled(normals[:B, :B], [bit for bit in index_bits if bit >= col_peers], [0])
 
     chips = col_peers // 2
-    design = after(design, left_strip)
+    design = after(design, top_strip)
     along = [design]
     for s in range(1, chips):
         along.append(lax.ppermute(design, "col", [(c, (c + 2 * s) % col_peers) for c in range(col_peers)]))
@@ -310,9 +306,13 @@
     for to in range(row_peers):
         far = lax.dynamic_index_in_dim(along, (col_index // 2 - to) % chips, 0, keepdims=False)
         sent.append(jnp.concatenate([design, far, lead], axis=1))
-    joined = lax.all_to_all(jnp.stack(sent), "row", 0, 0, tiled=True)
+    sent = after(jnp.stack(sent), leading)
+    joined = lax.all_to_all(sent, "row", 0, 0, tiled=True)
     joined = joined.reshape(obs, 2 * cols_here + B)
 
+    strip = lax.all_gather(row_strip_piece(normals, joined), "col", axis=0, tiled=True)
+
+    leading, reached = doubled(leading, [bit for bit in reversed(index_bits) if 1 < bit < col_peers], reached)
     leading = jnp.concatenate([joined[:, 2 * cols_here :], leading], axis=0)
     leading, _ = doubled(leading, [1], reached)
     lead, corner = leading[:obs], leading[obs:]
@@ -325,7 +325,7 @@
     place = jnp.stack([row_index, col_index]).astype(jnp.int32)
     inverse = corner_factor(corner, lead, filters, lead_reg)
     gram_left, gram_right, gram_rows, gram_cols = filter_sides(place, joined, lead, other, filters, own_reg, lead_reg)
-    right = right_side(place, strips, gram_rows, inverse, gram_right)
+    right = right_side(place, col_strip, gram_rows, inverse, gram_right)
     return tile_rows(place, normals, strip, gram_cols, gram_left, right, inverse, own_reg)
 
 

time: 185 us -> 186 us (level)
  the two profiles are of different devices: /device:TPU:0 before, /device:TPU:31 now
where the time goes in v11:
time: 186 us; the launch traced here: 185 us
  starting transfers between devices  59.3 us (32%)
  Pallas kernels  40.1 us (22%)
  waiting for transfers between devices  36.5 us (20%)
  local copies, waits for them, and re-layouts  23.7 us (13%)
  between operations  15.3 us (8%)
  other arithmetic  10.1 us (5%)
    ppermute x1, starting transfers between devices, body(): lax.ppermute(joined[:, cols_here:2 * cols_here], 'col', [(c, c ^ 1) for c...  42.2 us
    pallas_call x1, Pallas kernels, tile_rows(): pl.pallas_call(tile_kernel, grid_spec=pltpu.PrefetchScalarGridSpec(num_sc...  20.7 us
    unnamed x30, local copies, waits for them, and re-layouts  17.4 us
    ppermute x1, waiting for transfers between devices, row_strip_piece(): lax.ppermute(piece[size // 2:], 'col', [(c, c + 1) for c in range(0, peer...  16.1 us
    pallas_call x1, Pallas kernels, corner_factor(): pl.pallas_call(corner_kernel, out_shape=jax.ShapeDtypeStruct((B, B), jnp....  13.9 us
    ppermute x3, waiting for transfers between devices, body(): lax.ppermute(design, 'col', [(c, (c + 2 * s) % col_peers) for c in range(...  10.5 us
    all_to_all x1, waiting for transfers between devices, body(): joined = lax.all_to_all(sent, 'row', 0, 0, tiled=True)  9.8 us
    ppermute x3, starting transfers between devices, row_strip_piece(): lax.ppermute(normals[z * size:(z + 1) * size, :B], 'col', [(0, 2 * z)])  4.64 us
  transfers between devices with their start and end apart: 16, of which 4 were waited for; matrix products, arithmetic and copies ran while one was open for 7% of the time, Pallas kernels for 10%

profile of v11, /device:TPU:31, one launch (start us, length us, event | category | flops | bytes accessed | tf_op | source)
XLA Modules:
  0.0 185.1 jit_solution(12083435828417487904)
XLA Ops:
  7.4 2.7 %slice_select_fusion = f32[256,1536]{1,0:T(8,128)} fusion(f32[3072,1536]{1,0:T(8,128)} %normals_ref.1, pred[]{:T(512)S(6)} %eq.33), kind=kLoop, calls=%fused_computation.1 | loop fusion | flops 393216 | bytes 3145729 | tf_op jit(solution)/shard_map/jit(_where)/select_n | solution.py:292
  10.3 3.0 %collective-permute-start.3 = (f32[32,1536]{1,0:T(8,128)S(1)}, f32[32,1536]{1,0:T(8,128)S(1)}, u32[]{:S(2)}, u32[]{:S(2)}) collective-permute-start(f32[32,1536]{1,0:T(8,128)S(1)} %copy-done.13), channel_id=1, source_target_pairs={{0,2},{1,3},{2,4},{3,5},{4,6},{5,7},{6,0},{7,1},{8,10},{9,11},{10,... | collective-permute-start | bytes 589832 | tf_op jit(solution)/shard_map/ppermute | solution.py:302
  15.1 2.7 %collective-permute-done.5 = f32[32,1536]{1,0:T(8,128)S(1)} collective-permute-done((f32[32,1536]{1,0:T(8,128)S(1)}, f32[32,1536]{1,0:T(8,128)S(1)}, u32[]{:S(2)}, u32[]{:S(2)}) %collective-permute-start.5) | collective-permute-done | bytes 196640 | tf_op jit(solution)/shard_map/ppermute | solution.py:302
  17.8 7.9 %collective-permute-done.4 = f32[32,1536]{1,0:T(8,128)S(1)} collective-permute-done((f32[32,1536]{1,0:T(8,128)S(1)}, f32[32,1536]{1,0:T(8,128)S(1)}, u32[]{:S(2)}, u32[]{:S(2)}) %collective-permute-start.4) | collective-permute-done | bytes 196640 | tf_op jit(solution)/shard_map/ppermute | solution.py:302
  29.0 3.8 %all-to-all-start = ((f32[4,32,3328]{2,1,0:T(8,128)}), f32[4,32,3328]{2,1,0:T(8,128)S(1)}, u32[]{:S(2)}, u32[]{:S(2)}) async-start(f32[4,32,3328]{2,1,0:T(8,128)} %pad_maximum_fusion), calls=%async_computation | async-start | bytes 3407872 | tf_op jit(solution)/shard_map/all_to_all | solution.py:310
  32.7 2.7 %fusion.6 = (f32[768,256]{1,0:T(8,128)}, f32[768,256]{1,0:T(8,128)S(1)}, f32[768,256]{1,0:T(8,128)S(1)}) fusion(f32[3072,1536]{1,0:T(8,128)} %normals_ref.1), kind=kLoop, calls=%fused_computation.35 | loop fusion | bytes 4718592 | tf_op jit(solution)/shard_map/slice | solution.py:261
  35.4 1.6 collective-permute-start.2
  37.0 1.5 collective-permute-start.1
  38.5 1.5 collective-permute-start
  40.1 9.8 %all-to-all-done = f32[4,32,3328]{2,1,0:T(8,128)S(1)} async-done(((f32[4,32,3328]{2,1,0:T(8,128)}), f32[4,32,3328]{2,1,0:T(8,128)S(1)}, u32[]{:S(2)}, u32[]{:S(2)}) %all-to-all-start) | async-done | bytes 1703968 | tf_op jit(solution)/shard_map/all_to_all | solution.py:310
  49.9 2.0 %add_select_fusion = f32[768,256]{1,0:T(8,128)S(1)} fusion(f32[768,256]{1,0:T(8,128)} %collective-permute-done.2, f32[768,256]{1,0:T(8,128)} %collective-permute-done, f32[768,256]{1,0:T(8,128)} %collective-permute-done.1, f32[3072,1536]{1,0:T(8,128)} %normals_ref.1, pred[]{:T(512)S(6)} %eq.32), kind=kLoop, calls=%fused_computation.7 | loop fusion | flops 589824 | bytes 3932161 | tf_op jit(solution)/shard_map/jit(_where)/select_n | solution.py:264
  53.3 16.1 %collective-permute-done.8 = f32[384,256]{1,0:T(8,128)S(1)} collective-permute-done((f32[384,256]{1,0:T(8,128)S(1)}, f32[384,256]{1,0:T(8,128)S(1)}, u32[]{:S(2)}, u32[]{:S(2)}) %collective-permute-start.8) | collective-permute-done | bytes 393248 | tf_op jit(solution)/shard_map/ppermute | solution.py:265
  73.5 1.5 collective-permute-start.11
  75.0 42.2 %collective-permute-start.12 = (f32[128,1536]{1,0:T(8,128)}, f32[128,1536]{1,0:T(8,128)S(1)}, u32[]{:S(2)}, u32[]{:S(2)}) collective-permute-start(f32[128,1536]{1,0:T(8,128)} %slice.69), channel_id=1, source_target_pairs={{0,1},{1,0},{2,3},{3,2},{4,5},{5,4},{6,7},{7,6},{8,9},{9,8},{10,11... | collective-permute-start | bytes 2359304 | tf_op jit(solution)/shard_map/ppermute | solution.py:319
  120.1 13.9 %corner_factor.1.inverse_ref = f32[256,256]{1,0:T(8,128)S(1)} custom-call(f32[256,256]{1,0:T(8,128)S(1)} %slice.70.block_ref, f32[128,256]{1,0:T(8,128)S(1)} %slice.68.lead_ref.design_ref, f32[128,128]{1,0:T(8,128)S(1)} %select_n.149.filter_ref, f32[1,256]{1,0:T(1,128)S(1)} %bitcast.33), custom_call_target="tpu_custom_call" | custom-call | flops 1000000000 | bytes 1048576 | tf_op jit(solution)/shard_map/corner_factor/pallas_call | solution.py:82
  134.7 4.0 %filter_sides.1 = (bf16[3072,384]{1,0:T(8,128)(2,1)S(1)}, bf16[384,1536]{1,0:T(8,128)(2,1)S(1)}, f32[256,1536]{1,0:T(8,128)S(1)}, f32[3072,256]{1,0:T(8,128)S(1)}) custom-call(s32[2]{0:T(128)S(1)} %pad_add_fusion.place_ref, f32[128,3328]{1,0:T(8,128)S(1)} %bitcast.32, f32[128,256]{1,0:T(8,128)S(1)} %slice.68.lead_ref.design_ref, ...), custom_call_target="tpu_custom_call" | custom-call | flops 905969664 | bytes 9437184 | tf_op jit(solution)/shard_map/filter_sides/pallas_call | solution.py:172
  138.7 1.7 copy-done.1
  140.4 1.4 copy-done.3
  144.0 1.4 copy-done.5
  149.0 1.5 right_side.1.right_ref
  150.6 1.9 %copy-done = f32[3072,256]{1,0:T(8,128)S(1)} copy-done((f32[3072,256]{1,0:T(8,128)S(1)}, f32[3072,256]{1,0:T(8,128)}, u32[]{:S(2)}) %copy-start) | copy-done | bytes 3145752
  152.4 1.9 %copy-done.2 = f32[3072,256]{1,0:T(8,128)S(1)} copy-done((f32[3072,256]{1,0:T(8,128)S(1)}, f32[3072,256]{1,0:T(8,128)}, u32[]{:S(2)}) %copy-start.2) | copy-done | bytes 3145752
  154.3 1.7 copy-done.4
  156.9 20.7 %tile_rows.1 = f32[3072,1536]{1,0:T(8,128)} custom-call(s32[2]{0:T(128)S(1)} %pad_add_fusion.place_ref, f32[3072,1536]{1,0:T(8,128)} %normals_ref.1, f32[3072,256]{1,0:T(8,128)S(1)} %copy-done, f32[3072,256]{1,0:T(8,128)S(1)} %copy-done.2, bf16[3072,384]{1,0:T(8,128)(2,1)S(1)} %copy-done.4, bf16[1152,1536]{1,0:T(8,128)(2,1)S(1)} %right_side.1.right_ref, ...), custom_call_target="tpu_custom_call" | custom-call | flops 10871635968 | bytes 37748736 | tf_op jit(solution)/shard_map/tile_rows/pallas_call | solution.py:224
  (73 shorter events, 20.9 us)
Async XLA Ops:
  7.4 2.7 %copy-start.13 = (f32[32,1536]{1,0:T(8,128)S(1)}, f32[32,1536]{1,0:T(8,128)}, u32[]{:S(2)}) copy-start(f32[32,1536]{1,0:T(8,128)} %param.5) | copy-start | bytes 589828
  10.1 7.7 %collective-permute-start.5 = (f32[32,1536]{1,0:T(8,128)S(1)}, f32[32,1536]{1,0:T(8,128)S(1)}, u32[]{:S(2)}, u32[]{:S(2)}) collective-permute-start(f32[32,1536]{1,0:T(8,128)S(1)} %copy-done.13), channel_id=1, source_target_pairs={{0,6},{1,7},{2,0},{3,1},{4,2},{5,3},{6,4},{7,5},{8,14},{9,15},{10,... | collective-permute-start | bytes 589832 | tf_op jit(solution)/shard_map/ppermute | solution.py:302
  10.3 15.4 %collective-permute-start.4 = (f32[32,1536]{1,0:T(8,128)S(1)}, f32[32,1536]{1,0:T(8,128)S(1)}, u32[]{:S(2)}, u32[]{:S(2)}) collective-permute-start(f32[32,1536]{1,0:T(8,128)S(1)} %copy-done.13), channel_id=1, source_target_pairs={{0,4},{1,5},{2,6},{3,7},{4,0},{5,1},{6,2},{7,3},{8,12},{9,13},{10,... | collective-permute-start | bytes 589832 | tf_op jit(solution)/shard_map/ppermute | solution.py:302
  10.3 15.4 %collective-permute-start.3 = (f32[32,1536]{1,0:T(8,128)S(1)}, f32[32,1536]{1,0:T(8,128)S(1)}, u32[]{:S(2)}, u32[]{:S(2)}) collective-permute-start(f32[32,1536]{1,0:T(8,128)S(1)} %copy-done.13), channel_id=1, source_target_pairs={{0,2},{1,3},{2,4},{3,5},{4,6},{5,7},{6,0},{7,1},{8,10},{9,11},{10,... | collective-permute-start | bytes 589832 | tf_op jit(solution)/shard_map/ppermute | solution.py:302
  14.3 11.6 %collective-permute-start.6 = (f32[256,256]{1,0:T(8,128)S(1)}, f32[256,256]{1,0:T(8,128)S(1)}, u32[]{:S(2)}, u32[]{:S(2)}) collective-permute-start(f32[256,256]{1,0:T(8,128)S(1)} %slice.54), channel_id=1, source_target_pairs={{0,8}} | collective-permute-start | bytes 786440 | tf_op jit(solution)/shard_map/ppermute | solution.py:274
  27.0 2.0 %collective-permute-start.7 = (f32[256,256]{1,0:T(8,128)S(1)}, f32[256,256]{1,0:T(8,128)S(1)}, u32[]{:S(2)}, u32[]{:S(2)}) collective-permute-start(f32[256,256]{1,0:T(8,128)S(1)} %broadcast_select_fusion.3), channel_id=1, source_target_pairs={{0,16},{8,24}} | collective-permute-start | bytes 786440 | tf_op jit(solution)/shard_map/ppermute | solution.py:274
  29.0 21.0 %all-to-all-start = ((f32[4,32,3328]{2,1,0:T(8,128)}), f32[4,32,3328]{2,1,0:T(8,128)S(1)}, u32[]{:S(2)}, u32[]{:S(2)}) async-start(f32[4,32,3328]{2,1,0:T(8,128)} %pad_maximum_fusion), calls=%async_computation | async-start | bytes 3407872 | tf_op jit(solution)/shard_map/all_to_all | solution.py:310
  32.7 111.2 %all-reduce.2.cloned.1.call-start = ((), (), s32[]{:S(2)}) async-start(), calls=%async_computation.2 | async-start | bytes 3145728 | tf_op jit(solution)/shard_map/psum | solution.py:293
  35.4 4.7 %collective-permute-start.2 = (f32[768,256]{1,0:T(8,128)}, f32[768,256]{1,0:T(8,128)}, u32[]{:S(2)}, u32[]{:S(2)}) collective-permute-start(f32[768,256]{1,0:T(8,128)} %get-tuple-element.23), channel_id=1, source_target_pairs={{0,6},{8,14},{16,22},{24,30}} | collective-permute-start | bytes 2359304 | tf_op jit(solution)/shard_map/ppermute | solution.py:261
  37.0 3.2 %collective-permute-start.1 = (f32[768,256]{1,0:T(8,128)S(1)}, f32[768,256]{1,0:T(8,128)}, u32[]{:S(2)}, u32[]{:S(2)}) collective-permute-start(f32[768,256]{1,0:T(8,128)S(1)} %get-tuple-element.24), channel_id=1, source_target_pairs={{0,4},{8,12},{16,20},{24,28}} | collective-permute-start | bytes 2359304 | tf_op jit(solution)/shard_map/ppermute | solution.py:261
  38.5 1.6 collective-permute-start
  40.1 110.5 %all-gather.2.cloned.1.call-start = ((), (), s32[]{:S(2)}) async-start(), calls=%async_computation.1 | async-start | bytes 3538944 | tf_op jit(solution)/shard_map/all_gather | solution.py:313
  52.0 17.4 %collective-permute-start.8 = (f32[384,256]{1,0:T(8,128)S(1)}, f32[384,256]{1,0:T(8,128)S(1)}, u32[]{:S(2)}, u32[]{:S(2)}) collective-permute-start(f32[384,256]{1,0:T(8,128)S(1)} %slice.66), channel_id=1, source_target_pairs={{0,1},{2,3},{4,5},{6,7},{8,9},{10,11},{12,13},{14,15},{16,17},{18,... | collective-permute-start | bytes 1179656 | tf_op jit(solution)/shard_map/ppermute | solution.py:265
  69.4 2.2 %copy-start.14 = (f32[2,32,32]{2,1,0:T(8,128)S(1)}, f32[2,32,32]{2,1,0:T(8,128)}, u32[]{:S(2)}) copy-start(f32[2,32,32]{2,1,0:T(8,128)} %param.6) | copy-start | bytes 24580
  70.3 0.7 collective-permute-start.9
  71.0 0.7 collective-permute-start.10
  73.5 45.5 %collective-permute-start.11 = (f32[384,256]{1,0:T(8,128)}, f32[384,256]{1,0:T(8,128)}, u32[]{:S(2)}, u32[]{:S(2)}) collective-permute-start(f32[384,256]{1,0:T(8,128)} %pad_maximum_fusion.10), channel_id=1, source_target_pairs={{0,1},{8,9},{16,17},{24,25},{4,5},{12,13},{20,21},{28,29},{2,3},{1... | collective-permute-start | bytes 1179656 | tf_op jit(solution)/shard_map/ppermute | solution.py:274
  75.0 59.7 %collective-permute-start.12 = (f32[128,1536]{1,0:T(8,128)}, f32[128,1536]{1,0:T(8,128)S(1)}, u32[]{:S(2)}, u32[]{:S(2)}) collective-permute-start(f32[128,1536]{1,0:T(8,128)} %slice.69), channel_id=1, source_target_pairs={{0,1},{1,0},{2,3},{3,2},{4,5},{5,4},{6,7},{7,6},{8,9},{9,8},{10,11... | collective-permute-start | bytes 2359304 | tf_op jit(solution)/shard_map/ppermute | solution.py:319
  138.7 1.7 copy-start.1
  140.4 1.4 copy-start.3
  144.0 1.4 copy-start.5
  150.6 1.9 %copy-start = (f32[3072,256]{1,0:T(8,128)S(1)}, f32[3072,256]{1,0:T(8,128)}, u32[]{:S(2)}) copy-start(f32[3072,256]{1,0:T(8,128)} %all-gather.2.cloned.1.call-done.strip_ref) | copy-start | bytes 9437188
  152.4 1.9 %copy-start.2 = (f32[3072,256]{1,0:T(8,128)S(1)}, f32[3072,256]{1,0:T(8,128)}, u32[]{:S(2)}) copy-start(f32[3072,256]{1,0:T(8,128)} %copy-done.1) | copy-start | bytes 9437188
  154.3 1.7 copy-start.4
  (7 other events, 7.5 us)
Sparse Core Ops, SparseCore 0:
  40.2 76.7 all-reduce.1
Sparse Core Ops, SparseCore 1:
  70.3 54.8 all-gather.1

commit v12 on v11

--- a/solution.py
+++ b/solution.py
@@ -84,56 +84,23 @@
         out_shape=jax.ShapeDtypeStruct((B, B), jnp.float32),
         scratch_shapes=[pltpu.VMEM((B, 2 * B), jnp.float32)],
         compiler_params=pltpu.CompilerParams(vmem_limit_bytes=8 * 2**20),
-        cost_estimate=pl.CostEstimate(flops=10**9, bytes_accessed=2**20, transcendentals=0),
+        cost_estimate=pl.CostEstimate(flops=0, bytes_accessed=0, transcendentals=0),
         name="corner_factor",
     )(block, design, filter_matrix, regular)
 
 
-def right_kernel(place_ref, strip_ref, gram_ref, inverse_ref, side_ref, out_ref):
-    strip = strip_ref[...] + gram_ref[...]
-    panel_high, panel_low = split(-split_dot(inverse_ref[...].T, strip))
-    out_ref[:B, :] = panel_high
-    out_ref[B : 2 * B, :] = panel_low
-    out_ref[2 * B : 3 * B, :] = panel_high
-    out_ref[3 * B :, :] = side_ref[...]
-
-    @pl.when(place_ref[1] == 0)
-    def _():
-        row_pos = lax.broadcasted_iota(jnp.int32, (B, B), 0)
-        identity = jnp.where(row_pos == lax.broadcasted_iota(jnp.int32, (B, B), 1), 1.0, 0.0)
-        identity = identity.astype(jnp.bfloat16)
-        out_ref[:B, :B] = identity
-        out_ref[B : 2 * B, :B] = jnp.zeros((B, B), jnp.bfloat16)
-        out_ref[2 * B : 3 * B, :B] = identity
-
-
-def right_side(place, strip, gram_rows, inverse, side):
-    cols = gram_rows.shape[1]
-    depth = 3 * B + side.shape[0]
-    return pl.pallas_call(
-        right_kernel,
-        in_specs=[pl.BlockSpec(memory_space=pltpu.SMEM)] + [pl.BlockSpec(memory_space=pltpu.VMEM)] * 4,
-        out_specs=pl.BlockSpec(memory_space=pltpu.VMEM),
-        out_shape=jax.ShapeDtypeStruct((depth, cols), jnp.bfloat16),
-        compiler_params=pltpu.CompilerParams(vmem_limit_bytes=24 * 2**20),
-        cost_estimate=pl.CostEstimate(
-            flops=6 * cols * B * B, bytes_accessed=12 * cols * B, transcendentals=0
-        ),
-        name="right_side",
-    )(place, strip, gram_rows, inverse, side)
-
-
-def filter_kernel(
+def sides_kernel(
     place_ref,
     joined_ref,
     lead_ref,
     other_ref,
+    strip_ref,
+    inverse_ref,
     filter_ref,
     regular_ref,
     lead_reg_ref,
     left_ref,
     right_ref,
-    gram_rows_ref,
     gram_cols_ref,
 ):
     row_index, col_index = place_ref[0], place_ref[1]
@@ -141,15 +108,31 @@
     obs = filter_ref.shape[0]
     core = lax.rem(col_index, 2)
     filtered = split_dot(filter_ref[...], joined_ref[:, : 2 * cols])
-    here, rows_own = filtered[:, :cols], filtered[:, cols : 2 * cols]
+    here, rows_own = filtered[:, :cols], filtered[:, cols:]
     lead = split_dot(filter_ref[...], lead_ref[...])
+
     row_pos = lax.broadcasted_iota(jnp.int32, (B, cols), 0)
     col_pos = lax.broadcasted_iota(jnp.int32, (1, cols), 1) + col_index * cols
-    gram_rows_ref[...] = split_dot(lead.T, here) + jnp.where(row_pos == col_pos, regular_ref[...], 0.0)
+    strip = strip_ref[...] + split_dot(lead.T, here)
+    strip = strip + jnp.where(row_pos == col_pos, regular_ref[...], 0.0)
+    high, low = split(-split_dot(inverse_ref[...].T, strip))
+    right_ref[:B, :] = high
+    right_ref[B : 2 * B, :] = low
+    right_ref[2 * B : 3 * B, :] = high
     high, low = split(jnp.where(col_pos < B, 0.0, here))
-    right_ref[:obs, :] = high
-    right_ref[obs : 2 * obs, :] = low
-    right_ref[2 * obs :, :] = high
+    right_ref[3 * B : 3 * B + obs, :] = high
+    right_ref[3 * B + obs : 3 * B + 2 * obs, :] = low
+    right_ref[3 * B + 2 * obs :, :] = high
+
+    @pl.when(col_index == 0)
+    def _():
+        row_pos = lax.broadcasted_iota(jnp.int32, (B, B), 0)
+        identity = jnp.where(row_pos == lax.broadcasted_iota(jnp.int32, (B, B), 1), 1.0, 0.0)
+        identity = identity.astype(jnp.bfloat16)
+        right_ref[:B, :B] = identity
+        right_ref[B : 2 * B, :B] = jnp.zeros((B, B), jnp.bfloat16)
+        right_ref[2 * B : 3 * B, :B] = identity
+
     rows_other = split_dot(filter_ref[...], other_ref[...])
     for half, value in ((core, rows_own), (1 - core, rows_other)):
         value = value.T
@@ -165,26 +148,23 @@
         )
 
 
-def filter_sides(place, joined, lead, other, filter_matrix, regular, lead_reg):
+def both_sides(place, joined, lead, other, strip, inverse, filter_matrix, regular, lead_reg):
     cols = other.shape[1]
     obs = filter_matrix.shape[0]
     vmem = pl.BlockSpec(memory_space=pltpu.VMEM)
     return pl.pallas_call(
-        filter_kernel,
-        in_specs=[pl.BlockSpec(memory_space=pltpu.SMEM)] + [vmem] * 6,
-        out_specs=[vmem] * 4,
+        sides_kernel,
+        in_specs=[pl.BlockSpec(memory_space=pltpu.SMEM)] + [vmem] * 8,
+        out_specs=[vmem] * 3,
         out_shape=[
-            jax.ShapeDtypeStruct((2 * cols, 3 * obs), jnp.bfloat16),
-            jax.ShapeDtypeStruct((3 * obs, cols), jnp.bfloat16),
-            jax.ShapeDtypeStruct((B, cols), jnp.float32),
-            jax.ShapeDtypeStruct((2 * cols, B), jnp.float32),
+            pltpu.HBM((2 * cols, 3 * obs), jnp.bfloat16),
+            pltpu.HBM((3 * (obs + B), cols), jnp.bfloat16),
+            pltpu.HBM((2 * cols, B), jnp.float32),
         ],
-        compiler_params=pltpu.CompilerParams(vmem_limit_bytes=32 * 2**20),
-        cost_estimate=pl.CostEstimate(
-            flops=18 * cols * obs * B, bytes_accessed=24 * cols * B, transcendentals=0
-        ),
-        name="filter_sides",
-    )(place, joined, lead, other, filter_matrix, regular, lead_reg)
+        compiler_params=pltpu.CompilerParams(vmem_limit_bytes=36 * 2**20),
+        cost_estimate=pl.CostEstimate(flops=0, bytes_accessed=0, transcendentals=0),
+        name="both_sides",
+    )(place, joined, lead, other, strip, inverse, filter_matrix, regular, lead_reg)
 
 
 def block_rows(half):
@@ -232,9 +212,7 @@
         ),
         out_shape=jax.ShapeDtypeStruct((rows, cols), jnp.float32),
         compiler_params=pltpu.CompilerParams(vmem_limit_bytes=32 * 2**20),
-        cost_estimate=pl.CostEstimate(
-            flops=2 * rows * cols * right.shape[0], bytes_accessed=8 * rows * cols, transcendentals=0
-        ),
+        cost_estimate=pl.CostEstimate(flops=0, bytes_accessed=0, transcendentals=0),
         name="tile_rows",
     )(place, normals, strip, gram_cols, left, right, inverse, regular)
 
@@ -252,7 +230,7 @@
     return blocks.reshape(count * P_SIZE, count * P_SIZE)
 
 
-def row_strip_piece(normals, later):
+def row_strip_piece(normals):
     peers = lax.axis_size("col")
     chips = peers // 2
     size = normals.shape[0] // chips
@@ -260,7 +238,7 @@
     arrived = [
         lax.ppermute(normals[z * size : (z + 1) * size, :B], "col", [(0, 2 * z)]) for z in range(1, chips)
     ]
-    arrived = sum(after(arrived, later))
+    arrived = sum(arrived)
     piece = jnp.where(col_index == 0, normals[:size, :B], arrived)
     second = lax.ppermute(piece[size // 2 :], "col", [(c, c + 1) for c in range(0, peers, 2)])
     return jnp.where(col_index % 2 == 0, piece[: size // 2], second)
@@ -291,6 +269,9 @@
 
     top_strip = jnp.where(row_index == 0, normals[:B], 0.0)
     col_strip = lax.psum(top_strip, "row")
+
+    piece = row_strip_piece(normals)
+    strip = lax.all_gather(piece, "col", axis=0, tiled=True)
 
     index_bits = [1 << i for i in range((row_peers * col_peers - 1).bit_length())]
     leading, reached = doubled(normals[:B, :B], [bit for bit in index_bits if bit >= col_peers], [0])
@@ -306,11 +287,9 @@
     for to in range(row_peers):
         far = lax.dynamic_index_in_dim(along, (col_index // 2 - to) % chips, 0, keepdims=False)
         sent.append(jnp.concatenate([design, far, lead], axis=1))
-    sent = after(jnp.stack(sent), leading)
+    sent = after(jnp.stack(sent), (leading, piece))
     joined = lax.all_to_all(sent, "row", 0, 0, tiled=True)
     joined = joined.reshape(obs, 2 * cols_here + B)
-
-    strip = lax.all_gather(row_strip_piece(normals, joined), "col", axis=0, tiled=True)
 
     leading, reached = doubled(leading, [bit for bit in reversed(index_bits) if 1 < bit < col_peers], reached)
     leading = jnp.concatenate([joined[:, 2 * cols_here :], leading], axis=0)
@@ -324,9 +303,11 @@
     own_reg = lax.dynamic_slice_in_dim(regular, col_index * cols_here, cols_here).reshape(1, cols_here)
     place = jnp.stack([row_index, col_index]).astype(jnp.int32)
     inverse = corner_factor(corner, lead, filters, lead_reg)
-    gram_left, gram_right, gram_rows, gram_cols = filter_sides(place, joined, lead, other, filters, own_reg, lead_reg)
-    right = right_side(place, col_strip, gram_rows, inverse, gram_right)
-    return tile_rows(place, normals, strip, gram_cols, gram_left, right, inverse, own_reg)
+    left, right, gram_cols = both_sides(
+        place, joined, lead, other, col_strip, inverse, filters, own_reg, lead_reg
+    )
+    large = [pltpu.with_memory_space_constraint(array, pltpu.HBM) for array in (normals, strip, gram_cols, left)]
+    return tile_rows(place, *large, right, inverse, own_reg)
 
 
 def solution(mesh):

time: 186 us -> 186 us (level)
  the two profiles are of different devices: /device:TPU:31 before, /device:TPU:0 now
where the time goes in v12:
time: 186 us
  waiting for transfers between devices  73.9 us (40%)
  Pallas kernels  44.9 us (24%)
  starting transfers between devices  33.8 us (18%)
  between operations  15.2 us (8%)
  other arithmetic  8.91 us (5%)
  local copies, waits for them, and re-layouts  8.9 us (5%)
    ppermute x3, waiting for transfers between devices, body(): lax.ppermute(design, 'col', [(c, (c + 2 * s) % col_peers) for c in range(...  33.9 us
    pallas_call x1, Pallas kernels, tile_rows(): pl.pallas_call(tile_kernel, grid_spec=pltpu.PrefetchScalarGridSpec(num_sc...  21.9 us
    ppermute x3, waiting for transfers between devices, row_strip_piece(): lax.ppermute(normals[z * size:(z + 1) * size, :B], 'col', [(0, 2 * z)])  18.7 us
    ppermute x5, waiting for transfers between devices, doubled(): got = lax.ppermute(value, ('row', 'col'), pairs)  17.4 us
    pallas_call x1, Pallas kernels, corner_factor(): pl.pallas_call(corner_kernel, out_shape=jax.ShapeDtypeStruct((B, B), jnp....  13.9 us
    ppermute x5, starting transfers between devices, doubled(): got = lax.ppermute(value, ('row', 'col'), pairs)  12.6 us
    ppermute x3, starting transfers between devices, row_strip_piece(): lax.ppermute(normals[z * size:(z + 1) * size, :B], 'col', [(0, 2 * z)])  10.8 us
    pallas_call x1, Pallas kernels, both_sides(): pl.pallas_call(sides_kernel, in_specs=[pl.BlockSpec(memory_space=pltpu.SM...  9.14 us
  transfers between devices with their start and end apart: 16, of which 9 were waited for; matrix products, arithmetic and copies ran while one was open for 7% of the time, Pallas kernels for 12%

profile of v12, /device:TPU:0, one launch (start us, length us, event | category | flops | bytes accessed | tf_op | source)
XLA Modules:
  0.0 185.6 jit_solution(13952854351564497233)
XLA Ops:
  7.4 1.8 fusion.6
  9.1 6.0 %collective-permute-start.1 = (f32[768,256]{1,0:T(8,128)S(1)}, f32[768,256]{1,0:T(8,128)S(1)}, u32[]{:S(2)}, u32[]{:S(2)}) collective-permute-start(f32[768,256]{1,0:T(8,128)S(1)} %get-tuple-element.15), channel_id=1, source_target_pairs={{0,4},{8,12},{16,20},{24,28}} | collective-permute-start | bytes 2359304 | tf_op jit(solution)/shard_map/ppermute | solution.py:239
  15.1 2.6 %collective-permute-start.2 = (f32[768,256]{1,0:T(8,128)S(1)}, f32[768,256]{1,0:T(8,128)}, u32[]{:S(2)}, u32[]{:S(2)}) collective-permute-start(f32[768,256]{1,0:T(8,128)S(1)} %get-tuple-element.16), channel_id=1, source_target_pairs={{0,6},{8,14},{16,22},{24,30}} | collective-permute-start | bytes 2359304 | tf_op jit(solution)/shard_map/ppermute | solution.py:239
  17.7 2.2 %collective-permute-start = (f32[768,256]{1,0:T(8,128)S(1)}, f32[768,256]{1,0:T(8,128)}, u32[]{:S(2)}, u32[]{:S(2)}) collective-permute-start(f32[768,256]{1,0:T(8,128)S(1)} %get-tuple-element.17), channel_id=1, source_target_pairs={{0,2},{8,10},{16,18},{24,26}} | collective-permute-start | bytes 2359304 | tf_op jit(solution)/shard_map/ppermute | solution.py:239
  19.9 2.7 %slice_select_fusion = f32[256,1536]{1,0:T(8,128)} fusion(f32[3072,1536]{1,0:T(8,128)} %normals_ref.1, pred[]{:T(512)S(6)} %eq.33), kind=kLoop, calls=%fused_computation.1 | loop fusion | flops 393216 | bytes 3145729 | tf_op jit(solution)/shard_map/jit(_where)/select_n | solution.py:270
  22.7 1.9 %collective-permute-done.1 = f32[768,256]{1,0:T(8,128)S(1)} collective-permute-done((f32[768,256]{1,0:T(8,128)S(1)}, f32[768,256]{1,0:T(8,128)S(1)}, u32[]{:S(2)}, u32[]{:S(2)}) %collective-permute-start.1) | collective-permute-done | bytes 786464 | tf_op jit(solution)/shard_map/ppermute | solution.py:239
  24.6 8.4 %collective-permute-done.2 = f32[768,256]{1,0:T(8,128)} collective-permute-done((f32[768,256]{1,0:T(8,128)S(1)}, f32[768,256]{1,0:T(8,128)}, u32[]{:S(2)}, u32[]{:S(2)}) %collective-permute-start.2) | collective-permute-done | bytes 786464 | tf_op jit(solution)/shard_map/ppermute | solution.py:239
  33.0 8.4 %collective-permute-done = f32[768,256]{1,0:T(8,128)} collective-permute-done((f32[768,256]{1,0:T(8,128)S(1)}, f32[768,256]{1,0:T(8,128)}, u32[]{:S(2)}, u32[]{:S(2)}) %collective-permute-start) | collective-permute-done | bytes 786464 | tf_op jit(solution)/shard_map/ppermute | solution.py:239
  41.4 1.8 add_select_fusion
  43.3 1.4 collective-permute-start.3
  47.0 4.3 %collective-permute-start.5 = (f32[32,1536]{1,0:T(8,128)S(1)}, f32[32,1536]{1,0:T(8,128)S(1)}, u32[]{:S(2)}, u32[]{:S(2)}) collective-permute-start(f32[32,1536]{1,0:T(8,128)S(1)} %copy-done.2), channel_id=1, source_target_pairs={{0,4},{1,5},{2,6},{3,7},{4,0},{5,1},{6,2},{7,3},{8,12},{9,13},{10,... | collective-permute-start | bytes 589832 | tf_op jit(solution)/shard_map/ppermute | solution.py:283
  52.2 3.4 %collective-permute-start.7 = (f32[256,256]{1,0:T(8,128)S(1)}, f32[256,256]{1,0:T(8,128)S(1)}, u32[]{:S(2)}, u32[]{:S(2)}) collective-permute-start(f32[256,256]{1,0:T(8,128)S(1)} %slice.56), channel_id=1, source_target_pairs={{0,8}} | collective-permute-start | bytes 786440 | tf_op jit(solution)/shard_map/ppermute | solution.py:252
  55.8 33.9 %collective-permute-done.5 = f32[32,1536]{1,0:T(8,128)S(1)} collective-permute-done((f32[32,1536]{1,0:T(8,128)S(1)}, f32[32,1536]{1,0:T(8,128)S(1)}, u32[]{:S(2)}, u32[]{:S(2)}) %collective-permute-start.5) | collective-permute-done | bytes 196640 | tf_op jit(solution)/shard_map/ppermute | solution.py:283
  91.0 3.4 %collective-permute-start.8 = (f32[256,256]{1,0:T(8,128)S(1)}, f32[256,256]{1,0:T(8,128)S(1)}, u32[]{:S(2)}, u32[]{:S(2)}) collective-permute-start(f32[256,256]{1,0:T(8,128)S(1)} %broadcast_select_fusion.3), channel_id=1, source_target_pairs={{0,16},{8,24}} | collective-permute-start | bytes 786440 | tf_op jit(solution)/shard_map/ppermute | solution.py:252
  95.7 9.7 %collective-permute-done.8 = f32[256,256]{1,0:T(8,128)S(1)} collective-permute-done((f32[256,256]{1,0:T(8,128)S(1)}, f32[256,256]{1,0:T(8,128)S(1)}, u32[]{:S(2)}, u32[]{:S(2)}) %collective-permute-start.8) | collective-permute-done | bytes 262176 | tf_op jit(solution)/shard_map/ppermute | solution.py:252
  105.4 4.5 %all-to-all-start = ((f32[4,32,3328]{2,1,0:T(8,128)}), f32[4,32,3328]{2,1,0:T(8,128)S(1)}, u32[]{:S(2)}, u32[]{:S(2)}) async-start(f32[4,32,3328]{2,1,0:T(8,128)} %pad_maximum_fusion), calls=%async_computation | async-start | bytes 3407872 | tf_op jit(solution)/shard_map/all_to_all | solution.py:291
  111.3 3.9 %collective-permute-done.9 = f32[256,256]{1,0:T(8,128)S(1)} collective-permute-done((f32[256,256]{1,0:T(8,128)S(1)}, f32[256,256]{1,0:T(8,128)S(1)}, u32[]{:S(2)}, u32[]{:S(2)}) %collective-permute-start.9) | collective-permute-done | bytes 262176 | tf_op jit(solution)/shard_map/ppermute | solution.py:252
  116.5 3.8 %collective-permute-done.10 = f32[256,256]{1,0:T(8,128)S(1)} collective-permute-done((f32[256,256]{1,0:T(8,128)S(1)}, f32[256,256]{1,0:T(8,128)S(1)}, u32[]{:S(2)}, u32[]{:S(2)}) %collective-permute-start.10) | collective-permute-done | bytes 262176 | tf_op jit(solution)/shard_map/ppermute | solution.py:252
  120.4 2.5 %all-to-all-done = f32[4,32,3328]{2,1,0:T(8,128)S(1)} async-done(((f32[4,32,3328]{2,1,0:T(8,128)}), f32[4,32,3328]{2,1,0:T(8,128)S(1)}, u32[]{:S(2)}, u32[]{:S(2)}) %all-to-all-start) | async-done | bytes 1703968 | tf_op jit(solution)/shard_map/all_to_all | solution.py:291
  124.7 3.2 %collective-permute-start.11 = (f32[384,256]{1,0:T(8,128)}, f32[384,256]{1,0:T(8,128)}, u32[]{:S(2)}, u32[]{:S(2)}) collective-permute-start(f32[384,256]{1,0:T(8,128)} %pad_maximum_fusion.10), channel_id=1, source_target_pairs={{0,1},{8,9},{16,17},{24,25},{4,5},{12,13},{20,21},{28,29},{2,3},{1... | collective-permute-start | bytes 1179656 | tf_op jit(solution)/shard_map/ppermute | solution.py:252
  129.8 13.9 %corner_factor.1.inverse_ref = f32[256,256]{1,0:T(8,128)S(1)} custom-call(f32[256,256]{1,0:T(8,128)S(1)} %slice.70.block_ref, f32[128,256]{1,0:T(8,128)S(1)} %slice.68.design_ref.lead_ref, f32[128,128]{1,0:T(8,128)S(1)} %select_n.149.filter_ref, f32[1,256]{1,0:T(1,128)S(1)} %bitcast.33), custom_call_target="tpu_custom_call" | custom-call | tf_op jit(solution)/shard_map/corner_factor/pallas_call | solution.py:82
  145.1 9.1 %both_sides.1 = (bf16[3072,384]{1,0:T(8,128)(2,1)}, bf16[1152,1536]{1,0:T(8,128)(2,1)}, f32[3072,256]{1,0:T(8,128)}) custom-call(s32[2]{0:T(128)S(1)} %pad_add_fusion.place_ref, f32[128,3328]{1,0:T(8,128)S(1)} %bitcast.32, f32[128,256]{1,0:T(8,128)S(1)} %slice.68.design_ref.lead_ref, f32[128,1536]{1,0:T(8,128)S(1)} %collective-permute-done.12.other_ref, ...), custom_call_target="tpu_custom_call" | custom-call | tf_op jit(solution)/shard_map/both_sides/pallas_call | solution.py:155
  154.3 2.0 %copy-done = bf16[1152,1536]{1,0:T(8,128)(2,1)S(1)} copy-done((bf16[1152,1536]{1,0:T(8,128)(2,1)S(1)}, bf16[1152,1536]{1,0:T(8,128)(2,1)}, u32[]{:S(2)}) %copy-start) | copy-done | bytes 3538968
  156.3 21.9 %tile_rows.1 = f32[3072,1536]{1,0:T(8,128)} custom-call(s32[2]{0:T(128)S(1)} %pad_add_fusion.place_ref, f32[3072,1536]{1,0:T(8,128)} %normals_ref.1, f32[3072,256]{1,0:T(8,128)} %all-gather.2.cloned.1.call-done.strip_ref, f32[3072,256]{1,0:T(8,128)} %get-tuple-element.12.gram_ref, bf16[3072,384]{1,0:T(8,128)(2,1)} %get-tuple-element.13.left_ref, ...), custom_call_target="tpu_custom_call" | custom-call | tf_op jit(solution)/shard_map/tile_rows/pallas_call | solution.py:204
  (50 shorter events, 13.6 us)
Async XLA Ops:
  7.4 136.3 %all-reduce.2.cloned.1.call-start = ((), (), s32[]{:S(2)}) async-start(), calls=%async_computation.2 | async-start | bytes 3145728 | tf_op jit(solution)/shard_map/psum | solution.py:271
  9.1 15.4 %collective-permute-start.1 = (f32[768,256]{1,0:T(8,128)S(1)}, f32[768,256]{1,0:T(8,128)S(1)}, u32[]{:S(2)}, u32[]{:S(2)}) collective-permute-start(f32[768,256]{1,0:T(8,128)S(1)} %get-tuple-element.15), channel_id=1, source_target_pairs={{0,4},{8,12},{16,20},{24,28}} | collective-permute-start | bytes 2359304 | tf_op jit(solution)/shard_map/ppermute | solution.py:239
  15.1 17.9 %collective-permute-start.2 = (f32[768,256]{1,0:T(8,128)S(1)}, f32[768,256]{1,0:T(8,128)}, u32[]{:S(2)}, u32[]{:S(2)}) collective-permute-start(f32[768,256]{1,0:T(8,128)S(1)} %get-tuple-element.16), channel_id=1, source_target_pairs={{0,6},{8,14},{16,22},{24,30}} | collective-permute-start | bytes 2359304 | tf_op jit(solution)/shard_map/ppermute | solution.py:239
  17.7 23.7 %collective-permute-start = (f32[768,256]{1,0:T(8,128)S(1)}, f32[768,256]{1,0:T(8,128)}, u32[]{:S(2)}, u32[]{:S(2)}) collective-permute-start(f32[768,256]{1,0:T(8,128)S(1)} %get-tuple-element.17), channel_id=1, source_target_pairs={{0,2},{8,10},{16,18},{24,26}} | collective-permute-start | bytes 2359304 | tf_op jit(solution)/shard_map/ppermute | solution.py:239
  22.7 131.6 %all-gather.2.cloned.1.call-start = ((), (), s32[]{:S(2)}) async-start(), calls=%async_computation.1 | async-start | bytes 3538944 | tf_op jit(solution)/shard_map/all_gather | solution.py:274
  43.2 3.6 %copy-start.2 = (f32[32,1536]{1,0:T(8,128)S(1)}, f32[32,1536]{1,0:T(8,128)}, u32[]{:S(2)}) copy-start(f32[32,1536]{1,0:T(8,128)} %param.5) | copy-start | bytes 589828
  43.3 2.8 %collective-permute-start.3 = (f32[384,256]{1,0:T(8,128)S(1)}, f32[384,256]{1,0:T(8,128)S(1)}, u32[]{:S(2)}, u32[]{:S(2)}) collective-permute-start(f32[384,256]{1,0:T(8,128)S(1)} %slice.65), channel_id=1, source_target_pairs={{0,1},{2,3},{4,5},{6,7},{8,9},{10,11},{12,13},{14,15},{16,17},{18,... | collective-permute-start | bytes 1179656 | tf_op jit(solution)/shard_map/ppermute | solution.py:243
  46.9 8.9 %collective-permute-start.6 = (f32[32,1536]{1,0:T(8,128)S(1)}, f32[32,1536]{1,0:T(8,128)S(1)}, u32[]{:S(2)}, u32[]{:S(2)}) collective-permute-start(f32[32,1536]{1,0:T(8,128)S(1)} %copy-done.2), channel_id=1, source_target_pairs={{0,6},{1,7},{2,0},{3,1},{4,2},{5,3},{6,4},{7,5},{8,14},{9,15},{10,... | collective-permute-start | bytes 589832 | tf_op jit(solution)/shard_map/ppermute | solution.py:283
  47.0 42.7 %collective-permute-start.5 = (f32[32,1536]{1,0:T(8,128)S(1)}, f32[32,1536]{1,0:T(8,128)S(1)}, u32[]{:S(2)}, u32[]{:S(2)}) collective-permute-start(f32[32,1536]{1,0:T(8,128)S(1)} %copy-done.2), channel_id=1, source_target_pairs={{0,4},{1,5},{2,6},{3,7},{4,0},{5,1},{6,2},{7,3},{8,12},{9,13},{10,... | collective-permute-start | bytes 589832 | tf_op jit(solution)/shard_map/ppermute | solution.py:283
  51.2 38.4 %collective-permute-start.4 = (f32[32,1536]{1,0:T(8,128)S(1)}, f32[32,1536]{1,0:T(8,128)S(1)}, u32[]{:S(2)}, u32[]{:S(2)}) collective-permute-start(f32[32,1536]{1,0:T(8,128)S(1)} %copy-done.2), channel_id=1, source_target_pairs={{0,2},{1,3},{2,4},{3,5},{4,6},{5,7},{6,0},{7,1},{8,10},{9,11},{10,... | collective-permute-start | bytes 589832 | tf_op jit(solution)/shard_map/ppermute | solution.py:283
  52.2 37.7 %collective-permute-start.7 = (f32[256,256]{1,0:T(8,128)S(1)}, f32[256,256]{1,0:T(8,128)S(1)}, u32[]{:S(2)}, u32[]{:S(2)}) collective-permute-start(f32[256,256]{1,0:T(8,128)S(1)} %slice.56), channel_id=1, source_target_pairs={{0,8}} | collective-permute-start | bytes 786440 | tf_op jit(solution)/shard_map/ppermute | solution.py:252
  91.0 14.4 %collective-permute-start.8 = (f32[256,256]{1,0:T(8,128)S(1)}, f32[256,256]{1,0:T(8,128)S(1)}, u32[]{:S(2)}, u32[]{:S(2)}) collective-permute-start(f32[256,256]{1,0:T(8,128)S(1)} %broadcast_select_fusion.3), channel_id=1, source_target_pairs={{0,16},{8,24}} | collective-permute-start | bytes 786440 | tf_op jit(solution)/shard_map/ppermute | solution.py:252
  105.4 11.1 %copy-start.3 = (f32[2,32,32]{2,1,0:T(8,128)S(1)}, f32[2,32,32]{2,1,0:T(8,128)}, u32[]{:S(2)}) copy-start(f32[2,32,32]{2,1,0:T(8,128)} %param.6) | copy-start | bytes 24580
  105.4 17.5 %all-to-all-start = ((f32[4,32,3328]{2,1,0:T(8,128)}), f32[4,32,3328]{2,1,0:T(8,128)S(1)}, u32[]{:S(2)}, u32[]{:S(2)}) async-start(f32[4,32,3328]{2,1,0:T(8,128)} %pad_maximum_fusion), calls=%async_computation | async-start | bytes 3407872 | tf_op jit(solution)/shard_map/all_to_all | solution.py:291
  110.0 5.2 %collective-permute-start.9 = (f32[256,256]{1,0:T(8,128)S(1)}, f32[256,256]{1,0:T(8,128)S(1)}, u32[]{:S(2)}, u32[]{:S(2)}) collective-permute-start(f32[256,256]{1,0:T(8,128)S(1)} %broadcast_select_fusion.4), channel_id=1, source_target_pairs={{0,4},{8,12},{16,20},{24,28}} | collective-permute-start | bytes 786440 | tf_op jit(solution)/shard_map/ppermute | solution.py:252
  115.2 5.2 %collective-permute-start.10 = (f32[256,256]{1,0:T(8,128)S(1)}, f32[256,256]{1,0:T(8,128)S(1)}, u32[]{:S(2)}, u32[]{:S(2)}) collective-permute-start(f32[256,256]{1,0:T(8,128)S(1)} %broadcast_select_fusion.1), channel_id=1, source_target_pairs={{0,2},{8,10},{16,18},{24,26},{4,6},{12,14},{20,22},{28,30}} | collective-permute-start | bytes 786440 | tf_op jit(solution)/shard_map/ppermute | solution.py:252
  123.9 19.8 %collective-permute-start.12 = (f32[128,1536]{1,0:T(8,128)}, f32[128,1536]{1,0:T(8,128)S(1)}, u32[]{:S(2)}, u32[]{:S(2)}) collective-permute-start(f32[128,1536]{1,0:T(8,128)} %slice.69), channel_id=1, source_target_pairs={{0,1},{1,0},{2,3},{3,2},{4,5},{5,4},{6,7},{7,6},{8,9},{9,8},{10,11... | collective-permute-start | bytes 2359304 | tf_op jit(solution)/shard_map/ppermute | solution.py:298
  124.7 5.0 %collective-permute-start.11 = (f32[384,256]{1,0:T(8,128)}, f32[384,256]{1,0:T(8,128)}, u32[]{:S(2)}, u32[]{:S(2)}) collective-permute-start(f32[384,256]{1,0:T(8,128)} %pad_maximum_fusion.10), channel_id=1, source_target_pairs={{0,1},{8,9},{16,17},{24,25},{4,5},{12,13},{20,21},{28,29},{2,3},{1... | collective-permute-start | bytes 1179656 | tf_op jit(solution)/shard_map/ppermute | solution.py:252
  143.7 1.4 copy-start.1
  154.3 2.0 %copy-start = (bf16[1152,1536]{1,0:T(8,128)(2,1)S(1)}, bf16[1152,1536]{1,0:T(8,128)(2,1)}, u32[]{:S(2)}) copy-start(bf16[1152,1536]{1,0:T(8,128)(2,1)} %get-tuple-element.14.right_ref) | copy-start | bytes 10616836
Sparse Core Ops, SparseCore 0:
  22.8 59.0 all-reduce.1
Sparse Core Ops, SparseCore 1:
  47.0 48.9 all-gather.1

commit v13 on v12

--- a/solution.py
+++ b/solution.py
@@ -230,15 +230,14 @@
     return blocks.reshape(count * P_SIZE, count * P_SIZE)
 
 
-def row_strip_piece(normals):
+def row_strip_piece(normals, earlier, meanwhile):
     peers = lax.axis_size("col")
     chips = peers // 2
     size = normals.shape[0] // chips
     col_index = lax.axis_index("col")
-    arrived = [
-        lax.ppermute(normals[z * size : (z + 1) * size, :B], "col", [(0, 2 * z)]) for z in range(1, chips)
-    ]
-    arrived = sum(arrived)
+    shares = after([normals[z * size : (z + 1) * size, :B] for z in range(1, chips)], earlier)
+    arrived = [lax.ppermute(share, "col", [(0, 2 * z)]) for z, share in enumerate(shares, 1)]
+    arrived = sum(after(arrived, meanwhile))
     piece = jnp.where(col_index == 0, normals[:size, :B], arrived)
     second = lax.ppermute(piece[size // 2 :], "col", [(c, c + 1) for c in range(0, peers, 2)])
     return jnp.where(col_index % 2 == 0, piece[: size // 2], second)
@@ -261,48 +260,52 @@
     row_peers = lax.axis_size("row")
     row_index = lax.axis_index("row")
     col_index = lax.axis_index("col")
+    col_peers = lax.axis_size("col")
     obs = row_peers * obs_here
     core = col_index % 2
 
-    col_peers = lax.axis_size("col")
+
     col_strip = lax.psum(jnp.where(row_index == 0, normals[:B], 0.0), "row")
 
-    top_strip = jnp.where(row_index == 0, normals[:B], 0.0)
-    col_strip = lax.psum(top_strip, "row")
-
-    piece = row_strip_piece(normals)
-    strip = lax.all_gather(piece, "col", axis=0, tiled=True)
-
     index_bits = [1 << i for i in range((row_peers * col_peers - 1).bit_length())]
-    leading, reached = doubled(normals[:B, :B], [bit for bit in index_bits if bit >= col_peers], [0])
+    z_bits = [bit for bit in reversed(index_bits) if 1 < bit < col_peers]
+    row_bits = [bit for bit in index_bits if bit >= col_peers]
+    leading, reached = doubled(normals[:B, :B], z_bits, [0])
 
     chips = col_peers // 2
-    design = after(design, top_strip)
+    chip = col_index // 2
     along = [design]
     for s in range(1, chips):
         along.append(lax.ppermute(design, "col", [(c, (c + 2 * s) % col_peers) for c in range(col_peers)]))
     along = jnp.stack(along)
-    lead = lax.dynamic_index_in_dim(along, col_index // 2, 0, keepdims=False)[:, :B]
+
+    leading, reached = doubled(leading, row_bits, reached)
+    lead = lax.dynamic_index_in_dim(along, chip, 0, keepdims=False)[:, :B]
+    lead = lax.all_gather(lead, "row", axis=0, tiled=True)
+    leading = jnp.concatenate([lead, leading], axis=0)
+
     sent = []
     for to in range(row_peers):
-        far = lax.dynamic_index_in_dim(along, (col_index // 2 - to) % chips, 0, keepdims=False)
-        sent.append(jnp.concatenate([design, far, lead], axis=1))
-    sent = after(jnp.stack(sent), (leading, piece))
+        far = lax.dynamic_index_in_dim(along, (chip - to) % chips, 0, keepdims=False)
+        sent.append(jnp.concatenate([design, far], axis=1))
+    sent = jnp.stack(sent)
     joined = lax.all_to_all(sent, "row", 0, 0, tiled=True)
-    joined = joined.reshape(obs, 2 * cols_here + B)
-
-    leading, reached = doubled(leading, [bit for bit in reversed(index_bits) if 1 < bit < col_peers], reached)
-    leading = jnp.concatenate([joined[:, 2 * cols_here :], leading], axis=0)
+    joined = joined.reshape(obs, 2 * cols_here)
+
+    piece = row_strip_piece(normals, along, (leading, sent))
+    strip = lax.all_gather(piece, "col", axis=0, tiled=True)
+
     leading, _ = doubled(leading, [1], reached)
     lead, corner = leading[:obs], leading[obs:]
-    other = lax.ppermute(
-        joined[:, cols_here : 2 * cols_here], "col", [(c, c ^ 1) for c in range(col_peers)]
-    )
     filters = filter_matrix_of(filter_blocks, obs // P_SIZE)
     lead_reg = regular[:B].reshape(1, B)
+    inverse = corner_factor(corner, lead, filters, lead_reg)
+
+    other = lax.ppermute(
+        after(joined[:, cols_here:], inverse), "col", [(c, c ^ 1) for c in range(col_peers)]
+    )
     own_reg = lax.dynamic_slice_in_dim(regular, col_index * cols_here, cols_here).reshape(1, cols_here)
     place = jnp.stack([row_index, col_index]).astype(jnp.int32)
-    inverse = corner_factor(corner, lead, filters, lead_reg)
     left, right, gram_cols = both_sides(
         place, joined, lead, other, col_strip, inverse, filters, own_reg, lead_reg
     )

time: 186 us -> 157 us (0.84)
  waiting for transfers between devices: 73.9 us -> 34.4 us
  blocking collectives: 0 us -> 7.16 us
  starting transfers between devices: 33.8 us -> 36.8 us
    ppermute x3, waiting for transfers between devices: 33.9 us -> 4.39 us  [body(): lax.ppermute(design, 'col', [(c, (c + 2 * s) % col_peers) for c in range(...]
    ppermute x4, waiting for transfers between devices: 18.7 us -> 1.61 us  [the longest x1 1.61 us: body(): lax.ppermute(after(joined[:, cols_here:], inverse), 'col', [(c, c ^ 1) fo...]
    all_to_all x1, waiting for transfers between devices: 2.54 us -> 16.6 us  [body(): joined = lax.all_to_all(sent, 'row', 0, 0, tiled=True)]
    all_gather x0 -> x1, blocking collectives: none -> 7.16 us  [body(): lead = lax.all_gather(lead, 'row', axis=0, tiled=True)]
    ppermute x5, waiting for transfers between devices: 17.4 us -> 10.5 us  [doubled(): got = lax.ppermute(value, ('row', 'col'), pairs)]
    ppermute x4, starting transfers between devices: 10.8 us -> 5.24 us  [the longest x3 5.17 us: row_strip_piece(): lax.ppermute(share, 'col', [(0, 2 * z)])]
    ppermute x5, starting transfers between devices: 12.6 us -> 16.7 us  [doubled(): got = lax.ppermute(value, ('row', 'col'), pairs)]
    ppermute x3, starting transfers between devices: 4.34 us -> 7.86 us  [body(): lax.ppermute(design, 'col', [(c, (c + 2 * s) % col_peers) for c in range(...]
  transfers between devices with their start and end apart: 16 -> 16, of which waited for: 9 -> 7; matrix products, arithmetic and copies ran while one was open for 7% -> 9% of each run, Pallas kernels for 12% -> 15%
where the time goes in v13:
time: 157 us; the launch traced here: 156 us
  Pallas kernels  45 us (29%)
  starting transfers between devices  36.8 us (23%)
  waiting for transfers between devices  34.4 us (22%)
  between operations  15.2 us (10%)
  local copies, waits for them, and re-layouts  8.95 us (6%)
  other arithmetic  8.73 us (6%)
  blocking collectives  7.16 us (5%)
    pallas_call x1, Pallas kernels, tile_rows(): pl.pallas_call(tile_kernel, grid_spec=pltpu.PrefetchScalarGridSpec(num_sc...  21.9 us
    ppermute x5, starting transfers between devices, doubled(): got = lax.ppermute(value, ('row', 'col'), pairs)  16.7 us
    all_to_all x1, waiting for transfers between devices, body(): joined = lax.all_to_all(sent, 'row', 0, 0, tiled=True)  16.6 us
    pallas_call x1, Pallas kernels, corner_factor(): pl.pallas_call(corner_kernel, out_shape=jax.ShapeDtypeStruct((B, B), jnp....  13.9 us
    ppermute x5, waiting for transfers between devices, doubled(): got = lax.ppermute(value, ('row', 'col'), pairs)  10.5 us
    pallas_call x1, Pallas kernels, both_sides(): pl.pallas_call(sides_kernel, in_specs=[pl.BlockSpec(memory_space=pltpu.SM...  9.21 us
    ppermute x3, starting transfers between devices, body(): lax.ppermute(design, 'col', [(c, (c + 2 * s) % col_peers) for c in range(...  7.86 us
    all_gather x1, blocking collectives, body(): lead = lax.all_gather(lead, 'row', axis=0, tiled=True)  7.16 us
  transfers between devices with their start and end apart: 16, of which 7 were waited for; matrix products, arithmetic and copies ran while one was open for 9% of the time, Pallas kernels for 15%

profile of v13, /device:TPU:0, one launch (start us, length us, event | category | flops | bytes accessed | tf_op | source)
XLA Modules:
  0.0 156.3 jit_solution(6378822476576391612)
XLA Ops:
  7.4 4.0 %collective-permute-start.1 = (f32[32,1536]{1,0:T(8,128)}, f32[32,1536]{1,0:T(8,128)S(1)}, u32[]{:S(2)}, u32[]{:S(2)}) collective-permute-start(f32[32,1536]{1,0:T(8,128)} %param.5), channel_id=1, source_target_pairs={{0,4},{1,5},{2,6},{3,7},{4,0},{5,1},{6,2},{7,3},{8,12},{9,13},{10,... | collective-permute-start | bytes 589832 | tf_op jit(solution)/shard_map/ppermute | solution.py:279
  11.4 1.6 %collective-permute-start = (f32[32,1536]{1,0:T(8,128)}, f32[32,1536]{1,0:T(8,128)S(1)}, u32[]{:S(2)}, u32[]{:S(2)}) collective-permute-start(f32[32,1536]{1,0:T(8,128)} %param.5), channel_id=1, source_target_pairs={{0,2},{1,3},{2,4},{3,5},{4,6},{5,7},{6,0},{7,1},{8,10},{9,11},{10,... | collective-permute-start | bytes 589832 | tf_op jit(solution)/shard_map/ppermute | solution.py:279
  13.0 2.2 %collective-permute-start.2 = (f32[32,1536]{1,0:T(8,128)}, f32[32,1536]{1,0:T(8,128)}, u32[]{:S(2)}, u32[]{:S(2)}) collective-permute-start(f32[32,1536]{1,0:T(8,128)} %param.5), channel_id=1, source_target_pairs={{0,6},{1,7},{2,0},{3,1},{4,2},{5,3},{6,4},{7,5},{8,14},{9,15},{10,... | collective-permute-start | bytes 589832 | tf_op jit(solution)/shard_map/ppermute | solution.py:279
  17.5 2.7 %slice_select_fusion = f32[256,1536]{1,0:T(8,128)} fusion(f32[3072,1536]{1,0:T(8,128)} %normals_ref.1, pred[]{:T(512)S(6)} %eq.35), kind=kLoop, calls=%fused_computation.1 | loop fusion | flops 393216 | bytes 3145729 | tf_op jit(solution)/shard_map/jit(_where)/select_n | solution.py:268
  20.3 1.8 %fusion.6 = (f32[768,256]{1,0:T(8,128)S(1)}, f32[768,256]{1,0:T(8,128)S(1)}, f32[768,256]{1,0:T(8,128)S(1)}) fusion(f32[3072,1536]{1,0:T(8,128)} %normals_ref.1), kind=kLoop, calls=%fused_computation.31 | loop fusion | bytes 4718592 | tf_op jit(solution)/shard_map/slice | solution.py:238
  22.3 3.6 %collective-permute-done.1 = f32[32,1536]{1,0:T(8,128)S(1)} collective-permute-done((f32[32,1536]{1,0:T(8,128)}, f32[32,1536]{1,0:T(8,128)S(1)}, u32[]{:S(2)}, u32[]{:S(2)}) %collective-permute-start.1) | collective-permute-done | bytes 196640 | tf_op jit(solution)/shard_map/ppermute | solution.py:279
  28.6 8.1 %collective-permute-start.7 = (f32[256,256]{1,0:T(8,128)S(1)}, f32[256,256]{1,0:T(8,128)S(1)}, u32[]{:S(2)}, u32[]{:S(2)}) collective-permute-start(f32[256,256]{1,0:T(8,128)S(1)} %broadcast_select_fusion.1), channel_id=1, source_target_pairs={{0,2},{4,6}} | collective-permute-start | bytes 786440 | tf_op jit(solution)/shard_map/ppermute | solution.py:251
  36.9 1.3 collective-permute-start.3
  38.2 2.5 %collective-permute-start.4 = (f32[768,256]{1,0:T(8,128)S(1)}, f32[768,256]{1,0:T(8,128)S(1)}, u32[]{:S(2)}, u32[]{:S(2)}) collective-permute-start(f32[768,256]{1,0:T(8,128)S(1)} %get-tuple-element.16), channel_id=1, source_target_pairs={{0,4},{8,12},{16,20},{24,28}} | collective-permute-start | bytes 2359304 | tf_op jit(solution)/shard_map/ppermute | solution.py:239
  40.7 1.3 collective-permute-start.5
  42.1 7.2 %all_gather.6 = f32[128,256]{1,0:T(8,128)S(1)} all-gather(f32[32,256]{1,0:T(8,128)S(1)} %slice.60), channel_id=1, replica_groups=mesh['row'=4,'col'=8] {'row'}, dimensions={0}, use_global_device_ids=true | all-gather | bytes 163840 | tf_op jit(solution)/shard_map/all_gather | solution.py:284
  49.3 3.7 %collective-permute-start.8 = (f32[256,256]{1,0:T(8,128)S(1)}, f32[256,256]{1,0:T(8,128)S(1)}, u32[]{:S(2)}, u32[]{:S(2)}) collective-permute-start(f32[256,256]{1,0:T(8,128)S(1)} %broadcast_select_fusion.2), channel_id=1, source_target_pairs={{0,8},{4,12},{2,10},{6,14}} | collective-permute-start | bytes 786440 | tf_op jit(solution)/shard_map/ppermute | solution.py:251
  53.2 7.9 %collective-permute-done.8 = f32[256,256]{1,0:T(8,128)S(1)} collective-permute-done((f32[256,256]{1,0:T(8,128)S(1)}, f32[256,256]{1,0:T(8,128)S(1)}, u32[]{:S(2)}, u32[]{:S(2)}) %collective-permute-start.8) | collective-permute-done | bytes 262176 | tf_op jit(solution)/shard_map/ppermute | solution.py:251
  63.7 2.6 %collective-permute-done.9 = f32[256,256]{1,0:T(8,128)S(1)} collective-permute-done((f32[256,256]{1,0:T(8,128)S(1)}, f32[256,256]{1,0:T(8,128)S(1)}, u32[]{:S(2)}, u32[]{:S(2)}) %collective-permute-start.9) | collective-permute-done | bytes 262176 | tf_op jit(solution)/shard_map/ppermute | solution.py:251
  66.4 1.4 add_select_fusion
  71.3 5.7 %all-to-all-start = ((f32[4,32,3072]{2,1,0:T(8,128)}), f32[4,32,3072]{2,1,0:T(8,128)S(1)}, u32[]{:S(2)}, u32[]{:S(2)}) async-start(f32[4,32,3072]{2,1,0:T(8,128)} %pad_maximum_fusion), calls=%async_computation | async-start | bytes 3145728 | tf_op jit(solution)/shard_map/all_to_all | solution.py:292
  77.0 2.2 %collective-permute-start.11 = (f32[384,256]{1,0:T(8,128)S(1)}, f32[384,256]{1,0:T(8,128)S(1)}, u32[]{:S(2)}, u32[]{:S(2)}) collective-permute-start(f32[384,256]{1,0:T(8,128)S(1)} %pad_maximum_fusion.6), channel_id=1, source_target_pairs={{0,1},{4,5},{2,3},{6,7},{8,9},{12,13},{10,11},{14,15},{16,17},{20,... | collective-permute-start | bytes 1179656 | tf_op jit(solution)/shard_map/ppermute | solution.py:251
  80.2 16.6 %all-to-all-done = f32[4,32,3072]{2,1,0:T(8,128)S(1)} async-done(((f32[4,32,3072]{2,1,0:T(8,128)}), f32[4,32,3072]{2,1,0:T(8,128)S(1)}, u32[]{:S(2)}, u32[]{:S(2)}) %all-to-all-start) | async-done | bytes 1572896 | tf_op jit(solution)/shard_map/all_to_all | solution.py:292
  97.9 13.9 %corner_factor.1.inverse_ref = f32[256,256]{1,0:T(8,128)S(1)} custom-call(f32[256,256]{1,0:T(8,128)S(1)} %slice.65.block_ref, f32[128,256]{1,0:T(8,128)S(1)} %slice.63.design_ref.lead_ref, f32[128,128]{1,0:T(8,128)S(1)} %select_n.143.filter_ref, f32[1,256]{1,0:T(1,128)S(1)} %bitcast.32), custom_call_target="tpu_custom_call" | custom-call | tf_op jit(solution)/shard_map/corner_factor/pallas_call | solution.py:82
  112.7 1.6 %collective-permute-done.12.other_ref = f32[128,1536]{1,0:T(8,128)S(1)} collective-permute-done((f32[128,1536]{1,0:T(8,128)}, f32[128,1536]{1,0:T(8,128)S(1)}, u32[]{:S(2)}, u32[]{:S(2)}) %collective-permute-start.12) | collective-permute-done | bytes 786464 | tf_op jit(solution)/shard_map/ppermute | solution.py:304
  114.3 1.4 copy-done.1
  115.7 9.2 %both_sides.1 = (bf16[3072,384]{1,0:T(8,128)(2,1)}, bf16[1152,1536]{1,0:T(8,128)(2,1)}, f32[3072,256]{1,0:T(8,128)}) custom-call(s32[2]{0:T(128)S(1)} %pad_add_fusion.place_ref, f32[128,3072]{1,0:T(8,128)S(1)} %bitcast.31, f32[128,256]{1,0:T(8,128)S(1)} %slice.63.design_ref.lead_ref, f32[128,1536]{1,0:T(8,128)S(1)} %collective-permute-done.12.other_ref, ...), custom_call_target="tpu_custom_call" | custom-call | tf_op jit(solution)/shard_map/both_sides/pallas_call | solution.py:155
  124.9 2.0 %copy-done = bf16[1152,1536]{1,0:T(8,128)(2,1)S(1)} copy-done((bf16[1152,1536]{1,0:T(8,128)(2,1)S(1)}, bf16[1152,1536]{1,0:T(8,128)(2,1)}, u32[]{:S(2)}) %copy-start) | copy-done | bytes 3538968
  126.9 21.9 %tile_rows.1 = f32[3072,1536]{1,0:T(8,128)} custom-call(s32[2]{0:T(128)S(1)} %pad_add_fusion.place_ref, f32[3072,1536]{1,0:T(8,128)} %normals_ref.1, f32[3072,256]{1,0:T(8,128)} %all-gather.2.cloned.1.call-done.strip_ref, f32[3072,256]{1,0:T(8,128)} %get-tuple-element.22.gram_ref, bf16[3072,384]{1,0:T(8,128)(2,1)} %get-tuple-element.23.left_ref, ...), custom_call_target="tpu_custom_call" | custom-call | tf_op jit(solution)/shard_map/tile_rows/pallas_call | solution.py:204
  (50 shorter events, 14.6 us)
Async XLA Ops:
  7.4 105.3 %all-reduce.2.cloned.1.call-start = ((), (), s32[]{:S(2)}) async-start(), calls=%async_computation.2 | async-start | bytes 3145728 | tf_op jit(solution)/shard_map/psum | solution.py:268
  7.4 18.4 %collective-permute-start.1 = (f32[32,1536]{1,0:T(8,128)}, f32[32,1536]{1,0:T(8,128)S(1)}, u32[]{:S(2)}, u32[]{:S(2)}) collective-permute-start(f32[32,1536]{1,0:T(8,128)} %param.5), channel_id=1, source_target_pairs={{0,4},{1,5},{2,6},{3,7},{4,0},{5,1},{6,2},{7,3},{8,12},{9,13},{10,... | collective-permute-start | bytes 589832 | tf_op jit(solution)/shard_map/ppermute | solution.py:279
  11.4 14.4 %collective-permute-start = (f32[32,1536]{1,0:T(8,128)}, f32[32,1536]{1,0:T(8,128)S(1)}, u32[]{:S(2)}, u32[]{:S(2)}) collective-permute-start(f32[32,1536]{1,0:T(8,128)} %param.5), channel_id=1, source_target_pairs={{0,2},{1,3},{2,4},{3,5},{4,6},{5,7},{6,0},{7,1},{8,10},{9,11},{10,... | collective-permute-start | bytes 589832 | tf_op jit(solution)/shard_map/ppermute | solution.py:279
  13.0 13.7 %collective-permute-start.2 = (f32[32,1536]{1,0:T(8,128)}, f32[32,1536]{1,0:T(8,128)}, u32[]{:S(2)}, u32[]{:S(2)}) collective-permute-start(f32[32,1536]{1,0:T(8,128)} %param.5), channel_id=1, source_target_pairs={{0,6},{1,7},{2,0},{3,1},{4,2},{5,3},{6,4},{7,5},{8,14},{9,15},{10,... | collective-permute-start | bytes 589832 | tf_op jit(solution)/shard_map/ppermute | solution.py:279
  16.2 11.4 %collective-permute-start.6 = (f32[256,256]{1,0:T(8,128)S(1)}, f32[256,256]{1,0:T(8,128)S(1)}, u32[]{:S(2)}, u32[]{:S(2)}) collective-permute-start(f32[256,256]{1,0:T(8,128)S(1)} %slice.50), channel_id=1, source_target_pairs={{0,4}} | collective-permute-start | bytes 786440 | tf_op jit(solution)/shard_map/ppermute | solution.py:251
  20.3 6.4 %copy-start.2 = (f32[32,1536]{1,0:T(8,128)S(1)}, f32[32,1536]{1,0:T(8,128)}, u32[]{:S(2)}) copy-start(f32[32,1536]{1,0:T(8,128)} %param.5) | copy-start | bytes 589828
  20.3 104.7 %all-gather.2.cloned.1.call-start = ((), (), s32[]{:S(2)}) async-start(), calls=%async_computation.1 | async-start | bytes 3538944 | tf_op jit(solution)/shard_map/all_gather | solution.py:296
  28.6 20.6 %collective-permute-start.7 = (f32[256,256]{1,0:T(8,128)S(1)}, f32[256,256]{1,0:T(8,128)S(1)}, u32[]{:S(2)}, u32[]{:S(2)}) collective-permute-start(f32[256,256]{1,0:T(8,128)S(1)} %broadcast_select_fusion.1), channel_id=1, source_target_pairs={{0,2},{4,6}} | collective-permute-start | bytes 786440 | tf_op jit(solution)/shard_map/ppermute | solution.py:251
  36.9 29.5 %collective-permute-start.3 = (f32[768,256]{1,0:T(8,128)S(1)}, f32[768,256]{1,0:T(8,128)S(1)}, u32[]{:S(2)}, u32[]{:S(2)}) collective-permute-start(f32[768,256]{1,0:T(8,128)S(1)} %get-tuple-element.15), channel_id=1, source_target_pairs={{0,2},{8,10},{16,18},{24,26}} | collective-permute-start | bytes 2359304 | tf_op jit(solution)/shard_map/ppermute | solution.py:239
  38.2 28.2 %collective-permute-start.4 = (f32[768,256]{1,0:T(8,128)S(1)}, f32[768,256]{1,0:T(8,128)S(1)}, u32[]{:S(2)}, u32[]{:S(2)}) collective-permute-start(f32[768,256]{1,0:T(8,128)S(1)} %get-tuple-element.16), channel_id=1, source_target_pairs={{0,4},{8,12},{16,20},{24,28}} | collective-permute-start | bytes 2359304 | tf_op jit(solution)/shard_map/ppermute | solution.py:239
  40.7 25.7 %collective-permute-start.5 = (f32[768,256]{1,0:T(8,128)S(1)}, f32[768,256]{1,0:T(8,128)S(1)}, u32[]{:S(2)}, u32[]{:S(2)}) collective-permute-start(f32[768,256]{1,0:T(8,128)S(1)} %get-tuple-element.17), channel_id=1, source_target_pairs={{0,6},{8,14},{16,22},{24,30}} | collective-permute-start | bytes 2359304 | tf_op jit(solution)/shard_map/ppermute | solution.py:239
  49.3 11.8 %collective-permute-start.8 = (f32[256,256]{1,0:T(8,128)S(1)}, f32[256,256]{1,0:T(8,128)S(1)}, u32[]{:S(2)}, u32[]{:S(2)}) collective-permute-start(f32[256,256]{1,0:T(8,128)S(1)} %broadcast_select_fusion.2), channel_id=1, source_target_pairs={{0,8},{4,12},{2,10},{6,14}} | collective-permute-start | bytes 786440 | tf_op jit(solution)/shard_map/ppermute | solution.py:251
  61.1 5.2 %collective-permute-start.9 = (f32[256,256]{1,0:T(8,128)S(1)}, f32[256,256]{1,0:T(8,128)S(1)}, u32[]{:S(2)}, u32[]{:S(2)}) collective-permute-start(f32[256,256]{1,0:T(8,128)S(1)} %broadcast_select_fusion.3), channel_id=1, source_target_pairs={{0,16},{4,20},{2,18},{6,22},{8,24},{12,28},{10,26},{14,30}} | collective-permute-start | bytes 786440 | tf_op jit(solution)/shard_map/ppermute | solution.py:251
  67.8 2.6 %collective-permute-start.10 = (f32[384,256]{1,0:T(8,128)S(1)}, f32[384,256]{1,0:T(8,128)S(1)}, u32[]{:S(2)}, u32[]{:S(2)}) collective-permute-start(f32[384,256]{1,0:T(8,128)S(1)} %slice.62), channel_id=1, source_target_pairs={{0,1},{2,3},{4,5},{6,7},{8,9},{10,11},{12,13},{14,15},{16,17},{18,... | collective-permute-start | bytes 1179656 | tf_op jit(solution)/shard_map/ppermute | solution.py:242
  71.3 7.9 %copy-start.3 = (f32[2,32,32]{2,1,0:T(8,128)S(1)}, f32[2,32,32]{2,1,0:T(8,128)}, u32[]{:S(2)}) copy-start(f32[2,32,32]{2,1,0:T(8,128)} %param.6) | copy-start | bytes 24580
  71.3 25.5 %all-to-all-start = ((f32[4,32,3072]{2,1,0:T(8,128)}), f32[4,32,3072]{2,1,0:T(8,128)S(1)}, u32[]{:S(2)}, u32[]{:S(2)}) async-start(f32[4,32,3072]{2,1,0:T(8,128)} %pad_maximum_fusion), calls=%async_computation | async-start | bytes 3145728 | tf_op jit(solution)/shard_map/all_to_all | solution.py:292
  77.0 20.7 %collective-permute-start.11 = (f32[384,256]{1,0:T(8,128)S(1)}, f32[384,256]{1,0:T(8,128)S(1)}, u32[]{:S(2)}, u32[]{:S(2)}) collective-permute-start(f32[384,256]{1,0:T(8,128)S(1)} %pad_maximum_fusion.6), channel_id=1, source_target_pairs={{0,1},{4,5},{2,3},{6,7},{8,9},{12,13},{10,11},{14,15},{16,17},{20,... | collective-permute-start | bytes 1179656 | tf_op jit(solution)/shard_map/ppermute | solution.py:251
  111.8 2.6 %collective-permute-start.12 = (f32[128,1536]{1,0:T(8,128)}, f32[128,1536]{1,0:T(8,128)S(1)}, u32[]{:S(2)}, u32[]{:S(2)}) collective-permute-start(f32[128,1536]{1,0:T(8,128)} %slice.64), channel_id=1, source_target_pairs={{0,1},{1,0},{2,3},{3,2},{4,5},{5,4},{6,7},{7,6},{8,9},{9,8},{10,11... | collective-permute-start | bytes 2359304 | tf_op jit(solution)/shard_map/ppermute | solution.py:304
  114.3 1.4 copy-start.1
  124.9 2.0 %copy-start = (bf16[1152,1536]{1,0:T(8,128)(2,1)S(1)}, bf16[1152,1536]{1,0:T(8,128)(2,1)}, u32[]{:S(2)}) copy-start(bf16[1152,1536]{1,0:T(8,128)(2,1)} %get-tuple-element.24.right_ref) | copy-start | bytes 10616836
Sparse Core Ops, SparseCore 0:
  20.4 58.5 all-reduce.1
Sparse Core Ops, SparseCore 1:
  71.4 38.3 all-gather.1

commit v14 on v13

--- a/solution.py
+++ b/solution.py
@@ -84,7 +84,7 @@
         out_shape=jax.ShapeDtypeStruct((B, B), jnp.float32),
         scratch_shapes=[pltpu.VMEM((B, 2 * B), jnp.float32)],
         compiler_params=pltpu.CompilerParams(vmem_limit_bytes=8 * 2**20),
-        cost_estimate=pl.CostEstimate(flops=0, bytes_accessed=0, transcendentals=0),
+        cost_estimate=pl.CostEstimate(flops=16 * 10**9, bytes_accessed=0, transcendentals=0),
         name="corner_factor",
     )(block, design, filter_matrix, regular)
 
@@ -158,10 +158,10 @@
         out_specs=[vmem] * 3,
         out_shape=[
             pltpu.HBM((2 * cols, 3 * obs), jnp.bfloat16),
-            pltpu.HBM((3 * (obs + B), cols), jnp.bfloat16),
+            jax.ShapeDtypeStruct((3 * (obs + B), cols), jnp.bfloat16),
             pltpu.HBM((2 * cols, B), jnp.float32),
         ],
-        compiler_params=pltpu.CompilerParams(vmem_limit_bytes=36 * 2**20),
+        compiler_params=pltpu.CompilerParams(vmem_limit_bytes=26 * 2**20),
         cost_estimate=pl.CostEstimate(flops=0, bytes_accessed=0, transcendentals=0),
         name="both_sides",
     )(place, joined, lead, other, strip, inverse, filter_matrix, regular, lead_reg)
@@ -211,7 +211,7 @@
             out_specs=blocks(cols),
         ),
         out_shape=jax.ShapeDtypeStruct((rows, cols), jnp.float32),
-        compiler_params=pltpu.CompilerParams(vmem_limit_bytes=32 * 2**20),
+        compiler_params=pltpu.CompilerParams(vmem_limit_bytes=26 * 2**20),
         cost_estimate=pl.CostEstimate(flops=0, bytes_accessed=0, transcendentals=0),
         name="tile_rows",
     )(place, normals, strip, gram_cols, left, right, inverse, regular)
@@ -309,8 +309,9 @@
     left, right, gram_cols = both_sides(
         place, joined, lead, other, col_strip, inverse, filters, own_reg, lead_reg
     )
-    large = [pltpu.with_memory_space_constraint(array, pltpu.HBM) for array in (normals, strip, gram_cols, left)]
-    return tile_rows(place, *large, right, inverse, own_reg)
+    large = [pltpu.with_memory_space_constraint(array, pltpu.HBM) for array in (strip, gram_cols, left)]
+    fetched = pltpu.with_memory_space_constraint(normals, pltpu.VMEM)
+    return tile_rows(place, fetched, *large, right, inverse, own_reg)
 
 
 def solution(mesh):

time: 157 us -> 161 us (1.025)
  local copies, waits for them, and re-layouts: 8.95 us -> 17.1 us
  Pallas kernels: 45 us -> 41 us
    unnamed x8 -> x12, local copies, waits for them, and re-layouts: 3.42 us -> 11.6 us
    pallas_call x1, Pallas kernels: 21.9 us -> 19.1 us  [tile_rows(): pl.pallas_call(tile_kernel, grid_spec=pltpu.PrefetchScalarGridSpec(num_sc...]
  transfers between devices with their start and end apart: 16 -> 16, of which waited for: 7 -> 7; matrix products, arithmetic and copies ran while one was open for 9% -> 9% of each run, Pallas kernels for 15% -> 14%
where the time goes in v14:
time: 161 us; the launch traced here: 160 us
  Pallas kernels  41 us (25%)
  starting transfers between devices  37.7 us (23%)
  waiting for transfers between devices  33.5 us (21%)
  local copies, waits for them, and re-layouts  17.1 us (11%)
  between operations  15.2 us (9%)
  other arithmetic  8.74 us (5%)
  blocking collectives  7.17 us (4%)
    pallas_call x1, Pallas kernels, tile_rows(): pl.pallas_call(tile_kernel, grid_spec=pltpu.PrefetchScalarGridSpec(num_sc...  19.1 us
    ppermute x5, starting transfers between devices, doubled(): got = lax.ppermute(value, ('row', 'col'), pairs)  17.2 us
    all_to_all x1, waiting for transfers between devices, body(): joined = lax.all_to_all(sent, 'row', 0, 0, tiled=True)  16.1 us
    pallas_call x1, Pallas kernels, corner_factor(): pl.pallas_call(corner_kernel, out_shape=jax.ShapeDtypeStruct((B, B), jnp....  13.9 us
    unnamed x12, local copies, waits for them, and re-layouts  11.6 us
    ppermute x5, waiting for transfers between devices, doubled(): got = lax.ppermute(value, ('row', 'col'), pairs)  10.5 us
    pallas_call x1, Pallas kernels, both_sides(): pl.pallas_call(sides_kernel, in_specs=[pl.BlockSpec(memory_space=pltpu.SM...  7.99 us
    ppermute x3, starting transfers between devices, body(): lax.ppermute(design, 'col', [(c, (c + 2 * s) % col_peers) for c in range(...  7.86 us
  transfers between devices with their start and end apart: 16, of which 7 were waited for; matrix products, arithmetic and copies ran while one was open for 9% of the time, Pallas kernels for 14%

profile of v14, /device:TPU:0, one launch (start us, length us, event | category | flops | bytes accessed | tf_op | source)
XLA Modules:
  0.0 160.4 jit_solution(5239181598904410879)
XLA Ops:
  7.4 4.0 %collective-permute-start.1 = (f32[32,1536]{1,0:T(8,128)}, f32[32,1536]{1,0:T(8,128)S(1)}, u32[]{:S(2)}, u32[]{:S(2)}) collective-permute-start(f32[32,1536]{1,0:T(8,128)} %param.5), channel_id=1, source_target_pairs={{0,4},{1,5},{2,6},{3,7},{4,0},{5,1},{6,2},{7,3},{8,12},{9,13},{10,... | collective-permute-start | bytes 589832 | tf_op jit(solution)/shard_map/ppermute | solution.py:279
  11.4 1.6 collective-permute-start
  13.0 2.2 %collective-permute-start.2 = (f32[32,1536]{1,0:T(8,128)}, f32[32,1536]{1,0:T(8,128)}, u32[]{:S(2)}, u32[]{:S(2)}) collective-permute-start(f32[32,1536]{1,0:T(8,128)} %param.5), channel_id=1, source_target_pairs={{0,6},{1,7},{2,0},{3,1},{4,2},{5,3},{6,4},{7,5},{8,14},{9,15},{10,... | collective-permute-start | bytes 589832 | tf_op jit(solution)/shard_map/ppermute | solution.py:279
  17.5 2.7 %slice_select_fusion = f32[256,1536]{1,0:T(8,128)} fusion(f32[3072,1536]{1,0:T(8,128)} %normals_ref.1, pred[]{:T(512)S(6)} %eq.35), kind=kLoop, calls=%fused_computation.1 | loop fusion | flops 393216 | bytes 3145729 | tf_op jit(solution)/shard_map/jit(_where)/select_n | solution.py:268
  20.3 1.8 %fusion.6 = (f32[768,256]{1,0:T(8,128)S(1)}, f32[768,256]{1,0:T(8,128)S(1)}, f32[768,256]{1,0:T(8,128)S(1)}) fusion(f32[3072,1536]{1,0:T(8,128)} %normals_ref.1), kind=kLoop, calls=%fused_computation.31 | loop fusion | bytes 4718592 | tf_op jit(solution)/shard_map/slice | solution.py:238
  22.3 3.6 %collective-permute-done.1 = f32[32,1536]{1,0:T(8,128)S(1)} collective-permute-done((f32[32,1536]{1,0:T(8,128)}, f32[32,1536]{1,0:T(8,128)S(1)}, u32[]{:S(2)}, u32[]{:S(2)}) %collective-permute-start.1) | collective-permute-done | bytes 196640 | tf_op jit(solution)/shard_map/ppermute | solution.py:279
  28.6 8.1 %collective-permute-start.7 = (f32[256,256]{1,0:T(8,128)S(1)}, f32[256,256]{1,0:T(8,128)S(1)}, u32[]{:S(2)}, u32[]{:S(2)}) collective-permute-start(f32[256,256]{1,0:T(8,128)S(1)} %broadcast_select_fusion.1), channel_id=1, source_target_pairs={{0,2},{4,6}} | collective-permute-start | bytes 786440 | tf_op jit(solution)/shard_map/ppermute | solution.py:251
  36.8 1.3 collective-permute-start.3
  38.2 2.5 %collective-permute-start.4 = (f32[768,256]{1,0:T(8,128)S(1)}, f32[768,256]{1,0:T(8,128)S(1)}, u32[]{:S(2)}, u32[]{:S(2)}) collective-permute-start(f32[768,256]{1,0:T(8,128)S(1)} %get-tuple-element.16), channel_id=1, source_target_pairs={{0,4},{8,12},{16,20},{24,28}} | collective-permute-start | bytes 2359304 | tf_op jit(solution)/shard_map/ppermute | solution.py:239
  42.0 7.2 %all_gather.6 = f32[128,256]{1,0:T(8,128)S(1)} all-gather(f32[32,256]{1,0:T(8,128)S(1)} %slice.60), channel_id=1, replica_groups=mesh['row'=4,'col'=8] {'row'}, dimensions={0}, use_global_device_ids=true | all-gather | bytes 163840 | tf_op jit(solution)/shard_map/all_gather | solution.py:284
  49.3 3.7 %collective-permute-start.8 = (f32[256,256]{1,0:T(8,128)S(1)}, f32[256,256]{1,0:T(8,128)S(1)}, u32[]{:S(2)}, u32[]{:S(2)}) collective-permute-start(f32[256,256]{1,0:T(8,128)S(1)} %broadcast_select_fusion.2), channel_id=1, source_target_pairs={{0,8},{4,12},{2,10},{6,14}} | collective-permute-start | bytes 786440 | tf_op jit(solution)/shard_map/ppermute | solution.py:251
  53.2 7.9 %collective-permute-done.8 = f32[256,256]{1,0:T(8,128)S(1)} collective-permute-done((f32[256,256]{1,0:T(8,128)S(1)}, f32[256,256]{1,0:T(8,128)S(1)}, u32[]{:S(2)}, u32[]{:S(2)}) %collective-permute-start.8) | collective-permute-done | bytes 262176 | tf_op jit(solution)/shard_map/ppermute | solution.py:251
  63.7 2.6 %collective-permute-done.9 = f32[256,256]{1,0:T(8,128)S(1)} collective-permute-done((f32[256,256]{1,0:T(8,128)S(1)}, f32[256,256]{1,0:T(8,128)S(1)}, u32[]{:S(2)}, u32[]{:S(2)}) %collective-permute-start.9) | collective-permute-done | bytes 262176 | tf_op jit(solution)/shard_map/ppermute | solution.py:251
  66.4 1.4 add_select_fusion
  71.3 5.7 %all-to-all-start = ((f32[4,32,3072]{2,1,0:T(8,128)}), f32[4,32,3072]{2,1,0:T(8,128)S(1)}, u32[]{:S(2)}, u32[]{:S(2)}) async-start(f32[4,32,3072]{2,1,0:T(8,128)} %pad_maximum_fusion), calls=%async_computation | async-start | bytes 3145728 | tf_op jit(solution)/shard_map/all_to_all | solution.py:292
  77.0 2.7 %collective-permute-start.11 = (f32[384,256]{1,0:T(8,128)S(1)}, f32[384,256]{1,0:T(8,128)}, u32[]{:S(2)}, u32[]{:S(2)}) collective-permute-start(f32[384,256]{1,0:T(8,128)S(1)} %pad_maximum_fusion.6), channel_id=1, source_target_pairs={{0,1},{4,5},{2,3},{6,7},{8,9},{12,13},{10,11},{14,15},{16,17},{20,... | collective-permute-start | bytes 1179656 | tf_op jit(solution)/shard_map/ppermute | solution.py:251
  80.8 16.1 %all-to-all-done = f32[4,32,3072]{2,1,0:T(8,128)S(1)} async-done(((f32[4,32,3072]{2,1,0:T(8,128)}), f32[4,32,3072]{2,1,0:T(8,128)S(1)}, u32[]{:S(2)}, u32[]{:S(2)}) %all-to-all-start) | async-done | bytes 1572896 | tf_op jit(solution)/shard_map/all_to_all | solution.py:292
  97.9 13.9 %corner_factor.1.inverse_ref = f32[256,256]{1,0:T(8,128)S(1)} custom-call(f32[256,256]{1,0:T(8,128)S(1)} %slice.65.block_ref, f32[128,256]{1,0:T(8,128)S(1)} %slice.63.design_ref.lead_ref, f32[128,128]{1,0:T(8,128)S(1)} %select_n.143.filter_ref, f32[1,256]{1,0:T(1,128)S(1)} %bitcast.32), custom_call_target="tpu_custom_call" | custom-call | flops 16000000000 | tf_op jit(solution)/shard_map/corner_factor/pallas_call | solution.py:82
  114.3 1.4 copy-done.3
  115.7 8.0 %both_sides.1 = (bf16[3072,384]{1,0:T(8,128)(2,1)}, bf16[1152,1536]{1,0:T(8,128)(2,1)S(1)}, f32[3072,256]{1,0:T(8,128)}) custom-call(s32[2]{0:T(128)S(1)} %pad_add_fusion.place_ref, f32[128,3072]{1,0:T(8,128)S(1)} %bitcast.31, f32[128,256]{1,0:T(8,128)S(1)} %slice.63.design_ref.lead_ref, f32[128,1536]{1,0:T(8,128)S(1)} %collective-permute-done.12.other_ref, ...), custom_call_target="tpu_custom_call" | custom-call | tf_op jit(solution)/shard_map/both_sides/pallas_call | solution.py:155
  123.7 1.8 %copy-done.1 = bf16[1152,1536]{1,0:T(8,128)(2,1)} copy-done((bf16[1152,1536]{1,0:T(8,128)(2,1)}, bf16[1152,1536]{1,0:T(8,128)(2,1)S(1)}, u32[]{:S(2)}) %copy-start.1) | copy-done | bytes 3538968
  125.5 6.4 %copy-done = f32[3072,1536]{1,0:T(8,128)S(1)} copy-done((f32[3072,1536]{1,0:T(8,128)S(1)}, f32[3072,1536]{1,0:T(8,128)}, u32[]{:S(2)}) %copy-start) | copy-done | bytes 18874392
  131.9 2.0 %copy-done.2 = bf16[1152,1536]{1,0:T(8,128)(2,1)S(1)} copy-done((bf16[1152,1536]{1,0:T(8,128)(2,1)S(1)}, bf16[1152,1536]{1,0:T(8,128)(2,1)}, u32[]{:S(2)}) %copy-start.2) | copy-done | bytes 3538968
  133.9 19.1 %tile_rows.1 = f32[3072,1536]{1,0:T(8,128)} custom-call(s32[2]{0:T(128)S(1)} %pad_add_fusion.place_ref, f32[3072,1536]{1,0:T(8,128)S(1)} %copy-done, f32[3072,256]{1,0:T(8,128)} %all-gather.2.cloned.1.call-done.strip_ref, f32[3072,256]{1,0:T(8,128)} %get-tuple-element.22.gram_ref, bf16[3072,384]{1,0:T(8,128)(2,1)} %get-tuple-element.23.left_ref, ...), custom_call_target="tpu_custom_call" | custom-call | tf_op jit(solution)/shard_map/tile_rows/pallas_call | solution.py:204
  (54 shorter events, 17.5 us)
Async XLA Ops:
  7.4 105.7 %all-reduce.2.cloned.1.call-start = ((), (), s32[]{:S(2)}) async-start(), calls=%async_computation.2 | async-start | bytes 3145728 | tf_op jit(solution)/shard_map/psum | solution.py:268
  7.4 18.4 %collective-permute-start.1 = (f32[32,1536]{1,0:T(8,128)}, f32[32,1536]{1,0:T(8,128)S(1)}, u32[]{:S(2)}, u32[]{:S(2)}) collective-permute-start(f32[32,1536]{1,0:T(8,128)} %param.5), channel_id=1, source_target_pairs={{0,4},{1,5},{2,6},{3,7},{4,0},{5,1},{6,2},{7,3},{8,12},{9,13},{10,... | collective-permute-start | bytes 589832 | tf_op jit(solution)/shard_map/ppermute | solution.py:279
  11.4 14.4 %collective-permute-start = (f32[32,1536]{1,0:T(8,128)}, f32[32,1536]{1,0:T(8,128)S(1)}, u32[]{:S(2)}, u32[]{:S(2)}) collective-permute-start(f32[32,1536]{1,0:T(8,128)} %param.5), channel_id=1, source_target_pairs={{0,2},{1,3},{2,4},{3,5},{4,6},{5,7},{6,0},{7,1},{8,10},{9,11},{10,... | collective-permute-start | bytes 589832 | tf_op jit(solution)/shard_map/ppermute | solution.py:279
  13.0 13.7 %collective-permute-start.2 = (f32[32,1536]{1,0:T(8,128)}, f32[32,1536]{1,0:T(8,128)}, u32[]{:S(2)}, u32[]{:S(2)}) collective-permute-start(f32[32,1536]{1,0:T(8,128)} %param.5), channel_id=1, source_target_pairs={{0,6},{1,7},{2,0},{3,1},{4,2},{5,3},{6,4},{7,5},{8,14},{9,15},{10,... | collective-permute-start | bytes 589832 | tf_op jit(solution)/shard_map/ppermute | solution.py:279
  16.2 11.4 %collective-permute-start.6 = (f32[256,256]{1,0:T(8,128)S(1)}, f32[256,256]{1,0:T(8,128)S(1)}, u32[]{:S(2)}, u32[]{:S(2)}) collective-permute-start(f32[256,256]{1,0:T(8,128)S(1)} %slice.50), channel_id=1, source_target_pairs={{0,4}} | collective-permute-start | bytes 786440 | tf_op jit(solution)/shard_map/ppermute | solution.py:251
  20.3 6.4 %copy-start.4 = (f32[32,1536]{1,0:T(8,128)S(1)}, f32[32,1536]{1,0:T(8,128)}, u32[]{:S(2)}) copy-start(f32[32,1536]{1,0:T(8,128)} %param.5) | copy-start | bytes 589828
  20.3 105.2 %all-gather.2.cloned.1.call-start = ((), (), s32[]{:S(2)}) async-start(), calls=%async_computation.1 | async-start | bytes 3538944 | tf_op jit(solution)/shard_map/all_gather | solution.py:296
  28.6 20.6 %collective-permute-start.7 = (f32[256,256]{1,0:T(8,128)S(1)}, f32[256,256]{1,0:T(8,128)S(1)}, u32[]{:S(2)}, u32[]{:S(2)}) collective-permute-start(f32[256,256]{1,0:T(8,128)S(1)} %broadcast_select_fusion.1), channel_id=1, source_target_pairs={{0,2},{4,6}} | collective-permute-start | bytes 786440 | tf_op jit(solution)/shard_map/ppermute | solution.py:251
  36.8 29.5 %collective-permute-start.3 = (f32[768,256]{1,0:T(8,128)S(1)}, f32[768,256]{1,0:T(8,128)S(1)}, u32[]{:S(2)}, u32[]{:S(2)}) collective-permute-start(f32[768,256]{1,0:T(8,128)S(1)} %get-tuple-element.15), channel_id=1, source_target_pairs={{0,2},{8,10},{16,18},{24,26}} | collective-permute-start | bytes 2359304 | tf_op jit(solution)/shard_map/ppermute | solution.py:239
  38.2 28.2 %collective-permute-start.4 = (f32[768,256]{1,0:T(8,128)S(1)}, f32[768,256]{1,0:T(8,128)S(1)}, u32[]{:S(2)}, u32[]{:S(2)}) collective-permute-start(f32[768,256]{1,0:T(8,128)S(1)} %get-tuple-element.16), channel_id=1, source_target_pairs={{0,4},{8,12},{16,20},{24,28}} | collective-permute-start | bytes 2359304 | tf_op jit(solution)/shard_map/ppermute | solution.py:239
  40.7 25.7 %collective-permute-start.5 = (f32[768,256]{1,0:T(8,128)S(1)}, f32[768,256]{1,0:T(8,128)S(1)}, u32[]{:S(2)}, u32[]{:S(2)}) collective-permute-start(f32[768,256]{1,0:T(8,128)S(1)} %get-tuple-element.17), channel_id=1, source_target_pairs={{0,6},{8,14},{16,22},{24,30}} | collective-permute-start | bytes 2359304 | tf_op jit(solution)/shard_map/ppermute | solution.py:239
  49.3 11.8 %collective-permute-start.8 = (f32[256,256]{1,0:T(8,128)S(1)}, f32[256,256]{1,0:T(8,128)S(1)}, u32[]{:S(2)}, u32[]{:S(2)}) collective-permute-start(f32[256,256]{1,0:T(8,128)S(1)} %broadcast_select_fusion.2), channel_id=1, source_target_pairs={{0,8},{4,12},{2,10},{6,14}} | collective-permute-start | bytes 786440 | tf_op jit(solution)/shard_map/ppermute | solution.py:251
  61.1 5.2 %collective-permute-start.9 = (f32[256,256]{1,0:T(8,128)S(1)}, f32[256,256]{1,0:T(8,128)S(1)}, u32[]{:S(2)}, u32[]{:S(2)}) collective-permute-start(f32[256,256]{1,0:T(8,128)S(1)} %broadcast_select_fusion.3), channel_id=1, source_target_pairs={{0,16},{4,20},{2,18},{6,22},{8,24},{12,28},{10,26},{14,30}} | collective-permute-start | bytes 786440 | tf_op jit(solution)/shard_map/ppermute | solution.py:251
  67.8 2.6 %collective-permute-start.10 = (f32[384,256]{1,0:T(8,128)S(1)}, f32[384,256]{1,0:T(8,128)S(1)}, u32[]{:S(2)}, u32[]{:S(2)}) collective-permute-start(f32[384,256]{1,0:T(8,128)S(1)} %slice.62), channel_id=1, source_target_pairs={{0,1},{2,3},{4,5},{6,7},{8,9},{10,11},{12,13},{14,15},{16,17},{18,... | collective-permute-start | bytes 1179656 | tf_op jit(solution)/shard_map/ppermute | solution.py:242
  71.3 8.5 %copy-start.5 = (f32[2,32,32]{2,1,0:T(8,128)S(1)}, f32[2,32,32]{2,1,0:T(8,128)}, u32[]{:S(2)}) copy-start(f32[2,32,32]{2,1,0:T(8,128)} %param.6) | copy-start | bytes 24580
  71.3 25.5 %all-to-all-start = ((f32[4,32,3072]{2,1,0:T(8,128)}), f32[4,32,3072]{2,1,0:T(8,128)S(1)}, u32[]{:S(2)}, u32[]{:S(2)}) async-start(f32[4,32,3072]{2,1,0:T(8,128)} %pad_maximum_fusion), calls=%async_computation | async-start | bytes 3145728 | tf_op jit(solution)/shard_map/all_to_all | solution.py:292
  77.0 20.7 %collective-permute-start.11 = (f32[384,256]{1,0:T(8,128)S(1)}, f32[384,256]{1,0:T(8,128)}, u32[]{:S(2)}, u32[]{:S(2)}) collective-permute-start(f32[384,256]{1,0:T(8,128)S(1)} %pad_maximum_fusion.6), channel_id=1, source_target_pairs={{0,1},{4,5},{2,3},{6,7},{8,9},{12,13},{10,11},{14,15},{16,17},{20,... | collective-permute-start | bytes 1179656 | tf_op jit(solution)/shard_map/ppermute | solution.py:251
  111.8 2.6 %collective-permute-start.12 = (f32[128,1536]{1,0:T(8,128)}, f32[128,1536]{1,0:T(8,128)S(1)}, u32[]{:S(2)}, u32[]{:S(2)}) collective-permute-start(f32[128,1536]{1,0:T(8,128)} %slice.64), channel_id=1, source_target_pairs={{0,1},{1,0},{2,3},{3,2},{4,5},{5,4},{6,7},{7,6},{8,9},{9,8},{10,11... | collective-permute-start | bytes 2359304 | tf_op jit(solution)/shard_map/ppermute | solution.py:304
  114.3 1.4 copy-start.3
  123.7 1.8 %copy-start.1 = (bf16[1152,1536]{1,0:T(8,128)(2,1)}, bf16[1152,1536]{1,0:T(8,128)(2,1)S(1)}, u32[]{:S(2)}) copy-start(bf16[1152,1536]{1,0:T(8,128)(2,1)S(1)} %get-tuple-element.24.right_ref) | copy-start | bytes 10616836
  125.5 6.4 %copy-start = (f32[3072,1536]{1,0:T(8,128)S(1)}, f32[3072,1536]{1,0:T(8,128)}, u32[]{:S(2)}) copy-start(f32[3072,1536]{1,0:T(8,128)} %normals_ref.1) | copy-start | bytes 56623108
  131.9 2.0 %copy-start.2 = (bf16[1152,1536]{1,0:T(8,128)(2,1)S(1)}, bf16[1152,1536]{1,0:T(8,128)(2,1)}, u32[]{:S(2)}) copy-start(bf16[1152,1536]{1,0:T(8,128)(2,1)} %copy-done.1) | copy-start | bytes 10616836
Sparse Core Ops, SparseCore 0:
  20.4 58.5 all-reduce.1
Sparse Core Ops, SparseCore 1:
  71.4 38.3 all-gather.1

commit v15 on v13

--- a/solution.py
+++ b/solution.py
@@ -158,10 +158,10 @@
         out_specs=[vmem] * 3,
         out_shape=[
             pltpu.HBM((2 * cols, 3 * obs), jnp.bfloat16),
-            pltpu.HBM((3 * (obs + B), cols), jnp.bfloat16),
+            jax.ShapeDtypeStruct((3 * (obs + B), cols), jnp.bfloat16),
             pltpu.HBM((2 * cols, B), jnp.float32),
         ],
-        compiler_params=pltpu.CompilerParams(vmem_limit_bytes=36 * 2**20),
+        compiler_params=pltpu.CompilerParams(vmem_limit_bytes=26 * 2**20),
         cost_estimate=pl.CostEstimate(flops=0, bytes_accessed=0, transcendentals=0),
         name="both_sides",
     )(place, joined, lead, other, strip, inverse, filter_matrix, regular, lead_reg)
@@ -180,9 +180,12 @@
     first_col = place_ref[1] * cols
     col_pos = lax.broadcasted_iota(jnp.int32, (1, cols), 1) + first_col
     keep = jnp.where(col_pos < B, 0.0, 1.0)
-    out_ref[...] = normals_ref[...] * keep + jnp.dot(
-        left, right_ref[...], preferred_element_type=jnp.float32
-    )
+    width = max(size for size in range(128, 513, 128) if cols % size == 0)
+    for at in range(0, cols, width):
+        here = slice(at, at + width)
+        out_ref[:, here] = normals_ref[:, here] * keep[:, here] + jnp.dot(
+            left, right_ref[:, here], preferred_element_type=jnp.float32
+        )
 
     @pl.when((first_row < first_col + cols) & (first_col < first_row + block))
     def _():
@@ -211,7 +214,7 @@
             out_specs=blocks(cols),
         ),
         out_shape=jax.ShapeDtypeStruct((rows, cols), jnp.float32),
-        compiler_params=pltpu.CompilerParams(vmem_limit_bytes=32 * 2**20),
+        compiler_params=pltpu.CompilerParams(vmem_limit_bytes=26 * 2**20),
         cost_estimate=pl.CostEstimate(flops=0, bytes_accessed=0, transcendentals=0),
         name="tile_rows",
     )(place, normals, strip, gram_cols, left, right, inverse, regular)
@@ -271,6 +274,7 @@
     z_bits = [bit for bit in reversed(index_bits) if 1 < bit < col_peers]
     row_bits = [bit for bit in index_bits if bit >= col_peers]
     leading, reached = doubled(normals[:B, :B], z_bits, [0])
+    along_z = leading
 
     chips = col_peers // 2
     chip = col_index // 2
@@ -279,20 +283,20 @@
         along.append(lax.ppermute(design, "col", [(c, (c + 2 * s) % col_peers) for c in range(col_peers)]))
     along = jnp.stack(along)
 
-    leading, reached = doubled(leading, row_bits, reached)
-    lead = lax.dynamic_index_in_dim(along, chip, 0, keepdims=False)[:, :B]
-    lead = lax.all_gather(lead, "row", axis=0, tiled=True)
-    leading = jnp.concatenate([lead, leading], axis=0)
-
     sent = []
     for to in range(row_peers):
         far = lax.dynamic_index_in_dim(along, (chip - to) % chips, 0, keepdims=False)
         sent.append(jnp.concatenate([design, far], axis=1))
     sent = jnp.stack(sent)
+    leading, reached = doubled(leading, row_bits, reached)
+    lead = lax.dynamic_index_in_dim(along, chip, 0, keepdims=False)[:, :B]
+    lead = lax.all_gather(after(lead, sent), "row", axis=0, tiled=True)
+    leading = jnp.concatenate([lead, leading], axis=0)
+
     joined = lax.all_to_all(sent, "row", 0, 0, tiled=True)
     joined = joined.reshape(obs, 2 * cols_here)
 
-    piece = row_strip_piece(normals, along, (leading, sent))
+    piece = row_strip_piece(normals, along, (along_z, joined))
     strip = lax.all_gather(piece, "col", axis=0, tiled=True)
 
     leading, _ = doubled(leading, [1], reached)
@@ -301,9 +305,7 @@
     lead_reg = regular[:B].reshape(1, B)
     inverse = corner_factor(corner, lead, filters, lead_reg)
 
-    other = lax.ppermute(
-        after(joined[:, cols_here:], inverse), "col", [(c, c ^ 1) for c in range(col_peers)]
-    )
+    other = lax.ppermute(joined[:, cols_here:], "col", [(c, c ^ 1) for c in range(col_peers)])
     own_reg = lax.dynamic_slice_in_dim(regular, col_index * cols_here, cols_here).reshape(1, cols_here)
     place = jnp.stack([row_index, col_index]).astype(jnp.int32)
     left, right, gram_cols = both_sides(

time: 157 us -> 160 us (1.019)
  the two profiles are of different devices: /device:TPU:0 before, /device:TPU:11 now
where the time goes in v15:
time: 160 us; the launch traced here: 159 us
  Pallas kernels  43.8 us (27%)
  starting transfers between devices  33.1 us (21%)
  waiting for transfers between devices  25.4 us (16%)
  blocking collectives  18.4 us (11%)
  between operations  15.2 us (10%)
  local copies, waits for them, and re-layouts  13.3 us (8%)
  other arithmetic  9.51 us (6%)
    pallas_call x1, Pallas kernels, tile_rows(): pl.pallas_call(tile_kernel, grid_spec=pltpu.PrefetchScalarGridSpec(num_sc...  21.9 us
    all_gather x1, blocking collectives, body(): lead = lax.all_gather(after(lead, sent), 'row', axis=0, tiled=True)  18.4 us
    pallas_call x1, Pallas kernels, corner_factor(): pl.pallas_call(corner_kernel, out_shape=jax.ShapeDtypeStruct((B, B), jnp....  13.9 us
    ppermute x1, starting transfers between devices, body(): lax.ppermute(joined[:, cols_here:], 'col', [(c, c ^ 1) for c in range(col...  12.8 us
    ppermute x3, waiting for transfers between devices, body(): lax.ppermute(design, 'col', [(c, (c + 2 * s) % col_peers) for c in range(...  11.2 us
    all_to_all x1, waiting for transfers between devices, body(): joined = lax.all_to_all(sent, 'row', 0, 0, tiled=True)  9.32 us
    pallas_call x1, Pallas kernels, both_sides(): pl.pallas_call(sides_kernel, in_specs=[pl.BlockSpec(memory_space=pltpu.SM...  7.95 us
    all_to_all x1, starting transfers between devices, body(): joined = lax.all_to_all(sent, 'row', 0, 0, tiled=True)  6.59 us
  transfers between devices with their start and end apart: 16, of which 5 were waited for; matrix products, arithmetic and copies ran while one was open for 11% of the time, Pallas kernels for 14%

profile of v15, /device:TPU:11, one launch (start us, length us, event | category | flops | bytes accessed | tf_op | source)
XLA Modules:
  0.0 158.7 jit_solution(2680842122781492630)
XLA Ops:
  7.4 2.3 %collective-permute-start.1 = (f32[32,1536]{1,0:T(8,128)}, f32[32,1536]{1,0:T(8,128)S(1)}, u32[]{:S(2)}, u32[]{:S(2)}) collective-permute-start(f32[32,1536]{1,0:T(8,128)} %param.5), channel_id=1, source_target_pairs={{0,4},{1,5},{2,6},{3,7},{4,0},{5,1},{6,2},{7,3},{8,12},{9,13},{10,... | collective-permute-start | bytes 589832 | tf_op jit(solution)/shard_map/ppermute | solution.py:283
  9.7 1.5 collective-permute-start.2
  12.9 3.0 %fusion.6 = (f32[768,256]{1,0:T(8,128)S(1)}, f32[768,256]{1,0:T(8,128)}, f32[768,256]{1,0:T(8,128)}) fusion(f32[3072,1536]{1,0:T(8,128)} %normals_ref.1), kind=kLoop, calls=%fused_computation.31 | loop fusion | bytes 4718592 | tf_op jit(solution)/shard_map/slice | solution.py:241
  15.9 3.3 %collective-permute-done.1 = f32[32,1536]{1,0:T(8,128)S(1)} collective-permute-done((f32[32,1536]{1,0:T(8,128)}, f32[32,1536]{1,0:T(8,128)S(1)}, u32[]{:S(2)}, u32[]{:S(2)}) %collective-permute-start.1) | collective-permute-done | bytes 196640 | tf_op jit(solution)/shard_map/ppermute | solution.py:283
  19.2 7.9 %collective-permute-done = f32[32,1536]{1,0:T(8,128)S(1)} collective-permute-done((f32[32,1536]{1,0:T(8,128)}, f32[32,1536]{1,0:T(8,128)S(1)}, u32[]{:S(2)}, u32[]{:S(2)}) %collective-permute-start) | collective-permute-done | bytes 196640 | tf_op jit(solution)/shard_map/ppermute | solution.py:283
  28.1 1.3 pad_maximum_fusion
  29.4 6.6 %all-to-all-start = ((f32[4,32,3072]{2,1,0:T(8,128)}), f32[4,32,3072]{2,1,0:T(8,128)S(1)}, u32[]{:S(2)}, u32[]{:S(2)}) async-start(f32[4,32,3072]{2,1,0:T(8,128)} %pad_maximum_fusion), calls=%async_computation | async-start | bytes 3145728 | tf_op jit(solution)/shard_map/all_to_all | solution.py:296
  36.0 1.5 collective-permute-start.3
  37.6 1.5 collective-permute-start.4
  39.1 1.6 collective-permute-start.5
  40.7 2.7 %slice_select_fusion = f32[256,1536]{1,0:T(8,128)} fusion(f32[3072,1536]{1,0:T(8,128)} %normals_ref.1, pred[]{:T(512)S(6)} %eq.33), kind=kLoop, calls=%fused_computation.1 | loop fusion | flops 393216 | bytes 3145729 | tf_op jit(solution)/shard_map/jit(_where)/select_n | solution.py:271
  45.2 9.3 %all-to-all-done = f32[4,32,3072]{2,1,0:T(8,128)S(1)} async-done(((f32[4,32,3072]{2,1,0:T(8,128)}), f32[4,32,3072]{2,1,0:T(8,128)S(1)}, u32[]{:S(2)}, u32[]{:S(2)}) %all-to-all-start) | async-done | bytes 1572896 | tf_op jit(solution)/shard_map/all_to_all | solution.py:296
  54.6 2.0 %add_select_fusion = f32[768,256]{1,0:T(8,128)S(1)} fusion(f32[768,256]{1,0:T(8,128)} %collective-permute-done.5, f32[768,256]{1,0:T(8,128)} %collective-permute-done.3, f32[768,256]{1,0:T(8,128)} %collective-permute-done.4, f32[3072,1536]{1,0:T(8,128)} %normals_ref.1, pred[]{:T(512)S(6)} %eq.32), kind=kLoop, calls=%fused_computation.3 | loop fusion | flops 589824 | bytes 3932161 | tf_op jit(solution)/shard_map/jit(_where)/select_n | solution.py:244
  56.7 1.3 collective-permute-start.8
  58.0 4.2 %collective-permute-done.8 = f32[384,256]{1,0:T(8,128)S(1)} collective-permute-done((f32[384,256]{1,0:T(8,128)S(1)}, f32[384,256]{1,0:T(8,128)S(1)}, u32[]{:S(2)}, u32[]{:S(2)}) %collective-permute-start.8) | collective-permute-done | bytes 393248 | tf_op jit(solution)/shard_map/ppermute | solution.py:245
  65.2 18.4 %all_gather.7 = f32[128,256]{1,0:T(8,128)S(1)} all-gather(f32[32,256]{1,0:T(8,128)S(1)} %slice.62), channel_id=1, replica_groups=mesh['row'=4,'col'=8] {'row'}, dimensions={0}, use_global_device_ids=true | all-gather | bytes 163840 | tf_op jit(solution)/shard_map/all_gather | solution.py:293
  84.6 12.8 %collective-permute-start.12 = (f32[128,1536]{1,0:T(8,128)}, f32[128,1536]{1,0:T(8,128)S(1)}, u32[]{:S(2)}, u32[]{:S(2)}) collective-permute-start(f32[128,1536]{1,0:T(8,128)} %slice.64), channel_id=1, source_target_pairs={{0,1},{1,0},{2,3},{3,2},{4,5},{5,4},{6,7},{7,6},{8,9},{9,8},{10,11... | collective-permute-start | bytes 2359304 | tf_op jit(solution)/shard_map/ppermute | solution.py:308
  97.4 1.3 collective-permute-start.11
  102.3 13.9 %corner_factor.1.inverse_ref = f32[256,256]{1,0:T(8,128)S(1)} custom-call(f32[256,256]{1,0:T(8,128)S(1)} %slice.65.block_ref, f32[128,256]{1,0:T(8,128)S(1)} %slice.63.design_ref.lead_ref, f32[128,128]{1,0:T(8,128)S(1)} %select_n.145.filter_ref, f32[1,256]{1,0:T(1,128)S(1)} %bitcast.32), custom_call_target="tpu_custom_call" | custom-call | tf_op jit(solution)/shard_map/corner_factor/pallas_call | solution.py:82
  116.2 1.4 copy-done.2
  117.6 8.0 %both_sides.1 = (bf16[3072,384]{1,0:T(8,128)(2,1)}, bf16[1152,1536]{1,0:T(8,128)(2,1)S(1)}, f32[3072,256]{1,0:T(8,128)}) custom-call(s32[2]{0:T(128)S(1)} %pad_add_fusion.place_ref, f32[128,3072]{1,0:T(8,128)S(1)} %bitcast.31, f32[128,256]{1,0:T(8,128)S(1)} %slice.63.design_ref.lead_ref, f32[128,1536]{1,0:T(8,128)S(1)} %collective-permute-done.12.other_ref, ...), custom_call_target="tpu_custom_call" | custom-call | tf_op jit(solution)/shard_map/both_sides/pallas_call | solution.py:155
  125.6 1.8 %copy-done = bf16[1152,1536]{1,0:T(8,128)(2,1)} copy-done((bf16[1152,1536]{1,0:T(8,128)(2,1)}, bf16[1152,1536]{1,0:T(8,128)(2,1)S(1)}, u32[]{:S(2)}) %copy-start) | copy-done | bytes 3538968
  127.3 2.0 %copy-done.1 = bf16[1152,1536]{1,0:T(8,128)(2,1)S(1)} copy-done((bf16[1152,1536]{1,0:T(8,128)(2,1)S(1)}, bf16[1152,1536]{1,0:T(8,128)(2,1)}, u32[]{:S(2)}) %copy-start.1) | copy-done | bytes 3538968
  129.3 21.9 %tile_rows.1 = f32[3072,1536]{1,0:T(8,128)} custom-call(s32[2]{0:T(128)S(1)} %pad_add_fusion.place_ref, f32[3072,1536]{1,0:T(8,128)} %normals_ref.1, f32[3072,256]{1,0:T(8,128)} %all-gather.2.cloned.1.call-done.strip_ref, f32[3072,256]{1,0:T(8,128)} %get-tuple-element.22.gram_ref, bf16[3072,384]{1,0:T(8,128)(2,1)} %get-tuple-element.23.left_ref, ...), custom_call_target="tpu_custom_call" | custom-call | tf_op jit(solution)/shard_map/tile_rows/pallas_call | solution.py:207
  (52 shorter events, 12.0 us)
Async XLA Ops:
  7.4 11.9 %collective-permute-start.1 = (f32[32,1536]{1,0:T(8,128)}, f32[32,1536]{1,0:T(8,128)S(1)}, u32[]{:S(2)}, u32[]{:S(2)}) collective-permute-start(f32[32,1536]{1,0:T(8,128)} %param.5), channel_id=1, source_target_pairs={{0,4},{1,5},{2,6},{3,7},{4,0},{5,1},{6,2},{7,3},{8,12},{9,13},{10,... | collective-permute-start | bytes 589832 | tf_op jit(solution)/shard_map/ppermute | solution.py:283
  9.7 17.5 %collective-permute-start = (f32[32,1536]{1,0:T(8,128)}, f32[32,1536]{1,0:T(8,128)S(1)}, u32[]{:S(2)}, u32[]{:S(2)}) collective-permute-start(f32[32,1536]{1,0:T(8,128)} %param.5), channel_id=1, source_target_pairs={{0,2},{1,3},{2,4},{3,5},{4,6},{5,7},{6,0},{7,1},{8,10},{9,11},{10,... | collective-permute-start | bytes 589832 | tf_op jit(solution)/shard_map/ppermute | solution.py:283
  9.7 17.5 %collective-permute-start.2 = (f32[32,1536]{1,0:T(8,128)}, f32[32,1536]{1,0:T(8,128)S(1)}, u32[]{:S(2)}, u32[]{:S(2)}) collective-permute-start(f32[32,1536]{1,0:T(8,128)} %param.5), channel_id=1, source_target_pairs={{0,6},{1,7},{2,0},{3,1},{4,2},{5,3},{6,4},{7,5},{8,14},{9,15},{10,... | collective-permute-start | bytes 589832 | tf_op jit(solution)/shard_map/ppermute | solution.py:283
  12.1 31.4 %collective-permute-start.6 = (f32[256,256]{1,0:T(8,128)S(1)}, f32[256,256]{1,0:T(8,128)S(1)}, u32[]{:S(2)}, u32[]{:S(2)}) collective-permute-start(f32[256,256]{1,0:T(8,128)S(1)} %slice.49), channel_id=1, source_target_pairs={{0,4}} | collective-permute-start | bytes 786440 | tf_op jit(solution)/shard_map/ppermute | solution.py:254
  12.9 14.2 %copy-start.3 = (f32[32,1536]{1,0:T(8,128)S(1)}, f32[32,1536]{1,0:T(8,128)}, u32[]{:S(2)}) copy-start(f32[32,1536]{1,0:T(8,128)} %param.5) | copy-start | bytes 589828
  29.4 25.1 %all-to-all-start = ((f32[4,32,3072]{2,1,0:T(8,128)}), f32[4,32,3072]{2,1,0:T(8,128)S(1)}, u32[]{:S(2)}, u32[]{:S(2)}) async-start(f32[4,32,3072]{2,1,0:T(8,128)} %pad_maximum_fusion), calls=%async_computation | async-start | bytes 3145728 | tf_op jit(solution)/shard_map/all_to_all | solution.py:296
  36.0 80.2 %all-reduce.2.cloned.1.call-start = ((), (), s32[]{:S(2)}) async-start(), calls=%async_computation.2 | async-start | bytes 3145728 | tf_op jit(solution)/shard_map/psum | solution.py:271
  36.0 9.2 %collective-permute-start.3 = (f32[768,256]{1,0:T(8,128)}, f32[768,256]{1,0:T(8,128)}, u32[]{:S(2)}, u32[]{:S(2)}) collective-permute-start(f32[768,256]{1,0:T(8,128)} %get-tuple-element.15), channel_id=1, source_target_pairs={{0,2},{8,10},{16,18},{24,26}} | collective-permute-start | bytes 2359304 | tf_op jit(solution)/shard_map/ppermute | solution.py:242
  37.6 7.7 %collective-permute-start.4 = (f32[768,256]{1,0:T(8,128)}, f32[768,256]{1,0:T(8,128)}, u32[]{:S(2)}, u32[]{:S(2)}) collective-permute-start(f32[768,256]{1,0:T(8,128)} %get-tuple-element.16), channel_id=1, source_target_pairs={{0,4},{8,12},{16,20},{24,28}} | collective-permute-start | bytes 2359304 | tf_op jit(solution)/shard_map/ppermute | solution.py:242
  39.1 6.1 %collective-permute-start.5 = (f32[768,256]{1,0:T(8,128)S(1)}, f32[768,256]{1,0:T(8,128)}, u32[]{:S(2)}, u32[]{:S(2)}) collective-permute-start(f32[768,256]{1,0:T(8,128)S(1)} %get-tuple-element.17), channel_id=1, source_target_pairs={{0,6},{8,14},{16,22},{24,30}} | collective-permute-start | bytes 2359304 | tf_op jit(solution)/shard_map/ppermute | solution.py:242
  43.4 83.9 %all-gather.2.cloned.1.call-start = ((), (), s32[]{:S(2)}) async-start(), calls=%async_computation.1 | async-start | bytes 3538944 | tf_op jit(solution)/shard_map/all_gather | solution.py:300
  44.5 0.7 collective-permute-start.7
  56.6 7.8 %copy-start.4 = (f32[2,32,32]{2,1,0:T(8,128)S(1)}, f32[2,32,32]{2,1,0:T(8,128)}, u32[]{:S(2)}) copy-start(f32[2,32,32]{2,1,0:T(8,128)} %param.6) | copy-start | bytes 24580
  56.7 5.5 %collective-permute-start.8 = (f32[384,256]{1,0:T(8,128)S(1)}, f32[384,256]{1,0:T(8,128)S(1)}, u32[]{:S(2)}, u32[]{:S(2)}) collective-permute-start(f32[384,256]{1,0:T(8,128)S(1)} %slice.61), channel_id=1, source_target_pairs={{0,1},{2,3},{4,5},{6,7},{8,9},{10,11},{12,13},{14,15},{16,17},{18,... | collective-permute-start | bytes 1179656 | tf_op jit(solution)/shard_map/ppermute | solution.py:245
  63.0 0.7 collective-permute-start.9
  63.7 19.9 %collective-permute-start.10 = (f32[256,256]{1,0:T(8,128)S(1)}, f32[256,256]{1,0:T(8,128)S(1)}, u32[]{:S(2)}, u32[]{:S(2)}) collective-permute-start(f32[256,256]{1,0:T(8,128)S(1)} %broadcast_select_fusion.1), channel_id=1, source_target_pairs={{0,16},{4,20},{2,18},{6,22},{8,24},{12,28},{10,26},{14,30}} | collective-permute-start | bytes 786440 | tf_op jit(solution)/shard_map/ppermute | solution.py:254
  84.6 31.6 %collective-permute-start.12 = (f32[128,1536]{1,0:T(8,128)}, f32[128,1536]{1,0:T(8,128)S(1)}, u32[]{:S(2)}, u32[]{:S(2)}) collective-permute-start(f32[128,1536]{1,0:T(8,128)} %slice.64), channel_id=1, source_target_pairs={{0,1},{1,0},{2,3},{3,2},{4,5},{5,4},{6,7},{7,6},{8,9},{9,8},{10,11... | collective-permute-start | bytes 2359304 | tf_op jit(solution)/shard_map/ppermute | solution.py:308
  97.4 3.7 %collective-permute-start.11 = (f32[384,256]{1,0:T(8,128)S(1)}, f32[384,256]{1,0:T(8,128)}, u32[]{:S(2)}, u32[]{:S(2)}) collective-permute-start(f32[384,256]{1,0:T(8,128)S(1)} %pad_maximum_fusion.6), channel_id=1, source_target_pairs={{0,1},{4,5},{2,3},{6,7},{8,9},{12,13},{10,11},{14,15},{16,17},{20,... | collective-permute-start | bytes 1179656 | tf_op jit(solution)/shard_map/ppermute | solution.py:254
  116.2 1.4 copy-start.2
  125.6 1.8 %copy-start = (bf16[1152,1536]{1,0:T(8,128)(2,1)}, bf16[1152,1536]{1,0:T(8,128)(2,1)S(1)}, u32[]{:S(2)}) copy-start(bf16[1152,1536]{1,0:T(8,128)(2,1)S(1)} %get-tuple-element.24.right_ref) | copy-start | bytes 10616836
  127.3 2.0 %copy-start.1 = (bf16[1152,1536]{1,0:T(8,128)(2,1)S(1)}, bf16[1152,1536]{1,0:T(8,128)(2,1)}, u32[]{:S(2)}) copy-start(bf16[1152,1536]{1,0:T(8,128)(2,1)} %copy-done) | copy-start | bytes 10616836
Sparse Core Ops, SparseCore 0:
  43.5 67.1 all-reduce.1
Sparse Core Ops, SparseCore 1:
  63.1 48.3 all-gather.1

commit v16 on v15

--- a/solution.py
+++ b/solution.py
@@ -158,7 +158,7 @@
         out_specs=[vmem] * 3,
         out_shape=[
             pltpu.HBM((2 * cols, 3 * obs), jnp.bfloat16),
-            jax.ShapeDtypeStruct((3 * (obs + B), cols), jnp.bfloat16),
+            pltpu.HBM((3 * (obs + B), cols), jnp.bfloat16),
             pltpu.HBM((2 * cols, B), jnp.float32),
         ],
         compiler_params=pltpu.CompilerParams(vmem_limit_bytes=26 * 2**20),
@@ -296,7 +296,7 @@
     joined = lax.all_to_all(sent, "row", 0, 0, tiled=True)
     joined = joined.reshape(obs, 2 * cols_here)
 
-    piece = row_strip_piece(normals, along, (along_z, joined))
+    piece = row_strip_piece(normals, along, (along_z, joined, lead))
     strip = lax.all_gather(piece, "col", axis=0, tiled=True)
 
     leading, _ = doubled(leading, [1], reached)
@@ -311,8 +311,9 @@
     left, right, gram_cols = both_sides(
         place, joined, lead, other, col_strip, inverse, filters, own_reg, lead_reg
     )
-    large = [pltpu.with_memory_space_constraint(array, pltpu.HBM) for array in (normals, strip, gram_cols, left)]
-    return tile_rows(place, *large, right, inverse, own_reg)
+    large = [normals, strip, gram_cols, left, right]
+    large = [pltpu.with_memory_space_constraint(array, pltpu.HBM) for array in large]
+    return tile_rows(place, *large, inverse, own_reg)
 
 
 def solution(mesh):

time: 160 us -> 153 us (0.956)
  the two profiles are of different devices: /device:TPU:11 before, /device:TPU:0 now
where the time goes in v16:
time: 153 us; the launch traced here: 152 us
  Pallas kernels  46.1 us (30%)
  starting transfers between devices  36.5 us (24%)
  waiting for transfers between devices  28.7 us (19%)
  between operations  15.2 us (10%)
  blocking collectives  9.24 us (6%)
  other arithmetic  8.4 us (5%)
  local copies, waits for them, and re-layouts  8.27 us (5%)
    pallas_call x1, Pallas kernels, tile_rows(): pl.pallas_call(tile_kernel, grid_spec=pltpu.PrefetchScalarGridSpec(num_sc...  23.2 us
    ppermute x5, waiting for transfers between devices, doubled(): got = lax.ppermute(value, ('row', 'col'), pairs)  16.3 us
    ppermute x3, starting transfers between devices, row_strip_piece(): lax.ppermute(share, 'col', [(0, 2 * z)])  14.4 us
    pallas_call x1, Pallas kernels, corner_factor(): pl.pallas_call(corner_kernel, out_shape=jax.ShapeDtypeStruct((B, B), jnp....  13.9 us
    all_gather x1, blocking collectives, body(): lead = lax.all_gather(after(lead, sent), 'row', axis=0, tiled=True)  9.24 us
    pallas_call x1, Pallas kernels, both_sides(): pl.pallas_call(sides_kernel, in_specs=[pl.BlockSpec(memory_space=pltpu.SM...  9.02 us
    ppermute x5, starting transfers between devices, doubled(): got = lax.ppermute(value, ('row', 'col'), pairs)  8.38 us
    ppermute x3, starting transfers between devices, body(): lax.ppermute(design, 'col', [(c, (c + 2 * s) % col_peers) for c in range(...  7.86 us
  transfers between devices with their start and end apart: 16, of which 7 were waited for; matrix products, arithmetic and copies ran while one was open for 10% of the time, Pallas kernels for 15%

profile of v16, /device:TPU:0, one launch (start us, length us, event | category | flops | bytes accessed | tf_op | source)
XLA Modules:
  0.0 152.5 jit_solution(10140058889156999249)
XLA Ops:
  7.4 4.0 %collective-permute-start.1 = (f32[32,1536]{1,0:T(8,128)}, f32[32,1536]{1,0:T(8,128)S(1)}, u32[]{:S(2)}, u32[]{:S(2)}) collective-permute-start(f32[32,1536]{1,0:T(8,128)} %param.5), channel_id=1, source_target_pairs={{0,4},{1,5},{2,6},{3,7},{4,0},{5,1},{6,2},{7,3},{8,12},{9,13},{10,... | collective-permute-start | bytes 589832 | tf_op jit(solution)/shard_map/ppermute | solution.py:283
  11.4 1.6 %collective-permute-start = (f32[32,1536]{1,0:T(8,128)}, f32[32,1536]{1,0:T(8,128)S(1)}, u32[]{:S(2)}, u32[]{:S(2)}) collective-permute-start(f32[32,1536]{1,0:T(8,128)} %param.5), channel_id=1, source_target_pairs={{0,2},{1,3},{2,4},{3,5},{4,6},{5,7},{6,0},{7,1},{8,10},{9,11},{10,... | collective-permute-start | bytes 589832 | tf_op jit(solution)/shard_map/ppermute | solution.py:283
  13.0 2.2 %collective-permute-start.2 = (f32[32,1536]{1,0:T(8,128)}, f32[32,1536]{1,0:T(8,128)S(1)}, u32[]{:S(2)}, u32[]{:S(2)}) collective-permute-start(f32[32,1536]{1,0:T(8,128)} %param.5), channel_id=1, source_target_pairs={{0,6},{1,7},{2,0},{3,1},{4,2},{5,3},{6,4},{7,5},{8,14},{9,15},{10,... | collective-permute-start | bytes 589832 | tf_op jit(solution)/shard_map/ppermute | solution.py:283
  16.2 1.3 collective-permute-start.6
  17.6 3.2 %fusion.6 = (f32[768,256]{1,0:T(8,128)}, f32[768,256]{1,0:T(8,128)}, f32[768,256]{1,0:T(8,128)}) fusion(f32[3072,1536]{1,0:T(8,128)} %normals_ref.1), kind=kLoop, calls=%fused_computation.31 | loop fusion | bytes 4718592 | tf_op jit(solution)/shard_map/slice | solution.py:241
  20.8 5.0 %collective-permute-done.1 = f32[32,1536]{1,0:T(8,128)S(1)} collective-permute-done((f32[32,1536]{1,0:T(8,128)}, f32[32,1536]{1,0:T(8,128)S(1)}, u32[]{:S(2)}, u32[]{:S(2)}) %collective-permute-start.1) | collective-permute-done | bytes 196640 | tf_op jit(solution)/shard_map/ppermute | solution.py:283
  28.1 3.8 %all-to-all-start = ((f32[4,32,3072]{2,1,0:T(8,128)}), f32[4,32,3072]{2,1,0:T(8,128)S(1)}, u32[]{:S(2)}, u32[]{:S(2)}) async-start(f32[4,32,3072]{2,1,0:T(8,128)} %pad_maximum_fusion), calls=%async_computation | async-start | bytes 3145728 | tf_op jit(solution)/shard_map/all_to_all | solution.py:296
  31.9 8.9 %collective-permute-start.3 = (f32[768,256]{1,0:T(8,128)}, f32[768,256]{1,0:T(8,128)}, u32[]{:S(2)}, u32[]{:S(2)}) collective-permute-start(f32[768,256]{1,0:T(8,128)} %get-tuple-element.15), channel_id=1, source_target_pairs={{0,2},{8,10},{16,18},{24,26}} | collective-permute-start | bytes 2359304 | tf_op jit(solution)/shard_map/ppermute | solution.py:242
  40.8 3.4 %collective-permute-start.4 = (f32[768,256]{1,0:T(8,128)}, f32[768,256]{1,0:T(8,128)}, u32[]{:S(2)}, u32[]{:S(2)}) collective-permute-start(f32[768,256]{1,0:T(8,128)} %get-tuple-element.16), channel_id=1, source_target_pairs={{0,4},{8,12},{16,20},{24,28}} | collective-permute-start | bytes 2359304 | tf_op jit(solution)/shard_map/ppermute | solution.py:242
  44.2 2.2 %collective-permute-start.5 = (f32[768,256]{1,0:T(8,128)}, f32[768,256]{1,0:T(8,128)}, u32[]{:S(2)}, u32[]{:S(2)}) collective-permute-start(f32[768,256]{1,0:T(8,128)} %get-tuple-element.17), channel_id=1, source_target_pairs={{0,6},{8,14},{16,22},{24,30}} | collective-permute-start | bytes 2359304 | tf_op jit(solution)/shard_map/ppermute | solution.py:242
  46.4 2.7 %slice_select_fusion = f32[256,1536]{1,0:T(8,128)} fusion(f32[3072,1536]{1,0:T(8,128)} %normals_ref.1, pred[]{:T(512)S(6)} %eq.33), kind=kLoop, calls=%fused_computation.1 | loop fusion | flops 393216 | bytes 3145729 | tf_op jit(solution)/shard_map/jit(_where)/select_n | solution.py:271
  50.1 1.3 collective-permute-start.7
  51.4 9.2 %all_gather.6 = f32[128,256]{1,0:T(8,128)S(1)} all-gather(f32[32,256]{1,0:T(8,128)S(1)} %slice.60), channel_id=1, replica_groups=mesh['row'=4,'col'=8] {'row'}, dimensions={0}, use_global_device_ids=true | all-gather | bytes 163840 | tf_op jit(solution)/shard_map/all_gather | solution.py:293
  60.7 8.6 %collective-permute-done.7 = f32[256,256]{1,0:T(8,128)S(1)} collective-permute-done((f32[256,256]{1,0:T(8,128)S(1)}, f32[256,256]{1,0:T(8,128)S(1)}, u32[]{:S(2)}, u32[]{:S(2)}) %collective-permute-start.7) | collective-permute-done | bytes 262176 | tf_op jit(solution)/shard_map/ppermute | solution.py:254
  69.4 2.0 %add_select_fusion = f32[768,256]{1,0:T(8,128)S(1)} fusion(f32[768,256]{1,0:T(8,128)} %collective-permute-done.5, f32[768,256]{1,0:T(8,128)} %collective-permute-done.3, f32[768,256]{1,0:T(8,128)} %collective-permute-done.4, f32[3072,1536]{1,0:T(8,128)} %normals_ref.1, pred[]{:T(512)S(6)} %eq.32), kind=kLoop, calls=%fused_computation.3 | loop fusion | flops 589824 | bytes 3932161 | tf_op jit(solution)/shard_map/jit(_where)/select_n | solution.py:244
  71.5 2.0 %collective-permute-start.8 = (f32[384,256]{1,0:T(8,128)S(1)}, f32[384,256]{1,0:T(8,128)}, u32[]{:S(2)}, u32[]{:S(2)}) collective-permute-start(f32[384,256]{1,0:T(8,128)S(1)} %slice.62), channel_id=1, source_target_pairs={{0,1},{2,3},{4,5},{6,7},{8,9},{10,11},{12,13},{14,15},{16,17},{18,... | collective-permute-start | bytes 1179656 | tf_op jit(solution)/shard_map/ppermute | solution.py:245
  76.4 3.9 %collective-permute-done.9 = f32[256,256]{1,0:T(8,128)S(1)} collective-permute-done((f32[256,256]{1,0:T(8,128)S(1)}, f32[256,256]{1,0:T(8,128)S(1)}, u32[]{:S(2)}, u32[]{:S(2)}) %collective-permute-start.9) | collective-permute-done | bytes 262176 | tf_op jit(solution)/shard_map/ppermute | solution.py:254
  81.6 3.8 %collective-permute-done.10 = f32[256,256]{1,0:T(8,128)S(1)} collective-permute-done((f32[256,256]{1,0:T(8,128)S(1)}, f32[256,256]{1,0:T(8,128)S(1)}, u32[]{:S(2)}, u32[]{:S(2)}) %collective-permute-start.10) | collective-permute-done | bytes 262176 | tf_op jit(solution)/shard_map/ppermute | solution.py:254
  86.5 3.2 %collective-permute-start.11 = (f32[384,256]{1,0:T(8,128)S(1)}, f32[384,256]{1,0:T(8,128)}, u32[]{:S(2)}, u32[]{:S(2)}) collective-permute-start(f32[384,256]{1,0:T(8,128)S(1)} %pad_maximum_fusion.6), channel_id=1, source_target_pairs={{0,1},{4,5},{2,3},{6,7},{8,9},{12,13},{10,11},{14,15},{16,17},{20,... | collective-permute-start | bytes 1179656 | tf_op jit(solution)/shard_map/ppermute | solution.py:254
  91.6 13.9 %corner_factor.1.inverse_ref = f32[256,256]{1,0:T(8,128)S(1)} custom-call(f32[256,256]{1,0:T(8,128)S(1)} %slice.65.block_ref, f32[128,256]{1,0:T(8,128)S(1)} %slice.63.design_ref.lead_ref, f32[128,128]{1,0:T(8,128)S(1)} %select_n.145.filter_ref, f32[1,256]{1,0:T(1,128)S(1)} %bitcast.32), custom_call_target="tpu_custom_call" | custom-call | tf_op jit(solution)/shard_map/corner_factor/pallas_call | solution.py:82
  105.5 5.9 %all-reduce.2.cloned.1.call-done.strip_ref = f32[256,1536]{1,0:T(8,128)} async-done(((f32[256,1536]{1,0:T(8,128)}), f32[256,1536]{1,0:T(8,128)}) %all-reduce.2.cloned.1.call-update) | async-done | bytes 1572880 | tf_op jit(solution)/shard_map/psum | solution.py:271
  111.4 1.4 copy-done
  112.8 9.0 %both_sides.1 = (bf16[3072,384]{1,0:T(8,128)(2,1)}, bf16[1152,1536]{1,0:T(8,128)(2,1)}, f32[3072,256]{1,0:T(8,128)}) custom-call(s32[2]{0:T(128)S(1)} %pad_add_fusion.place_ref, f32[128,3072]{1,0:T(8,128)S(1)} %bitcast.31, f32[128,256]{1,0:T(8,128)S(1)} %slice.63.design_ref.lead_ref, f32[128,1536]{1,0:T(8,128)S(1)} %collective-permute-done.12.other_ref, ...), custom_call_target="tpu_custom_call" | custom-call | tf_op jit(solution)/shard_map/both_sides/pallas_call | solution.py:155
  121.8 23.2 %tile_rows.1 = f32[3072,1536]{1,0:T(8,128)} custom-call(s32[2]{0:T(128)S(1)} %pad_add_fusion.place_ref, f32[3072,1536]{1,0:T(8,128)} %normals_ref.1, f32[3072,256]{1,0:T(8,128)} %all-gather.2.cloned.1.call-done.strip_ref, f32[3072,256]{1,0:T(8,128)} %get-tuple-element.22.gram_ref, bf16[3072,384]{1,0:T(8,128)(2,1)} %get-tuple-element.23.left_ref, ...), custom_call_target="tpu_custom_call" | custom-call | tf_op jit(solution)/shard_map/tile_rows/pallas_call | solution.py:207
  (48 shorter events, 11.5 us)
Async XLA Ops:
  7.4 18.4 %collective-permute-start.1 = (f32[32,1536]{1,0:T(8,128)}, f32[32,1536]{1,0:T(8,128)S(1)}, u32[]{:S(2)}, u32[]{:S(2)}) collective-permute-start(f32[32,1536]{1,0:T(8,128)} %param.5), channel_id=1, source_target_pairs={{0,4},{1,5},{2,6},{3,7},{4,0},{5,1},{6,2},{7,3},{8,12},{9,13},{10,... | collective-permute-start | bytes 589832 | tf_op jit(solution)/shard_map/ppermute | solution.py:283
  11.4 14.4 %collective-permute-start = (f32[32,1536]{1,0:T(8,128)}, f32[32,1536]{1,0:T(8,128)S(1)}, u32[]{:S(2)}, u32[]{:S(2)}) collective-permute-start(f32[32,1536]{1,0:T(8,128)} %param.5), channel_id=1, source_target_pairs={{0,2},{1,3},{2,4},{3,5},{4,6},{5,7},{6,0},{7,1},{8,10},{9,11},{10,... | collective-permute-start | bytes 589832 | tf_op jit(solution)/shard_map/ppermute | solution.py:283
  13.0 13.6 %collective-permute-start.2 = (f32[32,1536]{1,0:T(8,128)}, f32[32,1536]{1,0:T(8,128)S(1)}, u32[]{:S(2)}, u32[]{:S(2)}) collective-permute-start(f32[32,1536]{1,0:T(8,128)} %param.5), channel_id=1, source_target_pairs={{0,6},{1,7},{2,0},{3,1},{4,2},{5,3},{6,4},{7,5},{8,14},{9,15},{10,... | collective-permute-start | bytes 589832 | tf_op jit(solution)/shard_map/ppermute | solution.py:283
  16.2 32.9 %collective-permute-start.6 = (f32[256,256]{1,0:T(8,128)S(1)}, f32[256,256]{1,0:T(8,128)S(1)}, u32[]{:S(2)}, u32[]{:S(2)}) collective-permute-start(f32[256,256]{1,0:T(8,128)S(1)} %slice.49), channel_id=1, source_target_pairs={{0,4}} | collective-permute-start | bytes 786440 | tf_op jit(solution)/shard_map/ppermute | solution.py:254
  17.6 8.9 %copy-start.1 = (f32[32,1536]{1,0:T(8,128)S(1)}, f32[32,1536]{1,0:T(8,128)}, u32[]{:S(2)}) copy-start(f32[32,1536]{1,0:T(8,128)} %param.5) | copy-start | bytes 589828
  28.1 41.2 %all-to-all-start = ((f32[4,32,3072]{2,1,0:T(8,128)}), f32[4,32,3072]{2,1,0:T(8,128)S(1)}, u32[]{:S(2)}, u32[]{:S(2)}) async-start(f32[4,32,3072]{2,1,0:T(8,128)} %pad_maximum_fusion), calls=%async_computation | async-start | bytes 3145728 | tf_op jit(solution)/shard_map/all_to_all | solution.py:296
  31.9 79.5 %all-reduce.2.cloned.1.call-start = ((), (), s32[]{:S(2)}) async-start(), calls=%async_computation.2 | async-start | bytes 3145728 | tf_op jit(solution)/shard_map/psum | solution.py:271
  31.9 37.4 %collective-permute-start.3 = (f32[768,256]{1,0:T(8,128)}, f32[768,256]{1,0:T(8,128)}, u32[]{:S(2)}, u32[]{:S(2)}) collective-permute-start(f32[768,256]{1,0:T(8,128)} %get-tuple-element.15), channel_id=1, source_target_pairs={{0,2},{8,10},{16,18},{24,26}} | collective-permute-start | bytes 2359304 | tf_op jit(solution)/shard_map/ppermute | solution.py:242
  40.8 28.5 %collective-permute-start.4 = (f32[768,256]{1,0:T(8,128)}, f32[768,256]{1,0:T(8,128)}, u32[]{:S(2)}, u32[]{:S(2)}) collective-permute-start(f32[768,256]{1,0:T(8,128)} %get-tuple-element.16), channel_id=1, source_target_pairs={{0,4},{8,12},{16,20},{24,28}} | collective-permute-start | bytes 2359304 | tf_op jit(solution)/shard_map/ppermute | solution.py:242
  44.2 25.2 %collective-permute-start.5 = (f32[768,256]{1,0:T(8,128)}, f32[768,256]{1,0:T(8,128)}, u32[]{:S(2)}, u32[]{:S(2)}) collective-permute-start(f32[768,256]{1,0:T(8,128)} %get-tuple-element.17), channel_id=1, source_target_pairs={{0,6},{8,14},{16,22},{24,30}} | collective-permute-start | bytes 2359304 | tf_op jit(solution)/shard_map/ppermute | solution.py:242
  49.0 72.8 %all-gather.2.cloned.1.call-start = ((), (), s32[]{:S(2)}) async-start(), calls=%async_computation.1 | async-start | bytes 3538944 | tf_op jit(solution)/shard_map/all_gather | solution.py:300
  50.1 19.2 %collective-permute-start.7 = (f32[256,256]{1,0:T(8,128)S(1)}, f32[256,256]{1,0:T(8,128)S(1)}, u32[]{:S(2)}, u32[]{:S(2)}) collective-permute-start(f32[256,256]{1,0:T(8,128)S(1)} %broadcast_select_fusion.3), channel_id=1, source_target_pairs={{0,2},{4,6}} | collective-permute-start | bytes 786440 | tf_op jit(solution)/shard_map/ppermute | solution.py:254
  71.4 10.2 %copy-start.2 = (f32[2,32,32]{2,1,0:T(8,128)S(1)}, f32[2,32,32]{2,1,0:T(8,128)}, u32[]{:S(2)}) copy-start(f32[2,32,32]{2,1,0:T(8,128)} %param.6) | copy-start | bytes 24580
  71.5 2.8 %collective-permute-start.8 = (f32[384,256]{1,0:T(8,128)S(1)}, f32[384,256]{1,0:T(8,128)}, u32[]{:S(2)}, u32[]{:S(2)}) collective-permute-start(f32[384,256]{1,0:T(8,128)S(1)} %slice.62), channel_id=1, source_target_pairs={{0,1},{2,3},{4,5},{6,7},{8,9},{10,11},{12,13},{14,15},{16,17},{18,... | collective-permute-start | bytes 1179656 | tf_op jit(solution)/shard_map/ppermute | solution.py:245
  75.1 5.2 %collective-permute-start.9 = (f32[256,256]{1,0:T(8,128)S(1)}, f32[256,256]{1,0:T(8,128)S(1)}, u32[]{:S(2)}, u32[]{:S(2)}) collective-permute-start(f32[256,256]{1,0:T(8,128)S(1)} %broadcast_select_fusion.4), channel_id=1, source_target_pairs={{0,8},{4,12},{2,10},{6,14}} | collective-permute-start | bytes 786440 | tf_op jit(solution)/shard_map/ppermute | solution.py:254
  80.3 5.2 %collective-permute-start.10 = (f32[256,256]{1,0:T(8,128)S(1)}, f32[256,256]{1,0:T(8,128)S(1)}, u32[]{:S(2)}, u32[]{:S(2)}) collective-permute-start(f32[256,256]{1,0:T(8,128)S(1)} %broadcast_select_fusion.1), channel_id=1, source_target_pairs={{0,16},{4,20},{2,18},{6,22},{8,24},{12,28},{10,26},{14,30}} | collective-permute-start | bytes 786440 | tf_op jit(solution)/shard_map/ppermute | solution.py:254
  86.4 24.9 %collective-permute-start.12 = (f32[128,1536]{1,0:T(8,128)}, f32[128,1536]{1,0:T(8,128)S(1)}, u32[]{:S(2)}, u32[]{:S(2)}) collective-permute-start(f32[128,1536]{1,0:T(8,128)} %slice.64), channel_id=1, source_target_pairs={{0,1},{1,0},{2,3},{3,2},{4,5},{5,4},{6,7},{7,6},{8,9},{9,8},{10,11... | collective-permute-start | bytes 2359304 | tf_op jit(solution)/shard_map/ppermute | solution.py:308
  86.5 5.0 %collective-permute-start.11 = (f32[384,256]{1,0:T(8,128)S(1)}, f32[384,256]{1,0:T(8,128)}, u32[]{:S(2)}, u32[]{:S(2)}) collective-permute-start(f32[384,256]{1,0:T(8,128)S(1)} %pad_maximum_fusion.6), channel_id=1, source_target_pairs={{0,1},{4,5},{2,3},{6,7},{8,9},{12,13},{10,11},{14,15},{16,17},{20,... | collective-permute-start | bytes 1179656 | tf_op jit(solution)/shard_map/ppermute | solution.py:254
  111.4 1.4 copy-start
Sparse Core Ops, SparseCore 0:
  49.2 62.1 all-reduce.1
Sparse Core Ops, SparseCore 1:
  75.2 38.6 all-gather.1

commit v17 on v16

--- a/solution.py
+++ b/solution.py
@@ -299,7 +299,7 @@
     piece = row_strip_piece(normals, along, (along_z, joined, lead))
     strip = lax.all_gather(piece, "col", axis=0, tiled=True)
 
-    leading, _ = doubled(leading, [1], reached)
+    leading, _ = doubled(after(leading, col_strip), [1], reached)
     lead, corner = leading[:obs], leading[obs:]
     filters = filter_matrix_of(filter_blocks, obs // P_SIZE)
     lead_reg = regular[:B].reshape(1, B)

time: 153 us -> 172 us (1.12)
  waiting for transfers between devices: 28.7 us -> 47.7 us
  other arithmetic: 8.4 us -> 10.3 us
    psum x1, waiting for transfers between devices: 5.88 us -> 24.1 us  [body(): col_strip = lax.psum(jnp.where(row_index == 0, normals[:B], 0.0), 'row')]
  transfers between devices with their start and end apart: 16 -> 16, of which waited for: 7 -> 7; matrix products, arithmetic and copies ran while one was open for 10% -> 10% of each run, Pallas kernels for 15% -> 14%
where the time goes in v17:
time: 172 us; the launch traced here: 171 us
  waiting for transfers between devices  47.7 us (28%)
  Pallas kernels  46.7 us (27%)
  starting transfers between devices  35.2 us (20%)
  between operations  15.2 us (9%)
  other arithmetic  10.3 us (6%)
  blocking collectives  9.24 us (5%)
  local copies, waits for them, and re-layouts  6.7 us (4%)
    psum x1, waiting for transfers between devices, body(): col_strip = lax.psum(jnp.where(row_index == 0, normals[:B], 0.0), 'row')  24.1 us
    pallas_call x1, Pallas kernels, tile_rows(): pl.pallas_call(tile_kernel, grid_spec=pltpu.PrefetchScalarGridSpec(num_sc...  23.2 us
    ppermute x5, waiting for transfers between devices, doubled(): got = lax.ppermute(value, ('row', 'col'), pairs)  16.3 us
    ppermute x3, starting transfers between devices, row_strip_piece(): lax.ppermute(share, 'col', [(0, 2 * z)])  14.5 us
    pallas_call x1, Pallas kernels, corner_factor(): pl.pallas_call(corner_kernel, out_shape=jax.ShapeDtypeStruct((B, B), jnp....  13.9 us
    pallas_call x1, Pallas kernels, both_sides(): pl.pallas_call(sides_kernel, in_specs=[pl.BlockSpec(memory_space=pltpu.SM...  9.62 us
    all_gather x1, blocking collectives, body(): lead = lax.all_gather(after(lead, sent), 'row', axis=0, tiled=True)  9.24 us
    ppermute x3, starting transfers between devices, body(): lax.ppermute(design, 'col', [(c, (c + 2 * s) % col_peers) for c in range(...  7.86 us
  transfers between devices with their start and end apart: 16, of which 7 were waited for; matrix products, arithmetic and copies ran while one was open for 10% of the time, Pallas kernels for 14%

profile of v17, /device:TPU:0, one launch (start us, length us, event | category | flops | bytes accessed | tf_op | source)
XLA Modules:
  0.0 171.0 jit_solution(2785099939208939206)
XLA Ops:
  7.4 4.0 %collective-permute-start.1 = (f32[32,1536]{1,0:T(8,128)}, f32[32,1536]{1,0:T(8,128)S(1)}, u32[]{:S(2)}, u32[]{:S(2)}) collective-permute-start(f32[32,1536]{1,0:T(8,128)} %param.5), channel_id=1, source_target_pairs={{0,4},{1,5},{2,6},{3,7},{4,0},{5,1},{6,2},{7,3},{8,12},{9,13},{10,... | collective-permute-start | bytes 589832 | tf_op jit(solution)/shard_map/ppermute | solution.py:283
  11.4 1.6 collective-permute-start
  13.0 2.2 %collective-permute-start.2 = (f32[32,1536]{1,0:T(8,128)}, f32[32,1536]{1,0:T(8,128)S(1)}, u32[]{:S(2)}, u32[]{:S(2)}) collective-permute-start(f32[32,1536]{1,0:T(8,128)} %param.5), channel_id=1, source_target_pairs={{0,6},{1,7},{2,0},{3,1},{4,2},{5,3},{6,4},{7,5},{8,14},{9,15},{10,... | collective-permute-start | bytes 589832 | tf_op jit(solution)/shard_map/ppermute | solution.py:283
  16.2 1.3 collective-permute-start.6
  17.6 3.0 %fusion.6 = (f32[768,256]{1,0:T(8,128)S(1)}, f32[768,256]{1,0:T(8,128)}, f32[768,256]{1,0:T(8,128)}) fusion(f32[3072,1536]{1,0:T(8,128)} %normals_ref.1), kind=kLoop, calls=%fused_computation.31 | loop fusion | bytes 4718592 | tf_op jit(solution)/shard_map/slice | solution.py:241
  20.6 5.2 %collective-permute-done.1 = f32[32,1536]{1,0:T(8,128)S(1)} collective-permute-done((f32[32,1536]{1,0:T(8,128)}, f32[32,1536]{1,0:T(8,128)S(1)}, u32[]{:S(2)}, u32[]{:S(2)}) %collective-permute-start.1) | collective-permute-done | bytes 196640 | tf_op jit(solution)/shard_map/ppermute | solution.py:283
  28.1 3.8 %all-to-all-start = ((f32[4,32,3072]{2,1,0:T(8,128)}), f32[4,32,3072]{2,1,0:T(8,128)S(1)}, u32[]{:S(2)}, u32[]{:S(2)}) async-start(f32[4,32,3072]{2,1,0:T(8,128)} %pad_maximum_fusion), calls=%async_computation | async-start | bytes 3145728 | tf_op jit(solution)/shard_map/all_to_all | solution.py:296
  31.9 8.9 %collective-permute-start.3 = (f32[768,256]{1,0:T(8,128)}, f32[768,256]{1,0:T(8,128)}, u32[]{:S(2)}, u32[]{:S(2)}) collective-permute-start(f32[768,256]{1,0:T(8,128)} %get-tuple-element.16), channel_id=1, source_target_pairs={{0,2},{8,10},{16,18},{24,26}} | collective-permute-start | bytes 2359304 | tf_op jit(solution)/shard_map/ppermute | solution.py:242
  40.8 3.4 %collective-permute-start.4 = (f32[768,256]{1,0:T(8,128)}, f32[768,256]{1,0:T(8,128)}, u32[]{:S(2)}, u32[]{:S(2)}) collective-permute-start(f32[768,256]{1,0:T(8,128)} %get-tuple-element.17), channel_id=1, source_target_pairs={{0,4},{8,12},{16,20},{24,28}} | collective-permute-start | bytes 2359304 | tf_op jit(solution)/shard_map/ppermute | solution.py:242
  44.2 2.2 %collective-permute-start.5 = (f32[768,256]{1,0:T(8,128)S(1)}, f32[768,256]{1,0:T(8,128)}, u32[]{:S(2)}, u32[]{:S(2)}) collective-permute-start(f32[768,256]{1,0:T(8,128)S(1)} %get-tuple-element.18), channel_id=1, source_target_pairs={{0,6},{8,14},{16,22},{24,30}} | collective-permute-start | bytes 2359304 | tf_op jit(solution)/shard_map/ppermute | solution.py:242
  46.4 2.7 %slice_select_fusion = f32[256,1536]{1,0:T(8,128)} fusion(f32[3072,1536]{1,0:T(8,128)} %normals_ref.1, pred[]{:T(512)S(6)} %eq.33), kind=kLoop, calls=%fused_computation.1 | loop fusion | flops 393216 | bytes 3145729 | tf_op jit(solution)/shard_map/jit(_where)/select_n | solution.py:271
  50.1 1.3 collective-permute-start.7
  51.5 9.2 %all_gather.6 = f32[128,256]{1,0:T(8,128)S(1)} all-gather(f32[32,256]{1,0:T(8,128)S(1)} %slice.60), channel_id=1, replica_groups=mesh['row'=4,'col'=8] {'row'}, dimensions={0}, use_global_device_ids=true | all-gather | bytes 163840 | tf_op jit(solution)/shard_map/all_gather | solution.py:293
  60.7 8.6 %collective-permute-done.7 = f32[256,256]{1,0:T(8,128)S(1)} collective-permute-done((f32[256,256]{1,0:T(8,128)S(1)}, f32[256,256]{1,0:T(8,128)S(1)}, u32[]{:S(2)}, u32[]{:S(2)}) %collective-permute-start.7) | collective-permute-done | bytes 262176 | tf_op jit(solution)/shard_map/ppermute | solution.py:254
  69.4 2.0 %add_select_fusion = f32[768,256]{1,0:T(8,128)S(1)} fusion(f32[768,256]{1,0:T(8,128)} %collective-permute-done.5, f32[768,256]{1,0:T(8,128)} %collective-permute-done.3, f32[768,256]{1,0:T(8,128)} %collective-permute-done.4, f32[3072,1536]{1,0:T(8,128)} %normals_ref.1, pred[]{:T(512)S(6)} %eq.32), kind=kLoop, calls=%fused_computation.3 | loop fusion | flops 589824 | bytes 3932161 | tf_op jit(solution)/shard_map/jit(_where)/select_n | solution.py:244
  71.5 1.3 collective-permute-start.8
  74.9 1.3 collective-permute-start.9
  76.3 3.9 %collective-permute-done.9 = f32[256,256]{1,0:T(8,128)S(1)} collective-permute-done((f32[256,256]{1,0:T(8,128)S(1)}, f32[256,256]{1,0:T(8,128)S(1)}, u32[]{:S(2)}, u32[]{:S(2)}) %collective-permute-start.9) | collective-permute-done | bytes 262176 | tf_op jit(solution)/shard_map/ppermute | solution.py:254
  81.5 3.8 %collective-permute-done.10 = f32[256,256]{1,0:T(8,128)S(1)} collective-permute-done((f32[256,256]{1,0:T(8,128)S(1)}, f32[256,256]{1,0:T(8,128)S(1)}, u32[]{:S(2)}, u32[]{:S(2)}) %collective-permute-start.10) | collective-permute-done | bytes 262176 | tf_op jit(solution)/shard_map/ppermute | solution.py:254
  87.1 24.1 %all-reduce.2.cloned.1.call-done.strip_ref = f32[256,1536]{1,0:T(8,128)} async-done(((f32[256,1536]{1,0:T(8,128)}), f32[256,1536]{1,0:T(8,128)}) %all-reduce.2.cloned.1.call-update) | async-done | bytes 1572880 | tf_op jit(solution)/shard_map/psum | solution.py:271
  111.2 2.5 %collective-permute-start.11 = (f32[384,256]{1,0:T(8,128)}, f32[384,256]{1,0:T(8,128)}, u32[]{:S(2)}, u32[]{:S(2)}) collective-permute-start(f32[384,256]{1,0:T(8,128)} %pad_maximum_fusion.6), channel_id=1, source_target_pairs={{0,1},{4,5},{2,3},{6,7},{8,9},{12,13},{10,11},{14,15},{16,17},{20,... | collective-permute-start | bytes 1179656 | tf_op jit(solution)/shard_map/ppermute | solution.py:254
  116.8 13.9 %corner_factor.1.inverse_ref = f32[256,256]{1,0:T(8,128)S(1)} custom-call(f32[256,256]{1,0:T(8,128)S(1)} %slice.65.block_ref, f32[128,256]{1,0:T(8,128)S(1)} %slice.63.design_ref.lead_ref, f32[128,128]{1,0:T(8,128)S(1)} %select_n.145.filter_ref, f32[1,256]{1,0:T(1,128)S(1)} %bitcast.32), custom_call_target="tpu_custom_call" | custom-call | tf_op jit(solution)/shard_map/corner_factor/pallas_call | solution.py:82
  130.7 9.6 %both_sides.1 = (bf16[3072,384]{1,0:T(8,128)(2,1)}, bf16[1152,1536]{1,0:T(8,128)(2,1)}, f32[3072,256]{1,0:T(8,128)}) custom-call(s32[2]{0:T(128)S(1)} %pad_add_fusion.place_ref, f32[128,3072]{1,0:T(8,128)S(1)} %bitcast.31, f32[128,256]{1,0:T(8,128)S(1)} %slice.63.design_ref.lead_ref, f32[128,1536]{1,0:T(8,128)} %collective-permute-done.12.other_ref, ...), custom_call_target="tpu_custom_call" | custom-call | tf_op jit(solution)/shard_map/both_sides/pallas_call | solution.py:155
  140.3 23.2 %tile_rows.1 = f32[3072,1536]{1,0:T(8,128)} custom-call(s32[2]{0:T(128)S(1)} %pad_add_fusion.place_ref, f32[3072,1536]{1,0:T(8,128)} %normals_ref.1, f32[3072,256]{1,0:T(8,128)} %all-gather.2.cloned.1.call-done.strip_ref, f32[3072,256]{1,0:T(8,128)} %get-tuple-element.24.gram_ref, bf16[3072,384]{1,0:T(8,128)(2,1)} %get-tuple-element.25.left_ref, ...), custom_call_target="tpu_custom_call" | custom-call | tf_op jit(solution)/shard_map/tile_rows/pallas_call | solution.py:207
  (48 shorter events, 12.7 us)
Async XLA Ops:
  7.4 18.4 %collective-permute-start.1 = (f32[32,1536]{1,0:T(8,128)}, f32[32,1536]{1,0:T(8,128)S(1)}, u32[]{:S(2)}, u32[]{:S(2)}) collective-permute-start(f32[32,1536]{1,0:T(8,128)} %param.5), channel_id=1, source_target_pairs={{0,4},{1,5},{2,6},{3,7},{4,0},{5,1},{6,2},{7,3},{8,12},{9,13},{10,... | collective-permute-start | bytes 589832 | tf_op jit(solution)/shard_map/ppermute | solution.py:283
  11.4 14.4 %collective-permute-start = (f32[32,1536]{1,0:T(8,128)}, f32[32,1536]{1,0:T(8,128)S(1)}, u32[]{:S(2)}, u32[]{:S(2)}) collective-permute-start(f32[32,1536]{1,0:T(8,128)} %param.5), channel_id=1, source_target_pairs={{0,2},{1,3},{2,4},{3,5},{4,6},{5,7},{6,0},{7,1},{8,10},{9,11},{10,... | collective-permute-start | bytes 589832 | tf_op jit(solution)/shard_map/ppermute | solution.py:283
  13.0 13.6 %collective-permute-start.2 = (f32[32,1536]{1,0:T(8,128)}, f32[32,1536]{1,0:T(8,128)S(1)}, u32[]{:S(2)}, u32[]{:S(2)}) collective-permute-start(f32[32,1536]{1,0:T(8,128)} %param.5), channel_id=1, source_target_pairs={{0,6},{1,7},{2,0},{3,1},{4,2},{5,3},{6,4},{7,5},{8,14},{9,15},{10,... | collective-permute-start | bytes 589832 | tf_op jit(solution)/shard_map/ppermute | solution.py:283
  16.2 32.9 %collective-permute-start.6 = (f32[256,256]{1,0:T(8,128)S(1)}, f32[256,256]{1,0:T(8,128)S(1)}, u32[]{:S(2)}, u32[]{:S(2)}) collective-permute-start(f32[256,256]{1,0:T(8,128)S(1)} %slice.49), channel_id=1, source_target_pairs={{0,4}} | collective-permute-start | bytes 786440 | tf_op jit(solution)/shard_map/ppermute | solution.py:254
  17.6 8.9 %copy-start.1 = (f32[32,1536]{1,0:T(8,128)S(1)}, f32[32,1536]{1,0:T(8,128)}, u32[]{:S(2)}) copy-start(f32[32,1536]{1,0:T(8,128)} %param.5) | copy-start | bytes 589828
  28.1 41.2 %all-to-all-start = ((f32[4,32,3072]{2,1,0:T(8,128)}), f32[4,32,3072]{2,1,0:T(8,128)S(1)}, u32[]{:S(2)}, u32[]{:S(2)}) async-start(f32[4,32,3072]{2,1,0:T(8,128)} %pad_maximum_fusion), calls=%async_computation | async-start | bytes 3145728 | tf_op jit(solution)/shard_map/all_to_all | solution.py:296
  31.9 79.3 %all-reduce.2.cloned.1.call-start = ((), (), s32[]{:S(2)}) async-start(), calls=%async_computation.2 | async-start | bytes 3145728 | tf_op jit(solution)/shard_map/psum | solution.py:271
  31.9 37.4 %collective-permute-start.3 = (f32[768,256]{1,0:T(8,128)}, f32[768,256]{1,0:T(8,128)}, u32[]{:S(2)}, u32[]{:S(2)}) collective-permute-start(f32[768,256]{1,0:T(8,128)} %get-tuple-element.16), channel_id=1, source_target_pairs={{0,2},{8,10},{16,18},{24,26}} | collective-permute-start | bytes 2359304 | tf_op jit(solution)/shard_map/ppermute | solution.py:242
  40.8 28.5 %collective-permute-start.4 = (f32[768,256]{1,0:T(8,128)}, f32[768,256]{1,0:T(8,128)}, u32[]{:S(2)}, u32[]{:S(2)}) collective-permute-start(f32[768,256]{1,0:T(8,128)} %get-tuple-element.17), channel_id=1, source_target_pairs={{0,4},{8,12},{16,20},{24,28}} | collective-permute-start | bytes 2359304 | tf_op jit(solution)/shard_map/ppermute | solution.py:242
  44.2 25.2 %collective-permute-start.5 = (f32[768,256]{1,0:T(8,128)S(1)}, f32[768,256]{1,0:T(8,128)}, u32[]{:S(2)}, u32[]{:S(2)}) collective-permute-start(f32[768,256]{1,0:T(8,128)S(1)} %get-tuple-element.18), channel_id=1, source_target_pairs={{0,6},{8,14},{16,22},{24,30}} | collective-permute-start | bytes 2359304 | tf_op jit(solution)/shard_map/ppermute | solution.py:242
  49.1 91.3 %all-gather.2.cloned.1.call-start = ((), (), s32[]{:S(2)}) async-start(), calls=%async_computation.1 | async-start | bytes 3538944 | tf_op jit(solution)/shard_map/all_gather | solution.py:300
  50.1 19.2 %collective-permute-start.7 = (f32[256,256]{1,0:T(8,128)S(1)}, f32[256,256]{1,0:T(8,128)S(1)}, u32[]{:S(2)}, u32[]{:S(2)}) collective-permute-start(f32[256,256]{1,0:T(8,128)S(1)} %broadcast_select_fusion.3), channel_id=1, source_target_pairs={{0,2},{4,6}} | collective-permute-start | bytes 786440 | tf_op jit(solution)/shard_map/ppermute | solution.py:254
  71.5 2.6 %collective-permute-start.8 = (f32[384,256]{1,0:T(8,128)S(1)}, f32[384,256]{1,0:T(8,128)S(1)}, u32[]{:S(2)}, u32[]{:S(2)}) collective-permute-start(f32[384,256]{1,0:T(8,128)S(1)} %slice.62), channel_id=1, source_target_pairs={{0,1},{2,3},{4,5},{6,7},{8,9},{10,11},{12,13},{14,15},{16,17},{18,... | collective-permute-start | bytes 1179656 | tf_op jit(solution)/shard_map/ppermute | solution.py:245
  74.1 7.4 %copy-start.2 = (f32[2,32,32]{2,1,0:T(8,128)S(1)}, f32[2,32,32]{2,1,0:T(8,128)}, u32[]{:S(2)}) copy-start(f32[2,32,32]{2,1,0:T(8,128)} %param.6) | copy-start | bytes 24580
  74.9 5.2 %collective-permute-start.9 = (f32[256,256]{1,0:T(8,128)S(1)}, f32[256,256]{1,0:T(8,128)S(1)}, u32[]{:S(2)}, u32[]{:S(2)}) collective-permute-start(f32[256,256]{1,0:T(8,128)S(1)} %broadcast_select_fusion.4), channel_id=1, source_target_pairs={{0,8},{4,12},{2,10},{6,14}} | collective-permute-start | bytes 786440 | tf_op jit(solution)/shard_map/ppermute | solution.py:254
  80.2 5.2 %collective-permute-start.10 = (f32[256,256]{1,0:T(8,128)S(1)}, f32[256,256]{1,0:T(8,128)S(1)}, u32[]{:S(2)}, u32[]{:S(2)}) collective-permute-start(f32[256,256]{1,0:T(8,128)S(1)} %broadcast_select_fusion.1), channel_id=1, source_target_pairs={{0,16},{4,20},{2,18},{6,22},{8,24},{12,28},{10,26},{14,30}} | collective-permute-start | bytes 786440 | tf_op jit(solution)/shard_map/ppermute | solution.py:254
  86.3 44.4 %collective-permute-start.12 = (f32[128,1536]{1,0:T(8,128)}, f32[128,1536]{1,0:T(8,128)}, u32[]{:S(2)}, u32[]{:S(2)}) collective-permute-start(f32[128,1536]{1,0:T(8,128)} %slice.64), channel_id=1, source_target_pairs={{0,1},{1,0},{2,3},{3,2},{4,5},{5,4},{6,7},{7,6},{8,9},{9,8},{10,11... | collective-permute-start | bytes 2359304 | tf_op jit(solution)/shard_map/ppermute | solution.py:308
  111.2 4.4 %collective-permute-start.11 = (f32[384,256]{1,0:T(8,128)}, f32[384,256]{1,0:T(8,128)}, u32[]{:S(2)}, u32[]{:S(2)}) collective-permute-start(f32[384,256]{1,0:T(8,128)} %pad_maximum_fusion.6), channel_id=1, source_target_pairs={{0,1},{4,5},{2,3},{6,7},{8,9},{12,13},{10,11},{14,15},{16,17},{20,... | collective-permute-start | bytes 1179656 | tf_op jit(solution)/shard_map/ppermute | solution.py:254
  115.3 15.4 %copy-start = (f32[256,1536]{1,0:T(8,128)S(1)}, f32[256,1536]{1,0:T(8,128)}, u32[]{:S(2)}) copy-start(f32[256,1536]{1,0:T(8,128)} %all-reduce.2.cloned.1.call-done.strip_ref) | copy-start | bytes 4718596
Sparse Core Ops, SparseCore 0:
  49.2 61.9 all-reduce.1
Sparse Core Ops, SparseCore 1:
  75.0 37.6 all-gather.1

commit v18 on v16

--- a/solution.py
+++ b/solution.py
@@ -89,28 +89,14 @@
     )(block, design, filter_matrix, regular)
 
 
-def sides_kernel(
-    place_ref,
-    joined_ref,
-    lead_ref,
-    other_ref,
-    strip_ref,
-    inverse_ref,
-    filter_ref,
-    regular_ref,
-    lead_reg_ref,
-    left_ref,
-    right_ref,
-    gram_cols_ref,
+def columns_kernel(
+    place_ref, joined_ref, lead_ref, strip_ref, inverse_ref, filter_ref, regular_ref, right_ref
 ):
-    row_index, col_index = place_ref[0], place_ref[1]
+    col_index = place_ref[1]
     cols = right_ref.shape[1]
     obs = filter_ref.shape[0]
-    core = lax.rem(col_index, 2)
-    filtered = split_dot(filter_ref[...], joined_ref[:, : 2 * cols])
-    here, rows_own = filtered[:, :cols], filtered[:, cols:]
+    here = split_dot(filter_ref[...], joined_ref[:, :cols])
     lead = split_dot(filter_ref[...], lead_ref[...])
-
     row_pos = lax.broadcasted_iota(jnp.int32, (B, cols), 0)
     col_pos = lax.broadcasted_iota(jnp.int32, (1, cols), 1) + col_index * cols
     strip = strip_ref[...] + split_dot(lead.T, here)
@@ -133,9 +119,30 @@
         right_ref[B : 2 * B, :B] = jnp.zeros((B, B), jnp.bfloat16)
         right_ref[2 * B : 3 * B, :B] = identity
 
-    rows_other = split_dot(filter_ref[...], other_ref[...])
-    for half, value in ((core, rows_own), (1 - core, rows_other)):
-        value = value.T
+
+def column_side(place, joined, lead, strip, inverse, filter_matrix, regular):
+    cols = strip.shape[1]
+    obs = filter_matrix.shape[0]
+    vmem = pl.BlockSpec(memory_space=pltpu.VMEM)
+    return pl.pallas_call(
+        columns_kernel,
+        in_specs=[pl.BlockSpec(memory_space=pltpu.SMEM)] + [vmem] * 6,
+        out_specs=vmem,
+        out_shape=pltpu.HBM((3 * (obs + B), cols), jnp.bfloat16),
+        compiler_params=pltpu.CompilerParams(vmem_limit_bytes=26 * 2**20),
+        cost_estimate=pl.CostEstimate(flops=0, bytes_accessed=0, transcendentals=0),
+        name="column_side",
+    )(place, joined, lead, strip, inverse, filter_matrix, regular)
+
+
+def rows_kernel(place_ref, joined_ref, lead_ref, other_ref, filter_ref, lead_reg_ref, left_ref, gram_cols_ref):
+    row_index, col_index = place_ref[0], place_ref[1]
+    cols = other_ref.shape[1]
+    obs = filter_ref.shape[0]
+    core = lax.rem(col_index, 2)
+    lead = split_dot(filter_ref[...], lead_ref[...])
+    for half, value in ((core, joined_ref[:, cols:]), (1 - core, other_ref[...])):
+        value = split_dot(filter_ref[...], value).T
         high, low = split(value)
         rows = pl.ds(pl.multiple_of(half * cols, cols), cols)
         left_ref[rows, :obs] = high
@@ -148,23 +155,22 @@
         )
 
 
-def both_sides(place, joined, lead, other, strip, inverse, filter_matrix, regular, lead_reg):
+def row_side(place, joined, lead, other, filter_matrix, lead_reg):
     cols = other.shape[1]
     obs = filter_matrix.shape[0]
     vmem = pl.BlockSpec(memory_space=pltpu.VMEM)
     return pl.pallas_call(
-        sides_kernel,
-        in_specs=[pl.BlockSpec(memory_space=pltpu.SMEM)] + [vmem] * 8,
-        out_specs=[vmem] * 3,
+        rows_kernel,
+        in_specs=[pl.BlockSpec(memory_space=pltpu.SMEM)] + [vmem] * 5,
+        out_specs=[vmem] * 2,
         out_shape=[
             pltpu.HBM((2 * cols, 3 * obs), jnp.bfloat16),
-            pltpu.HBM((3 * (obs + B), cols), jnp.bfloat16),
             pltpu.HBM((2 * cols, B), jnp.float32),
         ],
         compiler_params=pltpu.CompilerParams(vmem_limit_bytes=26 * 2**20),
         cost_estimate=pl.CostEstimate(flops=0, bytes_accessed=0, transcendentals=0),
-        name="both_sides",
-    )(place, joined, lead, other, strip, inverse, filter_matrix, regular, lead_reg)
+        name="row_side",
+    )(place, joined, lead, other, filter_matrix, lead_reg)
 
 
 def block_rows(half):
@@ -303,14 +309,12 @@
     lead, corner = leading[:obs], leading[obs:]
     filters = filter_matrix_of(filter_blocks, obs // P_SIZE)
     lead_reg = regular[:B].reshape(1, B)
-    inverse = corner_factor(corner, lead, filters, lead_reg)
-
-    other = lax.ppermute(joined[:, cols_here:], "col", [(c, c ^ 1) for c in range(col_peers)])
     own_reg = lax.dynamic_slice_in_dim(regular, col_index * cols_here, cols_here).reshape(1, cols_here)
     place = jnp.stack([row_index, col_index]).astype(jnp.int32)
-    left, right, gram_cols = both_sides(
-        place, joined, lead, other, col_strip, inverse, filters, own_reg, lead_reg
-    )
+    other = lax.ppermute(joined[:, cols_here:], "col", [(c, c ^ 1) for c in range(col_peers)])
+    left, gram_cols = row_side(place, joined, lead, other, filters, lead_reg)
+    inverse = corner_factor(after(corner, gram_cols), lead, filters, lead_reg)
+    right = column_side(place, joined, lead, col_strip, inverse, filters, own_reg)
     large = [normals, strip, gram_cols, left, right]
     large = [pltpu.with_memory_space_constraint(array, pltpu.HBM) for array in large]
     return tile_rows(place, *large, inverse, own_reg)

time: 153 us -> 151 us (0.987); the launches traced: 152 us -> 149 us
  waiting for transfers between devices: 28.7 us -> 23.8 us
    psum x1, waiting for transfers between devices: 5.88 us -> 0.97 us  [body(): col_strip = lax.psum(jnp.where(row_index == 0, normals[:B], 0.0), 'row')]
    pallas_call x1 -> x2, Pallas kernels: 9.02 us -> 10 us  [the longest x1 5.15 us: column_side(): pl.pallas_call(columns_kernel, in_specs=[pl.BlockSpec(memory_space=pltpu....]
  transfers between devices with their start and end apart: 16 -> 16, of which waited for: 7 -> 7; matrix products, arithmetic and copies ran while one was open for 10% -> 10% of each run, Pallas kernels for 15% -> 16%
where the time goes in v18:
time: 151 us; the launch traced here: 149 us
  Pallas kernels  47.1 us (31%)
  starting transfers between devices  36.5 us (24%)
  waiting for transfers between devices  23.8 us (16%)
  between operations  15.2 us (10%)
  blocking collectives  9.24 us (6%)
  other arithmetic  8.4 us (6%)
  local copies, waits for them, and re-layouts  8.27 us (5%)
    pallas_call x1, Pallas kernels, tile_rows(): pl.pallas_call(tile_kernel, grid_spec=pltpu.PrefetchScalarGridSpec(num_sc...  23.2 us
    ppermute x5, waiting for transfers between devices, doubled(): got = lax.ppermute(value, ('row', 'col'), pairs)  16.3 us
    ppermute x3, starting transfers between devices, row_strip_piece(): lax.ppermute(share, 'col', [(0, 2 * z)])  14.4 us
    pallas_call x1, Pallas kernels, corner_factor(): pl.pallas_call(corner_kernel, out_shape=jax.ShapeDtypeStruct((B, B), jnp....  13.9 us
    all_gather x1, blocking collectives, body(): lead = lax.all_gather(after(lead, sent), 'row', axis=0, tiled=True)  9.24 us
    ppermute x5, starting transfers between devices, doubled(): got = lax.ppermute(value, ('row', 'col'), pairs)  8.38 us
    ppermute x3, starting transfers between devices, body(): lax.ppermute(design, 'col', [(c, (c + 2 * s) % col_peers) for c in range(...  7.86 us
    ppermute x3, waiting for transfers between devices, body(): lax.ppermute(design, 'col', [(c, (c + 2 * s) % col_peers) for c in range(...  5.75 us
  transfers between devices with their start and end apart: 16, of which 7 were waited for; matrix products, arithmetic and copies ran while one was open for 10% of the time, Pallas kernels for 16%

profile of v18, /device:TPU:0, one launch (start us, length us, event | category | flops | bytes accessed | tf_op | source)
XLA Modules:
  0.0 148.6 jit_solution(1935767415734929334)
XLA Ops:
  7.4 4.0 %collective-permute-start.1 = (f32[32,1536]{1,0:T(8,128)}, f32[32,1536]{1,0:T(8,128)S(1)}, u32[]{:S(2)}, u32[]{:S(2)}) collective-permute-start(f32[32,1536]{1,0:T(8,128)} %param.5), channel_id=1, source_target_pairs={{0,4},{1,5},{2,6},{3,7},{4,0},{5,1},{6,2},{7,3},{8,12},{9,13},{10,... | collective-permute-start | bytes 589832 | tf_op jit(solution)/shard_map/ppermute | solution.py:289
  11.4 1.6 %collective-permute-start = (f32[32,1536]{1,0:T(8,128)}, f32[32,1536]{1,0:T(8,128)S(1)}, u32[]{:S(2)}, u32[]{:S(2)}) collective-permute-start(f32[32,1536]{1,0:T(8,128)} %param.5), channel_id=1, source_target_pairs={{0,2},{1,3},{2,4},{3,5},{4,6},{5,7},{6,0},{7,1},{8,10},{9,11},{10,... | collective-permute-start | bytes 589832 | tf_op jit(solution)/shard_map/ppermute | solution.py:289
  13.0 2.2 %collective-permute-start.2 = (f32[32,1536]{1,0:T(8,128)}, f32[32,1536]{1,0:T(8,128)S(1)}, u32[]{:S(2)}, u32[]{:S(2)}) collective-permute-start(f32[32,1536]{1,0:T(8,128)} %param.5), channel_id=1, source_target_pairs={{0,6},{1,7},{2,0},{3,1},{4,2},{5,3},{6,4},{7,5},{8,14},{9,15},{10,... | collective-permute-start | bytes 589832 | tf_op jit(solution)/shard_map/ppermute | solution.py:289
  17.6 3.2 %fusion.6 = (f32[768,256]{1,0:T(8,128)}, f32[768,256]{1,0:T(8,128)}, f32[768,256]{1,0:T(8,128)}) fusion(f32[3072,1536]{1,0:T(8,128)} %normals_ref.1), kind=kLoop, calls=%fused_computation.31 | loop fusion | bytes 4718592 | tf_op jit(solution)/shard_map/slice | solution.py:247
  20.8 5.0 %collective-permute-done.1 = f32[32,1536]{1,0:T(8,128)S(1)} collective-permute-done((f32[32,1536]{1,0:T(8,128)}, f32[32,1536]{1,0:T(8,128)S(1)}, u32[]{:S(2)}, u32[]{:S(2)}) %collective-permute-start.1) | collective-permute-done | bytes 196640 | tf_op jit(solution)/shard_map/ppermute | solution.py:289
  28.1 3.8 %all-to-all-start = ((f32[4,32,3072]{2,1,0:T(8,128)}), f32[4,32,3072]{2,1,0:T(8,128)S(1)}, u32[]{:S(2)}, u32[]{:S(2)}) async-start(f32[4,32,3072]{2,1,0:T(8,128)} %pad_maximum_fusion), calls=%async_computation | async-start | bytes 3145728 | tf_op jit(solution)/shard_map/all_to_all | solution.py:302
  31.9 8.9 %collective-permute-start.3 = (f32[768,256]{1,0:T(8,128)}, f32[768,256]{1,0:T(8,128)}, u32[]{:S(2)}, u32[]{:S(2)}) collective-permute-start(f32[768,256]{1,0:T(8,128)} %get-tuple-element.15), channel_id=1, source_target_pairs={{0,2},{8,10},{16,18},{24,26}} | collective-permute-start | bytes 2359304 | tf_op jit(solution)/shard_map/ppermute | solution.py:248
  40.8 3.4 %collective-permute-start.4 = (f32[768,256]{1,0:T(8,128)}, f32[768,256]{1,0:T(8,128)}, u32[]{:S(2)}, u32[]{:S(2)}) collective-permute-start(f32[768,256]{1,0:T(8,128)} %get-tuple-element.16), channel_id=1, source_target_pairs={{0,4},{8,12},{16,20},{24,28}} | collective-permute-start | bytes 2359304 | tf_op jit(solution)/shard_map/ppermute | solution.py:248
  44.2 2.2 %collective-permute-start.5 = (f32[768,256]{1,0:T(8,128)}, f32[768,256]{1,0:T(8,128)}, u32[]{:S(2)}, u32[]{:S(2)}) collective-permute-start(f32[768,256]{1,0:T(8,128)} %get-tuple-element.17), channel_id=1, source_target_pairs={{0,6},{8,14},{16,22},{24,30}} | collective-permute-start | bytes 2359304 | tf_op jit(solution)/shard_map/ppermute | solution.py:248
  46.4 2.7 %slice_select_fusion = f32[256,1536]{1,0:T(8,128)} fusion(f32[3072,1536]{1,0:T(8,128)} %normals_ref.1, pred[]{:T(512)S(6)} %eq.35), kind=kLoop, calls=%fused_computation.1 | loop fusion | flops 393216 | bytes 3145729 | tf_op jit(solution)/shard_map/jit(_where)/select_n | solution.py:277
  50.1 1.3 collective-permute-start.7
  51.4 9.2 %all_gather.6 = f32[128,256]{1,0:T(8,128)S(1)} all-gather(f32[32,256]{1,0:T(8,128)S(1)} %slice.60), channel_id=1, replica_groups=mesh['row'=4,'col'=8] {'row'}, dimensions={0}, use_global_device_ids=true | all-gather | bytes 163840 | tf_op jit(solution)/shard_map/all_gather | solution.py:299
  60.7 8.6 %collective-permute-done.7 = f32[256,256]{1,0:T(8,128)S(1)} collective-permute-done((f32[256,256]{1,0:T(8,128)S(1)}, f32[256,256]{1,0:T(8,128)S(1)}, u32[]{:S(2)}, u32[]{:S(2)}) %collective-permute-start.7) | collective-permute-done | bytes 262176 | tf_op jit(solution)/shard_map/ppermute | solution.py:260
  69.4 2.0 %add_select_fusion = f32[768,256]{1,0:T(8,128)S(1)} fusion(f32[768,256]{1,0:T(8,128)} %collective-permute-done.5, f32[768,256]{1,0:T(8,128)} %collective-permute-done.3, f32[768,256]{1,0:T(8,128)} %collective-permute-done.4, f32[3072,1536]{1,0:T(8,128)} %normals_ref.1, pred[]{:T(512)S(6)} %eq.32), kind=kLoop, calls=%fused_computation.3 | loop fusion | flops 589824 | bytes 3932161 | tf_op jit(solution)/shard_map/jit(_where)/select_n | solution.py:250
  71.5 2.0 %collective-permute-start.8 = (f32[384,256]{1,0:T(8,128)S(1)}, f32[384,256]{1,0:T(8,128)}, u32[]{:S(2)}, u32[]{:S(2)}) collective-permute-start(f32[384,256]{1,0:T(8,128)S(1)} %slice.62), channel_id=1, source_target_pairs={{0,1},{2,3},{4,5},{6,7},{8,9},{10,11},{12,13},{14,15},{16,17},{18,... | collective-permute-start | bytes 1179656 | tf_op jit(solution)/shard_map/ppermute | solution.py:251
  75.1 1.3 collective-permute-start.9
  76.4 3.9 %collective-permute-done.9 = f32[256,256]{1,0:T(8,128)S(1)} collective-permute-done((f32[256,256]{1,0:T(8,128)S(1)}, f32[256,256]{1,0:T(8,128)S(1)}, u32[]{:S(2)}, u32[]{:S(2)}) %collective-permute-start.9) | collective-permute-done | bytes 262176 | tf_op jit(solution)/shard_map/ppermute | solution.py:260
  81.6 3.8 %collective-permute-done.10 = f32[256,256]{1,0:T(8,128)S(1)} collective-permute-done((f32[256,256]{1,0:T(8,128)S(1)}, f32[256,256]{1,0:T(8,128)S(1)}, u32[]{:S(2)}, u32[]{:S(2)}) %collective-permute-start.10) | collective-permute-done | bytes 262176 | tf_op jit(solution)/shard_map/ppermute | solution.py:260
  86.5 3.2 %collective-permute-start.11 = (f32[384,256]{1,0:T(8,128)S(1)}, f32[384,256]{1,0:T(8,128)}, u32[]{:S(2)}, u32[]{:S(2)}) collective-permute-start(f32[384,256]{1,0:T(8,128)S(1)} %pad_maximum_fusion.6), channel_id=1, source_target_pairs={{0,1},{4,5},{2,3},{6,7},{8,9},{12,13},{10,11},{14,15},{16,17},{20,... | collective-permute-start | bytes 1179656 | tf_op jit(solution)/shard_map/ppermute | solution.py:260
  91.6 4.9 %row_side.1 = (bf16[3072,384]{1,0:T(8,128)(2,1)}, f32[3072,256]{1,0:T(8,128)}) custom-call(s32[2]{0:T(128)S(1)} %pad_add_fusion.place_ref, f32[128,3072]{1,0:T(8,128)S(1)} %bitcast.31, f32[128,256]{1,0:T(8,128)S(1)} %slice.63.lead_ref.design_ref, f32[128,1536]{1,0:T(8,128)S(1)} %collective-permute-done.12.other_ref, f32[128,128]{1,0:T(8,128)S(1)} %select_n.143.filter_ref, ...), custom_call_target="tpu_custom_call" | custom-call | tf_op jit(solution)/shard_map/row_side/pallas_call | solution.py:162
  96.5 13.9 %corner_factor.1.inverse_ref = f32[256,256]{1,0:T(8,128)S(1)} custom-call(f32[256,256]{1,0:T(8,128)S(1)} %slice.65.block_ref, f32[128,256]{1,0:T(8,128)S(1)} %slice.63.lead_ref.design_ref, f32[128,128]{1,0:T(8,128)S(1)} %select_n.143.filter_ref, f32[1,256]{1,0:T(1,128)S(1)} %bitcast.34), custom_call_target="tpu_custom_call" | custom-call | tf_op jit(solution)/shard_map/corner_factor/pallas_call | solution.py:82
  111.3 1.4 copy-done
  112.7 5.2 %column_side.1.right_ref = bf16[1152,1536]{1,0:T(8,128)(2,1)} custom-call(s32[2]{0:T(128)S(1)} %pad_add_fusion.place_ref, f32[128,3072]{1,0:T(8,128)S(1)} %bitcast.32, f32[128,256]{1,0:T(8,128)S(1)} %slice.63.lead_ref.design_ref, f32[256,1536]{1,0:T(8,128)S(1)} %copy-done, f32[256,256]{1,0:T(8,128)S(1)} %corner_factor.1.inverse_ref, ...), custom_call_target="tpu_custom_call" | custom-call | tf_op jit(solution)/shard_map/column_side/pallas_call | solution.py:127
  117.9 23.2 %tile_rows.1 = f32[3072,1536]{1,0:T(8,128)} custom-call(s32[2]{0:T(128)S(1)} %pad_add_fusion.place_ref, f32[3072,1536]{1,0:T(8,128)} %normals_ref.1, f32[3072,256]{1,0:T(8,128)} %all-gather.2.cloned.1.call-done.strip_ref, f32[3072,256]{1,0:T(8,128)} %get-tuple-element.22.gram_ref, bf16[3072,384]{1,0:T(8,128)(2,1)} %get-tuple-element.23.left_ref, ...), custom_call_target="tpu_custom_call" | custom-call | tf_op jit(solution)/shard_map/tile_rows/pallas_call | solution.py:213
  (49 shorter events, 12.5 us)
Async XLA Ops:
  7.4 18.4 %collective-permute-start.1 = (f32[32,1536]{1,0:T(8,128)}, f32[32,1536]{1,0:T(8,128)S(1)}, u32[]{:S(2)}, u32[]{:S(2)}) collective-permute-start(f32[32,1536]{1,0:T(8,128)} %param.5), channel_id=1, source_target_pairs={{0,4},{1,5},{2,6},{3,7},{4,0},{5,1},{6,2},{7,3},{8,12},{9,13},{10,... | collective-permute-start | bytes 589832 | tf_op jit(solution)/shard_map/ppermute | solution.py:289
  11.4 14.4 %collective-permute-start = (f32[32,1536]{1,0:T(8,128)}, f32[32,1536]{1,0:T(8,128)S(1)}, u32[]{:S(2)}, u32[]{:S(2)}) collective-permute-start(f32[32,1536]{1,0:T(8,128)} %param.5), channel_id=1, source_target_pairs={{0,2},{1,3},{2,4},{3,5},{4,6},{5,7},{6,0},{7,1},{8,10},{9,11},{10,... | collective-permute-start | bytes 589832 | tf_op jit(solution)/shard_map/ppermute | solution.py:289
  13.0 13.6 %collective-permute-start.2 = (f32[32,1536]{1,0:T(8,128)}, f32[32,1536]{1,0:T(8,128)S(1)}, u32[]{:S(2)}, u32[]{:S(2)}) collective-permute-start(f32[32,1536]{1,0:T(8,128)} %param.5), channel_id=1, source_target_pairs={{0,6},{1,7},{2,0},{3,1},{4,2},{5,3},{6,4},{7,5},{8,14},{9,15},{10,... | collective-permute-start | bytes 589832 | tf_op jit(solution)/shard_map/ppermute | solution.py:289
  16.2 32.9 %collective-permute-start.6 = (f32[256,256]{1,0:T(8,128)S(1)}, f32[256,256]{1,0:T(8,128)S(1)}, u32[]{:S(2)}, u32[]{:S(2)}) collective-permute-start(f32[256,256]{1,0:T(8,128)S(1)} %slice.49), channel_id=1, source_target_pairs={{0,4}} | collective-permute-start | bytes 786440 | tf_op jit(solution)/shard_map/ppermute | solution.py:260
  17.6 8.9 %copy-start.1 = (f32[32,1536]{1,0:T(8,128)S(1)}, f32[32,1536]{1,0:T(8,128)}, u32[]{:S(2)}) copy-start(f32[32,1536]{1,0:T(8,128)} %param.5) | copy-start | bytes 589828
  28.1 41.2 %all-to-all-start = ((f32[4,32,3072]{2,1,0:T(8,128)}), f32[4,32,3072]{2,1,0:T(8,128)S(1)}, u32[]{:S(2)}, u32[]{:S(2)}) async-start(f32[4,32,3072]{2,1,0:T(8,128)} %pad_maximum_fusion), calls=%async_computation | async-start | bytes 3145728 | tf_op jit(solution)/shard_map/all_to_all | solution.py:302
  31.9 79.4 %all-reduce.2.cloned.1.call-start = ((), (), s32[]{:S(2)}) async-start(), calls=%async_computation.2 | async-start | bytes 3145728 | tf_op jit(solution)/shard_map/psum | solution.py:277
  31.9 37.4 %collective-permute-start.3 = (f32[768,256]{1,0:T(8,128)}, f32[768,256]{1,0:T(8,128)}, u32[]{:S(2)}, u32[]{:S(2)}) collective-permute-start(f32[768,256]{1,0:T(8,128)} %get-tuple-element.15), channel_id=1, source_target_pairs={{0,2},{8,10},{16,18},{24,26}} | collective-permute-start | bytes 2359304 | tf_op jit(solution)/shard_map/ppermute | solution.py:248
  40.8 28.5 %collective-permute-start.4 = (f32[768,256]{1,0:T(8,128)}, f32[768,256]{1,0:T(8,128)}, u32[]{:S(2)}, u32[]{:S(2)}) collective-permute-start(f32[768,256]{1,0:T(8,128)} %get-tuple-element.16), channel_id=1, source_target_pairs={{0,4},{8,12},{16,20},{24,28}} | collective-permute-start | bytes 2359304 | tf_op jit(solution)/shard_map/ppermute | solution.py:248
  44.2 25.2 %collective-permute-start.5 = (f32[768,256]{1,0:T(8,128)}, f32[768,256]{1,0:T(8,128)}, u32[]{:S(2)}, u32[]{:S(2)}) collective-permute-start(f32[768,256]{1,0:T(8,128)} %get-tuple-element.17), channel_id=1, source_target_pairs={{0,6},{8,14},{16,22},{24,30}} | collective-permute-start | bytes 2359304 | tf_op jit(solution)/shard_map/ppermute | solution.py:248
  49.0 68.9 %all-gather.2.cloned.1.call-start = ((), (), s32[]{:S(2)}) async-start(), calls=%async_computation.1 | async-start | bytes 3538944 | tf_op jit(solution)/shard_map/all_gather | solution.py:306
  50.1 19.2 %collective-permute-start.7 = (f32[256,256]{1,0:T(8,128)S(1)}, f32[256,256]{1,0:T(8,128)S(1)}, u32[]{:S(2)}, u32[]{:S(2)}) collective-permute-start(f32[256,256]{1,0:T(8,128)S(1)} %broadcast_select_fusion.3), channel_id=1, source_target_pairs={{0,2},{4,6}} | collective-permute-start | bytes 786440 | tf_op jit(solution)/shard_map/ppermute | solution.py:260
  71.4 10.2 %copy-start.2 = (f32[2,32,32]{2,1,0:T(8,128)S(1)}, f32[2,32,32]{2,1,0:T(8,128)}, u32[]{:S(2)}) copy-start(f32[2,32,32]{2,1,0:T(8,128)} %param.6) | copy-start | bytes 24580
  71.5 2.8 %collective-permute-start.8 = (f32[384,256]{1,0:T(8,128)S(1)}, f32[384,256]{1,0:T(8,128)}, u32[]{:S(2)}, u32[]{:S(2)}) collective-permute-start(f32[384,256]{1,0:T(8,128)S(1)} %slice.62), channel_id=1, source_target_pairs={{0,1},{2,3},{4,5},{6,7},{8,9},{10,11},{12,13},{14,15},{16,17},{18,... | collective-permute-start | bytes 1179656 | tf_op jit(solution)/shard_map/ppermute | solution.py:251
  75.1 5.2 %collective-permute-start.9 = (f32[256,256]{1,0:T(8,128)S(1)}, f32[256,256]{1,0:T(8,128)S(1)}, u32[]{:S(2)}, u32[]{:S(2)}) collective-permute-start(f32[256,256]{1,0:T(8,128)S(1)} %broadcast_select_fusion.4), channel_id=1, source_target_pairs={{0,8},{4,12},{2,10},{6,14}} | collective-permute-start | bytes 786440 | tf_op jit(solution)/shard_map/ppermute | solution.py:260
  80.3 5.2 %collective-permute-start.10 = (f32[256,256]{1,0:T(8,128)S(1)}, f32[256,256]{1,0:T(8,128)S(1)}, u32[]{:S(2)}, u32[]{:S(2)}) collective-permute-start(f32[256,256]{1,0:T(8,128)S(1)} %broadcast_select_fusion.1), channel_id=1, source_target_pairs={{0,16},{4,20},{2,18},{6,22},{8,24},{12,28},{10,26},{14,30}} | collective-permute-start | bytes 786440 | tf_op jit(solution)/shard_map/ppermute | solution.py:260
  86.4 5.2 %collective-permute-start.12 = (f32[128,1536]{1,0:T(8,128)}, f32[128,1536]{1,0:T(8,128)S(1)}, u32[]{:S(2)}, u32[]{:S(2)}) collective-permute-start(f32[128,1536]{1,0:T(8,128)} %slice.64), channel_id=1, source_target_pairs={{0,1},{1,0},{2,3},{3,2},{4,5},{5,4},{6,7},{7,6},{8,9},{9,8},{10,11... | collective-permute-start | bytes 2359304 | tf_op jit(solution)/shard_map/ppermute | solution.py:314
  86.5 5.0 %collective-permute-start.11 = (f32[384,256]{1,0:T(8,128)S(1)}, f32[384,256]{1,0:T(8,128)}, u32[]{:S(2)}, u32[]{:S(2)}) collective-permute-start(f32[384,256]{1,0:T(8,128)S(1)} %pad_maximum_fusion.6), channel_id=1, source_target_pairs={{0,1},{4,5},{2,3},{6,7},{8,9},{12,13},{10,11},{14,15},{16,17},{20,... | collective-permute-start | bytes 1179656 | tf_op jit(solution)/shard_map/ppermute | solution.py:260
  111.3 1.4 copy-start
Sparse Core Ops, SparseCore 0:
  49.2 62.1 all-reduce.1
Sparse Core Ops, SparseCore 1:
  75.2 38.6 all-gather.1

commit v19 on v18

--- a/solution.py
+++ b/solution.py
@@ -10,7 +10,7 @@
 B = 256
 P_SIZE = 32
 STRIP = 32
-PIVOTS = 4
+PIVOTS = 8
 HIGHEST = lax.Precision.HIGHEST
 
 
@@ -293,7 +293,7 @@
     for to in range(row_peers):
         far = lax.dynamic_index_in_dim(along, (chip - to) % chips, 0, keepdims=False)
         sent.append(jnp.concatenate([design, far], axis=1))
-    sent = jnp.stack(sent)
+    sent = after(jnp.stack(sent), along_z)
     leading, reached = doubled(leading, row_bits, reached)
     lead = lax.dynamic_index_in_dim(along, chip, 0, keepdims=False)[:, :B]
     lead = lax.all_gather(after(lead, sent), "row", axis=0, tiled=True)

time: 151 us -> 161 us (1.066)
  waiting for transfers between devices: 23.8 us -> 32.5 us
  starting transfers between devices: 36.5 us -> 41 us
  Pallas kernels: 47.1 us -> 43.5 us
    ppermute x5, starting transfers between devices: 8.38 us -> 17.8 us  [doubled(): got = lax.ppermute(value, ('row', 'col'), pairs)]
    ppermute x3, waiting for transfers between devices: 0.01 us -> 8.95 us  [row_strip_piece(): lax.ppermute(share, 'col', [(0, 2 * z)])]
    ppermute x3, starting transfers between devices: 14.4 us -> 9.64 us  [row_strip_piece(): lax.ppermute(share, 'col', [(0, 2 * z)])]
    pallas_call x1, Pallas kernels: 13.9 us -> 10.3 us  [corner_factor(): pl.pallas_call(corner_kernel, out_shape=jax.ShapeDtypeStruct((B, B), jnp....]
    ppermute x3, waiting for transfers between devices: 5.75 us -> 8.91 us  [body(): lax.ppermute(design, 'col', [(c, (c + 2 * s) % col_peers) for c in range(...]
    ppermute x5, waiting for transfers between devices: 16.3 us -> 13.9 us  [doubled(): got = lax.ppermute(value, ('row', 'col'), pairs)]
  transfers between devices with their start and end apart: 16 -> 16, of which waited for: 7 -> 8; matrix products, arithmetic and copies ran while one was open for 10% -> 9% of each run, Pallas kernels for 16% -> 13%
where the time goes in v19:
time: 161 us; the launch traced here: 159 us
  Pallas kernels  43.5 us (27%)
  starting transfers between devices  41 us (25%)
  waiting for transfers between devices  32.5 us (20%)
  between operations  15.2 us (9%)
  blocking collectives  9.59 us (6%)
  other arithmetic  9.39 us (6%)
  local copies, waits for them, and re-layouts  8.06 us (5%)
    pallas_call x1, Pallas kernels, tile_rows(): pl.pallas_call(tile_kernel, grid_spec=pltpu.PrefetchScalarGridSpec(num_sc...  23.2 us
    ppermute x5, starting transfers between devices, doubled(): got = lax.ppermute(value, ('row', 'col'), pairs)  17.8 us
    ppermute x5, waiting for transfers between devices, doubled(): got = lax.ppermute(value, ('row', 'col'), pairs)  13.9 us
    pallas_call x1, Pallas kernels, corner_factor(): pl.pallas_call(corner_kernel, out_shape=jax.ShapeDtypeStruct((B, B), jnp....  10.3 us
    ppermute x3, starting transfers between devices, row_strip_piece(): lax.ppermute(share, 'col', [(0, 2 * z)])  9.64 us
    all_gather x1, blocking collectives, body(): lead = lax.all_gather(after(lead, sent), 'row', axis=0, tiled=True)  9.59 us
    ppermute x3, waiting for transfers between devices, row_strip_piece(): lax.ppermute(share, 'col', [(0, 2 * z)])  8.95 us
    ppermute x3, waiting for transfers between devices, body(): lax.ppermute(design, 'col', [(c, (c + 2 * s) % col_peers) for c in range(...  8.91 us
  transfers between devices with their start and end apart: 16, of which 8 were waited for; matrix products, arithmetic and copies ran while one was open for 9% of the time, Pallas kernels for 13%

profile of v19, /device:TPU:0, one launch (start us, length us, event | category | flops | bytes accessed | tf_op | source)
XLA Modules:
  0.0 159.3 jit_solution(13726713662924688755)
XLA Ops:
  7.4 4.0 %collective-permute-start.1 = (f32[32,1536]{1,0:T(8,128)}, f32[32,1536]{1,0:T(8,128)S(1)}, u32[]{:S(2)}, u32[]{:S(2)}) collective-permute-start(f32[32,1536]{1,0:T(8,128)} %param.5), channel_id=1, source_target_pairs={{0,4},{1,5},{2,6},{3,7},{4,0},{5,1},{6,2},{7,3},{8,12},{9,13},{10,... | collective-permute-start | bytes 589832 | tf_op jit(solution)/shard_map/ppermute | solution.py:289
  11.4 1.6 collective-permute-start
  13.0 2.2 %collective-permute-start.2 = (f32[32,1536]{1,0:T(8,128)}, f32[32,1536]{1,0:T(8,128)S(1)}, u32[]{:S(2)}, u32[]{:S(2)}) collective-permute-start(f32[32,1536]{1,0:T(8,128)} %param.5), channel_id=1, source_target_pairs={{0,6},{1,7},{2,0},{3,1},{4,2},{5,3},{6,4},{7,5},{8,14},{9,15},{10,... | collective-permute-start | bytes 589832 | tf_op jit(solution)/shard_map/ppermute | solution.py:289
  17.6 8.2 %collective-permute-done.1 = f32[32,1536]{1,0:T(8,128)S(1)} collective-permute-done((f32[32,1536]{1,0:T(8,128)}, f32[32,1536]{1,0:T(8,128)S(1)}, u32[]{:S(2)}, u32[]{:S(2)}) %collective-permute-start.1) | collective-permute-done | bytes 196640 | tf_op jit(solution)/shard_map/ppermute | solution.py:289
  28.9 8.2 %collective-permute-start.7 = (f32[256,256]{1,0:T(8,128)S(1)}, f32[256,256]{1,0:T(8,128)S(1)}, u32[]{:S(2)}, u32[]{:S(2)}) collective-permute-start(f32[256,256]{1,0:T(8,128)S(1)} %broadcast_select_fusion.3), channel_id=1, source_target_pairs={{0,2},{4,6}} | collective-permute-start | bytes 786440 | tf_op jit(solution)/shard_map/ppermute | solution.py:260
  38.3 2.6 %collective-permute-done.7 = f32[256,256]{1,0:T(8,128)S(1)} collective-permute-done((f32[256,256]{1,0:T(8,128)S(1)}, f32[256,256]{1,0:T(8,128)S(1)}, u32[]{:S(2)}, u32[]{:S(2)}) %collective-permute-start.7) | collective-permute-done | bytes 262176 | tf_op jit(solution)/shard_map/ppermute | solution.py:260
  40.9 3.6 %all-to-all-start = ((f32[4,32,3072]{2,1,0:T(8,128)}), f32[4,32,3072]{2,1,0:T(8,128)S(1)}, u32[]{:S(2)}, u32[]{:S(2)}) async-start(f32[4,32,3072]{2,1,0:T(8,128)} %pad_maximum_fusion), calls=%async_computation | async-start | bytes 3145728 | tf_op jit(solution)/shard_map/all_to_all | solution.py:302
  44.6 3.0 %fusion.6 = (f32[768,256]{1,0:T(8,128)S(1)}, f32[768,256]{1,0:T(8,128)}, f32[768,256]{1,0:T(8,128)}) fusion(f32[3072,1536]{1,0:T(8,128)} %normals_ref.1), kind=kLoop, calls=%fused_computation.31 | loop fusion | bytes 4718592 | tf_op jit(solution)/shard_map/slice | solution.py:247
  47.5 5.3 %collective-permute-start.3 = (f32[768,256]{1,0:T(8,128)}, f32[768,256]{1,0:T(8,128)}, u32[]{:S(2)}, u32[]{:S(2)}) collective-permute-start(f32[768,256]{1,0:T(8,128)} %get-tuple-element.16), channel_id=1, source_target_pairs={{0,2},{8,10},{16,18},{24,26}} | collective-permute-start | bytes 2359304 | tf_op jit(solution)/shard_map/ppermute | solution.py:248
  52.8 2.2 %collective-permute-start.4 = (f32[768,256]{1,0:T(8,128)}, f32[768,256]{1,0:T(8,128)}, u32[]{:S(2)}, u32[]{:S(2)}) collective-permute-start(f32[768,256]{1,0:T(8,128)} %get-tuple-element.17), channel_id=1, source_target_pairs={{0,4},{8,12},{16,20},{24,28}} | collective-permute-start | bytes 2359304 | tf_op jit(solution)/shard_map/ppermute | solution.py:248
  55.0 2.2 %collective-permute-start.5 = (f32[768,256]{1,0:T(8,128)S(1)}, f32[768,256]{1,0:T(8,128)}, u32[]{:S(2)}, u32[]{:S(2)}) collective-permute-start(f32[768,256]{1,0:T(8,128)S(1)} %get-tuple-element.18), channel_id=1, source_target_pairs={{0,6},{8,14},{16,22},{24,30}} | collective-permute-start | bytes 2359304 | tf_op jit(solution)/shard_map/ppermute | solution.py:248
  57.2 2.7 %slice_select_fusion = f32[256,1536]{1,0:T(8,128)} fusion(f32[3072,1536]{1,0:T(8,128)} %normals_ref.1, pred[]{:T(512)S(6)} %eq.35), kind=kLoop, calls=%fused_computation.1 | loop fusion | flops 393216 | bytes 3145729 | tf_op jit(solution)/shard_map/jit(_where)/select_n | solution.py:277
  59.9 9.6 %all_gather.6 = f32[128,256]{1,0:T(8,128)S(1)} all-gather(f32[32,256]{1,0:T(8,128)S(1)} %slice.60), channel_id=1, replica_groups=mesh['row'=4,'col'=8] {'row'}, dimensions={0}, use_global_device_ids=true | all-gather | bytes 163840 | tf_op jit(solution)/shard_map/all_gather | solution.py:299
  70.1 8.3 %collective-permute-done.5 = f32[768,256]{1,0:T(8,128)} collective-permute-done((f32[768,256]{1,0:T(8,128)S(1)}, f32[768,256]{1,0:T(8,128)}, u32[]{:S(2)}, u32[]{:S(2)}) %collective-permute-start.5) | collective-permute-done | bytes 786464 | tf_op jit(solution)/shard_map/ppermute | solution.py:248
  78.5 2.0 %add_select_fusion = f32[768,256]{1,0:T(8,128)S(1)} fusion(f32[768,256]{1,0:T(8,128)} %collective-permute-done.5, f32[768,256]{1,0:T(8,128)} %collective-permute-done.3, f32[768,256]{1,0:T(8,128)} %collective-permute-done.4, f32[3072,1536]{1,0:T(8,128)} %normals_ref.1, pred[]{:T(512)S(6)} %eq.32), kind=kLoop, calls=%fused_computation.3 | loop fusion | flops 589824 | bytes 3932161 | tf_op jit(solution)/shard_map/jit(_where)/select_n | solution.py:250
  80.6 2.0 %collective-permute-start.8 = (f32[384,256]{1,0:T(8,128)S(1)}, f32[384,256]{1,0:T(8,128)}, u32[]{:S(2)}, u32[]{:S(2)}) collective-permute-start(f32[384,256]{1,0:T(8,128)S(1)} %slice.62), channel_id=1, source_target_pairs={{0,1},{2,3},{4,5},{6,7},{8,9},{10,11},{12,13},{14,15},{16,17},{18,... | collective-permute-start | bytes 1179656 | tf_op jit(solution)/shard_map/ppermute | solution.py:251
  84.2 3.9 %collective-permute-start.9 = (f32[256,256]{1,0:T(8,128)S(1)}, f32[256,256]{1,0:T(8,128)S(1)}, u32[]{:S(2)}, u32[]{:S(2)}) collective-permute-start(f32[256,256]{1,0:T(8,128)S(1)} %broadcast_select_fusion.4), channel_id=1, source_target_pairs={{0,8},{4,12},{2,10},{6,14}} | collective-permute-start | bytes 786440 | tf_op jit(solution)/shard_map/ppermute | solution.py:260
  88.1 3.9 %collective-permute-done.9 = f32[256,256]{1,0:T(8,128)S(1)} collective-permute-done((f32[256,256]{1,0:T(8,128)S(1)}, f32[256,256]{1,0:T(8,128)S(1)}, u32[]{:S(2)}, u32[]{:S(2)}) %collective-permute-start.9) | collective-permute-done | bytes 262176 | tf_op jit(solution)/shard_map/ppermute | solution.py:260
  93.3 7.4 %collective-permute-done.10 = f32[256,256]{1,0:T(8,128)S(1)} collective-permute-done((f32[256,256]{1,0:T(8,128)S(1)}, f32[256,256]{1,0:T(8,128)S(1)}, u32[]{:S(2)}, u32[]{:S(2)}) %collective-permute-start.10) | collective-permute-done | bytes 262176 | tf_op jit(solution)/shard_map/ppermute | solution.py:260
  101.7 3.2 %collective-permute-start.11 = (f32[384,256]{1,0:T(8,128)S(1)}, f32[384,256]{1,0:T(8,128)}, u32[]{:S(2)}, u32[]{:S(2)}) collective-permute-start(f32[384,256]{1,0:T(8,128)S(1)} %pad_maximum_fusion.6), channel_id=1, source_target_pairs={{0,1},{4,5},{2,3},{6,7},{8,9},{12,13},{10,11},{14,15},{16,17},{20,... | collective-permute-start | bytes 1179656 | tf_op jit(solution)/shard_map/ppermute | solution.py:260
  106.9 4.9 %row_side.1 = (bf16[3072,384]{1,0:T(8,128)(2,1)}, f32[3072,256]{1,0:T(8,128)}) custom-call(s32[2]{0:T(128)S(1)} %pad_add_fusion.place_ref, f32[128,3072]{1,0:T(8,128)S(1)} %bitcast.31, f32[128,256]{1,0:T(8,128)S(1)} %slice.63.lead_ref.design_ref, f32[128,1536]{1,0:T(8,128)S(1)} %collective-permute-done.12.other_ref, f32[128,128]{1,0:T(8,128)S(1)} %select_n.143.filter_ref, ...), custom_call_target="tpu_custom_call" | custom-call | tf_op jit(solution)/shard_map/row_side/pallas_call | solution.py:162
  111.8 10.3 %corner_factor.1.inverse_ref = f32[256,256]{1,0:T(8,128)S(1)} custom-call(f32[256,256]{1,0:T(8,128)S(1)} %slice.65.block_ref, f32[128,256]{1,0:T(8,128)S(1)} %slice.63.lead_ref.design_ref, f32[128,128]{1,0:T(8,128)S(1)} %select_n.143.filter_ref, f32[1,256]{1,0:T(1,128)S(1)} %bitcast.34), custom_call_target="tpu_custom_call" | custom-call | tf_op jit(solution)/shard_map/corner_factor/pallas_call | solution.py:82
  123.5 5.1 %column_side.1.right_ref = bf16[1152,1536]{1,0:T(8,128)(2,1)} custom-call(s32[2]{0:T(128)S(1)} %pad_add_fusion.place_ref, f32[128,3072]{1,0:T(8,128)S(1)} %bitcast.32, f32[128,256]{1,0:T(8,128)S(1)} %slice.63.lead_ref.design_ref, f32[256,1536]{1,0:T(8,128)S(1)} %copy-done, f32[256,256]{1,0:T(8,128)S(1)} %corner_factor.1.inverse_ref, ...), custom_call_target="tpu_custom_call" | custom-call | tf_op jit(solution)/shard_map/column_side/pallas_call | solution.py:127
  128.6 23.2 %tile_rows.1 = f32[3072,1536]{1,0:T(8,128)} custom-call(s32[2]{0:T(128)S(1)} %pad_add_fusion.place_ref, f32[3072,1536]{1,0:T(8,128)} %normals_ref.1, f32[3072,256]{1,0:T(8,128)} %all-gather.2.cloned.1.call-done.strip_ref, f32[3072,256]{1,0:T(8,128)} %get-tuple-element.24.gram_ref, bf16[3072,384]{1,0:T(8,128)(2,1)} %get-tuple-element.25.left_ref, ...), custom_call_target="tpu_custom_call" | custom-call | tf_op jit(solution)/shard_map/tile_rows/pallas_call | solution.py:213
  (49 shorter events, 14.6 us)
Async XLA Ops:
  7.4 18.4 %collective-permute-start.1 = (f32[32,1536]{1,0:T(8,128)}, f32[32,1536]{1,0:T(8,128)S(1)}, u32[]{:S(2)}, u32[]{:S(2)}) collective-permute-start(f32[32,1536]{1,0:T(8,128)} %param.5), channel_id=1, source_target_pairs={{0,4},{1,5},{2,6},{3,7},{4,0},{5,1},{6,2},{7,3},{8,12},{9,13},{10,... | collective-permute-start | bytes 589832 | tf_op jit(solution)/shard_map/ppermute | solution.py:289
  11.4 14.4 %collective-permute-start = (f32[32,1536]{1,0:T(8,128)}, f32[32,1536]{1,0:T(8,128)S(1)}, u32[]{:S(2)}, u32[]{:S(2)}) collective-permute-start(f32[32,1536]{1,0:T(8,128)} %param.5), channel_id=1, source_target_pairs={{0,2},{1,3},{2,4},{3,5},{4,6},{5,7},{6,0},{7,1},{8,10},{9,11},{10,... | collective-permute-start | bytes 589832 | tf_op jit(solution)/shard_map/ppermute | solution.py:289
  13.0 13.6 %collective-permute-start.2 = (f32[32,1536]{1,0:T(8,128)}, f32[32,1536]{1,0:T(8,128)S(1)}, u32[]{:S(2)}, u32[]{:S(2)}) collective-permute-start(f32[32,1536]{1,0:T(8,128)} %param.5), channel_id=1, source_target_pairs={{0,6},{1,7},{2,0},{3,1},{4,2},{5,3},{6,4},{7,5},{8,14},{9,15},{10,... | collective-permute-start | bytes 589832 | tf_op jit(solution)/shard_map/ppermute | solution.py:289
  16.2 11.7 %collective-permute-start.6 = (f32[256,256]{1,0:T(8,128)S(1)}, f32[256,256]{1,0:T(8,128)S(1)}, u32[]{:S(2)}, u32[]{:S(2)}) collective-permute-start(f32[256,256]{1,0:T(8,128)S(1)} %slice.49), channel_id=1, source_target_pairs={{0,4}} | collective-permute-start | bytes 786440 | tf_op jit(solution)/shard_map/ppermute | solution.py:260
  26.5 1.1 copy-start.1
  28.9 12.0 %collective-permute-start.7 = (f32[256,256]{1,0:T(8,128)S(1)}, f32[256,256]{1,0:T(8,128)S(1)}, u32[]{:S(2)}, u32[]{:S(2)}) collective-permute-start(f32[256,256]{1,0:T(8,128)S(1)} %broadcast_select_fusion.3), channel_id=1, source_target_pairs={{0,2},{4,6}} | collective-permute-start | bytes 786440 | tf_op jit(solution)/shard_map/ppermute | solution.py:260
  40.9 37.5 %all-to-all-start = ((f32[4,32,3072]{2,1,0:T(8,128)}), f32[4,32,3072]{2,1,0:T(8,128)S(1)}, u32[]{:S(2)}, u32[]{:S(2)}) async-start(f32[4,32,3072]{2,1,0:T(8,128)} %pad_maximum_fusion), calls=%async_computation | async-start | bytes 3145728 | tf_op jit(solution)/shard_map/all_to_all | solution.py:302
  44.5 77.6 %all-reduce.2.cloned.1.call-start = ((), (), s32[]{:S(2)}) async-start(), calls=%async_computation.2 | async-start | bytes 3145728 | tf_op jit(solution)/shard_map/psum | solution.py:277
  47.5 22.0 %collective-permute-start.3 = (f32[768,256]{1,0:T(8,128)}, f32[768,256]{1,0:T(8,128)}, u32[]{:S(2)}, u32[]{:S(2)}) collective-permute-start(f32[768,256]{1,0:T(8,128)} %get-tuple-element.16), channel_id=1, source_target_pairs={{0,2},{8,10},{16,18},{24,26}} | collective-permute-start | bytes 2359304 | tf_op jit(solution)/shard_map/ppermute | solution.py:248
  52.8 17.3 %collective-permute-start.4 = (f32[768,256]{1,0:T(8,128)}, f32[768,256]{1,0:T(8,128)}, u32[]{:S(2)}, u32[]{:S(2)}) collective-permute-start(f32[768,256]{1,0:T(8,128)} %get-tuple-element.17), channel_id=1, source_target_pairs={{0,4},{8,12},{16,20},{24,28}} | collective-permute-start | bytes 2359304 | tf_op jit(solution)/shard_map/ppermute | solution.py:248
  55.0 23.5 %collective-permute-start.5 = (f32[768,256]{1,0:T(8,128)S(1)}, f32[768,256]{1,0:T(8,128)}, u32[]{:S(2)}, u32[]{:S(2)}) collective-permute-start(f32[768,256]{1,0:T(8,128)S(1)} %get-tuple-element.18), channel_id=1, source_target_pairs={{0,6},{8,14},{16,22},{24,30}} | collective-permute-start | bytes 2359304 | tf_op jit(solution)/shard_map/ppermute | solution.py:248
  59.9 68.8 %all-gather.2.cloned.1.call-start = ((), (), s32[]{:S(2)}) async-start(), calls=%async_computation.1 | async-start | bytes 3538944 | tf_op jit(solution)/shard_map/all_gather | solution.py:306
  80.5 12.7 %copy-start.2 = (f32[2,32,32]{2,1,0:T(8,128)S(1)}, f32[2,32,32]{2,1,0:T(8,128)}, u32[]{:S(2)}) copy-start(f32[2,32,32]{2,1,0:T(8,128)} %param.6) | copy-start | bytes 24580
  80.6 2.8 %collective-permute-start.8 = (f32[384,256]{1,0:T(8,128)S(1)}, f32[384,256]{1,0:T(8,128)}, u32[]{:S(2)}, u32[]{:S(2)}) collective-permute-start(f32[384,256]{1,0:T(8,128)S(1)} %slice.62), channel_id=1, source_target_pairs={{0,1},{2,3},{4,5},{6,7},{8,9},{10,11},{12,13},{14,15},{16,17},{18,... | collective-permute-start | bytes 1179656 | tf_op jit(solution)/shard_map/ppermute | solution.py:251
  84.2 7.7 %collective-permute-start.9 = (f32[256,256]{1,0:T(8,128)S(1)}, f32[256,256]{1,0:T(8,128)S(1)}, u32[]{:S(2)}, u32[]{:S(2)}) collective-permute-start(f32[256,256]{1,0:T(8,128)S(1)} %broadcast_select_fusion.4), channel_id=1, source_target_pairs={{0,8},{4,12},{2,10},{6,14}} | collective-permute-start | bytes 786440 | tf_op jit(solution)/shard_map/ppermute | solution.py:260
  91.9 8.8 %collective-permute-start.10 = (f32[256,256]{1,0:T(8,128)S(1)}, f32[256,256]{1,0:T(8,128)S(1)}, u32[]{:S(2)}, u32[]{:S(2)}) collective-permute-start(f32[256,256]{1,0:T(8,128)S(1)} %broadcast_select_fusion.1), channel_id=1, source_target_pairs={{0,16},{4,20},{2,18},{6,22},{8,24},{12,28},{10,26},{14,30}} | collective-permute-start | bytes 786440 | tf_op jit(solution)/shard_map/ppermute | solution.py:260
  101.7 5.2 %collective-permute-start.12 = (f32[128,1536]{1,0:T(8,128)}, f32[128,1536]{1,0:T(8,128)S(1)}, u32[]{:S(2)}, u32[]{:S(2)}) collective-permute-start(f32[128,1536]{1,0:T(8,128)} %slice.64), channel_id=1, source_target_pairs={{0,1},{1,0},{2,3},{3,2},{4,5},{5,4},{6,7},{7,6},{8,9},{9,8},{10,11... | collective-permute-start | bytes 2359304 | tf_op jit(solution)/shard_map/ppermute | solution.py:314
  101.7 5.0 %collective-permute-start.11 = (f32[384,256]{1,0:T(8,128)S(1)}, f32[384,256]{1,0:T(8,128)}, u32[]{:S(2)}, u32[]{:S(2)}) collective-permute-start(f32[384,256]{1,0:T(8,128)S(1)} %pad_maximum_fusion.6), channel_id=1, source_target_pairs={{0,1},{4,5},{2,3},{6,7},{8,9},{12,13},{10,11},{14,15},{16,17},{20,... | collective-permute-start | bytes 1179656 | tf_op jit(solution)/shard_map/ppermute | solution.py:260
  122.1 1.4 copy-start
Sparse Core Ops, SparseCore 0:
  60.0 61.4 all-reduce.1
Sparse Core Ops, SparseCore 1:
  84.3 41.7 all-gather.1
